TPU v7x, 128 devices: a whole 4x4x4 slice. The times are simulated.
128 devices in a mesh: dp: 16 (over x, z), seq: 8 (over y, core).
Axes of the slice: x: 4, y: 4, z: 4, core: 2. Of those that a mesh axis runs over, the one named last changes fastest.
Arguments:
- tokens: bfloat16 [16384, 7168], P(('dp', 'seq')), may hold values from -6 to 6
- cotangent: bfloat16 [16384, 7168], P(('dp', 'seq')), may hold values from -0.29882812 to 0.29882812
- chosen_expert_index: int32 [16384, 1], P(('dp', 'seq')), may hold values from 0 to 15; in each aligned block of 128 rows (0 to 127, 128 to 255, ...) at most 10 rows name the same one
- router_weight: float32 [16384, 1], P(('dp', 'seq')), may hold values from 0.2 to 1
- frozen_gate_weight: bfloat16 [16, 7168, 2048], P('dp', None, 'seq'), may hold values from -0.0625 to 0.0625
- frozen_up_weight: bfloat16 [16, 7168, 2048], P('dp', None, 'seq'), may hold values from -0.0625 to 0.0625
- frozen_down_weight: bfloat16 [16, 2048, 7168], P('dp', 'seq'), may hold values from -0.125 to 0.125
- gate_adapter_first: bfloat16 [16, 16, 7168], P('dp'), may hold values from -0.0625 to 0.0625
- gate_adapter_second: bfloat16 [16, 16, 2048], P('dp', None, 'seq'), may hold values from -1.5 to 1.5
- down_adapter_first: bfloat16 [16, 16, 2048], P('dp', None, 'seq'), may hold values from -0.125 to 0.125
- down_adapter_second: bfloat16 [16, 16, 7168], P('dp'), may hold values from -1.5 to 1.5
Outputs:
- grad_gate_a: float32 [16, 16, 7168], P('dp', None, 'seq')
- grad_gate_b: float32 [16, 16, 2048], P('dp', None, 'seq')
- grad_down_a: float32 [16, 16, 2048], P('dp', None, 'seq')
- grad_down_b: float32 [16, 16, 7168], P('dp', None, 'seq')
Inputs may be any that keep to these rules, and one draw needn't show every extreme that they name: `chosen_expert_index`: among the entries of the rows of one device (tokens b * 128 to (b + 1) * 128 - 1) no expert is named more than 10 times, and in some device's rows one expert is named exactly 10 times.
All inputs are finite; a program needn't handle non-finite values.
Results may differ from a plain program's by a relative error of at most 0.007.
Values may be sent and summed in bfloat16 or wider, within the bound.
No kernel may reach another device: no remote copies, remote signals or barrier semaphores. Data moves between devices by JAX's collectives and lax.ppermute only.
A program may use at most 256 MiB of HBM per device.

v0:
```python
import jax
import jax.numpy as jnp
from jax import lax
from jax.sharding import PartitionSpec as P


def contract_last(left, right):
    return lax.dot_general(
        left, right, (((1,), (1,)), ((), ())), preferred_element_type=jnp.float32
    )


def contract_first(left, right):
    return lax.dot_general(
        left, right, (((0,), (0,)), ((), ())), preferred_element_type=jnp.float32
    )


def expert_terms(rows_in, rows_back, gate_w, up_w, down_w, gate_a, gate_b, down_a, down_b):
    lowrank_in = contract_last(rows_in, gate_a).astype(jnp.bfloat16)
    gate_pre = jnp.dot(rows_in, gate_w, preferred_element_type=jnp.float32) + jnp.dot(
        lowrank_in, gate_b, preferred_element_type=jnp.float32
    )
    up_pre = jnp.dot(rows_in, up_w, preferred_element_type=jnp.float32)
    sigmoid_val = jax.nn.sigmoid(gate_pre)
    hidden = (gate_pre * sigmoid_val * up_pre).astype(jnp.bfloat16)
    lowrank_back = contract_last(rows_back, down_b).astype(jnp.bfloat16)
    hidden_grad = contract_last(rows_back, down_w) + jnp.dot(
        lowrank_back, down_a, preferred_element_type=jnp.float32
    )
    gate_grad = (
        hidden_grad * up_pre * sigmoid_val * (1.0 + gate_pre * (1.0 - sigmoid_val))
    ).astype(jnp.bfloat16)
    grad_gb = contract_first(lowrank_in, gate_grad)
    gate_back = contract_last(gate_grad, gate_b)
    grad_ga = jnp.dot(gate_back.T, rows_in, preferred_element_type=jnp.float32)
    grad_da = contract_first(lowrank_back, hidden)
    down_low = contract_last(hidden, down_a)
    grad_db = jnp.dot(down_low.T, rows_back, preferred_element_type=jnp.float32)
    return (grad_ga, grad_gb, grad_da, grad_db)


def body(
    tokens,
    cotangent,
    chosen_expert_index,
    router_weight,
    frozen_gate_weight,
    frozen_up_weight,
    frozen_down_weight,
    gate_adapter_first,
    gate_adapter_second,
    down_adapter_first,
    down_adapter_second,
):
    experts = lax.axis_size("dp")
    tok_count, top = chosen_expert_index.shape
    width = tokens.shape[1]
    capacity = 5 * tok_count * top // (4 * experts)
    flat_ids = chosen_expert_index.reshape(-1)
    onehot = (flat_ids[:, None] == jnp.arange(experts, dtype=jnp.int32)[None, :]).astype(jnp.int32)
    earlier = jnp.cumsum(onehot, axis=0) - onehot
    position = flat_ids * capacity + jnp.sum(earlier * onehot, axis=1)
    placing = (
        jnp.arange(experts * capacity, dtype=jnp.int32)[:, None] == position[None, :]
    ).astype(jnp.bfloat16)
    rows_in = tokens[:, None, :].reshape(-1, width)
    scaled = (
        (cotangent.astype(jnp.float32)[:, None, :] * router_weight[:, :, None])
        .astype(jnp.bfloat16)
        .reshape(-1, width)
    )
    incoming_buffer = (
        jnp.dot(placing, rows_in, preferred_element_type=jnp.float32)
        .astype(jnp.bfloat16)
        .reshape(experts, capacity, width)
    )
    return_buffer = (
        jnp.dot(placing, scaled, preferred_element_type=jnp.float32)
        .astype(jnp.bfloat16)
        .reshape(experts, capacity, width)
    )
    weights = (
        frozen_gate_weight[0],
        frozen_up_weight[0],
        frozen_down_weight[0],
        gate_adapter_first[0],
        gate_adapter_second[0],
        down_adapter_first[0],
        down_adapter_second[0],
    )
    groups = lax.axis_size("seq")
    wide_in = jnp.broadcast_to(
        incoming_buffer[:, None], (experts, groups, capacity, width)
    ).reshape(experts * groups, capacity, width)
    wide_back = jnp.broadcast_to(
        return_buffer[:, None], (experts, groups, capacity, width)
    ).reshape(experts * groups, capacity, width)
    received_in, received_back = (
        lax.all_to_all(wide_in, ("dp", "seq"), split_axis=0, concat_axis=0, tiled=True),
        lax.all_to_all(wide_back, ("dp", "seq"), split_axis=0, concat_axis=0, tiled=True),
    )
    terms = expert_terms(received_in.reshape(-1, width), received_back.reshape(-1, width), *weights)
    totals = tuple((new for new in terms))
    grad_ga, grad_gb, grad_da, grad_db = totals
    share_ga, share_db = (
        lax.psum_scatter(grad_ga, "seq", scatter_dimension=1, tiled=True),
        lax.psum_scatter(grad_db, "seq", scatter_dimension=1, tiled=True),
    )
    return (share_ga[None], grad_gb[None], grad_da[None], share_db[None])


def solution(mesh):
    return jax.shard_map(
        body,
        mesh=mesh,
        in_specs=(
            P(("dp", "seq"), None),
            P(("dp", "seq"), None),
            P(("dp", "seq"), None),
            P(("dp", "seq"), None),
            P("dp", None, "seq"),
            P("dp", None, "seq"),
            P("dp", "seq", None),
            P("dp", None, None),
            P("dp", None, "seq"),
            P("dp", None, "seq"),
            P("dp", None, None),
        ),
        out_specs=(
            P("dp", None, "seq"),
            P("dp", None, "seq"),
            P("dp", None, "seq"),
            P("dp", None, "seq"),
        ),
        check_vma=False,
    )
```

profile of v0, /device:TPU:1, one launch (start us, length us, event | category | flops | bytes accessed | tf_op | source)
XLA Modules:
  0.0 1119.8 jit_solution(17724396668406725511)
XLA Ops:
  7.2 0.0 copy-start
  7.2 0.9 fusion.19
  8.1 0.2 reduce_window_sum.11
  8.2 0.8 select_reduce_fusion
  9.1 0.7 multiply_add_fusion
  9.7 3.7 convolution_convert_fusion.1
  13.5 4.5 broadcast_in_dim.31
  17.9 11.0 broadcast_in_dim.32
  28.9 11.9 %all-to-all-start = ((bf16[128,10,7168]{2,1,0:T(8,128)(2,1)}), bf16[128,10,7168]{2,1,0:T(8,128)(2,1)}, u32[]{:S(2)}, u32[]{:S(2)}) async-start(bf16[128,10,7168]{2,1,0:T(8,128)(2,1)} %bitcast.57), calls=%async_computation | async-start | bytes 58720256 | tf_op jit(solution)/shard_map/all_to_all | solution.py:101
  40.8 0.0 copy-done
  40.9 2.2 convolution_convert_fusion
  43.0 4.5 broadcast_in_dim.33
  47.5 420.4 %all-to-all-done = bf16[128,10,7168]{2,1,0:T(8,128)(2,1)} async-done(((bf16[128,10,7168]{2,1,0:T(8,128)(2,1)}), bf16[128,10,7168]{2,1,0:T(8,128)(2,1)}, u32[]{:S(2)}, u32[]{:S(2)}) %all-to-all-start) | async-done | bytes 18350112 | tf_op jit(solution)/shard_map/all_to_all | solution.py:101
  467.9 11.0 broadcast_in_dim.34
  478.8 45.2 %all-to-all-start.1 = ((bf16[128,10,7168]{2,1,0:T(8,128)(2,1)}), bf16[128,10,7168]{2,1,0:T(8,128)(2,1)}, u32[]{:S(2)}, u32[]{:S(2)}) async-start(bf16[128,10,7168]{2,1,0:T(8,128)(2,1)} %bitcast.56), calls=%async_computation.1 | async-start | bytes 58720256 | tf_op jit(solution)/shard_map/all_to_all | solution.py:100
  524.0 0.0 copy-start.4
  524.0 0.2 reduce-scatter.3.cloned.1.call-start
  524.2 28.3 %reshape.42 = bf16[1280,7168]{1,0:T(8,128)(2,1)} reshape(bf16[128,10,7168]{2,1,0:T(8,128)(2,1)} %all-to-all-done) | data formatting | bytes 36700160 | tf_op jit(solution)/shard_map/reshape | solution.py:103
  552.5 0.0 copy-done.4
  552.5 0.0 copy-start.2
  552.5 11.2 convolution_convert_fusion.3
  563.7 0.3 copy-done.2
  564.0 8.3 fusion.4
  572.3 0.0 copy-start.5
  572.3 378.7 %all-to-all-done.1 = bf16[128,10,7168]{2,1,0:T(8,128)(2,1)} async-done(((bf16[128,10,7168]{2,1,0:T(8,128)(2,1)}), bf16[128,10,7168]{2,1,0:T(8,128)(2,1)}, u32[]{:S(2)}, u32[]{:S(2)}) %all-to-all-start.1) | async-done | bytes 18350112 | tf_op jit(solution)/shard_map/all_to_all | solution.py:100
  951.0 28.3 %reshape.44 = bf16[1280,7168]{1,0:T(8,128)(2,1)} reshape(bf16[128,10,7168]{2,1,0:T(8,128)(2,1)} %all-to-all-done.1) | data formatting | bytes 36700160 | tf_op jit(solution)/shard_map/reshape | solution.py:103
  979.3 0.0 copy-done.5
  979.3 0.0 copy-start.3
  979.3 0.0 copy-start.8
  979.3 11.2 convolution_convert_fusion.2
  990.5 0.2 copy-done.3
  990.8 1.0 copy-done.8
  991.8 0.0 copy-start.6
  991.8 5.0 fusion
  996.9 0.0 copy-done.6
  996.9 0.4 convolution_add_fusion
  997.2 0.0 copy-start.7
  997.3 0.0 copy-start.9
  997.3 7.6 multiply_convert_fusion.2
  1004.9 0.0 copy-done.7
  1004.9 0.0 copy-done.9
  1004.9 0.6 fusion.9
  1005.6 9.9 fusion.14
  1015.5 0.0 reduce-scatter.3.cloned.1.call-update
  1015.5 0.0 reduce-scatter.5.cloned.1.call-start
  1015.5 0.0 copy-start.1
  1015.5 10.0 fusion.11
  1025.6 0.0 reduce-scatter.5.cloned.1.call-update
  1025.6 0.8 convolution_bitcast_fusion.1
  1026.4 0.8 convolution_bitcast_fusion
  1027.2 53.0 %reduce-scatter.3.cloned.1.call-done = f32[16,896]{1,0:T(8,128)} async-done(((f32[16,7168]{1,0:T(8,128)}), f32[16,896]{1,0:T(8,128)}) %reduce-scatter.3.cloned.1.call-update) | async-done | bytes 57360 | tf_op jit(solution)/shard_map/reduce_scatter | solution.py:107
  1080.2 32.7 %reduce-scatter.5.cloned.1.call-done = f32[16,896]{1,0:T(8,128)} async-done(((f32[16,7168]{1,0:T(8,128)}), f32[16,896]{1,0:T(8,128)}) %reduce-scatter.5.cloned.1.call-update) | async-done | bytes 57360 | tf_op jit(solution)/shard_map/reduce_scatter | solution.py:108
  1113.0 0.0 copy-done.1
Async XLA Ops:
  7.2 33.7 %copy-start = (bf16[128,7168]{1,0:T(8,128)(2,1)S(1)}, bf16[128,7168]{1,0:T(8,128)(2,1)}, u32[]{:S(2)}) copy-start(bf16[128,7168]{1,0:T(8,128)(2,1)} %param.11) | copy-start | bytes 5505028
  28.9 438.9 %all-to-all-start = ((bf16[128,10,7168]{2,1,0:T(8,128)(2,1)}), bf16[128,10,7168]{2,1,0:T(8,128)(2,1)}, u32[]{:S(2)}, u32[]{:S(2)}) async-start(bf16[128,10,7168]{2,1,0:T(8,128)(2,1)} %bitcast.57), calls=%async_computation | async-start | bytes 58720256 | tf_op jit(solution)/shard_map/all_to_all | solution.py:101
  478.8 472.2 %all-to-all-start.1 = ((bf16[128,10,7168]{2,1,0:T(8,128)(2,1)}), bf16[128,10,7168]{2,1,0:T(8,128)(2,1)}, u32[]{:S(2)}, u32[]{:S(2)}) async-start(bf16[128,10,7168]{2,1,0:T(8,128)(2,1)} %bitcast.56), calls=%async_computation.1 | async-start | bytes 58720256 | tf_op jit(solution)/shard_map/all_to_all | solution.py:100
  524.0 28.5 %copy-start.4 = (bf16[1,16,7168]{2,1,0:T(8,128)(2,1)S(1)}, bf16[1,16,7168]{2,1,0:T(8,128)(2,1)}, u32[]{:S(2)}) copy-start(bf16[1,16,7168]{2,1,0:T(8,128)(2,1)} %param.21) | copy-start | bytes 688132
  524.0 556.2 %reduce-scatter.3.cloned.1.call-start = ((), (), s32[]{:S(2)}) async-start(), calls=%async_computation.4 | async-start | bytes 516096 | tf_op jit(solution)/shard_map/reduce_scatter | solution.py:107
  552.5 11.4 %copy-start.2 = (bf16[1280,7168]{1,0:T(8,128)(2,1)S(1)}, bf16[1280,7168]{1,0:T(8,128)(2,1)}, u32[]{:S(2)}) copy-start(bf16[1280,7168]{1,0:T(8,128)(2,1)} %reshape.42) | copy-start | bytes 55050244
  572.3 407.0 %copy-start.5 = (bf16[1,16,7168]{2,1,0:T(8,128)(2,1)S(1)}, bf16[1,16,7168]{2,1,0:T(8,128)(2,1)}, u32[]{:S(2)}) copy-start(bf16[1,16,7168]{2,1,0:T(8,128)(2,1)} %param.18) | copy-start | bytes 688132
  979.3 11.4 %copy-start.3 = (bf16[1280,7168]{1,0:T(8,128)(2,1)S(1)}, bf16[1280,7168]{1,0:T(8,128)(2,1)}, u32[]{:S(2)}) copy-start(bf16[1280,7168]{1,0:T(8,128)(2,1)} %reshape.44) | copy-start | bytes 55050244
  979.3 12.5 %copy-start.8 = (bf16[1,7168,256]{2,1,0:T(8,128)(2,1)S(1)}, bf16[1,7168,256]{2,1,0:T(8,128)(2,1)}, u32[]{:S(2)}) copy-start(bf16[1,7168,256]{2,1,0:T(8,128)(2,1)} %param.15) | copy-start | bytes 11010052
  991.8 5.0 copy-start.6
  997.2 7.6 copy-start.7
  997.3 7.6 copy-start.9
  1015.5 97.5 %reduce-scatter.5.cloned.1.call-start = ((), (), s32[]{:S(2)}) async-start(), calls=%async_computation.5 | async-start | bytes 516096 | tf_op jit(solution)/shard_map/reduce_scatter | solution.py:108
  1015.5 97.4 %copy-start.1 = (bf16[128,7168]{1,0:T(8,128)(2,1)S(1)}, bf16[128,7168]{1,0:T(8,128)(2,1)}, u32[]{:S(2)}) copy-start(bf16[128,7168]{1,0:T(8,128)(2,1)} %param.11) | copy-start | bytes 5505028
Sparse Core Ops, SparseCore 0:
  1015.6 64.5 reduce-scatter.2
  1083.3 29.6 reduce-scatter.4
where the time goes:
time: 1120 us
  waiting for transfers between devices  885 us (79%)
  local copies, waits for them, and re-layouts  89.1 us (8%)
  matrix products  71.9 us (6%)
  starting transfers between devices  57.3 us (5%)
  between operations  14.2 us (1%)
    all_to_all x1, waiting for transfers between devices, body(): lax.all_to_all(wide_back, ('dp', 'seq'), split_axis=0, concat_axis=0, til...  420 us
    all_to_all x1, waiting for transfers between devices, body(): lax.all_to_all(wide_in, ('dp', 'seq'), split_axis=0, concat_axis=0, tiled...  379 us
    reduce_scatter x1, waiting for transfers between devices, body(): lax.psum_scatter(grad_ga, 'seq', scatter_dimension=1, tiled=True)  53 us
    all_to_all x1, starting transfers between devices, body(): lax.all_to_all(wide_in, ('dp', 'seq'), split_axis=0, concat_axis=0, tiled...  45.2 us
    reduce_scatter x1, waiting for transfers between devices, body(): lax.psum_scatter(grad_db, 'seq', scatter_dimension=1, tiled=True)  32.7 us
    dot_general x3, matrix products, contract_last(): lax.dot_general(left, right, (((1,), (1,)), ((), ())), preferred_element_...  30.7 us
    reshape x1, local copies, waits for them, and re-layouts, body(): received_in.reshape(-1, width)  28.3 us
    reshape x1, local copies, waits for them, and re-layouts, body(): received_back.reshape(-1, width)  28.3 us
  transfers between devices with their start and end apart: 4, of which 4 were waited for; matrix products, arithmetic and copies ran while one was open for 6% of the time, Pallas kernels for 0%

commit v1 on v0

v1 whole, which is shorter than its diff:
```python
import jax
import jax.numpy as jnp
from jax import lax
from jax.sharding import PartitionSpec as P

PIECES = 4


def contract_last(left, right):
    return lax.dot_general(
        left, right, (((1,), (1,)), ((), ())), preferred_element_type=jnp.float32
    )


def contract_first(left, right):
    return lax.dot_general(
        left, right, (((0,), (0,)), ((), ())), preferred_element_type=jnp.float32
    )


def shift_y(value, step):
    size = lax.axis_size("seq")
    planes = size // 2
    pairs = [
        (y * 2 + c, ((y + step) % planes) * 2 + c) for y in range(planes) for c in range(2)
    ]
    return lax.ppermute(value, "seq", pairs)


def swap_core(value):
    size = lax.axis_size("seq")
    return lax.ppermute(value, "seq", [(i, i ^ 1) for i in range(size)])


def gather_y(rows):
    half = rows.shape[0] // 2
    before, after = shift_y(rows, 1), shift_y(rows, -1)
    far_a, far_b = shift_y(before[:half], 1), shift_y(after[half:], -1)
    return jnp.concatenate([rows, before, after, far_a, far_b], axis=0)


def body(
    tokens,
    cotangent,
    chosen_expert_index,
    router_weight,
    frozen_gate_weight,
    frozen_up_weight,
    frozen_down_weight,
    gate_adapter_first,
    gate_adapter_second,
    down_adapter_first,
    down_adapter_second,
):
    experts = lax.axis_size("dp")
    tok_count, top = chosen_expert_index.shape
    width = tokens.shape[1]
    part = width // PIECES
    capacity = 5 * tok_count * top // (4 * experts)
    slots = experts * capacity
    gate_w, up_w, down_w = frozen_gate_weight[0], frozen_up_weight[0], frozen_down_weight[0]
    gate_a, gate_b = gate_adapter_first[0], gate_adapter_second[0]
    down_a, down_b = down_adapter_first[0], down_adapter_second[0]
    weights = (
        (gate_w, up_w, down_w, gate_b, down_a),
        tuple(swap_core(w) for w in (gate_w, up_w, down_w, gate_b, down_a)),
    )

    flat_ids = chosen_expert_index.reshape(-1)
    onehot = (flat_ids[:, None] == jnp.arange(experts, dtype=jnp.int32)[None, :]).astype(jnp.int32)
    earlier = jnp.cumsum(onehot, axis=0) - onehot
    slot = jnp.sum(earlier * onehot, axis=1)
    at_row = jnp.arange(experts * PIECES * capacity, dtype=jnp.int32)
    row_expert = at_row // (PIECES * capacity)
    row_piece = at_row // capacity % PIECES
    row_slot = at_row % capacity
    hit = (row_expert[:, None] == flat_ids[None, :]) & (row_slot[:, None] == slot[None, :])
    placing = jnp.concatenate(
        [(hit & (row_piece == q)[:, None]).astype(jnp.bfloat16) for q in range(PIECES)], axis=1
    )
    at_slot = jnp.arange(slots, dtype=jnp.int32)
    home = (at_slot // capacity) * PIECES * capacity + at_slot % capacity
    taking = [
        ((home + q * capacity)[:, None] == at_row[None, :]).astype(jnp.bfloat16)
        for q in range(PIECES)
    ]

    def route(rows):
        stacked = jnp.concatenate([rows[:, q * part : (q + 1) * part] for q in range(PIECES)], axis=0)
        packed = jnp.dot(placing, stacked, preferred_element_type=jnp.float32).astype(jnp.bfloat16)
        packed = packed.reshape(experts, PIECES * capacity, part)
        got = lax.all_to_all(packed, "dp", split_axis=0, concat_axis=0, tiled=True)
        got = got.reshape(experts * PIECES * capacity, part)
        return jnp.concatenate(
            [
                jnp.dot(take, got, preferred_element_type=jnp.float32).astype(jnp.bfloat16)
                for take in taking
            ],
            axis=1,
        )

    rows_in = gather_y(route(tokens))
    scaled = (cotangent.astype(jnp.float32) * router_weight).astype(jnp.bfloat16)
    rows_back = gather_y(route(scaled))

    lowrank_in = contract_last(rows_in, gate_a).astype(jnp.bfloat16)
    lowrank_back = contract_last(rows_back, down_b).astype(jnp.bfloat16)
    sums, grads = 0.0, []
    for gw, uw, dw, gb, da in weights:
        gate_pre = jnp.dot(rows_in, gw, preferred_element_type=jnp.float32) + jnp.dot(
            lowrank_in, gb, preferred_element_type=jnp.float32
        )
        up_pre = jnp.dot(rows_in, uw, preferred_element_type=jnp.float32)
        sigmoid_val = jax.nn.sigmoid(gate_pre)
        hidden = (gate_pre * sigmoid_val * up_pre).astype(jnp.bfloat16)
        hidden_grad = contract_last(rows_back, dw) + jnp.dot(
            lowrank_back, da, preferred_element_type=jnp.float32
        )
        gate_grad = (
            hidden_grad * up_pre * sigmoid_val * (1.0 + gate_pre * (1.0 - sigmoid_val))
        ).astype(jnp.bfloat16)
        grads.append(
            jnp.stack([contract_first(lowrank_in, gate_grad), contract_first(lowrank_back, hidden)])
        )
        sums = sums + jnp.concatenate([contract_last(gb, gate_grad), contract_last(da, hidden)], axis=0)
    grad_hidden = grads[0] + swap_core(grads[1])

    def in_order(value, order):
        return jnp.concatenate([value[:, i * slots : (i + 1) * slots] for i in order], axis=1)

    sums = (
        sums
        + in_order(shift_y(sums, 1), (2, 0, 3, 1))
        + in_order(shift_y(sums, -1), (1, 3, 0, 2))
        + in_order(shift_y(sums, 2), (3, 2, 1, 0))
    )
    me = lax.axis_index("seq")
    share = width // lax.axis_size("seq")
    rank = gate_a.shape[0]

    def product(first):
        cols_in = lax.dynamic_slice_in_dim(rows_in, first, share, axis=1)
        cols_back = lax.dynamic_slice_in_dim(rows_back, first, share, axis=1)
        return jnp.stack(
            [
                jnp.dot(sums[:rank], cols_in, preferred_element_type=jnp.float32),
                jnp.dot(sums[rank:], cols_back, preferred_element_type=jnp.float32),
            ]
        )

    mine, theirs = product(me * share), product((me ^ 1) * share)
    wide = mine + swap_core(theirs)
    return (wide[:1], grad_hidden[:1], grad_hidden[1:], wide[1:])


def solution(mesh):
    return jax.shard_map(
        body,
        mesh=mesh,
        in_specs=(
            P(("dp", "seq"), None),
            P(("dp", "seq"), None),
            P(("dp", "seq"), None),
            P(("dp", "seq"), None),
            P("dp", None, "seq"),
            P("dp", None, "seq"),
            P("dp", "seq", None),
            P("dp", None, None),
            P("dp", None, "seq"),
            P("dp", None, "seq"),
            P("dp", None, None),
        ),
        out_specs=(
            P("dp", None, "seq"),
            P("dp", None, "seq"),
            P("dp", None, "seq"),
            P("dp", None, "seq"),
        ),
        check_vma=False,
    )
```

time: 1120 us -> 321 us (0.29)
  waiting for transfers between devices: 885 us -> 196 us
  local copies, waits for them, and re-layouts: 89.1 us -> 15.9 us
  matrix products: 71.9 us -> 52.9 us
  between operations: 14.2 us -> 1.08 us
  starting transfers between devices: 57.3 us -> 45.7 us
    all_to_all x2, waiting for transfers between devices: 799 us -> 51.6 us  [route(): got = lax.all_to_all(packed, 'dp', split_axis=0, concat_axis=0, tiled=True)]
    ppermute x0 -> x18, waiting for transfers between devices: none -> 145 us  [the longest x11 144 us: shift_y(): return lax.ppermute(value, 'seq', pairs)]
    reduce_scatter x2 -> x0, waiting for transfers between devices: 85.7 us -> none  [the longest x1 53 us: body(): lax.psum_scatter(grad_ga, 'seq', scatter_dimension=1, tiled=True)]
    reshape x2 -> x0, local copies, waits for them, and re-layouts: 56.6 us -> none  [the longest x1 28.3 us: body(): received_in.reshape(-1, width)]
    all_to_all x2, starting transfers between devices: 57.1 us -> 12.9 us  [route(): got = lax.all_to_all(packed, 'dp', split_axis=0, concat_axis=0, tiled=True)]
    ppermute x0 -> x18, starting transfers between devices: none -> 32.8 us  [the longest x7 19 us: swap_core(): return lax.ppermute(value, 'seq', [(i, i ^ 1) for i in range(size)])]
    broadcast_in_dim x4 -> x0, local copies, waits for them, and re-layouts: 30.9 us -> none  [the longest x2 15.5 us: body(): jnp.broadcast_to(return_buffer[:, None], (experts, groups, capacity, width))]
    dot_general x3 -> x8, matrix products: 30.7 us -> 13.7 us  [contract_last(): lax.dot_general(left, right, (((1,), (1,)), ((), ())), preferred_element_...]
  transfers between devices with their start and end apart: 4 -> 20, of which waited for: 4 -> 11; matrix products, arithmetic and copies ran while one was open for 6% -> 16% of each run, Pallas kernels for 0% -> 0%
where the time goes in v1:
time: 321 us; the launch traced here: 320 us
  waiting for transfers between devices  196 us (61%)
  matrix products  52.9 us (16%)
  starting transfers between devices  45.7 us (14%)
  local copies, waits for them, and re-layouts  15.9 us (5%)
  other arithmetic  8.29 us (3%)
    ppermute x11, waiting for transfers between devices, shift_y(): return lax.ppermute(value, 'seq', pairs)  144 us
    all_to_all x2, waiting for transfers between devices, route(): got = lax.all_to_all(packed, 'dp', split_axis=0, concat_axis=0, tiled=True)  51.6 us
    ppermute x7, starting transfers between devices, swap_core(): return lax.ppermute(value, 'seq', [(i, i ^ 1) for i in range(size)])  19 us
    ppermute x11, starting transfers between devices, shift_y(): return lax.ppermute(value, 'seq', pairs)  13.8 us
    dot_general x8, matrix products, contract_last(): lax.dot_general(left, right, (((1,), (1,)), ((), ())), preferred_element_...  13.7 us
    all_to_all x2, starting transfers between devices, route(): got = lax.all_to_all(packed, 'dp', split_axis=0, concat_axis=0, tiled=True)  12.9 us
    dot_general x8, matrix products, route(): jnp.dot(take, got, preferred_element_type=jnp.float32).astype(jnp.bfloat16)  12.6 us
    unnamed x28, local copies, waits for them, and re-layouts  9.77 us
  transfers between devices with their start and end apart: 20, of which 11 were waited for; matrix products, arithmetic and copies ran while one was open for 16% of the time, Pallas kernels for 0%

profile of v1, /device:TPU:1, one launch (start us, length us, event | category | flops | bytes accessed | tf_op | source)
XLA Modules:
  0.0 320.1 jit_solution(15129220906916544839)
XLA Ops:
  0.7 1.9 multiply_convert_fusion
  3.2 0.8 broadcast_and_fusion.3
  4.0 2.8 convolution_convert_fusion.1
  6.8 8.4 %all-to-all-start = ((bf16[16,40,1792]{2,1,0:T(8,128)(2,1)}), bf16[16,40,1792]{2,1,0:T(8,128)(2,1)S(1)}, u32[]{:S(2)}, u32[]{:S(2)}) async-start(bf16[16,40,1792]{2,1,0:T(8,128)(2,1)} %bitcast.101), calls=%async_computation | async-start | bytes 4587520 | tf_op jit(solution)/shard_map/all_to_all | solution.py:92
  15.2 1.6 fusion.87
  16.8 2.8 convolution_convert_fusion
  19.6 26.5 %all-to-all-done = bf16[16,40,1792]{2,1,0:T(8,128)(2,1)S(1)} async-done(((bf16[16,40,1792]{2,1,0:T(8,128)(2,1)}), bf16[16,40,1792]{2,1,0:T(8,128)(2,1)S(1)}, u32[]{:S(2)}, u32[]{:S(2)}) %all-to-all-start) | async-done | bytes 2293792 | tf_op jit(solution)/shard_map/all_to_all | solution.py:92
  46.1 4.5 %all-to-all-start.1 = ((bf16[16,40,1792]{2,1,0:T(8,128)(2,1)}), bf16[16,40,1792]{2,1,0:T(8,128)(2,1)}, u32[]{:S(2)}, u32[]{:S(2)}) async-start(bf16[16,40,1792]{2,1,0:T(8,128)(2,1)} %bitcast.100), calls=%async_computation.1 | async-start | bytes 4587520 | tf_op jit(solution)/shard_map/all_to_all | solution.py:92
  50.6 0.7 convolution_convert_fusion.6
  51.3 1.5 convolution_convert_fusion.7
  52.7 25.1 %all-to-all-done.1 = bf16[16,40,1792]{2,1,0:T(8,128)(2,1)} async-done(((bf16[16,40,1792]{2,1,0:T(8,128)(2,1)}), bf16[16,40,1792]{2,1,0:T(8,128)(2,1)}, u32[]{:S(2)}, u32[]{:S(2)}) %all-to-all-start.1) | async-done | bytes 2293792 | tf_op jit(solution)/shard_map/all_to_all | solution.py:92
  77.8 2.3 convolution_convert_fusion.2
  80.1 2.3 convolution_convert_fusion.3
  82.4 0.7 convolution_convert_fusion.8
  83.1 2.3 convolution_convert_fusion.4
  85.4 0.7 convolution_convert_fusion.9
  86.0 2.3 convolution_convert_fusion.5
  88.3 2.5 pad_maximum_fusion.1
  90.8 1.4 collective-permute-start.4
  92.2 2.4 pad_maximum_fusion
  94.5 1.2 collective-permute-start
  95.8 1.4 collective-permute-start.5
  97.2 6.5 %collective-permute-start.12 = (bf16[16,256]{1,0:T(8,128)(2,1)S(1)}, bf16[16,256]{1,0:T(8,128)(2,1)S(1)}, u32[]{:S(2)}, u32[]{:S(2)}) collective-permute-start(bf16[16,256]{1,0:T(8,128)(2,1)S(1)} %bitcast.102), channel_id=1, source_target_pairs={{0,1},{1,0},{2,3},{3,2},{4,5},{5,4},{6,7},{7,6},{8,9},{9,8},{10,11... | collective-permute-start | bytes 24584 | tf_op jit(solution)/shard_map/ppermute | solution.py:32
  103.8 34.3 %collective-permute-done.4 = bf16[160,7168]{1,0:T(8,128)(2,1)} collective-permute-done((bf16[160,7168]{1,0:T(8,128)(2,1)}, bf16[160,7168]{1,0:T(8,128)(2,1)}, u32[]{:S(2)}, u32[]{:S(2)}) %collective-permute-start.4) | collective-permute-done | bytes 2293792 | tf_op jit(solution)/shard_map/ppermute | solution.py:27
  138.1 1.4 collective-permute-start.1
  139.5 1.3 slice.128
  140.8 3.2 %constant_dynamic-update-slice_fusion.8 = bf16[640,7168]{1,0:T(8,128)(2,1)} fusion(bf16[640,7168]{1,0:T(8,128)(2,1)} %get-tuple-element.5, bf16[160,7168]{1,0:T(8,128)(2,1)} %collective-permute-done.4), kind=kLoop, calls=%fused_computation.108 | loop fusion | bytes 4587520
  144.0 43.1 %collective-permute-done = bf16[160,7168]{1,0:T(8,128)(2,1)S(1)} collective-permute-done((bf16[160,7168]{1,0:T(8,128)(2,1)}, bf16[160,7168]{1,0:T(8,128)(2,1)S(1)}, u32[]{:S(2)}, u32[]{:S(2)}) %collective-permute-start) | collective-permute-done | bytes 2293792 | tf_op jit(solution)/shard_map/ppermute | solution.py:27
  187.1 6.6 %collective-permute-start.10 = (bf16[7168,256]{1,0:T(8,128)(2,1)S(1)}, bf16[7168,256]{1,0:T(8,128)(2,1)}, u32[]{:S(2)}, u32[]{:S(2)}) collective-permute-start(bf16[7168,256]{1,0:T(8,128)(2,1)S(1)} %bitcast.108), channel_id=1, source_target_pairs={{0,1},{1,0},{2,3},{3,2},{4,5},{5,4},{6,7},{7,6},{8,9},{9,8},{10,11... | collective-permute-start | bytes 11010056 | tf_op jit(solution)/shard_map/ppermute | solution.py:32
  193.7 1.6 constant_dynamic-update-slice_fusion.3
  195.4 3.2 constant_dynamic-update-slice_fusion.7
  198.5 1.3 slice.129
  199.9 2.7 collective-permute-start.7
  202.6 1.6 constant_dynamic-update-slice_fusion.2
  204.3 19.1 %collective-permute-done.6 = bf16[80,7168]{1,0:T(8,128)(2,1)S(1)} collective-permute-done((bf16[80,7168]{1,0:T(8,128)(2,1)S(1)}, bf16[80,7168]{1,0:T(8,128)(2,1)S(1)}, u32[]{:S(2)}, u32[]{:S(2)}) %collective-permute-start.6) | collective-permute-done | bytes 1146912 | tf_op jit(solution)/shard_map/ppermute | solution.py:27
  223.4 0.8 collective-permute-start.9
  224.3 2.7 collective-permute-done.7
  227.0 0.8 collective-permute-start.2
  227.9 2.5 convolution_convert_fusion.10
  230.4 0.3 fusion.78
  230.7 24.2 %collective-permute-done.2 = bf16[80,7168]{1,0:T(8,128)(2,1)S(1)} collective-permute-done((bf16[80,7168]{1,0:T(8,128)(2,1)S(1)}, bf16[80,7168]{1,0:T(8,128)(2,1)S(1)}, u32[]{:S(2)}, u32[]{:S(2)}) %collective-permute-start.2) | collective-permute-done | bytes 1146912 | tf_op jit(solution)/shard_map/ppermute | solution.py:27
  254.9 1.2 collective-permute-start.3
  256.1 4.7 %convolution_add_fusion.2 = f32[640,256]{1,0:T(8,128)S(1)} fusion(f32[640,256]{1,0:T(8,128)S(1)} %fusion.78, bf16[640,7168]{1,0:T(8,128)(2,1)S(1)} %constant_dynamic-update-slice_fusion.5, bf16[1,7168,256]{2,1,0:T(8,128)(2,1)} %param.15), kind=kOutput, calls=%fused_computation.33 | convolution fusion | flops 2348974080 | bytes 14155776 | tf_op jit(solution)/shard_map/dot_general | solution.py:110
  260.9 19.0 %collective-permute-done.3 = bf16[80,7168]{1,0:T(8,128)(2,1)S(1)} collective-permute-done((bf16[80,7168]{1,0:T(8,128)(2,1)S(1)}, bf16[80,7168]{1,0:T(8,128)(2,1)S(1)}, u32[]{:S(2)}, u32[]{:S(2)}) %collective-permute-start.3) | collective-permute-done | bytes 1146912 | tf_op jit(solution)/shard_map/ppermute | solution.py:27
  279.9 2.6 collective-permute-start.8
  282.9 2.5 convolution_convert_fusion.11
  285.4 4.6 %convolution_add_fusion = f32[640,256]{1,0:T(8,128)S(1)} fusion(f32[640,256]{1,0:T(8,128)S(1)} %fusion.95, bf16[640,7168]{1,0:T(8,128)(2,1)S(1)} %constant_dynamic-update-slice_fusion.5, bf16[7168,256]{1,0:T(8,128)(2,1)} %collective-permute-done.11), kind=kOutput, calls=%fused_computation.28 | convolution fusion | flops 2348974080 | bytes 14155776 | tf_op jit(solution)/shard_map/dot_general | solution.py:110
  290.0 3.4 %multiply_convert_fusion.2 = (bf16[640,256]{1,0:T(8,128)(2,1)S(1)}, f32[640,256]{1,0:T(8,128)}) fusion(f32[640,256]{1,0:T(8,128)S(1)} %convolution_add_fusion.2, bf16[640,7168]{1,0:T(8,128)(2,1)S(1)} %constant_dynamic-update-slice_fusion.5, bf16[1,7168,256]{2,1,0:T(8,128)(2,1)S(1)} %copy-done.9), kind=kOutput, calls=%fused_computation.64 | convolution fusion | flops 2349793280 | bytes 14483456 | tf_op jit(solution)/shard_map/dot_general | solution.py:113
  293.6 0.3 fusion.84
  293.9 5.4 %multiply_convert_fusion.1 = (bf16[640,256]{1,0:T(8,128)(2,1)S(1)}, f32[640,256]{1,0:T(8,128)}) fusion(f32[640,256]{1,0:T(8,128)S(1)} %convolution_add_fusion, bf16[640,7168]{1,0:T(8,128)(2,1)S(1)} %constant_dynamic-update-slice_fusion.5, bf16[7168,256]{1,0:T(8,128)(2,1)} %collective-permute-done.10), kind=kOutput, calls=%fused_computation.62 | convolution fusion | flops 2349793280 | bytes 14483456 | tf_op jit(solution)/shard_map/dot_general | solution.py:113
  299.3 3.9 %fusion.20 = bf16[640,256]{1,0:T(8,128)(2,1)S(1)} fusion(f32[640,256]{1,0:T(8,128)} %get-tuple-element.37, f32[640,256]{1,0:T(8,128)S(1)} %fusion.84, bf16[640,7168]{1,0:T(8,128)(2,1)S(1)} %constant_dynamic-update-slice_fusion, f32[640,256]{1,0:T(8,128)S(1)} %convolution_add_fusion.2, bf16[1,256,7168]{2,1,0:T(8,128)(2,1)S(1)} %copy-done.10), kind=kOutput, calls=%fused_computation.38 | convolution fusion | flops 2350612480 | bytes 15138816 | tf_op jit(solution)/shard_map/dot_general | solution.py:10
  303.6 0.3 fusion.94
  304.0 4.1 %fusion.21 = bf16[640,256]{1,0:T(8,128)(2,1)S(1)} fusion(f32[640,256]{1,0:T(8,128)} %get-tuple-element.39, f32[640,256]{1,0:T(8,128)S(1)} %fusion.94, bf16[640,7168]{1,0:T(8,128)(2,1)S(1)} %constant_dynamic-update-slice_fusion, bf16[256,7168]{1,0:T(8,128)(2,1)S(1)} %collective-permute-done.8, f32[640,256]{1,0:T(8,128)S(1)} %convolution_add_fusion), kind=kOutput, calls=%fused_computation.39 | convolution fusion | flops 2350612480 | bytes 15138816 | tf_op jit(solution)/shard_map/dot_general | solution.py:10
  308.4 2.7 collective-permute-start.14
  311.0 0.9 collective-permute-start.15
  312.4 0.6 collective-permute-start.17
  313.2 0.7 collective-permute-done.17
  313.9 0.6 fusion.93
  314.7 1.1 collective-permute-done.15
  316.1 0.3 fusion.39
  316.7 1.8 collective-permute-start.16
  318.7 0.3 fusion.30
  319.0 0.4 collective-permute-done.16
  319.5 0.6 fusion.89
  (69 shorter events, 4.0 us)
Async XLA Ops:
  0.6 227.3 %copy-start = (bf16[1,16,7168]{2,1,0:T(8,128)(2,1)S(1)}, bf16[1,16,7168]{2,1,0:T(8,128)(2,1)}, u32[]{:S(2)}) copy-start(bf16[1,16,7168]{2,1,0:T(8,128)(2,1)} %param.18) | copy-start | bytes 688132
  0.7 2.1 copy-start.8
  6.8 39.3 %all-to-all-start = ((bf16[16,40,1792]{2,1,0:T(8,128)(2,1)}), bf16[16,40,1792]{2,1,0:T(8,128)(2,1)S(1)}, u32[]{:S(2)}, u32[]{:S(2)}) async-start(bf16[16,40,1792]{2,1,0:T(8,128)(2,1)} %bitcast.101), calls=%async_computation | async-start | bytes 4587520 | tf_op jit(solution)/shard_map/all_to_all | solution.py:92
  46.1 31.7 %all-to-all-start.1 = ((bf16[16,40,1792]{2,1,0:T(8,128)(2,1)}), bf16[16,40,1792]{2,1,0:T(8,128)(2,1)}, u32[]{:S(2)}, u32[]{:S(2)}) async-start(bf16[16,40,1792]{2,1,0:T(8,128)(2,1)} %bitcast.100), calls=%async_computation.1 | async-start | bytes 4587520 | tf_op jit(solution)/shard_map/all_to_all | solution.py:92
  88.3 3.8 %copy-start.4 = (bf16[160,1792]{1,0:T(8,128)(2,1)S(1)}, bf16[160,1792]{1,0:T(8,128)(2,1)}, u32[]{:S(2)}) copy-start(bf16[160,1792]{1,0:T(8,128)(2,1)} %convolution_convert_fusion.7) | copy-start | bytes 1720324
  90.8 6.4 %copy-start.6 = (bf16[1,16,256]{2,1,0:T(8,128)(2,1)S(1)}, bf16[1,16,256]{2,1,0:T(8,128)(2,1)}, u32[]{:S(2)}) copy-start(bf16[1,16,256]{2,1,0:T(8,128)(2,1)} %param.19) | copy-start | bytes 24580
  90.8 47.3 %collective-permute-start.4 = (bf16[160,7168]{1,0:T(8,128)(2,1)}, bf16[160,7168]{1,0:T(8,128)(2,1)}, u32[]{:S(2)}, u32[]{:S(2)}) collective-permute-start(bf16[160,7168]{1,0:T(8,128)(2,1)} %get-tuple-element.4), channel_id=1, source_target_pairs={{0,2},{1,3},{2,4},{3,5},{4,6},{5,7},{6,0},{7,1},{8,10},{9,11},{10,... | collective-permute-start | bytes 6881288 | tf_op jit(solution)/shard_map/ppermute | solution.py:27
  94.5 92.6 %collective-permute-start = (bf16[160,7168]{1,0:T(8,128)(2,1)}, bf16[160,7168]{1,0:T(8,128)(2,1)S(1)}, u32[]{:S(2)}, u32[]{:S(2)}) collective-permute-start(bf16[160,7168]{1,0:T(8,128)(2,1)} %get-tuple-element.6), channel_id=1, source_target_pairs={{0,2},{1,3},{2,4},{3,5},{4,6},{5,7},{6,0},{7,1},{8,10},{9,11},{10,... | collective-permute-start | bytes 6881288 | tf_op jit(solution)/shard_map/ppermute | solution.py:27
  95.8 99.5 %collective-permute-start.5 = (bf16[160,7168]{1,0:T(8,128)(2,1)}, bf16[160,7168]{1,0:T(8,128)(2,1)}, u32[]{:S(2)}, u32[]{:S(2)}) collective-permute-start(bf16[160,7168]{1,0:T(8,128)(2,1)} %get-tuple-element.4), channel_id=1, source_target_pairs={{0,6},{1,7},{2,0},{3,1},{4,2},{5,3},{6,4},{7,5},{8,14},{9,15},{10,... | collective-permute-start | bytes 6881288 | tf_op jit(solution)/shard_map/ppermute | solution.py:27
  97.2 185.4 %collective-permute-start.12 = (bf16[16,256]{1,0:T(8,128)(2,1)S(1)}, bf16[16,256]{1,0:T(8,128)(2,1)S(1)}, u32[]{:S(2)}, u32[]{:S(2)}) collective-permute-start(bf16[16,256]{1,0:T(8,128)(2,1)S(1)} %bitcast.102), channel_id=1, source_target_pairs={{0,1},{1,0},{2,3},{3,2},{4,5},{5,4},{6,7},{7,6},{8,9},{9,8},{10,11... | collective-permute-start | bytes 24584 | tf_op jit(solution)/shard_map/ppermute | solution.py:32
  103.7 181.7 %collective-permute-start.11 = (bf16[7168,256]{1,0:T(8,128)(2,1)}, bf16[7168,256]{1,0:T(8,128)(2,1)}, u32[]{:S(2)}, u32[]{:S(2)}) collective-permute-start(bf16[7168,256]{1,0:T(8,128)(2,1)} %bitcast.10), channel_id=1, source_target_pairs={{0,1},{1,0},{2,3},{3,2},{4,5},{5,4},{6,7},{7,6},{8,9},{9,8},{10,11... | collective-permute-start | bytes 11010056 | tf_op jit(solution)/shard_map/ppermute | solution.py:32
  103.7 83.4 %copy-start.9 = (bf16[1,7168,256]{2,1,0:T(8,128)(2,1)S(1)}, bf16[1,7168,256]{2,1,0:T(8,128)(2,1)}, u32[]{:S(2)}) copy-start(bf16[1,7168,256]{2,1,0:T(8,128)(2,1)} %param.16) | copy-start | bytes 11010052
  138.1 61.8 %collective-permute-start.1 = (bf16[160,7168]{1,0:T(8,128)(2,1)}, bf16[160,7168]{1,0:T(8,128)(2,1)S(1)}, u32[]{:S(2)}, u32[]{:S(2)}) collective-permute-start(bf16[160,7168]{1,0:T(8,128)(2,1)} %get-tuple-element.6), channel_id=1, source_target_pairs={{0,6},{1,7},{2,0},{3,1},{4,2},{5,3},{6,4},{7,5},{8,14},{9,15},{10,... | collective-permute-start | bytes 6881288 | tf_op jit(solution)/shard_map/ppermute | solution.py:27
  187.1 106.8 %collective-permute-start.10 = (bf16[7168,256]{1,0:T(8,128)(2,1)S(1)}, bf16[7168,256]{1,0:T(8,128)(2,1)}, u32[]{:S(2)}, u32[]{:S(2)}) collective-permute-start(bf16[7168,256]{1,0:T(8,128)(2,1)S(1)} %bitcast.108), channel_id=1, source_target_pairs={{0,1},{1,0},{2,3},{3,2},{4,5},{5,4},{6,7},{7,6},{8,9},{9,8},{10,11... | collective-permute-start | bytes 11010056 | tf_op jit(solution)/shard_map/ppermute | solution.py:32
  195.3 28.1 %collective-permute-start.6 = (bf16[80,7168]{1,0:T(8,128)(2,1)S(1)}, bf16[80,7168]{1,0:T(8,128)(2,1)S(1)}, u32[]{:S(2)}, u32[]{:S(2)}) collective-permute-start(bf16[80,7168]{1,0:T(8,128)(2,1)S(1)} %slice.128), channel_id=1, source_target_pairs={{0,2},{1,3},{2,4},{3,5},{4,6},{5,7},{6,0},{7,1},{8,10},{9,11},{10,... | collective-permute-start | bytes 3440648 | tf_op jit(solution)/shard_map/ppermute | solution.py:27
  198.5 24.8 %copy-start.7 = (bf16[1,16,256]{2,1,0:T(8,128)(2,1)S(1)}, bf16[1,16,256]{2,1,0:T(8,128)(2,1)}, u32[]{:S(2)}) copy-start(bf16[1,16,256]{2,1,0:T(8,128)(2,1)} %param.20) | copy-start | bytes 24580
  199.9 24.3 %copy-start.2 = (bf16[640,7168]{1,0:T(8,128)(2,1)S(1)}, bf16[640,7168]{1,0:T(8,128)(2,1)}, u32[]{:S(2)}) copy-start(bf16[640,7168]{1,0:T(8,128)(2,1)} %constant_dynamic-update-slice_fusion.7) | copy-start | bytes 27525124
  199.9 27.0 %collective-permute-start.7 = (bf16[80,7168]{1,0:T(8,128)(2,1)S(1)}, bf16[80,7168]{1,0:T(8,128)(2,1)S(1)}, u32[]{:S(2)}, u32[]{:S(2)}) collective-permute-start(bf16[80,7168]{1,0:T(8,128)(2,1)S(1)} %slice.129), channel_id=1, source_target_pairs={{0,6},{1,7},{2,0},{3,1},{4,2},{5,3},{6,4},{7,5},{8,14},{9,15},{10,... | collective-permute-start | bytes 3440648 | tf_op jit(solution)/shard_map/ppermute | solution.py:27
  223.4 80.0 %collective-permute-start.9 = (bf16[16,256]{1,0:T(8,128)(2,1)S(1)}, bf16[16,256]{1,0:T(8,128)(2,1)S(1)}, u32[]{:S(2)}, u32[]{:S(2)}) collective-permute-start(bf16[16,256]{1,0:T(8,128)(2,1)S(1)} %bitcast.103), channel_id=1, source_target_pairs={{0,1},{1,0},{2,3},{3,2},{4,5},{5,4},{6,7},{7,6},{8,9},{9,8},{10,11... | collective-permute-start | bytes 24584 | tf_op jit(solution)/shard_map/ppermute | solution.py:32
  227.0 27.9 %collective-permute-start.2 = (bf16[80,7168]{1,0:T(8,128)(2,1)S(1)}, bf16[80,7168]{1,0:T(8,128)(2,1)S(1)}, u32[]{:S(2)}, u32[]{:S(2)}) collective-permute-start(bf16[80,7168]{1,0:T(8,128)(2,1)S(1)} %slice.126), channel_id=1, source_target_pairs={{0,2},{1,3},{2,4},{3,5},{4,6},{5,7},{6,0},{7,1},{8,10},{9,11},{10,... | collective-permute-start | bytes 3440648 | tf_op jit(solution)/shard_map/ppermute | solution.py:27
  227.9 28.1 %copy-start.3 = (bf16[640,7168]{1,0:T(8,128)(2,1)S(1)}, bf16[640,7168]{1,0:T(8,128)(2,1)}, u32[]{:S(2)}) copy-start(bf16[640,7168]{1,0:T(8,128)(2,1)} %constant_dynamic-update-slice_fusion.2) | copy-start | bytes 27525124
  254.9 25.0 %collective-permute-start.3 = (bf16[80,7168]{1,0:T(8,128)(2,1)S(1)}, bf16[80,7168]{1,0:T(8,128)(2,1)S(1)}, u32[]{:S(2)}, u32[]{:S(2)}) collective-permute-start(bf16[80,7168]{1,0:T(8,128)(2,1)S(1)} %slice.127), channel_id=1, source_target_pairs={{0,6},{1,7},{2,0},{3,1},{4,2},{5,3},{6,4},{7,5},{8,14},{9,15},{10,... | collective-permute-start | bytes 3440648 | tf_op jit(solution)/shard_map/ppermute | solution.py:27
  256.1 23.8 %copy-start.10 = (bf16[1,256,7168]{2,1,0:T(8,128)(2,1)S(1)}, bf16[1,256,7168]{2,1,0:T(8,128)(2,1)}, u32[]{:S(2)}) copy-start(bf16[1,256,7168]{2,1,0:T(8,128)(2,1)} %param.17) | copy-start | bytes 11010052
  256.1 26.8 %copy-start.5 = (bf16[1,16,7168]{2,1,0:T(8,128)(2,1)S(1)}, bf16[1,16,7168]{2,1,0:T(8,128)(2,1)}, u32[]{:S(2)}) copy-start(bf16[1,16,7168]{2,1,0:T(8,128)(2,1)} %param.21) | copy-start | bytes 688132
  279.9 24.0 %collective-permute-start.8 = (bf16[256,7168]{1,0:T(8,128)(2,1)S(1)}, bf16[256,7168]{1,0:T(8,128)(2,1)S(1)}, u32[]{:S(2)}, u32[]{:S(2)}) collective-permute-start(bf16[256,7168]{1,0:T(8,128)(2,1)S(1)} %bitcast.109), channel_id=1, source_target_pairs={{0,1},{1,0},{2,3},{3,2},{4,5},{5,4},{6,7},{7,6},{8,9},{9,8},{10,11... | collective-permute-start | bytes 11010056 | tf_op jit(solution)/shard_map/ppermute | solution.py:32
  308.3 6.2 %collective-permute-start.13 = (f32[32,640]{1,0:T(8,128)S(1)}, f32[32,640]{1,0:T(8,128)S(1)}, u32[]{:S(2)}, u32[]{:S(2)}) collective-permute-start(f32[32,640]{1,0:T(8,128)S(1)} %maximum_add_fusion.1), channel_id=1, source_target_pairs={{0,2},{1,3},{2,4},{3,5},{4,6},{5,7},{6,0},{7,1},{8,10},{9,11},{10,... | collective-permute-start | bytes 245768 | tf_op jit(solution)/shard_map/ppermute | solution.py:27
  308.4 6.3 %collective-permute-start.14 = (f32[32,640]{1,0:T(8,128)S(1)}, f32[32,640]{1,0:T(8,128)S(1)}, u32[]{:S(2)}, u32[]{:S(2)}) collective-permute-start(f32[32,640]{1,0:T(8,128)S(1)} %maximum_add_fusion.1), channel_id=1, source_target_pairs={{0,6},{1,7},{2,0},{3,1},{4,2},{5,3},{6,4},{7,5},{8,14},{9,15},{10,... | collective-permute-start | bytes 245768 | tf_op jit(solution)/shard_map/ppermute | solution.py:27
  311.0 4.8 %collective-permute-start.15 = (f32[32,640]{1,0:T(8,128)S(1)}, f32[32,640]{1,0:T(8,128)S(1)}, u32[]{:S(2)}, u32[]{:S(2)}) collective-permute-start(f32[32,640]{1,0:T(8,128)S(1)} %maximum_add_fusion.1), channel_id=1, source_target_pairs={{0,4},{1,5},{2,6},{3,7},{4,0},{5,1},{6,2},{7,3},{8,12},{9,13},{10,... | collective-permute-start | bytes 245768 | tf_op jit(solution)/shard_map/ppermute | solution.py:27
  312.4 1.5 collective-permute-start.17
  313.1 7.1 %copy-start.1 = (bf16[1,16,7168]{2,1,0:T(8,128)(2,1)S(1)}, bf16[1,16,7168]{2,1,0:T(8,128)(2,1)}, u32[]{:S(2)}) copy-start(bf16[1,16,7168]{2,1,0:T(8,128)(2,1)} %param.18) | copy-start | bytes 688132
  316.7 2.8 collective-permute-start.16

commit v2 on v1

v2 whole, which is shorter than its diff:
```python
import functools

import jax
import jax.numpy as jnp
from jax import lax
from jax.experimental import pallas as pl
from jax.experimental.pallas import tpu as pltpu
from jax.sharding import PartitionSpec as P

PIECES = 4
EARLY = 4
CHUNKS = (2, 2, 3)
DEPTH = 1024
LANES = 128
COVER = 8
MIB = 1 << 20
VMEM_MIB = 56
BF16, F32 = jnp.bfloat16, jnp.float32


def dot(left, right):
    return jnp.dot(left, right, preferred_element_type=F32)


def contract_last(left, right):
    return lax.dot_general(left, right, (((1,), (1,)), ((), ())), preferred_element_type=F32)


def contract_first(left, right):
    return lax.dot_general(left, right, (((0,), (0,)), ((), ())), preferred_element_type=F32)


def shift_y(value, step):
    size = lax.axis_size("seq")
    planes = size // 2
    pairs = [
        (y * 2 + c, ((y + step) % planes) * 2 + c) for y in range(planes) for c in range(2)
    ]
    return lax.ppermute(value, "seq", pairs)


def swap_core(value):
    size = lax.axis_size("seq")
    return lax.ppermute(value, "seq", [(i, i ^ 1) for i in range(size)])


def first_step(rows):
    return shift_y(rows, 1), shift_y(rows, -1)


def split_kernel(before_ref, after_ref, low_ref, high_ref, sems):
    half = low_ref.shape[0]
    low = pltpu.make_async_copy(before_ref.at[pl.ds(0, half)], low_ref, sems.at[0])
    high = pltpu.make_async_copy(after_ref.at[pl.ds(half, half)], high_ref, sems.at[1])
    low.start()
    high.start()
    low.wait()
    high.wait()


def second_step(before, after):
    part = shape((before.shape[0] // 2, before.shape[1]), before.dtype)
    anywhere = pl.BlockSpec(memory_space=pl.ANY)
    low, high = call(
        split_kernel,
        (part, part),
        8,
        moved=2 * before.size * 2,
        in_specs=[anywhere] * 2,
        out_specs=(anywhere,) * 2,
        scratch_shapes=[pltpu.SemaphoreType.DMA((2,))],
    )(before, after)
    return shift_y(low, 1), shift_y(high, -1)


def shape(dims, dtype):
    return jax.ShapeDtypeStruct(dims, dtype)


def call(kernel, outs, mib, flops=0, moved=0, **rest):
    return pl.pallas_call(
        kernel,
        out_shape=outs,
        compiler_params=pltpu.CompilerParams(vmem_limit_bytes=mib * MIB),
        cost_estimate=pl.CostEstimate(flops=COVER * flops, bytes_accessed=COVER * moved, transcendentals=0),
        **rest,
    )


def whole(*dims):
    return pl.BlockSpec(dims, lambda *_: (0,) * len(dims))


def scale_kernel(cot_ref, weight_ref, code_ref, raw_ref, rest_ref):
    count = weight_ref.shape[1]
    column = jnp.broadcast_to(weight_ref[...], (count, count)).T[:, :1]
    early = cot_ref.shape[1] - rest_ref.shape[1]
    for base, size, out in ((0, early, raw_ref), (early, rest_ref.shape[1], rest_ref)):
        for at in range(0, size, 512):
            block = cot_ref[:, base + at : base + at + 512].astype(F32)
            out[:, at : at + 512] = (block * column).astype(BF16)
    codes = jnp.broadcast_to(code_ref[...], (count, count)).astype(F32).T
    raw_ref[:, early:] = codes[:, : raw_ref.shape[1] - early].astype(BF16)


def code_kernel(experts, capacity, ids_ref, code_ref):
    ids = ids_ref[...]
    count = ids.shape[1]
    onehot = (lax.broadcasted_iota(jnp.int32, (experts, count), 0) == ids).astype(F32)
    ahead = (
        lax.broadcasted_iota(jnp.int32, (count, count), 0)
        < lax.broadcasted_iota(jnp.int32, (count, count), 1)
    ).astype(BF16)
    earlier = dot(onehot.astype(BF16), ahead)
    slot = jnp.sum(earlier * onehot, axis=0, keepdims=True).astype(jnp.int32)
    code_ref[...] = ids * capacity + slot


def pack_kernel(spans, code_ref, want_ref, piece_ref, *refs):
    out = refs[-1]
    hit = code_ref[...] == want_ref[...]
    placing = jnp.concatenate(
        [(hit & (piece_ref[...] == q)).astype(BF16) for q in range(PIECES)], axis=1
    )
    at = 0
    for rows, (first, size) in zip(refs, spans):
        part = size // PIECES
        stacked = jnp.concatenate(
            [rows[:, first + q * part : first + (q + 1) * part] for q in range(PIECES)], axis=0
        )
        out[:, at : at + part] = dot(placing, stacked).astype(BF16)
        at += part


def unpack_kernel(got_ref, came_ref, *outs):
    count = got_ref.shape[0]
    take = (
        lax.broadcasted_iota(jnp.int32, (count, count), 1) == came_ref[...]
    ).astype(BF16)
    rows = count // PIECES
    at = 0
    for out in outs:
        part = out.shape[1] // PIECES
        taken = dot(take, got_ref[:, at : at + part]).astype(BF16)
        for q in range(PIECES):
            out[:, q * part : (q + 1) * part] = taken[q * rows : (q + 1) * rows]
        at += part


def pack_raw_kernel(want_ref, plane_ref, *refs):
    pieces, codes, out, placing = refs[:5], refs[5:10], refs[10], refs[11]

    @pl.when(pl.program_id(0) == 0)
    def _():
        code = jnp.concatenate([piece[...] for piece in codes], axis=0).astype(F32)
        count = code.shape[0] // 4
        for k in range(4):
            row = code[k * count : (k + 1) * count].T[:1].astype(jnp.int32)
            hit = (row == want_ref[...]) & (plane_ref[...] == k)
            placing[:, k * count : (k + 1) * count] = hit.astype(BF16)

    stacked = jnp.concatenate([piece[...] for piece in pieces], axis=0)
    out[...] = dot(placing[...], stacked).astype(BF16)


def gate_up_kernel(begins, last, *refs):
    pieces, (gate_o, gate_p, up_o, up_p, first) = refs[:5], refs[5:10]
    refs = refs[10:]
    if not begins:
        prev, refs = refs[:3], refs[3:]
    if last:
        (gb_o, gb_p, da_o, da_p), refs = refs[:4], refs[4:]
        (hidden_ref, factor_ref, low_ref, sums_ref), refs = refs[:4], refs[4:]
    gate, up, low = refs
    step = pl.program_id(0)
    units = gate_o.shape[1]

    @pl.when(step == 0)
    def _():
        for i, total in enumerate((gate, up, low)):
            total[...] = jnp.zeros_like(total) if begins else prev[i][...]

    rows = jnp.concatenate([piece[...] for piece in pieces], axis=0)
    gate[:, :units] += dot(rows, gate_o[...])
    gate[:, units:] += dot(rows, gate_p[...])
    up[:, :units] += dot(rows, up_o[...])
    up[:, units:] += dot(rows, up_p[...])
    low[...] += contract_last(rows, first[...])

    if last:

        @pl.when(step == pl.num_programs(0) - 1)
        def _():
            lowrank_in = low[...].astype(BF16)
            low_ref[...] = lowrank_in
            gate[:, :units] += dot(lowrank_in, gb_o[...])
            gate[:, units:] += dot(lowrank_in, gb_p[...])
            block = 32

            def some(i, carry):
                at = pl.ds(pl.multiple_of(i * block, block), block)
                gate_pre, up_pre = gate[at, :], up[at, :]
                sigmoid_val = jax.nn.sigmoid(gate_pre)
                slope = up_pre * sigmoid_val
                hidden_ref[at, :] = (gate_pre * slope).astype(BF16)
                factor_ref[at, :] = slope * (1.0 + gate_pre * (1.0 - sigmoid_val))
                return carry

            lax.fori_loop(0, gate.shape[0] // block, some, 0)
            sums_ref[...] = contract_last(da_o[...], hidden_ref[:, :units]) + contract_last(
                da_p[...], hidden_ref[:, units:]
            )


def halves(value):
    high = value.astype(BF16)
    return high, (value - high.astype(F32)).astype(BF16)


def order_of(came_ref):
    count = came_ref.shape[0]
    return (lax.broadcasted_iota(jnp.int32, (count, count), 1) == came_ref[...]).astype(BF16)


def raw_kernel(got_ref, came_ref, down_o, down_p, first, total_ref, low_ref, total, low):
    units = down_o.shape[0]
    step = pl.program_id(0)

    @pl.when(step == 0)
    def _():
        total[...] = jnp.zeros_like(total)
        low[...] = jnp.zeros_like(low)

    rows = got_ref[...]
    total[:, :units] += contract_last(rows, down_o[...])
    total[:, units:] += contract_last(rows, down_p[...])
    low[...] += contract_last(rows, first[...])

    @pl.when(step == pl.num_programs(0) - 1)
    def _():
        order = order_of(came_ref)
        for source, out in ((total, total_ref), (low, low_ref)):
            high_part, low_part = halves(source[...])
            out[...] = dot(order, high_part) + dot(order, low_part)


def back_kernel(last, pieces, *refs):
    refs = list(refs)

    def take(number):
        taken = refs[:number]
        del refs[:number]
        return taken

    rows_refs, (down_o, down_p, first) = take(pieces), take(3)
    prev, (factor_ref, hidden_ref, low_in_ref) = take(2), take(3)
    gb_o, gb_p, da_o, da_p = take(4)
    if last:
        sums_before, grads_before, sums_back = take(3)
    sums_ref, grads_ref, total, low = refs
    step = pl.program_id(0)
    units = down_o.shape[0]

    @pl.when(step == 0)
    def _():
        total[...] = prev[0][...]
        low[...] = prev[1][...]

    rows = jnp.concatenate([piece[...] for piece in rows_refs], axis=0)
    total[:, :units] += contract_last(rows, down_o[...])
    total[:, units:] += contract_last(rows, down_p[...])
    low[...] += contract_last(rows, first[...])

    @pl.when(step == pl.num_programs(0) - 1)
    def _():
        lowrank_back = low[...].astype(BF16)
        rank = lowrank_back.shape[1]
        total_o = total[:, :units] + dot(lowrank_back, da_o[...])
        grad_o = (total_o * factor_ref[:, :units]).astype(BF16)
        total_p = total[:, units:] + dot(lowrank_back, da_p[...])
        grad_p = (total_p * factor_ref[:, units:]).astype(BF16)
        lowrank_in = low_in_ref[...]
        sums = contract_last(gb_o[...], grad_o) + contract_last(gb_p[...], grad_p)
        grads_o = contract_first(lowrank_in, grad_o)
        grads_p = contract_first(lowrank_in, grad_p)
        grads_b = contract_first(lowrank_back, hidden_ref[...])
        if last:
            done = sums_before.shape[1]
            sums_ref[:rank, :done] = sums_before[...]
            sums_ref[:rank, done:] = sums
            sums_ref[rank:, :] = sums_back[...]
            grads_ref[:rank, :units] = grads_before[:rank, :units] + grads_o
            grads_ref[:rank, units:] = grads_before[:rank, units:] + grads_p
            grads_ref[rank:, :] = grads_before[rank:, :] + grads_b
        else:
            sums_ref[...] = sums
            grads_ref[:rank, :units] = grads_o
            grads_ref[:rank, units:] = grads_p
            grads_ref[rank:, :] = grads_b


def product_kernel(rank, me_ref, sums_ref, came_ref, *refs):
    sides = ((refs[:5], refs[5:10], refs[10:15]), (refs[15:16], refs[16:21]))
    mine_ref, theirs_ref, buffer, sems = refs[21:]
    span = buffer.shape[2]
    me = me_ref[0]
    plane = lax.div(me, 2)

    def copies(which):
        found, number = [], 0
        begin, end = which * span, (which + 1) * span
        for side, chunks in enumerate(sides):
            base = 0
            for pieces in chunks:
                size = pieces[0].shape[1]
                low, high = max(begin, base), min(end, base + size)
                at = 0
                for piece in pieces:
                    rows = piece.shape[0]
                    if low < high:
                        found.append(
                            pltpu.make_async_copy(
                                piece.at[:, pl.ds(low - base, high - low)],
                                buffer.at[side, pl.ds(at, rows), pl.ds(low - begin, high - low)],
                                sems.at[number],
                            )
                        )
                        number += 1
                    at += rows
                base += size
        return found

    for which in range(4):

        @pl.when(plane == which)
        def _():
            found = copies(which)
            for copy in found:
                copy.start()
            for copy in found:
                copy.wait()

    high, low = halves(sums_ref[...])
    half = span // 2
    even = lax.rem(me, 2) == 0
    crossed = lax.broadcasted_iota(jnp.int32, (rank, span), 1) + plane * span < sides[1][0][0].shape[1]
    for side in range(2):
        at = slice(side * rank, (side + 1) * rank)
        both = jnp.concatenate([high[at], low[at]], axis=0)
        wide = dot(both, buffer[side])
        wide = wide[:rank] + wide[rank:]
        if side == 1:
            moved = dot(dot(both, order_of(came_ref)).astype(BF16), buffer[side])
            wide = jnp.where(crossed, moved[:rank] + moved[rank:], wide)
        mine_ref[side] = jnp.where(even, wide[:, :half], wide[:, half:])
        theirs_ref[side] = jnp.where(even, wide[:, half:], wide[:, :half])


def body(
    tokens,
    cotangent,
    chosen_expert_index,
    router_weight,
    frozen_gate_weight,
    frozen_up_weight,
    frozen_down_weight,
    gate_adapter_first,
    gate_adapter_second,
    down_adapter_first,
    down_adapter_second,
):
    tie = lax.optimization_barrier
    experts = lax.axis_size("dp")
    count, top = chosen_expert_index.shape
    width = tokens.shape[1]
    early = width // DEPTH * EARLY // 7 * DEPTH
    spans, at = [], 0
    for sevenths in CHUNKS:
        size = width // DEPTH * sevenths // 7 * DEPTH
        spans.append((at, size))
        at += size
    capacity = 5 * count * top // (4 * experts)
    slots = experts * capacity
    every = 4 * slots
    gate_w, up_w, down_w = frozen_gate_weight[0], frozen_up_weight[0], frozen_down_weight[0]
    gate_a, gate_b = gate_adapter_first[0], gate_adapter_second[0]
    down_a, down_b = down_adapter_first[0], down_adapter_second[0]
    rank, units = gate_b.shape

    at_row = jnp.arange(every, dtype=jnp.int32)[:, None]
    want = at_row // (4 * capacity) * capacity + at_row % capacity
    quarter = at_row // capacity % 4
    came = at_row % slots // capacity * 4 * capacity + at_row // slots * capacity + at_row % capacity

    code = call(
        functools.partial(code_kernel, experts, capacity), shape((1, count), jnp.int32), 16, moved=1024
    )(chosen_expert_index.reshape(1, count))
    raw, scaled = call(
        scale_kernel,
        (shape((count, early + LANES), BF16), shape((count, width - early), BF16)),
        16,
        moved=4 * count * width,
    )(cotangent, router_weight.reshape(1, count), code)
    raw_steps = first_step(raw)

    def pack(*sources):
        spans = [(first, size) for _, first, size in sources]
        part = sum(size for _, size in spans) // PIECES
        return call(
            functools.partial(pack_kernel, spans),
            shape((every, part), BF16),
            32,
            flops=2 * every * PIECES * count * part,
            moved=2 * (PIECES * count + every) * part,
            grid=(1,),
            in_specs=[whole(1, count), whole(every, 1), whole(every, 1)]
            + [whole(*rows.shape) for rows, _, _ in sources],
            out_specs=whole(every, part),
        )(code, want, quarter, *[rows for rows, _, _ in sources])

    def across_dp(packed):
        sent = packed.reshape(experts, -1, packed.shape[1])
        return lax.all_to_all(sent, "dp", split_axis=0, concat_axis=0, tiled=True).reshape(packed.shape)

    def unpack(got, *sizes):
        return call(
            unpack_kernel,
            tuple(shape((slots, size), BF16) for size in sizes),
            32,
            flops=2 * every * every * got.shape[1],
            moved=4 * every * got.shape[1],
        )(got, came)

    mine = (gate_w, up_w, down_w, jnp.concatenate([gate_b, down_a], axis=0))
    raw_far = second_step(*raw_steps)
    sent = pack(*[(tokens, *span) for span in spans], (scaled, 0, width - early))
    got = across_dp(sent)
    raw_pieces = (raw, *raw_steps, *raw_far)
    wide = early // PIECES
    packed_raw = call(
        pack_raw_kernel,
        shape((every, early), BF16),
        VMEM_MIB,
        flops=2 * every * 4 * count * early,
        moved=2 * (4 * count + every) * early,
        grid=(PIECES,),
        in_specs=[whole(every, 1), whole(every, 1)]
        + [pl.BlockSpec((piece.shape[0], wide), lambda i: (0, i)) for piece in raw_pieces]
        + [
            pl.BlockSpec((piece.shape[0], LANES), lambda i: (0, early // LANES))
            for piece in raw_pieces
        ],
        out_specs=pl.BlockSpec((every, wide), lambda i: (0, i)),
        scratch_shapes=[pltpu.VMEM((every, 4 * count), BF16)],
    )(want, quarter, *raw_pieces, *raw_pieces)
    got, theirs, packed_raw = tie((got, tuple(swap_core(w) for w in mine), packed_raw))
    gate_p, up_p, down_p, small_p = theirs
    small = (gate_b, small_p[:rank], down_a, small_p[rank:])
    *rows, rows_back = unpack(got, *[size for _, size in spans], width - early)

    def piece_specs(pieces):
        return [pl.BlockSpec((piece.shape[0], DEPTH), lambda i: (0, i)) for piece in pieces]

    def tall(first):
        return pl.BlockSpec((DEPTH, units), lambda i: (first // DEPTH + i, 0))

    def flat(rows, first):
        return pl.BlockSpec((rows, DEPTH), lambda i: (0, first // DEPTH + i))

    totals = (shape((every, 2 * units), F32), shape((every, 2 * units), F32), shape((every, rank), F32))
    scratch = [pltpu.VMEM(s.shape, s.dtype) for s in totals]
    def gate_up(chunk, pieces, before):
        begins, last = chunk == 0, chunk == len(spans) - 1
        first, size = spans[chunk]
        outs = totals
        if last:
            outs = (
                shape((every, 2 * units), BF16),
                totals[0],
                shape((every, rank), BF16),
                shape((rank, every), F32),
            )
        extra = (before if before else ()) + (small if last else ())
        return call(
            functools.partial(gate_up_kernel, begins, last),
            outs,
            VMEM_MIB,
            flops=2 * every * size * 4 * units,
            moved=2 * size * (every + 4 * units),
            grid=(size // DEPTH,),
            in_specs=piece_specs(pieces)
            + [tall(first)] * 4
            + [flat(rank, first)]
            + [whole(*value.shape) for value in extra],
            out_specs=tuple(whole(*s.shape) for s in outs),
            scratch_shapes=scratch if last else [],
        )(*pieces, gate_w, gate_p, up_w, up_p, gate_a, *extra)

    packed_raw, rows[0] = tie((packed_raw, rows[0]))
    got_raw = across_dp(packed_raw)
    steps_0 = first_step(rows[0])
    steps_0, rows[1] = tie((steps_0, rows[1]))
    far_0 = second_step(*steps_0)
    steps_1 = first_step(rows[1])
    steps_1, far_0, rows[2] = tie((steps_1, far_0, rows[2]))
    far_1 = second_step(*steps_1)
    steps_2 = first_step(rows[2])
    pieces_0 = (rows[0], *steps_0, *far_0)
    part_0 = gate_up(0, pieces_0, None)
    steps_2, part_0 = tie((steps_2, part_0))
    far_2 = second_step(*steps_2)
    pieces_1 = (rows[1], *steps_1, *far_1)
    part_1 = gate_up(1, pieces_1, part_0)
    far_2, part_1, rows_back = tie((far_2, part_1, rows_back))
    steps_3 = first_step(rows_back)
    pieces_2 = (rows[2], *steps_2, *far_2)
    hidden, factor, low_in, sums_back = gate_up(2, pieces_2, part_1)
    steps_3, hidden = tie((steps_3, hidden))
    far_3 = second_step(*steps_3)

    back_0, low_0 = call(
        raw_kernel,
        (totals[0], totals[2]),
        VMEM_MIB,
        flops=2 * every * early * 2 * units,
        moved=2 * early * (every + 2 * units),
        grid=(early // DEPTH,),
        in_specs=[
            pl.BlockSpec((every, DEPTH), lambda i: (0, i)),
            whole(every, 1),
            flat(units, 0),
            flat(units, 0),
            flat(rank, 0),
        ],
        out_specs=(whole(every, 2 * units), whole(every, rank)),
        scratch_shapes=[scratch[0], scratch[2]],
    )(got_raw, came, down_w, down_p, down_b)

    def back(last, pieces, at, *before):
        rows = sum(piece.shape[0] for piece in pieces)

        def block(columns):
            return pl.BlockSpec((rows, columns), lambda i: (at // rows, 0))

        outs = (shape((2 * rank if last else rank, every if last else rows), F32), shape((2 * rank, 2 * units), F32))
        return call(
            functools.partial(back_kernel, last, len(pieces)),
            outs,
            VMEM_MIB,
            flops=2 * rows * (width - early) * 2 * units,
            moved=2 * (width - early) * (rows + 2 * units),
            grid=((width - early) // DEPTH,),
            in_specs=piece_specs(pieces)
            + [flat(units, early)] * 2
            + [flat(rank, early)]
            + [block(2 * units), block(rank), block(2 * units), block(2 * units), block(rank)]
            + [whole(rank, units)] * 4
            + [whole(*value.shape) for value in before],
            out_specs=tuple(whole(*s.shape) for s in outs),
            scratch_shapes=[pltpu.VMEM((rows, 2 * units), F32), pltpu.VMEM((rows, rank), F32)],
        )(*pieces, down_w, down_p, down_b, back_0, low_0, factor, hidden, low_in, *small, *before)

    pieces_3 = (rows_back, *steps_3, *far_3)
    near = back(False, pieces_3[:3], 0)
    sums, grads = back(True, pieces_3[3:], 3 * slots, *near, sums_back)

    def in_order(value, order):
        return jnp.concatenate([value[:, i * slots : (i + 1) * slots] for i in order], axis=1)

    sums = (
        sums
        + in_order(shift_y(sums, 1), (2, 0, 3, 1))
        + in_order(shift_y(sums, -1), (1, 3, 0, 2))
        + in_order(shift_y(sums, 2), (3, 2, 1, 0))
    )
    me = lax.axis_index("seq").astype(jnp.int32).reshape(1)
    share = width // lax.axis_size("seq")
    anywhere = pl.BlockSpec(memory_space=pl.ANY)
    chunks = (*pieces_0, *pieces_1, *pieces_2, got_raw, *pieces_3)
    own, other = call(
        functools.partial(product_kernel, rank),
        (shape((2, rank, share), F32),) * 2,
        VMEM_MIB,
        flops=8 * rank * every * share,
        moved=8 * every * share,
        in_specs=[pl.BlockSpec(memory_space=pltpu.SMEM), whole(2 * rank, every), whole(every, 1)]
        + [anywhere] * len(chunks),
        scratch_shapes=[
            pltpu.VMEM((2, every, 2 * share), BF16),
            pltpu.SemaphoreType.DMA((21,)),
        ],
    )(me, sums, came, *chunks)
    result = own + swap_core(other)
    grad_hidden = grads[:, :units] + swap_core(grads[:, units:])
    return (result[:1], grad_hidden[None, :rank], grad_hidden[None, rank:], result[1:])


def solution(mesh):
    return jax.shard_map(
        body,
        mesh=mesh,
        in_specs=(
            P(("dp", "seq"), None),
            P(("dp", "seq"), None),
            P(("dp", "seq"), None),
            P(("dp", "seq"), None),
            P("dp", None, "seq"),
            P("dp", None, "seq"),
            P("dp", "seq", None),
            P("dp", None, None),
            P("dp", None, "seq"),
            P("dp", None, "seq"),
            P("dp", None, None),
        ),
        out_specs=(
            P("dp", None, "seq"),
            P("dp", None, "seq"),
            P("dp", None, "seq"),
            P("dp", None, "seq"),
        ),
        check_vma=False,
    )
```

time: 321 us -> 229 us (0.71); the launches traced: 320 us -> 225 us
  waiting for transfers between devices: 196 us -> 64.8 us
  Pallas kernels: 0 us -> 72.8 us
  matrix products: 52.9 us -> 0 us
  starting transfers between devices: 45.7 us -> 67.8 us
  other arithmetic: 8.29 us -> 4.84 us
    ppermute x11 -> x23, waiting for transfers between devices: 144 us -> 56.7 us  [shift_y(): return lax.ppermute(value, 'seq', pairs)]
    pallas_call x0 -> x17, Pallas kernels: none -> 72.8 us  [the longest x3 26.9 us: gate_up(): call(functools.partial(gate_up_kernel, begins, last), outs, VMEM_MIB, flo...]
    dot_general x34 -> x0, matrix products: 52.9 us -> none  [the longest x8 13.7 us: contract_last(): lax.dot_general(left, right, (((1,), (1,)), ((), ())), preferred_element_...]
    all_to_all x2, waiting for transfers between devices: 51.6 us -> 7.56 us  [across_dp(): lax.all_to_all(sent, 'dp', split_axis=0, concat_axis=0, tiled=True)]
    ppermute x11 -> x23, starting transfers between devices: 13.8 us -> 30.7 us  [shift_y(): return lax.ppermute(value, 'seq', pairs)]
    all_to_all x2, starting transfers between devices: 12.9 us -> 19.6 us  [across_dp(): lax.all_to_all(sent, 'dp', split_axis=0, concat_axis=0, tiled=True)]
    concatenate x2 -> x1, other arithmetic: 4.81 us -> 0.01 us  [body(): mine = (gate_w, up_w, down_w, jnp.concatenate([gate_b, down_a], axis=0))]
    slice x8 -> x3, local copies, waits for them, and re-layouts: 5.78 us -> 2.01 us  [the longest x1 0.76 us: body(): grad_hidden = grads[:, :units] + swap_core(grads[:, units:])]
  transfers between devices with their start and end apart: 20 -> 31, of which waited for: 11 -> 13; matrix products, arithmetic and copies ran while one was open for 16% -> 2% of each run, Pallas kernels for 0% -> 26%
where the time goes in v2:
time: 229 us; the launch traced here: 225 us
  Pallas kernels  72.8 us (32%)
  starting transfers between devices  67.8 us (30%)
  waiting for transfers between devices  64.8 us (28%)
  local copies, waits for them, and re-layouts  13.4 us (6%)
  other arithmetic  4.84 us (2%)
    ppermute x23, waiting for transfers between devices, shift_y(): return lax.ppermute(value, 'seq', pairs)  56.7 us
    ppermute x23, starting transfers between devices, shift_y(): return lax.ppermute(value, 'seq', pairs)  30.7 us
    pallas_call x3, Pallas kernels, gate_up(): call(functools.partial(gate_up_kernel, begins, last), outs, VMEM_MIB, flo...  26.9 us
    all_to_all x2, starting transfers between devices, across_dp(): lax.all_to_all(sent, 'dp', split_axis=0, concat_axis=0, tiled=True)  19.6 us
    ppermute x6, starting transfers between devices, swap_core(): return lax.ppermute(value, 'seq', [(i, i ^ 1) for i in range(size)])  17.4 us
    pallas_call x2, Pallas kernels, back(): call(functools.partial(back_kernel, last, len(pieces)), outs, VMEM_MIB, f...  13 us
    unnamed x58, local copies, waits for them, and re-layouts  10.6 us
    pallas_call x1, Pallas kernels, body(): call(raw_kernel, (totals[0], totals[2]), VMEM_MIB, flops=2 * every * earl...  10.3 us
  transfers between devices with their start and end apart: 31, of which 13 were waited for; matrix products, arithmetic and copies ran while one was open for 2% of the time, Pallas kernels for 26%

profile of v2, /device:TPU:1, one launch (start us, length us, event | category | flops | bytes accessed | tf_op | source)
XLA Modules:
  0.0 224.6 jit_solution(5203996392509643124)
XLA Ops:
  0.6 0.6 copy-done.19
  1.4 1.5 copy-done.9
  2.9 0.7 copy-done.17
  3.6 1.5 shard_map.139
  5.0 2.1 collective-permute-start.4
  7.2 1.4 collective-permute-start.5
  8.6 1.1 collective-permute-start
  10.5 2.0 shard_map.140
  12.6 1.7 copy-done.4
  14.2 7.8 %all-to-all-start = ((bf16[16,40,2560]{2,1,0:T(8,128)(2,1)}), bf16[16,40,2560]{2,1,0:T(8,128)(2,1)S(1)}, u32[]{:S(2)}, u32[]{:S(2)}) async-start(bf16[16,40,2560]{2,1,0:T(8,128)(2,1)} %bitcast.19), calls=%async_computation | async-start | bytes 6553600 | tf_op jit(solution)/shard_map/all_to_all | solution.py:423
  22.0 10.3 %collective-permute-done.4.before_ref.refs_1_.refs_6_ = bf16[128,4224]{1,0:T(8,128)(2,1)} collective-permute-done((bf16[128,4224]{1,0:T(8,128)(2,1)}, bf16[128,4224]{1,0:T(8,128)(2,1)}, u32[]{:S(2)}, u32[]{:S(2)}) %collective-permute-start.4) | collective-permute-done | bytes 1081376 | tf_op jit(solution)/shard_map/ppermute | solution.py:39
  32.4 1.2 shard_map.141
  33.6 0.9 collective-permute-start.6
  34.5 1.8 collective-permute-start.7
  36.4 1.2 fusion.18.came_ref
  37.5 9.7 %collective-permute-done.6.refs_3_.refs_8_ = bf16[64,4224]{1,0:T(8,128)(2,1)S(1)} collective-permute-done((bf16[64,4224]{1,0:T(8,128)(2,1)S(1)}, bf16[64,4224]{1,0:T(8,128)(2,1)S(1)}, u32[]{:S(2)}, u32[]{:S(2)}) %collective-permute-start.6) | collective-permute-done | bytes 540704 | tf_op jit(solution)/shard_map/ppermute | solution.py:39
  47.2 2.3 %collective-permute-start.3 = (bf16[32,256]{1,0:T(8,128)(2,1)S(1)}, bf16[32,256]{1,0:T(8,128)(2,1)S(1)}, u32[]{:S(2)}, u32[]{:S(2)}) collective-permute-start(bf16[32,256]{1,0:T(8,128)(2,1)S(1)} %pad_maximum_fusion), channel_id=1, source_target_pairs={{0,1},{1,0},{2,3},{3,2},{4,5},{5,4},{6,7},{7,6},{8,9},{9,8},{10,11... | collective-permute-start | bytes 49160 | tf_op jit(solution)/shard_map/ppermute | solution.py:44
  49.6 0.9 copy-done.28
  50.4 7.7 %shard_map.142 = bf16[640,4096]{1,0:T(8,128)(2,1)} custom-call(s32[640,1]{1,0:T(8,128)} %copy-done.16, s32[640,1]{1,0:T(8,128)} %copy-done.15, bf16[128,4224]{1,0:T(8,128)(2,1)} %get-tuple-element.69.refs_0_.refs_5_, bf16[128,4224]{1,0:T(8,128)(2,1)} %collective-permute-done.4.before_ref.refs_1_.refs_6_, ...), custom_call_target="tpu_custom_call" | custom-call | flops 21474836480 | bytes 75497472 | tf_op jit(solution)/shard_map/pallas_call | solution.py:440
  58.1 7.6 %all-to-all-done = bf16[16,40,2560]{2,1,0:T(8,128)(2,1)S(1)} async-done(((bf16[16,40,2560]{2,1,0:T(8,128)(2,1)}), bf16[16,40,2560]{2,1,0:T(8,128)(2,1)S(1)}, u32[]{:S(2)}, u32[]{:S(2)}) %all-to-all-start) | async-done | bytes 3276832 | tf_op jit(solution)/shard_map/all_to_all | solution.py:423
  65.7 1.0 copy-done.10
  66.7 2.8 %shard_map.143 = (bf16[160,2048]{1,0:T(8,128)(2,1)S(1)}, bf16[160,2048]{1,0:T(8,128)(2,1)}, bf16[160,3072]{1,0:T(8,128)(2,1)S(1)}, bf16[160,3072]{1,0:T(8,128)(2,1)S(1)}) custom-call(bf16[640,2560]{1,0:T(8,128)(2,1)S(1)} %bitcast.18, s32[640,1]{1,0:T(8,128)S(1)} %copy-done.10), custom_call_target="tpu_custom_call" | custom-call | flops 16777216000 | bytes 52428800 | tf_op jit(solution)/shard_map/pallas_call | solution.py:426
  69.5 1.0 copy-done.11
  70.5 0.9 copy-done.12
  71.4 2.7 %collective-permute-start.9 = (bf16[160,2048]{1,0:T(8,128)(2,1)S(1)}, bf16[160,2048]{1,0:T(8,128)(2,1)S(1)}, u32[]{:S(2)}, u32[]{:S(2)}) collective-permute-start(bf16[160,2048]{1,0:T(8,128)(2,1)S(1)} %get-tuple-element.75.refs_0_), channel_id=1, source_target_pairs={{0,6},{1,7},{2,0},{3,1},{4,2},{5,3},{6,4},{7,5},{8,14},{9,15},{10,... | collective-permute-start | bytes 1966088 | tf_op jit(solution)/shard_map/ppermute | solution.py:39
  74.1 13.1 %collective-permute-done.8.before_ref.refs_1_ = bf16[160,2048]{1,0:T(8,128)(2,1)S(1)} collective-permute-done((bf16[160,2048]{1,0:T(8,128)(2,1)S(1)}, bf16[160,2048]{1,0:T(8,128)(2,1)S(1)}, u32[]{:S(2)}, u32[]{:S(2)}) %collective-permute-start.8) | collective-permute-done | bytes 655392 | tf_op jit(solution)/shard_map/ppermute | solution.py:39
  87.3 2.7 %collective-permute-start.11 = (bf16[160,2048]{1,0:T(8,128)(2,1)}, bf16[160,2048]{1,0:T(8,128)(2,1)S(1)}, u32[]{:S(2)}, u32[]{:S(2)}) collective-permute-start(bf16[160,2048]{1,0:T(8,128)(2,1)} %get-tuple-element.77.refs_0_.refs_5_), channel_id=1, source_target_pairs={{0,6},{1,7},{2,0},{3,1},{4,2},{5,3},{6,4},{7,5},{8,14},{9,15},{10,... | collective-permute-start | bytes 1966088 | tf_op jit(solution)/shard_map/ppermute | solution.py:39
  90.3 2.7 %collective-permute-start.13 = (bf16[80,2048]{1,0:T(8,128)(2,1)S(1)}, bf16[80,2048]{1,0:T(8,128)(2,1)}, u32[]{:S(2)}, u32[]{:S(2)}) collective-permute-start(bf16[80,2048]{1,0:T(8,128)(2,1)S(1)} %get-tuple-element.81), channel_id=1, source_target_pairs={{0,6},{1,7},{2,0},{3,1},{4,2},{5,3},{6,4},{7,5},{8,14},{9,15},{10,... | collective-permute-start | bytes 983048 | tf_op jit(solution)/shard_map/ppermute | solution.py:39
  92.9 11.9 %all-to-all-start.1 = ((bf16[16,40,4096]{2,1,0:T(8,128)(2,1)}), bf16[16,40,4096]{2,1,0:T(8,128)(2,1)}, u32[]{:S(2)}, u32[]{:S(2)}) async-start(bf16[16,40,4096]{2,1,0:T(8,128)(2,1)} %bitcast.22), calls=%async_computation.1 | async-start | bytes 10485760 | tf_op jit(solution)/shard_map/all_to_all | solution.py:423
  105.4 4.0 %collective-permute-done.12.refs_3_ = bf16[80,2048]{1,0:T(8,128)(2,1)} collective-permute-done((bf16[80,2048]{1,0:T(8,128)(2,1)S(1)}, bf16[80,2048]{1,0:T(8,128)(2,1)}, u32[]{:S(2)}, u32[]{:S(2)}) %collective-permute-start.12) | collective-permute-done | bytes 327712 | tf_op jit(solution)/shard_map/ppermute | solution.py:39
  109.8 2.4 %collective-permute-start.15 = (bf16[160,3072]{1,0:T(8,128)(2,1)}, bf16[160,3072]{1,0:T(8,128)(2,1)S(1)}, u32[]{:S(2)}, u32[]{:S(2)}) collective-permute-start(bf16[160,3072]{1,0:T(8,128)(2,1)} %copy-done.11), channel_id=1, source_target_pairs={{0,6},{1,7},{2,0},{3,1},{4,2},{5,3},{6,4},{7,5},{8,14},{9,15},{10,... | collective-permute-start | bytes 2949128 | tf_op jit(solution)/shard_map/ppermute | solution.py:39
  112.5 2.7 %collective-permute-start.19 = (bf16[80,2048]{1,0:T(8,128)(2,1)S(1)}, bf16[80,2048]{1,0:T(8,128)(2,1)S(1)}, u32[]{:S(2)}, u32[]{:S(2)}) collective-permute-start(bf16[80,2048]{1,0:T(8,128)(2,1)S(1)} %get-tuple-element.98), channel_id=1, source_target_pairs={{0,6},{1,7},{2,0},{3,1},{4,2},{5,3},{6,4},{7,5},{8,14},{9,15},{10,... | collective-permute-start | bytes 983048 | tf_op jit(solution)/shard_map/ppermute | solution.py:39
  115.2 6.8 %shard_map.145 = (f32[640,512]{1,0:T(8,128)}, f32[640,512]{1,0:T(8,128)}, f32[640,16]{1,0:T(8,128)}) custom-call(bf16[160,2048]{1,0:T(8,128)(2,1)} %copy-done.14, bf16[160,2048]{1,0:T(8,128)(2,1)} %copy-done.5, bf16[160,2048]{1,0:T(8,128)(2,1)} %copy-done.6, bf16[80,2048]{1,0:T(8,128)(2,1)} %collective-permute-done.12.refs_3_, ...), custom_call_target="tpu_custom_call" | custom-call | flops 21474836480 | bytes 54525952 | tf_op jit(solution)/shard_map/pallas_call | solution.py:484
  122.0 8.8 %collective-permute-done.14.before_ref.refs_1_.refs_11_ = bf16[160,3072]{1,0:T(8,128)(2,1)S(1)} collective-permute-done((bf16[160,3072]{1,0:T(8,128)(2,1)}, bf16[160,3072]{1,0:T(8,128)(2,1)S(1)}, u32[]{:S(2)}, u32[]{:S(2)}) %collective-permute-start.14) | collective-permute-done | bytes 983072 | tf_op jit(solution)/shard_map/ppermute | solution.py:39
  130.8 0.6 shard_map.146
  131.7 2.5 %collective-permute-start.17 = (bf16[80,3072]{1,0:T(8,128)(2,1)S(1)}, bf16[80,3072]{1,0:T(8,128)(2,1)S(1)}, u32[]{:S(2)}, u32[]{:S(2)}) collective-permute-start(bf16[80,3072]{1,0:T(8,128)(2,1)S(1)} %get-tuple-element.94), channel_id=1, source_target_pairs={{0,6},{1,7},{2,0},{3,1},{4,2},{5,3},{6,4},{7,5},{8,14},{9,15},{10,... | collective-permute-start | bytes 1474568 | tf_op jit(solution)/shard_map/ppermute | solution.py:39
  134.2 3.6 %collective-permute-done.18.refs_3_.refs_8_ = bf16[80,2048]{1,0:T(8,128)(2,1)S(1)} collective-permute-done((bf16[80,2048]{1,0:T(8,128)(2,1)S(1)}, bf16[80,2048]{1,0:T(8,128)(2,1)S(1)}, u32[]{:S(2)}, u32[]{:S(2)}) %collective-permute-start.18) | collective-permute-done | bytes 327712 | tf_op jit(solution)/shard_map/ppermute | solution.py:39
  137.8 0.7 copy-done.23
  138.5 0.7 copy-done.24
  139.3 8.3 %shard_map.148 = (f32[640,512]{1,0:T(8,128)}, f32[640,512]{1,0:T(8,128)}, f32[640,16]{1,0:T(8,128)}) custom-call(bf16[160,2048]{1,0:T(8,128)(2,1)} %get-tuple-element.77.refs_0_.refs_5_, bf16[160,2048]{1,0:T(8,128)(2,1)} %copy-done.7, bf16[160,2048]{1,0:T(8,128)(2,1)} %copy-done.8, bf16[80,2048]{1,0:T(8,128)(2,1)} %copy-done.23, ...), custom_call_target="tpu_custom_call" | custom-call | flops 21474836480 | bytes 54525952 | tf_op jit(solution)/shard_map/pallas_call | solution.py:484
  147.6 0.8 collective-permute-done.16.refs_3_.refs_13_
  148.5 2.6 %collective-permute-start.21 = (bf16[160,3072]{1,0:T(8,128)(2,1)S(1)}, bf16[160,3072]{1,0:T(8,128)(2,1)S(1)}, u32[]{:S(2)}, u32[]{:S(2)}) collective-permute-start(bf16[160,3072]{1,0:T(8,128)(2,1)S(1)} %copy-done.13), channel_id=1, source_target_pairs={{0,6},{1,7},{2,0},{3,1},{4,2},{5,3},{6,4},{7,5},{8,14},{9,15},{10,... | collective-permute-start | bytes 2949128 | tf_op jit(solution)/shard_map/ppermute | solution.py:39
  151.1 11.9 %shard_map.149 = (bf16[640,512]{1,0:T(8,128)(2,1)}, f32[640,512]{1,0:T(8,128)}, bf16[640,16]{1,0:T(8,128)(2,1)}, f32[16,640]{1,0:T(8,128)}) custom-call(bf16[160,3072]{1,0:T(8,128)(2,1)} %copy-done.11, bf16[160,3072]{1,0:T(8,128)(2,1)} %copy-done, bf16[160,3072]{1,0:T(8,128)(2,1)} %copy-done.1, bf16[80,3072]{1,0:T(8,128)(2,1)} %copy-done.20, ...), custom_call_target="tpu_custom_call" | custom-call | flops 32212254720 | bytes 81788928 | tf_op jit(solution)/shard_map/pallas_call | solution.py:484
  163.0 2.3 %collective-permute-done.20.before_ref.refs_1_.refs_17_ = bf16[160,3072]{1,0:T(8,128)(2,1)S(1)} collective-permute-done((bf16[160,3072]{1,0:T(8,128)(2,1)S(1)}, bf16[160,3072]{1,0:T(8,128)(2,1)S(1)}, u32[]{:S(2)}, u32[]{:S(2)}) %collective-permute-start.20) | collective-permute-done | bytes 983072 | tf_op jit(solution)/shard_map/ppermute | solution.py:39
  165.3 0.6 shard_map.150
  166.2 2.5 %collective-permute-start.23 = (bf16[80,3072]{1,0:T(8,128)(2,1)S(1)}, bf16[80,3072]{1,0:T(8,128)(2,1)}, u32[]{:S(2)}, u32[]{:S(2)}) collective-permute-start(bf16[80,3072]{1,0:T(8,128)(2,1)S(1)} %get-tuple-element.117), channel_id=1, source_target_pairs={{0,6},{1,7},{2,0},{3,1},{4,2},{5,3},{6,4},{7,5},{8,14},{9,15},{10,... | collective-permute-start | bytes 1474568 | tf_op jit(solution)/shard_map/ppermute | solution.py:39
  168.8 10.3 %shard_map.151 = (f32[640,512]{1,0:T(8,128)}, f32[640,16]{1,0:T(8,128)}) custom-call(bf16[640,4096]{1,0:T(8,128)(2,1)} %bitcast.13.got_ref.refs_15_, s32[640,1]{1,0:T(8,128)} %fusion.18.came_ref, bf16[256,7168]{1,0:T(8,128)(2,1)} %bitcast.40, bf16[256,7168]{1,0:T(8,128)(2,1)} %collective-permute-done.2.down_p.refs_4_.refs_3_, bf16[16,7168]{1,0:T(8,128)(2,1)} %bitcast.46), custom_call_target="tpu_custom_call" | custom-call | flops 21474836480 | bytes 75497472 | tf_op jit(solution)/shard_map/pallas_call | solution.py:521
  179.1 7.4 %shard_map.152 = (f32[16,480]{1,0:T(8,128)}, f32[32,512]{1,0:T(8,128)}) custom-call(bf16[160,3072]{1,0:T(8,128)(2,1)} %copy-done.12, bf16[160,3072]{1,0:T(8,128)(2,1)} %copy-done.2, bf16[160,3072]{1,0:T(8,128)(2,1)} %copy-done.3, bf16[256,7168]{1,0:T(8,128)(2,1)} %bitcast.41, bf16[256,7168]{1,0:T(8,128)(2,1)} %collective-permute-done.2.down_p.refs_4_.refs_3_, ...), custom_call_target="tpu_custom_call" | custom-call | flops 12079595520 | bytes 48758784 | tf_op jit(solution)/shard_map/pallas_call | solution.py:546
  186.6 0.8 copy-done.22
  187.4 5.5 %shard_map.153 = (f32[32,640]{1,0:T(8,128)}, f32[32,512]{1,0:T(8,128)}) custom-call(bf16[80,3072]{1,0:T(8,128)(2,1)} %copy-done.22, bf16[80,3072]{1,0:T(8,128)(2,1)} %collective-permute-done.23.refs_1_.refs_20_, bf16[256,7168]{1,0:T(8,128)(2,1)} %bitcast.42, bf16[256,7168]{1,0:T(8,128)(2,1)} %collective-permute-done.2.down_p.refs_4_.refs_3_, ...), custom_call_target="tpu_custom_call" | custom-call | flops 4026531840 | bytes 33030144 | tf_op jit(solution)/shard_map/pallas_call | solution.py:546
  192.9 0.8 slice.76
  193.7 12.4 %collective-permute-start.28 = (f32[32,256]{1,0:T(8,128)S(1)}, f32[32,256]{1,0:T(8,128)S(1)}, u32[]{:S(2)}, u32[]{:S(2)}) collective-permute-start(f32[32,256]{1,0:T(8,128)S(1)} %slice.76), channel_id=1, source_target_pairs={{0,1},{1,0},{2,3},{3,2},{4,5},{5,4},{6,7},{7,6},{8,9},{9,8},{10,11... | collective-permute-start | bytes 98312 | tf_op jit(solution)/shard_map/ppermute | solution.py:44
  206.1 0.9 collective-permute-start.26
  207.0 0.7 collective-permute-start.25
  207.7 0.8 collective-permute-start.24
  208.5 0.8 slice_add_fusion
  209.2 2.6 %collective-permute-done.26 = f32[32,640]{1,0:T(8,128)S(1)} collective-permute-done((f32[32,640]{1,0:T(8,128)}, f32[32,640]{1,0:T(8,128)S(1)}, u32[]{:S(2)}, u32[]{:S(2)}) %collective-permute-start.26) | collective-permute-done | bytes 81952 | tf_op jit(solution)/shard_map/ppermute | solution.py:39
  212.0 0.7 collective-permute-done.25
  212.7 0.7 collective-permute-done.24
  213.5 1.7 fusion.27.sums_ref
  215.2 5.6 %shard_map.154 = (f32[2,16,896]{2,1,0:T(8,128)}, f32[2,16,896]{2,1,0:T(8,128)}) custom-call(s32[1]{0:T(128)} %bitcast.me_ref, f32[32,640]{1,0:T(8,128)} %fusion.27.sums_ref, s32[640,1]{1,0:T(8,128)} %fusion.18.came_ref, bf16[160,2048]{1,0:T(8,128)(2,1)} %copy-done.14, bf16[160,2048]{1,0:T(8,128)(2,1)} %copy-done.5, bf16[160,2048]{1,0:T(8,128)(2,1)} %copy-done.6, ...), custom_call_target="tpu_custom_call" | custom-call | flops 587202560 | bytes 36700160 | tf_op jit(solution)/shard_map/pallas_call | solution.py:580
  220.8 1.1 collective-permute-start.27
  223.1 0.9 add.145
  224.0 0.6 fusion.28
  (86 shorter events, 4.8 us)
Async XLA Ops:
  0.6 0.7 copy-start.19
  1.4 1.5 copy-start.9
  2.9 0.7 copy-start.17
  3.6 6.9 %copy-start.18 = (bf16[128,7168]{1,0:T(8,128)(2,1)S(1)}, bf16[128,7168]{1,0:T(8,128)(2,1)}, u32[]{:S(2)}) copy-start(bf16[128,7168]{1,0:T(8,128)(2,1)} %refs_2_.1) | copy-start | bytes 5505028
  5.0 27.3 %collective-permute-start.4 = (bf16[128,4224]{1,0:T(8,128)(2,1)}, bf16[128,4224]{1,0:T(8,128)(2,1)}, u32[]{:S(2)}, u32[]{:S(2)}) collective-permute-start(bf16[128,4224]{1,0:T(8,128)(2,1)} %get-tuple-element.69.refs_0_.refs_5_), channel_id=1, source_target_pairs={{0,2},{1,3},{2,4},{3,5},{4,6},{5,7},{6,0},{7,1},{8,10},{9,11},{10,... | collective-permute-start | bytes 3244040 | tf_op jit(solution)/shard_map/ppermute | solution.py:39
  7.2 25.2 %collective-permute-start.5 = (bf16[128,4224]{1,0:T(8,128)(2,1)}, bf16[128,4224]{1,0:T(8,128)(2,1)}, u32[]{:S(2)}, u32[]{:S(2)}) collective-permute-start(bf16[128,4224]{1,0:T(8,128)(2,1)} %get-tuple-element.69.refs_0_.refs_5_), channel_id=1, source_target_pairs={{0,6},{1,7},{2,0},{3,1},{4,2},{5,3},{6,4},{7,5},{8,14},{9,15},{10,... | collective-permute-start | bytes 3244040 | tf_op jit(solution)/shard_map/ppermute | solution.py:39
  8.6 57.1 %collective-permute-start = (bf16[7168,256]{1,0:T(8,128)(2,1)}, bf16[7168,256]{1,0:T(8,128)(2,1)}, u32[]{:S(2)}, u32[]{:S(2)}) collective-permute-start(bf16[7168,256]{1,0:T(8,128)(2,1)} %bitcast.31), channel_id=1, source_target_pairs={{0,1},{1,0},{2,3},{3,2},{4,5},{5,4},{6,7},{7,6},{8,9},{9,8},{10,11... | collective-permute-start | bytes 11010056 | tf_op jit(solution)/shard_map/ppermute | solution.py:44
  9.7 56.0 %collective-permute-start.1 = (bf16[7168,256]{1,0:T(8,128)(2,1)}, bf16[7168,256]{1,0:T(8,128)(2,1)}, u32[]{:S(2)}, u32[]{:S(2)}) collective-permute-start(bf16[7168,256]{1,0:T(8,128)(2,1)} %bitcast.35), channel_id=1, source_target_pairs={{0,1},{1,0},{2,3},{3,2},{4,5},{5,4},{6,7},{7,6},{8,9},{9,8},{10,11... | collective-permute-start | bytes 11010056 | tf_op jit(solution)/shard_map/ppermute | solution.py:44
  9.7 56.0 %collective-permute-start.2 = (bf16[256,7168]{1,0:T(8,128)(2,1)}, bf16[256,7168]{1,0:T(8,128)(2,1)}, u32[]{:S(2)}, u32[]{:S(2)}) collective-permute-start(bf16[256,7168]{1,0:T(8,128)(2,1)} %bitcast.39), channel_id=1, source_target_pairs={{0,1},{1,0},{2,3},{3,2},{4,5},{5,4},{6,7},{7,6},{8,9},{9,8},{10,11... | collective-permute-start | bytes 11010056 | tf_op jit(solution)/shard_map/ppermute | solution.py:44
  10.5 2.0 copy-start.15
  10.5 2.0 copy-start.16
  12.6 1.7 copy-start.4
  14.2 51.5 %all-to-all-start = ((bf16[16,40,2560]{2,1,0:T(8,128)(2,1)}), bf16[16,40,2560]{2,1,0:T(8,128)(2,1)S(1)}, u32[]{:S(2)}, u32[]{:S(2)}) async-start(bf16[16,40,2560]{2,1,0:T(8,128)(2,1)} %bitcast.19), calls=%async_computation | async-start | bytes 6553600 | tf_op jit(solution)/shard_map/all_to_all | solution.py:423
  22.0 14.3 %copy-start.25 = (bf16[1,16,256]{2,1,0:T(8,128)(2,1)S(1)}, bf16[1,16,256]{2,1,0:T(8,128)(2,1)}, u32[]{:S(2)}) copy-start(bf16[1,16,256]{2,1,0:T(8,128)(2,1)} %param.19) | copy-start | bytes 24580
  22.0 14.3 %copy-start.26 = (bf16[1,16,256]{2,1,0:T(8,128)(2,1)S(1)}, bf16[1,16,256]{2,1,0:T(8,128)(2,1)}, u32[]{:S(2)}) copy-start(bf16[1,16,256]{2,1,0:T(8,128)(2,1)} %param.20) | copy-start | bytes 24580
  33.6 13.6 %collective-permute-start.6 = (bf16[64,4224]{1,0:T(8,128)(2,1)S(1)}, bf16[64,4224]{1,0:T(8,128)(2,1)S(1)}, u32[]{:S(2)}, u32[]{:S(2)}) collective-permute-start(bf16[64,4224]{1,0:T(8,128)(2,1)S(1)} %get-tuple-element.70), channel_id=1, source_target_pairs={{0,2},{1,3},{2,4},{3,5},{4,6},{5,7},{6,0},{7,1},{8,10},{9,11},{10,... | collective-permute-start | bytes 1622024 | tf_op jit(solution)/shard_map/ppermute | solution.py:39
  34.5 15.1 %collective-permute-start.7 = (bf16[64,4224]{1,0:T(8,128)(2,1)S(1)}, bf16[64,4224]{1,0:T(8,128)(2,1)S(1)}, u32[]{:S(2)}, u32[]{:S(2)}) collective-permute-start(bf16[64,4224]{1,0:T(8,128)(2,1)S(1)} %get-tuple-element.71), channel_id=1, source_target_pairs={{0,6},{1,7},{2,0},{3,1},{4,2},{5,3},{6,4},{7,5},{8,14},{9,15},{10,... | collective-permute-start | bytes 1622024 | tf_op jit(solution)/shard_map/ppermute | solution.py:39
  47.2 2.3 %copy-start.27 = (bf16[64,4224]{1,0:T(8,128)(2,1)}, bf16[64,4224]{1,0:T(8,128)(2,1)S(1)}, u32[]{:S(2)}) copy-start(bf16[64,4224]{1,0:T(8,128)(2,1)S(1)} %collective-permute-done.6.refs_3_.refs_8_) | copy-start | bytes 1622020
  47.2 10.9 %collective-permute-start.3 = (bf16[32,256]{1,0:T(8,128)(2,1)S(1)}, bf16[32,256]{1,0:T(8,128)(2,1)S(1)}, u32[]{:S(2)}, u32[]{:S(2)}) collective-permute-start(bf16[32,256]{1,0:T(8,128)(2,1)S(1)} %pad_maximum_fusion), channel_id=1, source_target_pairs={{0,1},{1,0},{2,3},{3,2},{4,5},{5,4},{6,7},{7,6},{8,9},{9,8},{10,11... | collective-permute-start | bytes 49160 | tf_op jit(solution)/shard_map/ppermute | solution.py:44
  49.6 0.9 copy-start.28
  65.7 1.0 copy-start.10
  69.5 1.0 copy-start.11
  70.5 1.0 copy-start.12
  71.4 15.8 %copy-start.14 = (bf16[160,2048]{1,0:T(8,128)(2,1)}, bf16[160,2048]{1,0:T(8,128)(2,1)S(1)}, u32[]{:S(2)}) copy-start(bf16[160,2048]{1,0:T(8,128)(2,1)S(1)} %get-tuple-element.75.refs_0_) | copy-start | bytes 1966084
  71.4 15.8 %collective-permute-start.8 = (bf16[160,2048]{1,0:T(8,128)(2,1)S(1)}, bf16[160,2048]{1,0:T(8,128)(2,1)S(1)}, u32[]{:S(2)}, u32[]{:S(2)}) collective-permute-start(bf16[160,2048]{1,0:T(8,128)(2,1)S(1)} %get-tuple-element.75.refs_0_), channel_id=1, source_target_pairs={{0,2},{1,3},{2,4},{3,5},{4,6},{5,7},{6,0},{7,1},{8,10},{9,11},{10,... | collective-permute-start | bytes 1966088 | tf_op jit(solution)/shard_map/ppermute | solution.py:39
  71.4 15.8 %collective-permute-start.9 = (bf16[160,2048]{1,0:T(8,128)(2,1)S(1)}, bf16[160,2048]{1,0:T(8,128)(2,1)S(1)}, u32[]{:S(2)}, u32[]{:S(2)}) collective-permute-start(bf16[160,2048]{1,0:T(8,128)(2,1)S(1)} %get-tuple-element.75.refs_0_), channel_id=1, source_target_pairs={{0,6},{1,7},{2,0},{3,1},{4,2},{5,3},{6,4},{7,5},{8,14},{9,15},{10,... | collective-permute-start | bytes 1966088 | tf_op jit(solution)/shard_map/ppermute | solution.py:39
  87.2 5.7 %copy-start.5 = (bf16[160,2048]{1,0:T(8,128)(2,1)}, bf16[160,2048]{1,0:T(8,128)(2,1)S(1)}, u32[]{:S(2)}) copy-start(bf16[160,2048]{1,0:T(8,128)(2,1)S(1)} %collective-permute-done.8.before_ref.refs_1_) | copy-start | bytes 1966084
  87.2 5.7 %copy-start.6 = (bf16[160,2048]{1,0:T(8,128)(2,1)}, bf16[160,2048]{1,0:T(8,128)(2,1)S(1)}, u32[]{:S(2)}) copy-start(bf16[160,2048]{1,0:T(8,128)(2,1)S(1)} %collective-permute-done.9.after_ref.refs_2_) | copy-start | bytes 1966084
  87.2 22.2 %collective-permute-start.10 = (bf16[160,2048]{1,0:T(8,128)(2,1)}, bf16[160,2048]{1,0:T(8,128)(2,1)S(1)}, u32[]{:S(2)}, u32[]{:S(2)}) collective-permute-start(bf16[160,2048]{1,0:T(8,128)(2,1)} %get-tuple-element.77.refs_0_.refs_5_), channel_id=1, source_target_pairs={{0,2},{1,3},{2,4},{3,5},{4,6},{5,7},{6,0},{7,1},{8,10},{9,11},{10,... | collective-permute-start | bytes 1966088 | tf_op jit(solution)/shard_map/ppermute | solution.py:39
  87.3 22.2 %collective-permute-start.11 = (bf16[160,2048]{1,0:T(8,128)(2,1)}, bf16[160,2048]{1,0:T(8,128)(2,1)S(1)}, u32[]{:S(2)}, u32[]{:S(2)}) collective-permute-start(bf16[160,2048]{1,0:T(8,128)(2,1)} %get-tuple-element.77.refs_0_.refs_5_), channel_id=1, source_target_pairs={{0,6},{1,7},{2,0},{3,1},{4,2},{5,3},{6,4},{7,5},{8,14},{9,15},{10,... | collective-permute-start | bytes 1966088 | tf_op jit(solution)/shard_map/ppermute | solution.py:39
  90.2 19.3 %collective-permute-start.12 = (bf16[80,2048]{1,0:T(8,128)(2,1)S(1)}, bf16[80,2048]{1,0:T(8,128)(2,1)}, u32[]{:S(2)}, u32[]{:S(2)}) collective-permute-start(bf16[80,2048]{1,0:T(8,128)(2,1)S(1)} %get-tuple-element.80), channel_id=1, source_target_pairs={{0,2},{1,3},{2,4},{3,5},{4,6},{5,7},{6,0},{7,1},{8,10},{9,11},{10,... | collective-permute-start | bytes 983048 | tf_op jit(solution)/shard_map/ppermute | solution.py:39
  90.3 19.2 %collective-permute-start.13 = (bf16[80,2048]{1,0:T(8,128)(2,1)S(1)}, bf16[80,2048]{1,0:T(8,128)(2,1)}, u32[]{:S(2)}, u32[]{:S(2)}) collective-permute-start(bf16[80,2048]{1,0:T(8,128)(2,1)S(1)} %get-tuple-element.81), channel_id=1, source_target_pairs={{0,6},{1,7},{2,0},{3,1},{4,2},{5,3},{6,4},{7,5},{8,14},{9,15},{10,... | collective-permute-start | bytes 983048 | tf_op jit(solution)/shard_map/ppermute | solution.py:39
  92.9 75.9 %all-to-all-start.1 = ((bf16[16,40,4096]{2,1,0:T(8,128)(2,1)}), bf16[16,40,4096]{2,1,0:T(8,128)(2,1)}, u32[]{:S(2)}, u32[]{:S(2)}) async-start(bf16[16,40,4096]{2,1,0:T(8,128)(2,1)} %bitcast.22), calls=%async_computation.1 | async-start | bytes 10485760 | tf_op jit(solution)/shard_map/all_to_all | solution.py:423
  109.4 12.5 %copy-start.7 = (bf16[160,2048]{1,0:T(8,128)(2,1)}, bf16[160,2048]{1,0:T(8,128)(2,1)S(1)}, u32[]{:S(2)}) copy-start(bf16[160,2048]{1,0:T(8,128)(2,1)S(1)} %collective-permute-done.10.before_ref.refs_1_.refs_6_) | copy-start | bytes 1966084
  109.5 12.5 %copy-start.8 = (bf16[160,2048]{1,0:T(8,128)(2,1)}, bf16[160,2048]{1,0:T(8,128)(2,1)S(1)}, u32[]{:S(2)}) copy-start(bf16[160,2048]{1,0:T(8,128)(2,1)S(1)} %collective-permute-done.11.after_ref.refs_2_.refs_7_) | copy-start | bytes 1966084
  109.5 21.3 %collective-permute-start.14 = (bf16[160,3072]{1,0:T(8,128)(2,1)}, bf16[160,3072]{1,0:T(8,128)(2,1)S(1)}, u32[]{:S(2)}, u32[]{:S(2)}) collective-permute-start(bf16[160,3072]{1,0:T(8,128)(2,1)} %copy-done.11), channel_id=1, source_target_pairs={{0,2},{1,3},{2,4},{3,5},{4,6},{5,7},{6,0},{7,1},{8,10},{9,11},{10,... | collective-permute-start | bytes 2949128 | tf_op jit(solution)/shard_map/ppermute | solution.py:39
  109.8 21.0 %collective-permute-start.15 = (bf16[160,3072]{1,0:T(8,128)(2,1)}, bf16[160,3072]{1,0:T(8,128)(2,1)S(1)}, u32[]{:S(2)}, u32[]{:S(2)}) collective-permute-start(bf16[160,3072]{1,0:T(8,128)(2,1)} %copy-done.11), channel_id=1, source_target_pairs={{0,6},{1,7},{2,0},{3,1},{4,2},{5,3},{6,4},{7,5},{8,14},{9,15},{10,... | collective-permute-start | bytes 2949128 | tf_op jit(solution)/shard_map/ppermute | solution.py:39
  112.4 25.4 %collective-permute-start.18 = (bf16[80,2048]{1,0:T(8,128)(2,1)S(1)}, bf16[80,2048]{1,0:T(8,128)(2,1)S(1)}, u32[]{:S(2)}, u32[]{:S(2)}) collective-permute-start(bf16[80,2048]{1,0:T(8,128)(2,1)S(1)} %get-tuple-element.97), channel_id=1, source_target_pairs={{0,2},{1,3},{2,4},{3,5},{4,6},{5,7},{6,0},{7,1},{8,10},{9,11},{10,... | collective-permute-start | bytes 983048 | tf_op jit(solution)/shard_map/ppermute | solution.py:39
  112.5 25.3 %collective-permute-start.19 = (bf16[80,2048]{1,0:T(8,128)(2,1)S(1)}, bf16[80,2048]{1,0:T(8,128)(2,1)S(1)}, u32[]{:S(2)}, u32[]{:S(2)}) collective-permute-start(bf16[80,2048]{1,0:T(8,128)(2,1)S(1)} %get-tuple-element.98), channel_id=1, source_target_pairs={{0,6},{1,7},{2,0},{3,1},{4,2},{5,3},{6,4},{7,5},{8,14},{9,15},{10,... | collective-permute-start | bytes 983048 | tf_op jit(solution)/shard_map/ppermute | solution.py:39
  130.8 16.8 %copy-start = (bf16[160,3072]{1,0:T(8,128)(2,1)}, bf16[160,3072]{1,0:T(8,128)(2,1)S(1)}, u32[]{:S(2)}) copy-start(bf16[160,3072]{1,0:T(8,128)(2,1)S(1)} %collective-permute-done.14.before_ref.refs_1_.refs_11_) | copy-start | bytes 2949124
  130.8 16.8 %copy-start.1 = (bf16[160,3072]{1,0:T(8,128)(2,1)}, bf16[160,3072]{1,0:T(8,128)(2,1)S(1)}, u32[]{:S(2)}) copy-start(bf16[160,3072]{1,0:T(8,128)(2,1)S(1)} %collective-permute-done.15.after_ref.refs_2_.refs_12_) | copy-start | bytes 2949124
  131.5 16.9 %collective-permute-start.16 = (bf16[80,3072]{1,0:T(8,128)(2,1)S(1)}, bf16[80,3072]{1,0:T(8,128)(2,1)S(1)}, u32[]{:S(2)}, u32[]{:S(2)}) collective-permute-start(bf16[80,3072]{1,0:T(8,128)(2,1)S(1)} %get-tuple-element.93), channel_id=1, source_target_pairs={{0,2},{1,3},{2,4},{3,5},{4,6},{5,7},{6,0},{7,1},{8,10},{9,11},{10,... | collective-permute-start | bytes 1474568 | tf_op jit(solution)/shard_map/ppermute | solution.py:39
  131.7 16.7 %copy-start.13 = (bf16[160,3072]{1,0:T(8,128)(2,1)S(1)}, bf16[160,3072]{1,0:T(8,128)(2,1)}, u32[]{:S(2)}) copy-start(bf16[160,3072]{1,0:T(8,128)(2,1)} %copy-done.12) | copy-start | bytes 2949124
  131.7 16.7 %collective-permute-start.17 = (bf16[80,3072]{1,0:T(8,128)(2,1)S(1)}, bf16[80,3072]{1,0:T(8,128)(2,1)S(1)}, u32[]{:S(2)}, u32[]{:S(2)}) collective-permute-start(bf16[80,3072]{1,0:T(8,128)(2,1)S(1)} %get-tuple-element.94), channel_id=1, source_target_pairs={{0,6},{1,7},{2,0},{3,1},{4,2},{5,3},{6,4},{7,5},{8,14},{9,15},{10,... | collective-permute-start | bytes 1474568 | tf_op jit(solution)/shard_map/ppermute | solution.py:39
  137.8 0.7 copy-start.23
  138.5 0.7 copy-start.24
  148.3 2.8 %copy-start.20 = (bf16[80,3072]{1,0:T(8,128)(2,1)}, bf16[80,3072]{1,0:T(8,128)(2,1)S(1)}, u32[]{:S(2)}) copy-start(bf16[80,3072]{1,0:T(8,128)(2,1)S(1)} %collective-permute-done.16.refs_3_.refs_13_) | copy-start | bytes 1474564
  148.4 2.8 %copy-start.21 = (bf16[80,3072]{1,0:T(8,128)(2,1)}, bf16[80,3072]{1,0:T(8,128)(2,1)S(1)}, u32[]{:S(2)}) copy-start(bf16[80,3072]{1,0:T(8,128)(2,1)S(1)} %collective-permute-done.17.refs_4_.refs_14_) | copy-start | bytes 1474564
  148.4 16.9 %collective-permute-start.20 = (bf16[160,3072]{1,0:T(8,128)(2,1)S(1)}, bf16[160,3072]{1,0:T(8,128)(2,1)S(1)}, u32[]{:S(2)}, u32[]{:S(2)}) collective-permute-start(bf16[160,3072]{1,0:T(8,128)(2,1)S(1)} %copy-done.13), channel_id=1, source_target_pairs={{0,2},{1,3},{2,4},{3,5},{4,6},{5,7},{6,0},{7,1},{8,10},{9,11},{10,... | collective-permute-start | bytes 2949128 | tf_op jit(solution)/shard_map/ppermute | solution.py:39
  148.5 16.7 %collective-permute-start.21 = (bf16[160,3072]{1,0:T(8,128)(2,1)S(1)}, bf16[160,3072]{1,0:T(8,128)(2,1)S(1)}, u32[]{:S(2)}, u32[]{:S(2)}) collective-permute-start(bf16[160,3072]{1,0:T(8,128)(2,1)S(1)} %copy-done.13), channel_id=1, source_target_pairs={{0,6},{1,7},{2,0},{3,1},{4,2},{5,3},{6,4},{7,5},{8,14},{9,15},{10,... | collective-permute-start | bytes 2949128 | tf_op jit(solution)/shard_map/ppermute | solution.py:39
  165.3 13.8 %copy-start.2 = (bf16[160,3072]{1,0:T(8,128)(2,1)}, bf16[160,3072]{1,0:T(8,128)(2,1)S(1)}, u32[]{:S(2)}) copy-start(bf16[160,3072]{1,0:T(8,128)(2,1)S(1)} %collective-permute-done.20.before_ref.refs_1_.refs_17_) | copy-start | bytes 2949124
  165.3 13.8 %copy-start.3 = (bf16[160,3072]{1,0:T(8,128)(2,1)}, bf16[160,3072]{1,0:T(8,128)(2,1)S(1)}, u32[]{:S(2)}) copy-start(bf16[160,3072]{1,0:T(8,128)(2,1)S(1)} %collective-permute-done.21.after_ref.refs_2_.refs_18_) | copy-start | bytes 2949124
  165.9 20.6 %collective-permute-start.22 = (bf16[80,3072]{1,0:T(8,128)(2,1)S(1)}, bf16[80,3072]{1,0:T(8,128)(2,1)S(1)}, u32[]{:S(2)}, u32[]{:S(2)}) collective-permute-start(bf16[80,3072]{1,0:T(8,128)(2,1)S(1)} %get-tuple-element.116), channel_id=1, source_target_pairs={{0,2},{1,3},{2,4},{3,5},{4,6},{5,7},{6,0},{7,1},{8,10},{9,11},{10,... | collective-permute-start | bytes 1474568 | tf_op jit(solution)/shard_map/ppermute | solution.py:39
  166.2 20.3 %collective-permute-start.23 = (bf16[80,3072]{1,0:T(8,128)(2,1)S(1)}, bf16[80,3072]{1,0:T(8,128)(2,1)}, u32[]{:S(2)}, u32[]{:S(2)}) collective-permute-start(bf16[80,3072]{1,0:T(8,128)(2,1)S(1)} %get-tuple-element.117), channel_id=1, source_target_pairs={{0,6},{1,7},{2,0},{3,1},{4,2},{5,3},{6,4},{7,5},{8,14},{9,15},{10,... | collective-permute-start | bytes 1474568 | tf_op jit(solution)/shard_map/ppermute | solution.py:39
  186.5 0.8 copy-start.22
  193.7 14.8 %collective-permute-start.28 = (f32[32,256]{1,0:T(8,128)S(1)}, f32[32,256]{1,0:T(8,128)S(1)}, u32[]{:S(2)}, u32[]{:S(2)}) collective-permute-start(f32[32,256]{1,0:T(8,128)S(1)} %slice.76), channel_id=1, source_target_pairs={{0,1},{1,0},{2,3},{3,2},{4,5},{5,4},{6,7},{7,6},{8,9},{9,8},{10,11... | collective-permute-start | bytes 98312 | tf_op jit(solution)/shard_map/ppermute | solution.py:44
  206.1 5.8 %collective-permute-start.26 = (f32[32,640]{1,0:T(8,128)}, f32[32,640]{1,0:T(8,128)S(1)}, u32[]{:S(2)}, u32[]{:S(2)}) collective-permute-start(f32[32,640]{1,0:T(8,128)} %get-tuple-element.128), channel_id=1, source_target_pairs={{0,4},{1,5},{2,6},{3,7},{4,0},{5,1},{6,2},{7,3},{8,12},{9,13},{10,... | collective-permute-start | bytes 245768 | tf_op jit(solution)/shard_map/ppermute | solution.py:39
  207.0 5.6 %collective-permute-start.25 = (f32[32,640]{1,0:T(8,128)}, f32[32,640]{1,0:T(8,128)S(1)}, u32[]{:S(2)}, u32[]{:S(2)}) collective-permute-start(f32[32,640]{1,0:T(8,128)} %get-tuple-element.128), channel_id=1, source_target_pairs={{0,6},{1,7},{2,0},{3,1},{4,2},{5,3},{6,4},{7,5},{8,14},{9,15},{10,... | collective-permute-start | bytes 245768 | tf_op jit(solution)/shard_map/ppermute | solution.py:39
  207.7 5.7 %collective-permute-start.24 = (f32[32,640]{1,0:T(8,128)}, f32[32,640]{1,0:T(8,128)S(1)}, u32[]{:S(2)}, u32[]{:S(2)}) collective-permute-start(f32[32,640]{1,0:T(8,128)} %get-tuple-element.128), channel_id=1, source_target_pairs={{0,2},{1,3},{2,4},{3,5},{4,6},{5,7},{6,0},{7,1},{8,10},{9,11},{10,... | collective-permute-start | bytes 245768 | tf_op jit(solution)/shard_map/ppermute | solution.py:39
  220.8 2.2 collective-permute-start.27

commit v3 on v2

--- a/solution.py
+++ b/solution.py
@@ -1,4 +1,5 @@
 import functools
+import math
 
 import jax
 import jax.numpy as jnp
@@ -8,13 +9,12 @@
 from jax.sharding import PartitionSpec as P
 
 PIECES = 4
-EARLY = 4
-CHUNKS = (2, 2, 3)
-DEPTH = 1024
+FIRST = 4
+UNIT = 1024
 LANES = 128
 COVER = 8
 MIB = 1 << 20
-VMEM_MIB = 56
+VMEM_MIB = 58
 BF16, F32 = jnp.bfloat16, jnp.float32
 
 
@@ -48,27 +48,22 @@
     return shift_y(rows, 1), shift_y(rows, -1)
 
 
-def split_kernel(before_ref, after_ref, low_ref, high_ref, sems):
-    half = low_ref.shape[0]
-    low = pltpu.make_async_copy(before_ref.at[pl.ds(0, half)], low_ref, sems.at[0])
-    high = pltpu.make_async_copy(after_ref.at[pl.ds(half, half)], high_ref, sems.at[1])
-    low.start()
-    high.start()
-    low.wait()
-    high.wait()
+def split_kernel(before_ref, after_ref, low_ref, high_ref):
+    low_ref[...] = before_ref[...]
+    high_ref[...] = after_ref[...]
 
 
 def second_step(before, after):
-    part = shape((before.shape[0] // 2, before.shape[1]), before.dtype)
-    anywhere = pl.BlockSpec(memory_space=pl.ANY)
+    rows, columns = before.shape[0] // 2, before.shape[1]
+    part = pl.BlockSpec((rows, columns), lambda i: (0, 0))
     low, high = call(
         split_kernel,
-        (part, part),
-        8,
-        moved=2 * before.size * 2,
-        in_specs=[anywhere] * 2,
-        out_specs=(anywhere,) * 2,
-        scratch_shapes=[pltpu.SemaphoreType.DMA((2,))],
+        (shape((rows, columns), before.dtype),) * 2,
+        16,
+        moved=2 * before.size,
+        grid=(1,),
+        in_specs=[part, pl.BlockSpec((rows, columns), lambda i: (1, 0))],
+        out_specs=(part,) * 2,
     )(before, after)
     return shift_y(low, 1), shift_y(high, -1)
 
@@ -91,16 +86,17 @@
     return pl.BlockSpec(dims, lambda *_: (0,) * len(dims))
 
 
-def scale_kernel(cot_ref, weight_ref, code_ref, raw_ref, rest_ref):
+def scale_kernel(cot_ref, weight_ref, code_ref, rest_ref, raw_ref):
     count = weight_ref.shape[1]
     column = jnp.broadcast_to(weight_ref[...], (count, count)).T[:, :1]
-    early = cot_ref.shape[1] - rest_ref.shape[1]
-    for base, size, out in ((0, early, raw_ref), (early, rest_ref.shape[1], rest_ref)):
+    rest = rest_ref.shape[1]
+    late = cot_ref.shape[1] - rest
+    for base, size, out in ((rest, late, raw_ref), (0, rest, rest_ref)):
         for at in range(0, size, 512):
             block = cot_ref[:, base + at : base + at + 512].astype(F32)
             out[:, at : at + 512] = (block * column).astype(BF16)
     codes = jnp.broadcast_to(code_ref[...], (count, count)).astype(F32).T
-    raw_ref[:, early:] = codes[:, : raw_ref.shape[1] - early].astype(BF16)
+    raw_ref[:, late:] = codes[:, : raw_ref.shape[1] - late].astype(BF16)
 
 
 def code_kernel(experts, capacity, ids_ref, code_ref):
@@ -256,8 +252,8 @@
     prev, (factor_ref, hidden_ref, low_in_ref) = take(2), take(3)
     gb_o, gb_p, da_o, da_p = take(4)
     if last:
-        sums_before, grads_before, sums_back = take(3)
-    sums_ref, grads_ref, total, low = refs
+        sums_before, *grads_before, sums_back = take(4)
+    sums_ref, grads_o_ref, grads_p_ref, total, low = refs
     step = pl.program_id(0)
     units = down_o.shape[0]
 
@@ -289,27 +285,28 @@
             sums_ref[:rank, :done] = sums_before[...]
             sums_ref[:rank, done:] = sums
             sums_ref[rank:, :] = sums_back[...]
-            grads_ref[:rank, :units] = grads_before[:rank, :units] + grads_o
-            grads_ref[:rank, units:] = grads_before[:rank, units:] + grads_p
-            grads_ref[rank:, :] = grads_before[rank:, :] + grads_b
         else:
             sums_ref[...] = sums
-            grads_ref[:rank, :units] = grads_o
-            grads_ref[:rank, units:] = grads_p
-            grads_ref[rank:, :] = grads_b
-
-
-def product_kernel(rank, me_ref, sums_ref, came_ref, *refs):
-    sides = ((refs[:5], refs[5:10], refs[10:15]), (refs[15:16], refs[16:21]))
-    mine_ref, theirs_ref, buffer, sems = refs[21:]
-    span = buffer.shape[2]
-    me = me_ref[0]
-    plane = lax.div(me, 2)
+        for i, (out, top) in enumerate(((grads_o_ref, grads_o), (grads_p_ref, grads_p))):
+            bottom = grads_b[:, i * units : (i + 1) * units]
+            if last:
+                top = top + grads_before[i][:rank, :]
+                bottom = bottom + grads_before[i][rank:, :]
+            out[:rank, :] = top
+            out[rank:, :] = bottom
+
+
+def select_kernel(counts, me_ref, *refs):
+    number = sum(sum(side) for side in counts)
+    ins, outs, sems = list(refs[:number]), refs[number:-1], refs[-1]
+    sides = [[[ins.pop(0) for _ in range(pieces)] for pieces in side] for side in counts]
+    span = outs[0].shape[1]
+    plane = lax.div(me_ref[0], 2)
 
     def copies(which):
-        found, number = [], 0
+        found = []
         begin, end = which * span, (which + 1) * span
-        for side, chunks in enumerate(sides):
+        for chunks, out in zip(sides, outs):
             base = 0
             for pieces in chunks:
                 size = pieces[0].shape[1]
@@ -321,11 +318,10 @@
                         found.append(
                             pltpu.make_async_copy(
                                 piece.at[:, pl.ds(low - base, high - low)],
-                                buffer.at[side, pl.ds(at, rows), pl.ds(low - begin, high - low)],
-                                sems.at[number],
+                                out.at[pl.ds(at, rows), pl.ds(low - begin, high - low)],
+                                sems.at[len(found)],
                             )
                         )
-                        number += 1
                     at += rows
                 base += size
         return found
@@ -340,20 +336,42 @@
             for copy in found:
                 copy.wait()
 
-    high, low = halves(sums_ref[...])
+
+def product_kernel(rest, me_ref, came_ref, tok_ref, cot_ref, own_ref, *refs):
+    others, (mine_ref, theirs_ref) = refs[:3], refs[3:]
+    rank, span = mine_ref.shape[1], tok_ref.shape[1]
+    slots = tok_ref.shape[0] // 4
+    me = me_ref[0]
+    sums = own_ref[...]
+    for other, order in zip(others, ((2, 0, 3, 1), (1, 3, 0, 2), (3, 2, 1, 0))):
+        value = other[...]
+        sums = sums + jnp.concatenate([value[:, i * slots : (i + 1) * slots] for i in order], axis=1)
+    high, low = halves(sums)
     half = span // 2
     even = lax.rem(me, 2) == 0
-    crossed = lax.broadcasted_iota(jnp.int32, (rank, span), 1) + plane * span < sides[1][0][0].shape[1]
-    for side in range(2):
+    crossed = lax.broadcasted_iota(jnp.int32, (rank, span), 1) + lax.div(me, 2) * span >= rest
+    for side, rows_ref in enumerate((tok_ref, cot_ref)):
         at = slice(side * rank, (side + 1) * rank)
         both = jnp.concatenate([high[at], low[at]], axis=0)
-        wide = dot(both, buffer[side])
-        wide = wide[:rank] + wide[rank:]
+        rows = rows_ref[...]
         if side == 1:
-            moved = dot(dot(both, order_of(came_ref)).astype(BF16), buffer[side])
-            wide = jnp.where(crossed, moved[:rank] + moved[rank:], wide)
+            both = jnp.concatenate([both, dot(both, order_of(came_ref)).astype(BF16)], axis=0)
+        wide = dot(both, rows)
+        if side == 1:
+            moved = wide[2 * rank : 3 * rank] + wide[3 * rank :]
+        wide = wide[:rank] + wide[rank : 2 * rank]
+        if side == 1:
+            wide = jnp.where(crossed, moved, wide)
         mine_ref[side] = jnp.where(even, wide[:, :half], wide[:, half:])
         theirs_ref[side] = jnp.where(even, wide[:, half:], wide[:, :half])
+
+
+def final_kernel(own_ref, other_ref, grads_ref, more_ref, ga_ref, gb_ref, da_ref, db_ref):
+    rank = ga_ref.shape[1]
+    ga_ref[0] = own_ref[0] + other_ref[0]
+    db_ref[0] = own_ref[1] + other_ref[1]
+    gb_ref[0] = grads_ref[:rank, :] + more_ref[:rank, :]
+    da_ref[0] = grads_ref[rank:, :] + more_ref[rank:, :]
 
 
 def body(
@@ -373,12 +391,9 @@
     experts = lax.axis_size("dp")
     count, top = chosen_expert_index.shape
     width = tokens.shape[1]
-    early = width // DEPTH * EARLY // 7 * DEPTH
-    spans, at = [], 0
-    for sevenths in CHUNKS:
-        size = width // DEPTH * sevenths // 7 * DEPTH
-        spans.append((at, size))
-        at += size
+    first = width // UNIT * FIRST // 7 * UNIT
+    spans = ((0, first), (first, width - first))
+    rest, late = first, width - first
     capacity = 5 * count * top // (4 * experts)
     slots = experts * capacity
     every = 4 * slots
@@ -395,21 +410,21 @@
     code = call(
         functools.partial(code_kernel, experts, capacity), shape((1, count), jnp.int32), 16, moved=1024
     )(chosen_expert_index.reshape(1, count))
-    raw, scaled = call(
+    scaled, raw = call(
         scale_kernel,
-        (shape((count, early + LANES), BF16), shape((count, width - early), BF16)),
+        (shape((count, rest), BF16), shape((count, late + LANES), BF16)),
         16,
         moved=4 * count * width,
     )(cotangent, router_weight.reshape(1, count), code)
     raw_steps = first_step(raw)
 
-    def pack(*sources):
+    def pack(code, *sources):
         spans = [(first, size) for _, first, size in sources]
         part = sum(size for _, size in spans) // PIECES
         return call(
             functools.partial(pack_kernel, spans),
             shape((every, part), BF16),
-            32,
+            VMEM_MIB,
             flops=2 * every * PIECES * count * part,
             moved=2 * (PIECES * count + every) * part,
             grid=(1,),
@@ -426,28 +441,37 @@
         return call(
             unpack_kernel,
             tuple(shape((slots, size), BF16) for size in sizes),
-            32,
-            flops=2 * every * every * got.shape[1],
-            moved=4 * every * got.shape[1],
+            VMEM_MIB,
+            flops=2 * every * every * got.shape[1] // COVER,
+            moved=4 * every * got.shape[1] // COVER,
         )(got, came)
 
     mine = (gate_w, up_w, down_w, jnp.concatenate([gate_b, down_a], axis=0))
+    got = across_dp(pack(code, (tokens, *spans[0])))
+    code, raw_steps = tie((code, raw_steps))
     raw_far = second_step(*raw_steps)
-    sent = pack(*[(tokens, *span) for span in spans], (scaled, 0, width - early))
+    sent = pack(code, (tokens, *spans[1]), (scaled, 0, rest))
+    got, sent = tie((got, sent))
+    (rows_0,) = unpack(got, first)
+    rows_0, sent = tie((rows_0, sent))
+    steps_0 = first_step(rows_0)
     got = across_dp(sent)
+    raw_far, steps_0 = tie((raw_far, steps_0))
+    far_0 = second_step(*steps_0)
+
     raw_pieces = (raw, *raw_steps, *raw_far)
-    wide = early // PIECES
+    wide = late // PIECES
     packed_raw = call(
         pack_raw_kernel,
-        shape((every, early), BF16),
+        shape((every, late), BF16),
         VMEM_MIB,
-        flops=2 * every * 4 * count * early,
-        moved=2 * (4 * count + every) * early,
+        flops=2 * every * 4 * count * late,
+        moved=2 * (4 * count + every) * late,
         grid=(PIECES,),
         in_specs=[whole(every, 1), whole(every, 1)]
         + [pl.BlockSpec((piece.shape[0], wide), lambda i: (0, i)) for piece in raw_pieces]
         + [
-            pl.BlockSpec((piece.shape[0], LANES), lambda i: (0, early // LANES))
+            pl.BlockSpec((piece.shape[0], LANES), lambda i: (0, late // LANES))
             for piece in raw_pieces
         ],
         out_specs=pl.BlockSpec((every, wide), lambda i: (0, i)),
@@ -456,22 +480,23 @@
     got, theirs, packed_raw = tie((got, tuple(swap_core(w) for w in mine), packed_raw))
     gate_p, up_p, down_p, small_p = theirs
     small = (gate_b, small_p[:rank], down_a, small_p[rank:])
-    *rows, rows_back = unpack(got, *[size for _, size in spans], width - early)
-
-    def piece_specs(pieces):
-        return [pl.BlockSpec((piece.shape[0], DEPTH), lambda i: (0, i)) for piece in pieces]
-
-    def tall(first):
-        return pl.BlockSpec((DEPTH, units), lambda i: (first // DEPTH + i, 0))
-
-    def flat(rows, first):
-        return pl.BlockSpec((rows, DEPTH), lambda i: (0, first // DEPTH + i))
+    rows_1, rows_2 = unpack(got, width - first, rest)
+
+    def piece_specs(pieces, depth):
+        return [pl.BlockSpec((piece.shape[0], depth), lambda i: (0, i)) for piece in pieces]
+
+    def tall(depth, first):
+        return pl.BlockSpec((depth, units), lambda i: (first // depth + i, 0))
+
+    def flat(rows, depth, first):
+        return pl.BlockSpec((rows, depth), lambda i: (0, first // depth + i))
 
     totals = (shape((every, 2 * units), F32), shape((every, 2 * units), F32), shape((every, rank), F32))
     scratch = [pltpu.VMEM(s.shape, s.dtype) for s in totals]
     def gate_up(chunk, pieces, before):
         begins, last = chunk == 0, chunk == len(spans) - 1
         first, size = spans[chunk]
+        depth = math.gcd(first, size) if first else size // 2
         outs = totals
         if last:
             outs = (
@@ -487,50 +512,43 @@
             VMEM_MIB,
             flops=2 * every * size * 4 * units,
             moved=2 * size * (every + 4 * units),
-            grid=(size // DEPTH,),
-            in_specs=piece_specs(pieces)
-            + [tall(first)] * 4
-            + [flat(rank, first)]
+            grid=(size // depth,),
+            in_specs=piece_specs(pieces, depth)
+            + [tall(depth, first)] * 4
+            + [flat(rank, depth, first)]
             + [whole(*value.shape) for value in extra],
             out_specs=tuple(whole(*s.shape) for s in outs),
             scratch_shapes=scratch if last else [],
         )(*pieces, gate_w, gate_p, up_w, up_p, gate_a, *extra)
 
-    packed_raw, rows[0] = tie((packed_raw, rows[0]))
+    packed_raw, rows_1, far_0 = tie((packed_raw, rows_1, far_0))
     got_raw = across_dp(packed_raw)
-    steps_0 = first_step(rows[0])
-    steps_0, rows[1] = tie((steps_0, rows[1]))
-    far_0 = second_step(*steps_0)
-    steps_1 = first_step(rows[1])
-    steps_1, far_0, rows[2] = tie((steps_1, far_0, rows[2]))
+    steps_1 = first_step(rows_1)
+    steps_1, rows_0 = tie((steps_1, rows_0))
+    pieces_0 = (rows_0, *steps_0, *far_0)
+    part_0 = gate_up(0, pieces_0, None)
     far_1 = second_step(*steps_1)
-    steps_2 = first_step(rows[2])
-    pieces_0 = (rows[0], *steps_0, *far_0)
-    part_0 = gate_up(0, pieces_0, None)
-    steps_2, part_0 = tie((steps_2, part_0))
+    far_1, rows_2 = tie((far_1, rows_2))
+    steps_2 = first_step(rows_2)
+    pieces_1 = (rows_1, *steps_1, *far_1)
+    hidden, factor, low_in, sums_back = gate_up(1, pieces_1, part_0)
+    steps_2, hidden = tie((steps_2, hidden))
     far_2 = second_step(*steps_2)
-    pieces_1 = (rows[1], *steps_1, *far_1)
-    part_1 = gate_up(1, pieces_1, part_0)
-    far_2, part_1, rows_back = tie((far_2, part_1, rows_back))
-    steps_3 = first_step(rows_back)
-    pieces_2 = (rows[2], *steps_2, *far_2)
-    hidden, factor, low_in, sums_back = gate_up(2, pieces_2, part_1)
-    steps_3, hidden = tie((steps_3, hidden))
-    far_3 = second_step(*steps_3)
-
+
+    depth = math.gcd(rest, late)
     back_0, low_0 = call(
         raw_kernel,
         (totals[0], totals[2]),
         VMEM_MIB,
-        flops=2 * every * early * 2 * units,
-        moved=2 * early * (every + 2 * units),
-        grid=(early // DEPTH,),
+        flops=2 * every * late * 2 * units,
+        moved=2 * late * (every + 2 * units),
+        grid=(late // depth,),
         in_specs=[
-            pl.BlockSpec((every, DEPTH), lambda i: (0, i)),
+            pl.BlockSpec((every, depth), lambda i: (0, i)),
             whole(every, 1),
-            flat(units, 0),
-            flat(units, 0),
-            flat(rank, 0),
+            flat(units, depth, rest),
+            flat(units, depth, rest),
+            flat(rank, depth, rest),
         ],
         out_specs=(whole(every, 2 * units), whole(every, rank)),
         scratch_shapes=[scratch[0], scratch[2]],
@@ -542,17 +560,21 @@
         def block(columns):
             return pl.BlockSpec((rows, columns), lambda i: (at // rows, 0))
 
-        outs = (shape((2 * rank if last else rank, every if last else rows), F32), shape((2 * rank, 2 * units), F32))
+        outs = (
+            shape((2 * rank if last else rank, every if last else rows), F32),
+            *[shape((2 * rank, units), F32)] * 2,
+        )
+        depth = rest // 2
         return call(
             functools.partial(back_kernel, last, len(pieces)),
             outs,
             VMEM_MIB,
-            flops=2 * rows * (width - early) * 2 * units,
-            moved=2 * (width - early) * (rows + 2 * units),
-            grid=((width - early) // DEPTH,),
-            in_specs=piece_specs(pieces)
-            + [flat(units, early)] * 2
-            + [flat(rank, early)]
+            flops=2 * rows * rest * 2 * units,
+            moved=2 * rest * (rows + 2 * units),
+            grid=(rest // depth,),
+            in_specs=piece_specs(pieces, depth)
+            + [flat(units, depth, 0)] * 2
+            + [flat(rank, depth, 0)]
             + [block(2 * units), block(rank), block(2 * units), block(2 * units), block(rank)]
             + [whole(rank, units)] * 4
             + [whole(*value.shape) for value in before],
@@ -560,39 +582,46 @@
             scratch_shapes=[pltpu.VMEM((rows, 2 * units), F32), pltpu.VMEM((rows, rank), F32)],
         )(*pieces, down_w, down_p, down_b, back_0, low_0, factor, hidden, low_in, *small, *before)
 
-    pieces_3 = (rows_back, *steps_3, *far_3)
-    near = back(False, pieces_3[:3], 0)
-    sums, grads = back(True, pieces_3[3:], 3 * slots, *near, sums_back)
-
-    def in_order(value, order):
-        return jnp.concatenate([value[:, i * slots : (i + 1) * slots] for i in order], axis=1)
-
-    sums = (
-        sums
-        + in_order(shift_y(sums, 1), (2, 0, 3, 1))
-        + in_order(shift_y(sums, -1), (1, 3, 0, 2))
-        + in_order(shift_y(sums, 2), (3, 2, 1, 0))
-    )
+    pieces_2 = (rows_2, *steps_2, *far_2)
+    near = back(False, pieces_2[:3], 0)
+    sums, grads, for_other = back(True, pieces_2[3:], 3 * slots, *near, sums_back)
+
     me = lax.axis_index("seq").astype(jnp.int32).reshape(1)
     share = width // lax.axis_size("seq")
-    anywhere = pl.BlockSpec(memory_space=pl.ANY)
-    chunks = (*pieces_0, *pieces_1, *pieces_2, got_raw, *pieces_3)
+    scalar = pl.BlockSpec(memory_space=pltpu.SMEM)
+    chunks = (*pieces_0, *pieces_1, *pieces_2, got_raw)
+    tok, cot = call(
+        functools.partial(select_kernel, ((5, 5), (5, 1))),
+        (shape((every, 2 * share), BF16),) * 2,
+        VMEM_MIB,
+        moved=16 * every * share,
+        in_specs=[scalar] + [pl.BlockSpec(memory_space=pl.ANY)] * len(chunks),
+        out_specs=(whole(every, 2 * share),) * 2,
+        scratch_shapes=[pltpu.SemaphoreType.DMA((len(chunks),))],
+    )(me, *chunks)
     own, other = call(
-        functools.partial(product_kernel, rank),
+        functools.partial(product_kernel, rest),
         (shape((2, rank, share), F32),) * 2,
-        VMEM_MIB,
+        16,
         flops=8 * rank * every * share,
         moved=8 * every * share,
-        in_specs=[pl.BlockSpec(memory_space=pltpu.SMEM), whole(2 * rank, every), whole(every, 1)]
-        + [anywhere] * len(chunks),
-        scratch_shapes=[
-            pltpu.VMEM((2, every, 2 * share), BF16),
-            pltpu.SemaphoreType.DMA((21,)),
-        ],
-    )(me, sums, came, *chunks)
-    result = own + swap_core(other)
-    grad_hidden = grads[:, :units] + swap_core(grads[:, units:])
-    return (result[:1], grad_hidden[None, :rank], grad_hidden[None, rank:], result[1:])
+        in_specs=[scalar, whole(every, 1)]
+        + [whole(every, 2 * share)] * 2
+        + [whole(2 * rank, every)] * 4,
+    )(me, came, tok, cot, sums, shift_y(sums, 1), shift_y(sums, -1), shift_y(sums, 2))
+    return tuple(
+        call(
+            final_kernel,
+            (
+                shape((1, rank, share), F32),
+                shape((1, rank, units), F32),
+                shape((1, rank, units), F32),
+                shape((1, rank, share), F32),
+            ),
+            8,
+            moved=24 * rank * share,
+        )(own, swap_core(other), grads, swap_core(for_other))
+    )
 
 
 def solution(mesh):

time: 229 us -> 209 us (0.913); the launches traced: 225 us -> 208 us
  starting transfers between devices: 67.8 us -> 53.3 us
  Pallas kernels: 72.8 us -> 78.6 us
  local copies, waits for them, and re-layouts: 13.4 us -> 9.36 us
  other arithmetic: 4.84 us -> 2.29 us
    ppermute x23 -> x19, starting transfers between devices: 30.7 us -> 24.5 us  [shift_y(): return lax.ppermute(value, 'seq', pairs)]
    pallas_call x1 -> x2, Pallas kernels: 2.77 us -> 8.49 us  [unpack(): call(unpack_kernel, tuple((shape((slots, size), BF16) for size in sizes))...]
    ppermute x6, starting transfers between devices: 17.4 us -> 12 us  [swap_core(): return lax.ppermute(value, 'seq', [(i, i ^ 1) for i in range(size)])]
    pallas_call x3 -> x2, Pallas kernels: 26.9 us -> 23 us  [gate_up(): call(functools.partial(gate_up_kernel, begins, last), outs, VMEM_MIB, flo...]
    pallas_call x10 -> x12, Pallas kernels: 30 us -> 33.8 us  [the longest x1 9.05 us: body(): call(raw_kernel, (totals[0], totals[2]), VMEM_MIB, flops=2 * every * late...]
    add x3 -> x0, other arithmetic: 3.37 us -> none  [the longest x1 1.69 us: body(): sums + in_order(shift_y(sums, 1), (2, 0, 3, 1))]
    all_to_all x2 -> x3, starting transfers between devices: 19.6 us -> 16.7 us  [across_dp(): lax.all_to_all(sent, 'dp', split_axis=0, concat_axis=0, tiled=True)]
    all_to_all x2 -> x3, waiting for transfers between devices: 7.56 us -> 4.89 us  [across_dp(): lax.all_to_all(sent, 'dp', split_axis=0, concat_axis=0, tiled=True)]
  transfers between devices with their start and end apart: 31 -> 28, of which waited for: 13 -> 8; matrix products, arithmetic and copies ran while one was open for 2% -> 1% of each run, Pallas kernels for 26% -> 34%
where the time goes in v3:
time: 209 us; the launch traced here: 208 us
  Pallas kernels  78.6 us (38%)
  waiting for transfers between devices  63.7 us (30%)
  starting transfers between devices  53.3 us (26%)
  local copies, waits for them, and re-layouts  9.36 us (4%)
  other arithmetic  2.29 us (1%)
    ppermute x19, waiting for transfers between devices, shift_y(): return lax.ppermute(value, 'seq', pairs)  57.6 us
    ppermute x19, starting transfers between devices, shift_y(): return lax.ppermute(value, 'seq', pairs)  24.5 us
    pallas_call x2, Pallas kernels, gate_up(): call(functools.partial(gate_up_kernel, begins, last), outs, VMEM_MIB, flo...  23 us
    all_to_all x3, starting transfers between devices, across_dp(): lax.all_to_all(sent, 'dp', split_axis=0, concat_axis=0, tiled=True)  16.7 us
    pallas_call x2, Pallas kernels, back(): call(functools.partial(back_kernel, last, len(pieces)), outs, VMEM_MIB, f...  13.2 us
    ppermute x6, starting transfers between devices, swap_core(): return lax.ppermute(value, 'seq', [(i, i ^ 1) for i in range(size)])  12 us
    pallas_call x1, Pallas kernels, body(): call(raw_kernel, (totals[0], totals[2]), VMEM_MIB, flops=2 * every * late...  9.05 us
    pallas_call x2, Pallas kernels, pack(): call(functools.partial(pack_kernel, spans), shape((every, part), BF16), V...  8.82 us
  transfers between devices with their start and end apart: 28, of which 8 were waited for; matrix products, arithmetic and copies ran while one was open for 1% of the time, Pallas kernels for 34%

profile of v3, /device:TPU:1, one launch (start us, length us, event | category | flops | bytes accessed | tf_op | source)
XLA Modules:
  0.0 208.1 jit_solution(12427893830645968779)
XLA Ops:
  0.6 0.6 copy-done.18
  1.3 0.1 shard_map.138.code_ref
  1.4 0.0 copy-start.8
  1.4 1.5 copy-done.8
  2.9 0.7 copy-done.14
  3.6 0.4 shard_map.140
  4.0 1.0 copy-done.16
  5.1 2.1 %collective-permute-start = (bf16[128,3200]{1,0:T(8,128)(2,1)S(1)}, bf16[128,3200]{1,0:T(8,128)(2,1)S(1)}, u32[]{:S(2)}, u32[]{:S(2)}) collective-permute-start(bf16[128,3200]{1,0:T(8,128)(2,1)S(1)} %get-tuple-element.65.refs_0_.refs_5_), channel_id=1, source_target_pairs={{0,2},{1,3},{2,4},{3,5},{4,6},{5,7},{6,0},{7,1},{8,10},{9,11},{10,... | collective-permute-start | bytes 2457608 | tf_op jit(solution)/shard_map/ppermute | solution.py:39
  7.2 1.4 collective-permute-start.1
  8.6 1.1 add_select_fusion
  9.7 3.8 %shard_map.139 = bf16[640,1024]{1,0:T(8,128)(2,1)} custom-call(s32[1,128]{1,0:T(1,128)} %copy-done.15, s32[640,1]{1,0:T(8,128)} %get-tuple-element.129.want_ref, s32[640,1]{1,0:T(8,128)} %get-tuple-element.128.piece_ref.plane_ref, bf16[128,7168]{1,0:T(8,128)(2,1)} %refs_0_.3), custom_call_target="tpu_custom_call" | custom-call | flops 5368709120 | bytes 18874368 | tf_op jit(solution)/shard_map/pallas_call | solution.py:424
  13.5 7.6 %all-to-all-start = ((bf16[16,40,1024]{2,1,0:T(8,128)(2,1)}), bf16[16,40,1024]{2,1,0:T(8,128)(2,1)}, u32[]{:S(2)}, u32[]{:S(2)}) async-start(bf16[16,40,1024]{2,1,0:T(8,128)(2,1)} %bitcast.20), calls=%async_computation | async-start | bytes 2621440 | tf_op jit(solution)/shard_map/all_to_all | solution.py:438
  21.2 1.5 collective-permute-start.4
  22.7 0.1 collective-permute-start.2
  22.8 0.4 collective-permute-start.3
  23.2 1.2 fusion.16.came_ref
  24.4 2.0 collective-permute-done.before_ref.refs_1_.refs_6_
  26.4 0.0 collective-permute-done.1.after_ref.refs_2_.refs_7_
  26.4 0.1 shard_map.143
  26.5 1.0 collective-permute-start.6
  27.5 1.7 collective-permute-start.7
  29.3 5.0 %shard_map.141 = bf16[640,1792]{1,0:T(8,128)(2,1)} custom-call(s32[1,128]{1,0:T(1,128)} %copy-done.15, s32[640,1]{1,0:T(8,128)} %get-tuple-element.129.want_ref, s32[640,1]{1,0:T(8,128)} %get-tuple-element.128.piece_ref.plane_ref, bf16[128,7168]{1,0:T(8,128)(2,1)} %refs_0_.3, bf16[128,4096]{1,0:T(8,128)(2,1)} %copy-done.16), custom_call_target="tpu_custom_call" | custom-call | flops 9395240960 | bytes 33030144 | tf_op jit(solution)/shard_map/pallas_call | solution.py:424
  34.3 4.9 %all-to-all-done = bf16[16,40,1024]{2,1,0:T(8,128)(2,1)} async-done(((bf16[16,40,1024]{2,1,0:T(8,128)(2,1)}), bf16[16,40,1024]{2,1,0:T(8,128)(2,1)}, u32[]{:S(2)}, u32[]{:S(2)}) %all-to-all-start) | async-done | bytes 1310752 | tf_op jit(solution)/shard_map/all_to_all | solution.py:438
  39.2 3.7 %shard_map.142.refs_0_ = bf16[160,4096]{1,0:T(8,128)(2,1)} custom-call(bf16[640,1024]{1,0:T(8,128)(2,1)} %bitcast.3.got_ref, s32[640,1]{1,0:T(8,128)} %fusion.16.came_ref), custom_call_target="tpu_custom_call" | custom-call | flops 838860800 | bytes 2621440 | tf_op jit(solution)/shard_map/pallas_call | solution.py:441
  42.9 0.0 collective-permute-done.6.refs_3_.refs_8_
  42.9 0.0 collective-permute-start.8
  43.0 0.8 copy-done.24
  43.7 2.0 collective-permute-start.9
  45.7 4.6 %all-to-all-start.1 = ((bf16[16,40,1792]{2,1,0:T(8,128)(2,1)}), bf16[16,40,1792]{2,1,0:T(8,128)(2,1)}, u32[]{:S(2)}, u32[]{:S(2)}) async-start(bf16[16,40,1792]{2,1,0:T(8,128)(2,1)} %bitcast.19), calls=%async_computation.1 | async-start | bytes 4587520 | tf_op jit(solution)/shard_map/all_to_all | solution.py:438
  50.3 20.7 %collective-permute-done.8.before_ref.refs_1_ = bf16[160,4096]{1,0:T(8,128)(2,1)S(1)} collective-permute-done((bf16[160,4096]{1,0:T(8,128)(2,1)}, bf16[160,4096]{1,0:T(8,128)(2,1)S(1)}, u32[]{:S(2)}, u32[]{:S(2)}) %collective-permute-start.8) | collective-permute-done | bytes 1310752 | tf_op jit(solution)/shard_map/ppermute | solution.py:39
  71.0 4.5 %collective-permute-start.5 = (bf16[32,256]{1,0:T(8,128)(2,1)S(1)}, bf16[32,256]{1,0:T(8,128)(2,1)S(1)}, u32[]{:S(2)}, u32[]{:S(2)}) collective-permute-start(bf16[32,256]{1,0:T(8,128)(2,1)S(1)} %pad_maximum_fusion), channel_id=1, source_target_pairs={{0,1},{1,0},{2,3},{3,2},{4,5},{5,4},{6,7},{7,6},{8,9},{9,8},{10,11... | collective-permute-start | bytes 49160 | tf_op jit(solution)/shard_map/ppermute | solution.py:44
  75.6 1.0 shard_map.146
  76.6 2.7 %collective-permute-start.11 = (bf16[80,4096]{1,0:T(8,128)(2,1)S(1)}, bf16[80,4096]{1,0:T(8,128)(2,1)}, u32[]{:S(2)}, u32[]{:S(2)}) collective-permute-start(bf16[80,4096]{1,0:T(8,128)(2,1)S(1)} %get-tuple-element.84), channel_id=1, source_target_pairs={{0,6},{1,7},{2,0},{3,1},{4,2},{5,3},{6,4},{7,5},{8,14},{9,15},{10,... | collective-permute-start | bytes 1966088 | tf_op jit(solution)/shard_map/ppermute | solution.py:39
  79.3 7.0 %shard_map.144 = bf16[640,3072]{1,0:T(8,128)(2,1)} custom-call(s32[640,1]{1,0:T(8,128)} %get-tuple-element.129.want_ref, s32[640,1]{1,0:T(8,128)} %get-tuple-element.128.piece_ref.plane_ref, bf16[128,3200]{1,0:T(8,128)(2,1)} %copy-done.17, bf16[128,3200]{1,0:T(8,128)(2,1)} %copy-done.10, bf16[128,3200]{1,0:T(8,128)(2,1)} %copy-done.11, ...), custom_call_target="tpu_custom_call" | custom-call | flops 16106127360 | bytes 56623104 | tf_op jit(solution)/shard_map/pallas_call | solution.py:464
  86.3 4.8 %shard_map.145 = (bf16[160,3072]{1,0:T(8,128)(2,1)}, bf16[160,4096]{1,0:T(8,128)(2,1)}) custom-call(bf16[640,1792]{1,0:T(8,128)(2,1)} %bitcast.6.got_ref, s32[640,1]{1,0:T(8,128)} %fusion.16.came_ref), custom_call_target="tpu_custom_call" | custom-call | flops 1468006400 | bytes 4587520 | tf_op jit(solution)/shard_map/pallas_call | solution.py:441
  91.0 3.4 %collective-permute-done.10.refs_3_ = bf16[80,4096]{1,0:T(8,128)(2,1)} collective-permute-done((bf16[80,4096]{1,0:T(8,128)(2,1)}, bf16[80,4096]{1,0:T(8,128)(2,1)}, u32[]{:S(2)}, u32[]{:S(2)}) %collective-permute-start.10) | collective-permute-done | bytes 655392 | tf_op jit(solution)/shard_map/ppermute | solution.py:39
  94.5 2.7 %collective-permute-start.13 = (bf16[160,3072]{1,0:T(8,128)(2,1)}, bf16[160,3072]{1,0:T(8,128)(2,1)S(1)}, u32[]{:S(2)}, u32[]{:S(2)}) collective-permute-start(bf16[160,3072]{1,0:T(8,128)(2,1)} %get-tuple-element.85.refs_0_.refs_5_), channel_id=1, source_target_pairs={{0,6},{1,7},{2,0},{3,1},{4,2},{5,3},{6,4},{7,5},{8,14},{9,15},{10,... | collective-permute-start | bytes 2949128 | tf_op jit(solution)/shard_map/ppermute | solution.py:39
  97.2 4.5 %all-to-all-start.2 = ((bf16[16,40,3072]{2,1,0:T(8,128)(2,1)}), bf16[16,40,3072]{2,1,0:T(8,128)(2,1)}, u32[]{:S(2)}, u32[]{:S(2)}) async-start(bf16[16,40,3072]{2,1,0:T(8,128)(2,1)} %bitcast.18), calls=%async_computation.2 | async-start | bytes 7864320 | tf_op jit(solution)/shard_map/all_to_all | solution.py:438
  101.7 0.6 fusion.28
  102.3 16.2 %collective-permute-done.12.before_ref.refs_1_.refs_6_ = bf16[160,3072]{1,0:T(8,128)(2,1)S(1)} collective-permute-done((bf16[160,3072]{1,0:T(8,128)(2,1)}, bf16[160,3072]{1,0:T(8,128)(2,1)S(1)}, u32[]{:S(2)}, u32[]{:S(2)}) %collective-permute-start.12) | collective-permute-done | bytes 983072 | tf_op jit(solution)/shard_map/ppermute | solution.py:39
  118.5 0.1 shard_map.147
  118.6 0.1 collective-permute-start.14
  118.7 2.7 %collective-permute-start.15 = (bf16[80,3072]{1,0:T(8,128)(2,1)S(1)}, bf16[80,3072]{1,0:T(8,128)(2,1)S(1)}, u32[]{:S(2)}, u32[]{:S(2)}) collective-permute-start(bf16[80,3072]{1,0:T(8,128)(2,1)S(1)} %get-tuple-element.92), channel_id=1, source_target_pairs={{0,6},{1,7},{2,0},{3,1},{4,2},{5,3},{6,4},{7,5},{8,14},{9,15},{10,... | collective-permute-start | bytes 1474568 | tf_op jit(solution)/shard_map/ppermute | solution.py:39
  121.3 11.1 %shard_map.148 = (f32[640,512]{1,0:T(8,128)}, f32[640,512]{1,0:T(8,128)}, f32[640,16]{1,0:T(8,128)}) custom-call(bf16[160,4096]{1,0:T(8,128)(2,1)} %shard_map.142.refs_0_, bf16[160,4096]{1,0:T(8,128)(2,1)} %copy-done, bf16[160,4096]{1,0:T(8,128)(2,1)} %copy-done.1, bf16[80,4096]{1,0:T(8,128)(2,1)} %collective-permute-done.10.refs_3_, ...), custom_call_target="tpu_custom_call" | custom-call | flops 42949672960 | bytes 109051904 | tf_op jit(solution)/shard_map/pallas_call | solution.py:509
  132.5 0.8 copy-done.21
  133.3 2.7 %collective-permute-start.17 = (bf16[160,4096]{1,0:T(8,128)(2,1)S(1)}, bf16[160,4096]{1,0:T(8,128)(2,1)S(1)}, u32[]{:S(2)}, u32[]{:S(2)}) collective-permute-start(bf16[160,4096]{1,0:T(8,128)(2,1)S(1)} %copy-done.19), channel_id=1, source_target_pairs={{0,6},{1,7},{2,0},{3,1},{4,2},{5,3},{6,4},{7,5},{8,14},{9,15},{10,... | collective-permute-start | bytes 3932168 | tf_op jit(solution)/shard_map/ppermute | solution.py:39
  136.0 11.9 %shard_map.149 = (bf16[640,512]{1,0:T(8,128)(2,1)}, f32[640,512]{1,0:T(8,128)}, bf16[640,16]{1,0:T(8,128)(2,1)}, f32[16,640]{1,0:T(8,128)}) custom-call(bf16[160,3072]{1,0:T(8,128)(2,1)} %get-tuple-element.85.refs_0_.refs_5_, bf16[160,3072]{1,0:T(8,128)(2,1)} %copy-done.4, bf16[160,3072]{1,0:T(8,128)(2,1)} %copy-done.5, bf16[80,3072]{1,0:T(8,128)(2,1)} %copy-done.20, ...), custom_call_target="tpu_custom_call" | custom-call | flops 32212254720 | bytes 81788928 | tf_op jit(solution)/shard_map/pallas_call | solution.py:509
  147.9 14.8 %collective-permute-done.16.before_ref.refs_11_.refs_1_ = bf16[160,4096]{1,0:T(8,128)(2,1)S(1)} collective-permute-done((bf16[160,4096]{1,0:T(8,128)(2,1)S(1)}, bf16[160,4096]{1,0:T(8,128)(2,1)S(1)}, u32[]{:S(2)}, u32[]{:S(2)}) %collective-permute-start.16) | collective-permute-done | bytes 1310752 | tf_op jit(solution)/shard_map/ppermute | solution.py:39
  162.7 1.1 shard_map.150
  163.8 2.7 %collective-permute-start.19 = (bf16[80,4096]{1,0:T(8,128)(2,1)S(1)}, bf16[80,4096]{1,0:T(8,128)(2,1)}, u32[]{:S(2)}, u32[]{:S(2)}) collective-permute-start(bf16[80,4096]{1,0:T(8,128)(2,1)S(1)} %get-tuple-element.107), channel_id=1, source_target_pairs={{0,6},{1,7},{2,0},{3,1},{4,2},{5,3},{6,4},{7,5},{8,14},{9,15},{10,... | collective-permute-start | bytes 1966088 | tf_op jit(solution)/shard_map/ppermute | solution.py:39
  166.4 9.0 %shard_map.152 = (f32[640,512]{1,0:T(8,128)}, f32[640,16]{1,0:T(8,128)}) custom-call(bf16[640,3072]{1,0:T(8,128)(2,1)} %bitcast.14.refs_15_.got_ref, s32[640,1]{1,0:T(8,128)} %fusion.16.came_ref, bf16[256,7168]{1,0:T(8,128)(2,1)} %bitcast.36, bf16[256,7168]{1,0:T(8,128)(2,1)} %collective-permute-done.4.down_p.refs_4_.refs_3_, bf16[16,7168]{1,0:T(8,128)(2,1)} %bitcast.41), custom_call_target="tpu_custom_call" | custom-call | flops 16106127360 | bytes 56623104 | tf_op jit(solution)/shard_map/pallas_call | solution.py:539
  175.5 7.9 %shard_map.153 = (f32[16,480]{1,0:T(8,128)}, f32[32,256]{1,0:T(8,128)}, f32[32,256]{1,0:T(8,128)}) custom-call(bf16[160,4096]{1,0:T(8,128)(2,1)} %get-tuple-element.96.refs_10_.refs_0_, bf16[160,4096]{1,0:T(8,128)(2,1)} %copy-done.2, bf16[160,4096]{1,0:T(8,128)(2,1)} %copy-done.3, bf16[256,7168]{1,0:T(8,128)(2,1)} %bitcast.37, ...), custom_call_target="tpu_custom_call" | custom-call | flops 16106127360 | bytes 65011712 | tf_op jit(solution)/shard_map/pallas_call | solution.py:568
  183.4 5.3 %shard_map.154 = (f32[32,640]{1,0:T(8,128)}, f32[32,256]{1,0:T(8,128)}, f32[32,256]{1,0:T(8,128)}) custom-call(bf16[80,4096]{1,0:T(8,128)(2,1)} %collective-permute-done.18.refs_13_.refs_0_, bf16[80,4096]{1,0:T(8,128)(2,1)} %collective-permute-done.19.refs_14_.refs_1_, bf16[256,7168]{1,0:T(8,128)(2,1)} %bitcast.38, ...), custom_call_target="tpu_custom_call" | custom-call | flops 5368709120 | bytes 44040192 | tf_op jit(solution)/shard_map/pallas_call | solution.py:568
  188.7 0.1 collective-permute-start.20
  188.8 2.7 %collective-permute-start.21 = (f32[32,640]{1,0:T(8,128)}, f32[32,640]{1,0:T(8,128)S(1)}, u32[]{:S(2)}, u32[]{:S(2)}) collective-permute-start(f32[32,640]{1,0:T(8,128)} %get-tuple-element.121.own_ref), channel_id=1, source_target_pairs={{0,6},{1,7},{2,0},{3,1},{4,2},{5,3},{6,4},{7,5},{8,14},{9,15},{10,... | collective-permute-start | bytes 245768 | tf_op jit(solution)/shard_map/ppermute | solution.py:39
  191.4 4.6 %shard_map.151 = (bf16[640,1792]{1,0:T(8,128)(2,1)}, bf16[640,1792]{1,0:T(8,128)(2,1)}) custom-call(s32[1]{0:T(128)} %bitcast.me_ref, bf16[160,4096]{1,0:T(8,128)(2,1)} %shard_map.142.refs_0_, bf16[160,4096]{1,0:T(8,128)(2,1)} %copy-done, bf16[160,4096]{1,0:T(8,128)(2,1)} %copy-done.1, bf16[80,4096]{1,0:T(8,128)(2,1)} %collective-permute-done.10.refs_3_, ...), custom_call_target="tpu_custom_call" | custom-call | bytes 73400320 | tf_op jit(solution)/shard_map/pallas_call | solution.py:593
  196.1 0.4 collective-permute-done.22.refs_2_
  196.4 1.6 copy-done.6
  198.1 1.6 copy-done.7
  199.7 1.1 shard_map.155
  200.8 5.3 %collective-permute-start.23 = (f32[2,16,896]{2,1,0:T(8,128)S(1)}, f32[2,16,896]{2,1,0:T(8,128)S(1)}, u32[]{:S(2)}, u32[]{:S(2)}) collective-permute-start(f32[2,16,896]{2,1,0:T(8,128)S(1)} %get-tuple-element.123), channel_id=1, source_target_pairs={{0,1},{1,0},{2,3},{3,2},{4,5},{5,4},{6,7},{7,6},{8,9},{9,8},{10,11... | collective-permute-start | bytes 344072 | tf_op jit(solution)/shard_map/ppermute | solution.py:44
  206.2 0.1 collective-permute-start.24
  206.3 1.1 collective-permute-done.24.more_ref
  207.4 0.7 shard_map.156
  (69 shorter events, 0.1 us)
Async XLA Ops:
  0.6 0.7 copy-start.18
  1.4 8.3 %copy-start.15 = (s32[1,128]{1,0:T(1,128)}, s32[1,128]{1,0:T(1,128)S(1)}, u32[]{:S(2)}) copy-start(s32[1,128]{1,0:T(1,128)S(1)} %shard_map.138.code_ref) | copy-start | bytes 1540
  1.4 1.5 copy-start.8
  2.9 0.7 copy-start.14
  4.0 1.0 copy-start.16
  5.1 8.5 %copy-start.17 = (bf16[128,3200]{1,0:T(8,128)(2,1)}, bf16[128,3200]{1,0:T(8,128)(2,1)S(1)}, u32[]{:S(2)}) copy-start(bf16[128,3200]{1,0:T(8,128)(2,1)S(1)} %get-tuple-element.65.refs_0_.refs_5_) | copy-start | bytes 2457604
  5.1 21.4 %collective-permute-start = (bf16[128,3200]{1,0:T(8,128)(2,1)S(1)}, bf16[128,3200]{1,0:T(8,128)(2,1)S(1)}, u32[]{:S(2)}, u32[]{:S(2)}) collective-permute-start(bf16[128,3200]{1,0:T(8,128)(2,1)S(1)} %get-tuple-element.65.refs_0_.refs_5_), channel_id=1, source_target_pairs={{0,2},{1,3},{2,4},{3,5},{4,6},{5,7},{6,0},{7,1},{8,10},{9,11},{10,... | collective-permute-start | bytes 2457608 | tf_op jit(solution)/shard_map/ppermute | solution.py:39
  7.2 19.3 %collective-permute-start.1 = (bf16[128,3200]{1,0:T(8,128)(2,1)S(1)}, bf16[128,3200]{1,0:T(8,128)(2,1)S(1)}, u32[]{:S(2)}, u32[]{:S(2)}) collective-permute-start(bf16[128,3200]{1,0:T(8,128)(2,1)S(1)} %get-tuple-element.65.refs_0_.refs_5_), channel_id=1, source_target_pairs={{0,6},{1,7},{2,0},{3,1},{4,2},{5,3},{6,4},{7,5},{8,14},{9,15},{10,... | collective-permute-start | bytes 2457608 | tf_op jit(solution)/shard_map/ppermute | solution.py:39
  13.5 25.7 %all-to-all-start = ((bf16[16,40,1024]{2,1,0:T(8,128)(2,1)}), bf16[16,40,1024]{2,1,0:T(8,128)(2,1)}, u32[]{:S(2)}, u32[]{:S(2)}) async-start(bf16[16,40,1024]{2,1,0:T(8,128)(2,1)} %bitcast.20), calls=%async_computation | async-start | bytes 2621440 | tf_op jit(solution)/shard_map/all_to_all | solution.py:438
  21.2 65.1 %collective-permute-start.4 = (bf16[256,7168]{1,0:T(8,128)(2,1)}, bf16[256,7168]{1,0:T(8,128)(2,1)}, u32[]{:S(2)}, u32[]{:S(2)}) collective-permute-start(bf16[256,7168]{1,0:T(8,128)(2,1)} %bitcast.35), channel_id=1, source_target_pairs={{0,1},{1,0},{2,3},{3,2},{4,5},{5,4},{6,7},{7,6},{8,9},{9,8},{10,11... | collective-permute-start | bytes 11010056 | tf_op jit(solution)/shard_map/ppermute | solution.py:44
  22.7 63.6 %collective-permute-start.2 = (bf16[7168,256]{1,0:T(8,128)(2,1)}, bf16[7168,256]{1,0:T(8,128)(2,1)}, u32[]{:S(2)}, u32[]{:S(2)}) collective-permute-start(bf16[7168,256]{1,0:T(8,128)(2,1)} %bitcast.29), channel_id=1, source_target_pairs={{0,1},{1,0},{2,3},{3,2},{4,5},{5,4},{6,7},{7,6},{8,9},{9,8},{10,11... | collective-permute-start | bytes 11010056 | tf_op jit(solution)/shard_map/ppermute | solution.py:44
  22.8 63.5 %collective-permute-start.3 = (bf16[7168,256]{1,0:T(8,128)(2,1)}, bf16[7168,256]{1,0:T(8,128)(2,1)}, u32[]{:S(2)}, u32[]{:S(2)}) collective-permute-start(bf16[7168,256]{1,0:T(8,128)(2,1)} %bitcast.32), channel_id=1, source_target_pairs={{0,1},{1,0},{2,3},{3,2},{4,5},{5,4},{6,7},{7,6},{8,9},{9,8},{10,11... | collective-permute-start | bytes 11010056 | tf_op jit(solution)/shard_map/ppermute | solution.py:44
  26.4 7.9 %copy-start.10 = (bf16[128,3200]{1,0:T(8,128)(2,1)}, bf16[128,3200]{1,0:T(8,128)(2,1)S(1)}, u32[]{:S(2)}) copy-start(bf16[128,3200]{1,0:T(8,128)(2,1)S(1)} %collective-permute-done.before_ref.refs_1_.refs_6_) | copy-start | bytes 2457604
  26.4 7.9 %copy-start.11 = (bf16[128,3200]{1,0:T(8,128)(2,1)}, bf16[128,3200]{1,0:T(8,128)(2,1)S(1)}, u32[]{:S(2)}) copy-start(bf16[128,3200]{1,0:T(8,128)(2,1)S(1)} %collective-permute-done.1.after_ref.refs_2_.refs_7_) | copy-start | bytes 2457604
  26.5 16.4 %collective-permute-start.6 = (bf16[64,3200]{1,0:T(8,128)(2,1)S(1)}, bf16[64,3200]{1,0:T(8,128)(2,1)S(1)}, u32[]{:S(2)}, u32[]{:S(2)}) collective-permute-start(bf16[64,3200]{1,0:T(8,128)(2,1)S(1)} %get-tuple-element.73), channel_id=1, source_target_pairs={{0,2},{1,3},{2,4},{3,5},{4,6},{5,7},{6,0},{7,1},{8,10},{9,11},{10,... | collective-permute-start | bytes 1228808 | tf_op jit(solution)/shard_map/ppermute | solution.py:39
  27.5 16.2 %collective-permute-start.7 = (bf16[64,3200]{1,0:T(8,128)(2,1)S(1)}, bf16[64,3200]{1,0:T(8,128)(2,1)S(1)}, u32[]{:S(2)}, u32[]{:S(2)}) collective-permute-start(bf16[64,3200]{1,0:T(8,128)(2,1)S(1)} %get-tuple-element.74), channel_id=1, source_target_pairs={{0,6},{1,7},{2,0},{3,1},{4,2},{5,3},{6,4},{7,5},{8,14},{9,15},{10,... | collective-permute-start | bytes 1228808 | tf_op jit(solution)/shard_map/ppermute | solution.py:39
  42.9 0.8 copy-start.24
  42.9 28.1 %collective-permute-start.8 = (bf16[160,4096]{1,0:T(8,128)(2,1)}, bf16[160,4096]{1,0:T(8,128)(2,1)S(1)}, u32[]{:S(2)}, u32[]{:S(2)}) collective-permute-start(bf16[160,4096]{1,0:T(8,128)(2,1)} %shard_map.142.refs_0_), channel_id=1, source_target_pairs={{0,2},{1,3},{2,4},{3,5},{4,6},{5,7},{6,0},{7,1},{8,10},{9,11},{10,... | collective-permute-start | bytes 3932168 | tf_op jit(solution)/shard_map/ppermute | solution.py:39
  43.7 2.0 copy-start.25
  43.7 31.8 %collective-permute-start.9 = (bf16[160,4096]{1,0:T(8,128)(2,1)}, bf16[160,4096]{1,0:T(8,128)(2,1)S(1)}, u32[]{:S(2)}, u32[]{:S(2)}) collective-permute-start(bf16[160,4096]{1,0:T(8,128)(2,1)} %shard_map.142.refs_0_), channel_id=1, source_target_pairs={{0,6},{1,7},{2,0},{3,1},{4,2},{5,3},{6,4},{7,5},{8,14},{9,15},{10,... | collective-permute-start | bytes 3932168 | tf_op jit(solution)/shard_map/ppermute | solution.py:39
  45.7 4.6 %copy-start.22 = (bf16[1,16,256]{2,1,0:T(8,128)(2,1)S(1)}, bf16[1,16,256]{2,1,0:T(8,128)(2,1)}, u32[]{:S(2)}) copy-start(bf16[1,16,256]{2,1,0:T(8,128)(2,1)} %param.19) | copy-start | bytes 24580
  45.7 4.6 %copy-start.23 = (bf16[1,16,256]{2,1,0:T(8,128)(2,1)S(1)}, bf16[1,16,256]{2,1,0:T(8,128)(2,1)}, u32[]{:S(2)}) copy-start(bf16[1,16,256]{2,1,0:T(8,128)(2,1)} %param.20) | copy-start | bytes 24580
  45.7 40.6 %all-to-all-start.1 = ((bf16[16,40,1792]{2,1,0:T(8,128)(2,1)}), bf16[16,40,1792]{2,1,0:T(8,128)(2,1)}, u32[]{:S(2)}, u32[]{:S(2)}) async-start(bf16[16,40,1792]{2,1,0:T(8,128)(2,1)} %bitcast.19), calls=%async_computation.1 | async-start | bytes 4587520 | tf_op jit(solution)/shard_map/all_to_all | solution.py:438
  71.0 15.2 %copy-start = (bf16[160,4096]{1,0:T(8,128)(2,1)}, bf16[160,4096]{1,0:T(8,128)(2,1)S(1)}, u32[]{:S(2)}) copy-start(bf16[160,4096]{1,0:T(8,128)(2,1)S(1)} %collective-permute-done.8.before_ref.refs_1_) | copy-start | bytes 3932164
  71.0 5.6 %collective-permute-start.5 = (bf16[32,256]{1,0:T(8,128)(2,1)S(1)}, bf16[32,256]{1,0:T(8,128)(2,1)S(1)}, u32[]{:S(2)}, u32[]{:S(2)}) collective-permute-start(bf16[32,256]{1,0:T(8,128)(2,1)S(1)} %pad_maximum_fusion), channel_id=1, source_target_pairs={{0,1},{1,0},{2,3},{3,2},{4,5},{5,4},{6,7},{7,6},{8,9},{9,8},{10,11... | collective-permute-start | bytes 49160 | tf_op jit(solution)/shard_map/ppermute | solution.py:44
  75.6 10.7 %copy-start.1 = (bf16[160,4096]{1,0:T(8,128)(2,1)}, bf16[160,4096]{1,0:T(8,128)(2,1)S(1)}, u32[]{:S(2)}) copy-start(bf16[160,4096]{1,0:T(8,128)(2,1)S(1)} %collective-permute-done.9.after_ref.refs_2_) | copy-start | bytes 3932164
  76.6 17.9 %collective-permute-start.10 = (bf16[80,4096]{1,0:T(8,128)(2,1)}, bf16[80,4096]{1,0:T(8,128)(2,1)}, u32[]{:S(2)}, u32[]{:S(2)}) collective-permute-start(bf16[80,4096]{1,0:T(8,128)(2,1)} %get-tuple-element.83), channel_id=1, source_target_pairs={{0,2},{1,3},{2,4},{3,5},{4,6},{5,7},{6,0},{7,1},{8,10},{9,11},{10,... | collective-permute-start | bytes 1966088 | tf_op jit(solution)/shard_map/ppermute | solution.py:39
  76.6 17.9 %collective-permute-start.11 = (bf16[80,4096]{1,0:T(8,128)(2,1)S(1)}, bf16[80,4096]{1,0:T(8,128)(2,1)}, u32[]{:S(2)}, u32[]{:S(2)}) collective-permute-start(bf16[80,4096]{1,0:T(8,128)(2,1)S(1)} %get-tuple-element.84), channel_id=1, source_target_pairs={{0,6},{1,7},{2,0},{3,1},{4,2},{5,3},{6,4},{7,5},{8,14},{9,15},{10,... | collective-permute-start | bytes 1966088 | tf_op jit(solution)/shard_map/ppermute | solution.py:39
  94.5 24.0 %collective-permute-start.12 = (bf16[160,3072]{1,0:T(8,128)(2,1)}, bf16[160,3072]{1,0:T(8,128)(2,1)S(1)}, u32[]{:S(2)}, u32[]{:S(2)}) collective-permute-start(bf16[160,3072]{1,0:T(8,128)(2,1)} %get-tuple-element.85.refs_0_.refs_5_), channel_id=1, source_target_pairs={{0,2},{1,3},{2,4},{3,5},{4,6},{5,7},{6,0},{7,1},{8,10},{9,11},{10,... | collective-permute-start | bytes 2949128 | tf_op jit(solution)/shard_map/ppermute | solution.py:39
  94.5 24.0 %collective-permute-start.13 = (bf16[160,3072]{1,0:T(8,128)(2,1)}, bf16[160,3072]{1,0:T(8,128)(2,1)S(1)}, u32[]{:S(2)}, u32[]{:S(2)}) collective-permute-start(bf16[160,3072]{1,0:T(8,128)(2,1)} %get-tuple-element.85.refs_0_.refs_5_), channel_id=1, source_target_pairs={{0,6},{1,7},{2,0},{3,1},{4,2},{5,3},{6,4},{7,5},{8,14},{9,15},{10,... | collective-permute-start | bytes 2949128 | tf_op jit(solution)/shard_map/ppermute | solution.py:39
  97.2 69.3 %all-to-all-start.2 = ((bf16[16,40,3072]{2,1,0:T(8,128)(2,1)}), bf16[16,40,3072]{2,1,0:T(8,128)(2,1)}, u32[]{:S(2)}, u32[]{:S(2)}) async-start(bf16[16,40,3072]{2,1,0:T(8,128)(2,1)} %bitcast.18), calls=%async_computation.2 | async-start | bytes 7864320 | tf_op jit(solution)/shard_map/all_to_all | solution.py:438
  118.5 14.0 %copy-start.4 = (bf16[160,3072]{1,0:T(8,128)(2,1)}, bf16[160,3072]{1,0:T(8,128)(2,1)S(1)}, u32[]{:S(2)}) copy-start(bf16[160,3072]{1,0:T(8,128)(2,1)S(1)} %collective-permute-done.12.before_ref.refs_1_.refs_6_) | copy-start | bytes 2949124
  118.5 14.0 %copy-start.5 = (bf16[160,3072]{1,0:T(8,128)(2,1)}, bf16[160,3072]{1,0:T(8,128)(2,1)S(1)}, u32[]{:S(2)}) copy-start(bf16[160,3072]{1,0:T(8,128)(2,1)S(1)} %collective-permute-done.13.after_ref.refs_2_.refs_7_) | copy-start | bytes 2949124
  118.6 13.9 %collective-permute-start.14 = (bf16[80,3072]{1,0:T(8,128)(2,1)S(1)}, bf16[80,3072]{1,0:T(8,128)(2,1)S(1)}, u32[]{:S(2)}, u32[]{:S(2)}) collective-permute-start(bf16[80,3072]{1,0:T(8,128)(2,1)S(1)} %get-tuple-element.91), channel_id=1, source_target_pairs={{0,2},{1,3},{2,4},{3,5},{4,6},{5,7},{6,0},{7,1},{8,10},{9,11},{10,... | collective-permute-start | bytes 1474568 | tf_op jit(solution)/shard_map/ppermute | solution.py:39
  118.7 13.8 %collective-permute-start.15 = (bf16[80,3072]{1,0:T(8,128)(2,1)S(1)}, bf16[80,3072]{1,0:T(8,128)(2,1)S(1)}, u32[]{:S(2)}, u32[]{:S(2)}) collective-permute-start(bf16[80,3072]{1,0:T(8,128)(2,1)S(1)} %get-tuple-element.92), channel_id=1, source_target_pairs={{0,6},{1,7},{2,0},{3,1},{4,2},{5,3},{6,4},{7,5},{8,14},{9,15},{10,... | collective-permute-start | bytes 1474568 | tf_op jit(solution)/shard_map/ppermute | solution.py:39
  121.3 12.0 %copy-start.19 = (bf16[160,4096]{1,0:T(8,128)(2,1)S(1)}, bf16[160,4096]{1,0:T(8,128)(2,1)}, u32[]{:S(2)}) copy-start(bf16[160,4096]{1,0:T(8,128)(2,1)} %get-tuple-element.96.refs_10_.refs_0_) | copy-start | bytes 3932164
  132.5 3.5 %copy-start.20 = (bf16[80,3072]{1,0:T(8,128)(2,1)}, bf16[80,3072]{1,0:T(8,128)(2,1)S(1)}, u32[]{:S(2)}) copy-start(bf16[80,3072]{1,0:T(8,128)(2,1)S(1)} %collective-permute-done.14.refs_3_.refs_8_) | copy-start | bytes 1474564
  132.5 0.8 copy-start.21
  133.3 29.4 %collective-permute-start.16 = (bf16[160,4096]{1,0:T(8,128)(2,1)S(1)}, bf16[160,4096]{1,0:T(8,128)(2,1)S(1)}, u32[]{:S(2)}, u32[]{:S(2)}) collective-permute-start(bf16[160,4096]{1,0:T(8,128)(2,1)S(1)} %copy-done.19), channel_id=1, source_target_pairs={{0,2},{1,3},{2,4},{3,5},{4,6},{5,7},{6,0},{7,1},{8,10},{9,11},{10,... | collective-permute-start | bytes 3932168 | tf_op jit(solution)/shard_map/ppermute | solution.py:39
  133.3 29.4 %collective-permute-start.17 = (bf16[160,4096]{1,0:T(8,128)(2,1)S(1)}, bf16[160,4096]{1,0:T(8,128)(2,1)S(1)}, u32[]{:S(2)}, u32[]{:S(2)}) collective-permute-start(bf16[160,4096]{1,0:T(8,128)(2,1)S(1)} %copy-done.19), channel_id=1, source_target_pairs={{0,6},{1,7},{2,0},{3,1},{4,2},{5,3},{6,4},{7,5},{8,14},{9,15},{10,... | collective-permute-start | bytes 3932168 | tf_op jit(solution)/shard_map/ppermute | solution.py:39
  162.7 12.8 %copy-start.2 = (bf16[160,4096]{1,0:T(8,128)(2,1)}, bf16[160,4096]{1,0:T(8,128)(2,1)S(1)}, u32[]{:S(2)}) copy-start(bf16[160,4096]{1,0:T(8,128)(2,1)S(1)} %collective-permute-done.16.before_ref.refs_11_.refs_1_) | copy-start | bytes 3932164
  162.7 12.8 %copy-start.3 = (bf16[160,4096]{1,0:T(8,128)(2,1)}, bf16[160,4096]{1,0:T(8,128)(2,1)S(1)}, u32[]{:S(2)}) copy-start(bf16[160,4096]{1,0:T(8,128)(2,1)S(1)} %collective-permute-done.17.after_ref.refs_12_.refs_2_) | copy-start | bytes 3932164
  163.8 19.6 %collective-permute-start.18 = (bf16[80,4096]{1,0:T(8,128)(2,1)}, bf16[80,4096]{1,0:T(8,128)(2,1)}, u32[]{:S(2)}, u32[]{:S(2)}) collective-permute-start(bf16[80,4096]{1,0:T(8,128)(2,1)} %get-tuple-element.106), channel_id=1, source_target_pairs={{0,2},{1,3},{2,4},{3,5},{4,6},{5,7},{6,0},{7,1},{8,10},{9,11},{10,... | collective-permute-start | bytes 1966088 | tf_op jit(solution)/shard_map/ppermute | solution.py:39
  163.8 19.6 %collective-permute-start.19 = (bf16[80,4096]{1,0:T(8,128)(2,1)S(1)}, bf16[80,4096]{1,0:T(8,128)(2,1)}, u32[]{:S(2)}, u32[]{:S(2)}) collective-permute-start(bf16[80,4096]{1,0:T(8,128)(2,1)S(1)} %get-tuple-element.107), channel_id=1, source_target_pairs={{0,6},{1,7},{2,0},{3,1},{4,2},{5,3},{6,4},{7,5},{8,14},{9,15},{10,... | collective-permute-start | bytes 1966088 | tf_op jit(solution)/shard_map/ppermute | solution.py:39
  188.7 7.4 %collective-permute-start.20 = (f32[32,640]{1,0:T(8,128)}, f32[32,640]{1,0:T(8,128)S(1)}, u32[]{:S(2)}, u32[]{:S(2)}) collective-permute-start(f32[32,640]{1,0:T(8,128)} %get-tuple-element.121.own_ref), channel_id=1, source_target_pairs={{0,2},{1,3},{2,4},{3,5},{4,6},{5,7},{6,0},{7,1},{8,10},{9,11},{10,... | collective-permute-start | bytes 245768 | tf_op jit(solution)/shard_map/ppermute | solution.py:39
  188.8 7.3 %collective-permute-start.21 = (f32[32,640]{1,0:T(8,128)}, f32[32,640]{1,0:T(8,128)S(1)}, u32[]{:S(2)}, u32[]{:S(2)}) collective-permute-start(f32[32,640]{1,0:T(8,128)} %get-tuple-element.121.own_ref), channel_id=1, source_target_pairs={{0,6},{1,7},{2,0},{3,1},{4,2},{5,3},{6,4},{7,5},{8,14},{9,15},{10,... | collective-permute-start | bytes 245768 | tf_op jit(solution)/shard_map/ppermute | solution.py:39
  191.4 5.0 %collective-permute-start.22 = (f32[32,640]{1,0:T(8,128)}, f32[32,640]{1,0:T(8,128)S(1)}, u32[]{:S(2)}, u32[]{:S(2)}) collective-permute-start(f32[32,640]{1,0:T(8,128)} %get-tuple-element.121.own_ref), channel_id=1, source_target_pairs={{0,4},{1,5},{2,6},{3,7},{4,0},{5,1},{6,2},{7,3},{8,12},{9,13},{10,... | collective-permute-start | bytes 245768 | tf_op jit(solution)/shard_map/ppermute | solution.py:39
  191.4 5.0 %copy-start.9 = (s32[640,1]{1,0:T(8,128)S(1)}, s32[640,1]{1,0:T(8,128)}, u32[]{:S(2)}) copy-start(s32[640,1]{1,0:T(8,128)} %fusion.16.came_ref) | copy-start | bytes 7684
  191.4 5.0 %copy-start.12 = (f32[32,640]{1,0:T(8,128)S(1)}, f32[32,640]{1,0:T(8,128)}, u32[]{:S(2)}) copy-start(f32[32,640]{1,0:T(8,128)} %get-tuple-element.121.own_ref) | copy-start | bytes 245764
  196.4 1.6 copy-start.6
  198.1 1.6 copy-start.7
  199.7 6.4 %copy-start.26 = (f32[32,256]{1,0:T(8,128)S(1)}, f32[32,256]{1,0:T(8,128)}, u32[]{:S(2)}) copy-start(f32[32,256]{1,0:T(8,128)} %get-tuple-element.125) | copy-start | bytes 98308
  199.7 7.7 %copy-start.13 = (f32[32,256]{1,0:T(8,128)S(1)}, f32[32,256]{1,0:T(8,128)}, u32[]{:S(2)}) copy-start(f32[32,256]{1,0:T(8,128)} %get-tuple-element.124.grads_ref) | copy-start | bytes 98308
  200.8 6.6 %collective-permute-start.23 = (f32[2,16,896]{2,1,0:T(8,128)S(1)}, f32[2,16,896]{2,1,0:T(8,128)S(1)}, u32[]{:S(2)}, u32[]{:S(2)}) collective-permute-start(f32[2,16,896]{2,1,0:T(8,128)S(1)} %get-tuple-element.123), channel_id=1, source_target_pairs={{0,1},{1,0},{2,3},{3,2},{4,5},{5,4},{6,7},{7,6},{8,9},{9,8},{10,11... | collective-permute-start | bytes 344072 | tf_op jit(solution)/shard_map/ppermute | solution.py:44
  206.2 1.2 collective-permute-start.24

commit v4 on v3

--- a/solution.py
+++ b/solution.py
@@ -3,6 +3,7 @@
 
 import jax
 import jax.numpy as jnp
+import numpy as np
 from jax import lax
 from jax.experimental import pallas as pl
 from jax.experimental.pallas import tpu as pltpu
@@ -402,7 +403,7 @@
     down_a, down_b = down_adapter_first[0], down_adapter_second[0]
     rank, units = gate_b.shape
 
-    at_row = jnp.arange(every, dtype=jnp.int32)[:, None]
+    at_row = np.arange(every, dtype=np.int32)[:, None]
     want = at_row // (4 * capacity) * capacity + at_row % capacity
     quarter = at_row // capacity % 4
     came = at_row % slots // capacity * 4 * capacity + at_row // slots * capacity + at_row % capacity
@@ -424,7 +425,7 @@
         return call(
             functools.partial(pack_kernel, spans),
             shape((every, part), BF16),
-            VMEM_MIB,
+            32,
             flops=2 * every * PIECES * count * part,
             moved=2 * (PIECES * count + every) * part,
             grid=(1,),
@@ -521,7 +522,7 @@
             scratch_shapes=scratch if last else [],
         )(*pieces, gate_w, gate_p, up_w, up_p, gate_a, *extra)
 
-    packed_raw, rows_1, far_0 = tie((packed_raw, rows_1, far_0))
+    rows_1, far_0 = tie((rows_1, far_0))
     got_raw = across_dp(packed_raw)
     steps_1 = first_step(rows_1)
     steps_1, rows_0 = tie((steps_1, rows_0))
@@ -532,9 +533,6 @@
     steps_2 = first_step(rows_2)
     pieces_1 = (rows_1, *steps_1, *far_1)
     hidden, factor, low_in, sums_back = gate_up(1, pieces_1, part_0)
-    steps_2, hidden = tie((steps_2, hidden))
-    far_2 = second_step(*steps_2)
-
     depth = math.gcd(rest, late)
     back_0, low_0 = call(
         raw_kernel,
@@ -553,6 +551,8 @@
         out_specs=(whole(every, 2 * units), whole(every, rank)),
         scratch_shapes=[scratch[0], scratch[2]],
     )(got_raw, came, down_w, down_p, down_b)
+    steps_2, hidden, back_0 = tie((steps_2, hidden, back_0))
+    far_2 = second_step(*steps_2)
 
     def back(last, pieces, at, *before):
         rows = sum(piece.shape[0] for piece in pieces)
@@ -592,11 +592,11 @@
     chunks = (*pieces_0, *pieces_1, *pieces_2, got_raw)
     tok, cot = call(
         functools.partial(select_kernel, ((5, 5), (5, 1))),
-        (shape((every, 2 * share), BF16),) * 2,
+        (pltpu.VMEM((every, 2 * share), BF16),) * 2,
         VMEM_MIB,
         moved=16 * every * share,
         in_specs=[scalar] + [pl.BlockSpec(memory_space=pl.ANY)] * len(chunks),
-        out_specs=(whole(every, 2 * share),) * 2,
+        out_specs=(pl.BlockSpec(memory_space=pltpu.VMEM),) * 2,
         scratch_shapes=[pltpu.SemaphoreType.DMA((len(chunks),))],
     )(me, *chunks)
     own, other = call(
@@ -606,7 +606,7 @@
         flops=8 * rank * every * share,
         moved=8 * every * share,
         in_specs=[scalar, whole(every, 1)]
-        + [whole(every, 2 * share)] * 2
+        + [pl.BlockSpec(memory_space=pltpu.VMEM)] * 2
         + [whole(2 * rank, every)] * 4,
     )(me, came, tok, cot, sums, shift_y(sums, 1), shift_y(sums, -1), shift_y(sums, 2))
     return tuple(

time: 209 us -> 199 us (0.952)
  Pallas kernels: 78.6 us -> 71.9 us
  waiting for transfers between devices: 63.7 us -> 59.3 us
  starting transfers between devices: 53.3 us -> 56 us
  other arithmetic: 2.29 us -> 0.01 us
    pallas_call x3, Pallas kernels: 13.4 us -> 6.14 us  [the longest x2 3.69 us: pack(): call(functools.partial(pack_kernel, spans), shape((every, part), BF16), 3...]
    ppermute x19, waiting for transfers between devices: 57.6 us -> 51.6 us  [shift_y(): return lax.ppermute(value, 'seq', pairs)]
    unnamed x54 -> x56, local copies, waits for them, and re-layouts: 8.76 us -> 9.75 us
  transfers between devices with their start and end apart: 28 -> 28, of which waited for: 8 -> 10; matrix products, arithmetic and copies ran while one was open for 1% -> 0% of each run, Pallas kernels for 34% -> 32%
where the time goes in v4:
time: 199 us; the launch traced here: 198 us
  Pallas kernels  71.9 us (36%)
  waiting for transfers between devices  59.3 us (30%)
  starting transfers between devices  56 us (28%)
  local copies, waits for them, and re-layouts  10.4 us (5%)
    ppermute x19, waiting for transfers between devices, shift_y(): return lax.ppermute(value, 'seq', pairs)  51.6 us
    ppermute x19, starting transfers between devices, shift_y(): return lax.ppermute(value, 'seq', pairs)  25.9 us
    pallas_call x2, Pallas kernels, gate_up(): call(functools.partial(gate_up_kernel, begins, last), outs, VMEM_MIB, flo...  22.9 us
    all_to_all x3, starting transfers between devices, across_dp(): lax.all_to_all(sent, 'dp', split_axis=0, concat_axis=0, tiled=True)  17.7 us
    pallas_call x2, Pallas kernels, back(): call(functools.partial(back_kernel, last, len(pieces)), outs, VMEM_MIB, f...  13.1 us
    ppermute x6, starting transfers between devices, swap_core(): return lax.ppermute(value, 'seq', [(i, i ^ 1) for i in range(size)])  12.4 us
    unnamed x56, local copies, waits for them, and re-layouts  9.75 us
    pallas_call x1, Pallas kernels, body(): call(raw_kernel, (totals[0], totals[2]), VMEM_MIB, flops=2 * every * late...  9.07 us
  transfers between devices with their start and end apart: 28, of which 10 were waited for; matrix products, arithmetic and copies ran while one was open for 0% of the time, Pallas kernels for 32%

profile of v4, /device:TPU:1, one launch (start us, length us, event | category | flops | bytes accessed | tf_op | source)
XLA Modules:
  0.0 198.5 jit_solution(571078260336047285)
XLA Ops:
  0.6 0.6 copy-done.16
  1.3 0.1 shard_map.165.code_ref
  1.4 1.5 copy-done.7
  2.9 0.7 copy-done.13
  3.6 1.3 shard_map.167
  4.9 2.1 %collective-permute-start = (bf16[128,3200]{1,0:T(8,128)(2,1)}, bf16[128,3200]{1,0:T(8,128)(2,1)S(1)}, u32[]{:S(2)}, u32[]{:S(2)}) collective-permute-start(bf16[128,3200]{1,0:T(8,128)(2,1)} %get-tuple-element.65.refs_0_.refs_5_), channel_id=1, source_target_pairs={{0,2},{1,3},{2,4},{3,5},{4,6},{5,7},{6,0},{7,1},{8,10},{9,11},{10,... | collective-permute-start | bytes 2457608 | tf_op jit(solution)/shard_map/ppermute | solution.py:40
  7.0 1.4 collective-permute-start.1
  8.5 1.0 copy-done.17
  9.5 1.0 copy-done.19
  10.4 2.0 %shard_map.166 = bf16[640,1024]{1,0:T(8,128)(2,1)} custom-call(s32[1,128]{1,0:T(1,128)S(1)} %shard_map.165.code_ref, s32[640,1]{1,0:T(8,128)S(1)} %copy-done.17, s32[640,1]{1,0:T(8,128)S(1)} %copy-done.19, bf16[128,7168]{1,0:T(8,128)(2,1)S(1)} %copy-done.14), custom_call_target="tpu_custom_call" | custom-call | flops 5368709120 | bytes 18874368 | tf_op jit(solution)/shard_map/pallas_call | solution.py:425
  12.5 7.8 %all-to-all-start = ((bf16[16,40,1024]{2,1,0:T(8,128)(2,1)}), bf16[16,40,1024]{2,1,0:T(8,128)(2,1)}, u32[]{:S(2)}, u32[]{:S(2)}) async-start(bf16[16,40,1024]{2,1,0:T(8,128)(2,1)} %bitcast.2), calls=%async_computation | async-start | bytes 2621440 | tf_op jit(solution)/shard_map/all_to_all | solution.py:439
  20.3 1.5 collective-permute-start.4
  21.8 0.1 collective-permute-start.2
  21.9 0.4 collective-permute-start.3
  22.3 4.3 %collective-permute-done.before_ref.refs_1_.refs_6_ = bf16[128,3200]{1,0:T(8,128)(2,1)S(1)} collective-permute-done((bf16[128,3200]{1,0:T(8,128)(2,1)}, bf16[128,3200]{1,0:T(8,128)(2,1)S(1)}, u32[]{:S(2)}, u32[]{:S(2)}) %collective-permute-start) | collective-permute-done | bytes 819232 | tf_op jit(solution)/shard_map/ppermute | solution.py:40
  26.6 0.9 shard_map.170
  27.5 0.8 collective-permute-start.6
  28.3 1.9 collective-permute-start.7
  30.2 1.5 copy-done.15
  31.7 1.0 copy-done.20
  32.6 1.6 shard_map.168
  34.3 1.4 copy-done.6
  35.7 2.6 %all-to-all-done = bf16[16,40,1024]{2,1,0:T(8,128)(2,1)} async-done(((bf16[16,40,1024]{2,1,0:T(8,128)(2,1)}), bf16[16,40,1024]{2,1,0:T(8,128)(2,1)}, u32[]{:S(2)}, u32[]{:S(2)}) %all-to-all-start) | async-done | bytes 1310752 | tf_op jit(solution)/shard_map/all_to_all | solution.py:439
  38.3 3.7 %shard_map.169.refs_0_ = bf16[160,4096]{1,0:T(8,128)(2,1)} custom-call(bf16[640,1024]{1,0:T(8,128)(2,1)} %bitcast.3.got_ref, s32[640,1]{1,0:T(8,128)} %constant.12.clone.came_ref), custom_call_target="tpu_custom_call" | custom-call | flops 838860800 | bytes 2621440 | tf_op jit(solution)/shard_map/pallas_call | solution.py:442
  42.0 2.7 %collective-permute-start.9 = (bf16[160,4096]{1,0:T(8,128)(2,1)}, bf16[160,4096]{1,0:T(8,128)(2,1)S(1)}, u32[]{:S(2)}, u32[]{:S(2)}) collective-permute-start(bf16[160,4096]{1,0:T(8,128)(2,1)} %shard_map.169.refs_0_), channel_id=1, source_target_pairs={{0,6},{1,7},{2,0},{3,1},{4,2},{5,3},{6,4},{7,5},{8,14},{9,15},{10,... | collective-permute-start | bytes 3932168 | tf_op jit(solution)/shard_map/ppermute | solution.py:40
  44.7 5.0 %all-to-all-start.1 = ((bf16[16,40,1792]{2,1,0:T(8,128)(2,1)}), bf16[16,40,1792]{2,1,0:T(8,128)(2,1)}, u32[]{:S(2)}, u32[]{:S(2)}) async-start(bf16[16,40,1792]{2,1,0:T(8,128)(2,1)} %bitcast.16), calls=%async_computation.1 | async-start | bytes 4587520 | tf_op jit(solution)/shard_map/all_to_all | solution.py:439
  49.8 20.3 %collective-permute-done.8.before_ref.refs_1_ = bf16[160,4096]{1,0:T(8,128)(2,1)S(1)} collective-permute-done((bf16[160,4096]{1,0:T(8,128)(2,1)}, bf16[160,4096]{1,0:T(8,128)(2,1)S(1)}, u32[]{:S(2)}, u32[]{:S(2)}) %collective-permute-start.8) | collective-permute-done | bytes 1310752 | tf_op jit(solution)/shard_map/ppermute | solution.py:40
  70.1 4.5 %collective-permute-start.5 = (bf16[32,256]{1,0:T(8,128)(2,1)S(1)}, bf16[32,256]{1,0:T(8,128)(2,1)S(1)}, u32[]{:S(2)}, u32[]{:S(2)}) collective-permute-start(bf16[32,256]{1,0:T(8,128)(2,1)S(1)} %pad_maximum_fusion), channel_id=1, source_target_pairs={{0,1},{1,0},{2,3},{3,2},{4,5},{5,4},{6,7},{7,6},{8,9},{9,8},{10,11... | collective-permute-start | bytes 49160 | tf_op jit(solution)/shard_map/ppermute | solution.py:45
  74.6 1.0 shard_map.173
  75.7 2.7 %collective-permute-start.11 = (bf16[80,4096]{1,0:T(8,128)(2,1)S(1)}, bf16[80,4096]{1,0:T(8,128)(2,1)}, u32[]{:S(2)}, u32[]{:S(2)}) collective-permute-start(bf16[80,4096]{1,0:T(8,128)(2,1)S(1)} %get-tuple-element.83), channel_id=1, source_target_pairs={{0,6},{1,7},{2,0},{3,1},{4,2},{5,3},{6,4},{7,5},{8,14},{9,15},{10,... | collective-permute-start | bytes 1966088 | tf_op jit(solution)/shard_map/ppermute | solution.py:40
  78.4 7.0 %shard_map.171 = bf16[640,3072]{1,0:T(8,128)(2,1)} custom-call(s32[640,1]{1,0:T(8,128)} %constant.10.clone.want_ref, s32[640,1]{1,0:T(8,128)} %constant.11.clone.piece_ref.plane_ref, bf16[128,3200]{1,0:T(8,128)(2,1)} %get-tuple-element.65.refs_0_.refs_5_, bf16[128,3200]{1,0:T(8,128)(2,1)} %copy-done.8, bf16[128,3200]{1,0:T(8,128)(2,1)} %copy-done.9, ...), custom_call_target="tpu_custom_call" | custom-call | flops 16106127360 | bytes 56623104 | tf_op jit(solution)/shard_map/pallas_call | solution.py:465
  85.4 4.8 %shard_map.172 = (bf16[160,3072]{1,0:T(8,128)(2,1)}, bf16[160,4096]{1,0:T(8,128)(2,1)}) custom-call(bf16[640,1792]{1,0:T(8,128)(2,1)} %bitcast.6.got_ref, s32[640,1]{1,0:T(8,128)} %constant.12.clone.came_ref), custom_call_target="tpu_custom_call" | custom-call | flops 1468006400 | bytes 4587520 | tf_op jit(solution)/shard_map/pallas_call | solution.py:442
  90.1 3.4 %collective-permute-done.10.refs_3_ = bf16[80,4096]{1,0:T(8,128)(2,1)} collective-permute-done((bf16[80,4096]{1,0:T(8,128)(2,1)}, bf16[80,4096]{1,0:T(8,128)(2,1)}, u32[]{:S(2)}, u32[]{:S(2)}) %collective-permute-start.10) | collective-permute-done | bytes 655392 | tf_op jit(solution)/shard_map/ppermute | solution.py:40
  93.6 2.7 %collective-permute-start.13 = (bf16[160,3072]{1,0:T(8,128)(2,1)}, bf16[160,3072]{1,0:T(8,128)(2,1)S(1)}, u32[]{:S(2)}, u32[]{:S(2)}) collective-permute-start(bf16[160,3072]{1,0:T(8,128)(2,1)} %get-tuple-element.84.refs_0_.refs_5_), channel_id=1, source_target_pairs={{0,6},{1,7},{2,0},{3,1},{4,2},{5,3},{6,4},{7,5},{8,14},{9,15},{10,... | collective-permute-start | bytes 2949128 | tf_op jit(solution)/shard_map/ppermute | solution.py:40
  96.2 4.9 %all-to-all-start.2 = ((bf16[16,40,3072]{2,1,0:T(8,128)(2,1)}), bf16[16,40,3072]{2,1,0:T(8,128)(2,1)}, u32[]{:S(2)}, u32[]{:S(2)}) async-start(bf16[16,40,3072]{2,1,0:T(8,128)(2,1)} %bitcast.19), calls=%async_computation.2 | async-start | bytes 7864320 | tf_op jit(solution)/shard_map/all_to_all | solution.py:439
  101.1 0.6 fusion
  101.8 15.8 %collective-permute-done.12.before_ref.refs_1_.refs_6_ = bf16[160,3072]{1,0:T(8,128)(2,1)S(1)} collective-permute-done((bf16[160,3072]{1,0:T(8,128)(2,1)}, bf16[160,3072]{1,0:T(8,128)(2,1)S(1)}, u32[]{:S(2)}, u32[]{:S(2)}) %collective-permute-start.12) | collective-permute-done | bytes 983072 | tf_op jit(solution)/shard_map/ppermute | solution.py:40
  117.7 0.1 collective-permute-start.14
  117.8 2.7 %collective-permute-start.15 = (bf16[80,3072]{1,0:T(8,128)(2,1)S(1)}, bf16[80,3072]{1,0:T(8,128)(2,1)S(1)}, u32[]{:S(2)}, u32[]{:S(2)}) collective-permute-start(bf16[80,3072]{1,0:T(8,128)(2,1)S(1)} %get-tuple-element.91), channel_id=1, source_target_pairs={{0,6},{1,7},{2,0},{3,1},{4,2},{5,3},{6,4},{7,5},{8,14},{9,15},{10,... | collective-permute-start | bytes 1474568 | tf_op jit(solution)/shard_map/ppermute | solution.py:40
  120.4 11.0 %shard_map.175 = (f32[640,512]{1,0:T(8,128)}, f32[640,512]{1,0:T(8,128)}, f32[640,16]{1,0:T(8,128)}) custom-call(bf16[160,4096]{1,0:T(8,128)(2,1)} %shard_map.169.refs_0_, bf16[160,4096]{1,0:T(8,128)(2,1)} %copy-done, bf16[160,4096]{1,0:T(8,128)(2,1)} %copy-done.1, bf16[80,4096]{1,0:T(8,128)(2,1)} %collective-permute-done.10.refs_3_, ...), custom_call_target="tpu_custom_call" | custom-call | flops 42949672960 | bytes 109051904 | tf_op jit(solution)/shard_map/pallas_call | solution.py:510
  131.5 0.1 collective-permute-start.16
  131.6 2.7 %collective-permute-start.17 = (bf16[160,4096]{1,0:T(8,128)(2,1)}, bf16[160,4096]{1,0:T(8,128)(2,1)S(1)}, u32[]{:S(2)}, u32[]{:S(2)}) collective-permute-start(bf16[160,4096]{1,0:T(8,128)(2,1)} %get-tuple-element.95.refs_10_.refs_0_), channel_id=1, source_target_pairs={{0,6},{1,7},{2,0},{3,1},{4,2},{5,3},{6,4},{7,5},{8,14},{9,15},{10,... | collective-permute-start | bytes 3932168 | tf_op jit(solution)/shard_map/ppermute | solution.py:40
  134.3 11.9 %shard_map.176 = (bf16[640,512]{1,0:T(8,128)(2,1)}, f32[640,512]{1,0:T(8,128)}, bf16[640,16]{1,0:T(8,128)(2,1)}, f32[16,640]{1,0:T(8,128)}) custom-call(bf16[160,3072]{1,0:T(8,128)(2,1)} %get-tuple-element.84.refs_0_.refs_5_, bf16[160,3072]{1,0:T(8,128)(2,1)} %copy-done.4, bf16[160,3072]{1,0:T(8,128)(2,1)} %copy-done.5, bf16[80,3072]{1,0:T(8,128)(2,1)} %copy-done.23, ...), custom_call_target="tpu_custom_call" | custom-call | flops 32212254720 | bytes 81788928 | tf_op jit(solution)/shard_map/pallas_call | solution.py:510
  146.1 4.0 %all-to-all-done.2 = bf16[16,40,3072]{2,1,0:T(8,128)(2,1)} async-done(((bf16[16,40,3072]{2,1,0:T(8,128)(2,1)}), bf16[16,40,3072]{2,1,0:T(8,128)(2,1)}, u32[]{:S(2)}, u32[]{:S(2)}) %all-to-all-start.2) | async-done | bytes 3932192 | tf_op jit(solution)/shard_map/all_to_all | solution.py:439
  150.1 9.1 %shard_map.177 = (f32[640,512]{1,0:T(8,128)}, f32[640,16]{1,0:T(8,128)}) custom-call(bf16[640,3072]{1,0:T(8,128)(2,1)} %bitcast.14.got_ref.refs_15_, s32[640,1]{1,0:T(8,128)} %constant.12.clone.came_ref, bf16[256,7168]{1,0:T(8,128)(2,1)} %bitcast.35, bf16[256,7168]{1,0:T(8,128)(2,1)} %collective-permute-done.4.down_p.refs_4_.refs_3_, bf16[16,7168]{1,0:T(8,128)(2,1)} %bitcast.40), custom_call_target="tpu_custom_call" | custom-call | flops 16106127360 | bytes 56623104 | tf_op jit(solution)/shard_map/pallas_call | solution.py:537
  159.1 2.0 %collective-permute-done.16.before_ref.refs_11_.refs_1_ = bf16[160,4096]{1,0:T(8,128)(2,1)S(1)} collective-permute-done((bf16[160,4096]{1,0:T(8,128)(2,1)}, bf16[160,4096]{1,0:T(8,128)(2,1)S(1)}, u32[]{:S(2)}, u32[]{:S(2)}) %collective-permute-start.16) | collective-permute-done | bytes 1310752 | tf_op jit(solution)/shard_map/ppermute | solution.py:40
  161.1 0.1 shard_map.178
  161.2 0.1 collective-permute-start.18
  161.3 2.7 %collective-permute-start.19 = (bf16[80,4096]{1,0:T(8,128)(2,1)S(1)}, bf16[80,4096]{1,0:T(8,128)(2,1)S(1)}, u32[]{:S(2)}, u32[]{:S(2)}) collective-permute-start(bf16[80,4096]{1,0:T(8,128)(2,1)S(1)} %get-tuple-element.109), channel_id=1, source_target_pairs={{0,6},{1,7},{2,0},{3,1},{4,2},{5,3},{6,4},{7,5},{8,14},{9,15},{10,... | collective-permute-start | bytes 1966088 | tf_op jit(solution)/shard_map/ppermute | solution.py:40
  164.0 7.8 %shard_map.180 = (f32[16,480]{1,0:T(8,128)}, f32[32,256]{1,0:T(8,128)}, f32[32,256]{1,0:T(8,128)}) custom-call(bf16[160,4096]{1,0:T(8,128)(2,1)} %get-tuple-element.95.refs_10_.refs_0_, bf16[160,4096]{1,0:T(8,128)(2,1)} %copy-done.2, bf16[160,4096]{1,0:T(8,128)(2,1)} %copy-done.3, bf16[256,7168]{1,0:T(8,128)(2,1)} %bitcast.36, ...), custom_call_target="tpu_custom_call" | custom-call | flops 16106127360 | bytes 65011712 | tf_op jit(solution)/shard_map/pallas_call | solution.py:568
  171.8 3.9 %collective-permute-done.18.refs_13_.refs_0_ = bf16[80,4096]{1,0:T(8,128)(2,1)S(1)} collective-permute-done((bf16[80,4096]{1,0:T(8,128)(2,1)S(1)}, bf16[80,4096]{1,0:T(8,128)(2,1)S(1)}, u32[]{:S(2)}, u32[]{:S(2)}) %collective-permute-start.18) | collective-permute-done | bytes 655392 | tf_op jit(solution)/shard_map/ppermute | solution.py:40
  175.7 0.8 copy-done.21
  176.5 0.2 copy-done.22
  176.8 5.3 %shard_map.181 = (f32[32,640]{1,0:T(8,128)}, f32[32,256]{1,0:T(8,128)}, f32[32,256]{1,0:T(8,128)}) custom-call(bf16[80,4096]{1,0:T(8,128)(2,1)} %copy-done.21, bf16[80,4096]{1,0:T(8,128)(2,1)} %copy-done.22, bf16[256,7168]{1,0:T(8,128)(2,1)} %bitcast.37, bf16[256,7168]{1,0:T(8,128)(2,1)} %collective-permute-done.4.down_p.refs_4_.refs_3_, ...), custom_call_target="tpu_custom_call" | custom-call | flops 5368709120 | bytes 44040192 | tf_op jit(solution)/shard_map/pallas_call | solution.py:568
  182.0 0.1 collective-permute-start.20
  182.2 2.6 %collective-permute-start.21 = (f32[32,640]{1,0:T(8,128)}, f32[32,640]{1,0:T(8,128)S(1)}, u32[]{:S(2)}, u32[]{:S(2)}) collective-permute-start(f32[32,640]{1,0:T(8,128)} %get-tuple-element.121.own_ref), channel_id=1, source_target_pairs={{0,6},{1,7},{2,0},{3,1},{4,2},{5,3},{6,4},{7,5},{8,14},{9,15},{10,... | collective-permute-start | bytes 245768 | tf_op jit(solution)/shard_map/ppermute | solution.py:40
  184.8 0.7 collective-permute-start.22
  185.5 2.5 %shard_map.179 = (bf16[640,1792]{1,0:T(8,128)(2,1)S(1)}, bf16[640,1792]{1,0:T(8,128)(2,1)S(1)}) custom-call(s32[1]{0:T(128)} %bitcast.me_ref, bf16[160,4096]{1,0:T(8,128)(2,1)} %shard_map.169.refs_0_, bf16[160,4096]{1,0:T(8,128)(2,1)} %copy-done, bf16[160,4096]{1,0:T(8,128)(2,1)} %copy-done.1, bf16[80,4096]{1,0:T(8,128)(2,1)} %collective-permute-done.10.refs_3_, ...), custom_call_target="tpu_custom_call" | custom-call | bytes 73400320 | tf_op jit(solution)/shard_map/pallas_call | solution.py:593
  187.9 1.8 collective-permute-done.22.refs_2_
  189.8 1.1 shard_map.182
  190.9 5.7 %collective-permute-start.23 = (f32[2,16,896]{2,1,0:T(8,128)S(1)}, f32[2,16,896]{2,1,0:T(8,128)S(1)}, u32[]{:S(2)}, u32[]{:S(2)}) collective-permute-start(f32[2,16,896]{2,1,0:T(8,128)S(1)} %get-tuple-element.123), channel_id=1, source_target_pairs={{0,1},{1,0},{2,3},{3,2},{4,5},{5,4},{6,7},{7,6},{8,9},{9,8},{10,11... | collective-permute-start | bytes 344072 | tf_op jit(solution)/shard_map/ppermute | solution.py:45
  196.6 0.1 collective-permute-start.24
  196.7 1.1 collective-permute-done.24.more_ref
  197.8 0.7 shard_map.183
  (69 shorter events, 0.2 us)
Async XLA Ops:
  0.6 0.7 copy-start.16
  1.4 1.5 copy-start.7
  2.9 0.7 copy-start.13
  3.6 4.9 %copy-start.14 = (bf16[128,7168]{1,0:T(8,128)(2,1)S(1)}, bf16[128,7168]{1,0:T(8,128)(2,1)}, u32[]{:S(2)}) copy-start(bf16[128,7168]{1,0:T(8,128)(2,1)} %refs_0_.3) | copy-start | bytes 5505028
  4.9 21.7 %collective-permute-start = (bf16[128,3200]{1,0:T(8,128)(2,1)}, bf16[128,3200]{1,0:T(8,128)(2,1)S(1)}, u32[]{:S(2)}, u32[]{:S(2)}) collective-permute-start(bf16[128,3200]{1,0:T(8,128)(2,1)} %get-tuple-element.65.refs_0_.refs_5_), channel_id=1, source_target_pairs={{0,2},{1,3},{2,4},{3,5},{4,6},{5,7},{6,0},{7,1},{8,10},{9,11},{10,... | collective-permute-start | bytes 2457608 | tf_op jit(solution)/shard_map/ppermute | solution.py:40
  7.0 19.6 %collective-permute-start.1 = (bf16[128,3200]{1,0:T(8,128)(2,1)}, bf16[128,3200]{1,0:T(8,128)(2,1)S(1)}, u32[]{:S(2)}, u32[]{:S(2)}) collective-permute-start(bf16[128,3200]{1,0:T(8,128)(2,1)} %get-tuple-element.65.refs_0_.refs_5_), channel_id=1, source_target_pairs={{0,6},{1,7},{2,0},{3,1},{4,2},{5,3},{6,4},{7,5},{8,14},{9,15},{10,... | collective-permute-start | bytes 2457608 | tf_op jit(solution)/shard_map/ppermute | solution.py:40
  8.5 1.0 copy-start.17
  9.5 1.0 copy-start.19
  12.5 17.7 %copy-start.18 = (s32[640,1]{1,0:T(8,128)S(1)}, s32[640,1]{1,0:T(8,128)}, u32[]{:S(2)}) copy-start(s32[640,1]{1,0:T(8,128)} %constant.10.clone.want_ref) | copy-start | bytes 7684
  12.5 25.8 %all-to-all-start = ((bf16[16,40,1024]{2,1,0:T(8,128)(2,1)}), bf16[16,40,1024]{2,1,0:T(8,128)(2,1)}, u32[]{:S(2)}, u32[]{:S(2)}) async-start(bf16[16,40,1024]{2,1,0:T(8,128)(2,1)} %bitcast.2), calls=%async_computation | async-start | bytes 2621440 | tf_op jit(solution)/shard_map/all_to_all | solution.py:439
  20.3 65.1 %collective-permute-start.4 = (bf16[256,7168]{1,0:T(8,128)(2,1)}, bf16[256,7168]{1,0:T(8,128)(2,1)}, u32[]{:S(2)}, u32[]{:S(2)}) collective-permute-start(bf16[256,7168]{1,0:T(8,128)(2,1)} %bitcast.34), channel_id=1, source_target_pairs={{0,1},{1,0},{2,3},{3,2},{4,5},{5,4},{6,7},{7,6},{8,9},{9,8},{10,11... | collective-permute-start | bytes 11010056 | tf_op jit(solution)/shard_map/ppermute | solution.py:45
  21.8 63.5 %collective-permute-start.2 = (bf16[7168,256]{1,0:T(8,128)(2,1)}, bf16[7168,256]{1,0:T(8,128)(2,1)}, u32[]{:S(2)}, u32[]{:S(2)}) collective-permute-start(bf16[7168,256]{1,0:T(8,128)(2,1)} %bitcast.28), channel_id=1, source_target_pairs={{0,1},{1,0},{2,3},{3,2},{4,5},{5,4},{6,7},{7,6},{8,9},{9,8},{10,11... | collective-permute-start | bytes 11010056 | tf_op jit(solution)/shard_map/ppermute | solution.py:45
  21.9 63.5 %collective-permute-start.3 = (bf16[7168,256]{1,0:T(8,128)(2,1)}, bf16[7168,256]{1,0:T(8,128)(2,1)}, u32[]{:S(2)}, u32[]{:S(2)}) collective-permute-start(bf16[7168,256]{1,0:T(8,128)(2,1)} %bitcast.31), channel_id=1, source_target_pairs={{0,1},{1,0},{2,3},{3,2},{4,5},{5,4},{6,7},{7,6},{8,9},{9,8},{10,11... | collective-permute-start | bytes 11010056 | tf_op jit(solution)/shard_map/ppermute | solution.py:45
  26.6 7.7 %copy-start.8 = (bf16[128,3200]{1,0:T(8,128)(2,1)}, bf16[128,3200]{1,0:T(8,128)(2,1)S(1)}, u32[]{:S(2)}) copy-start(bf16[128,3200]{1,0:T(8,128)(2,1)S(1)} %collective-permute-done.before_ref.refs_1_.refs_6_) | copy-start | bytes 2457604
  26.6 7.7 %copy-start.9 = (bf16[128,3200]{1,0:T(8,128)(2,1)}, bf16[128,3200]{1,0:T(8,128)(2,1)S(1)}, u32[]{:S(2)}) copy-start(bf16[128,3200]{1,0:T(8,128)(2,1)S(1)} %collective-permute-done.1.after_ref.refs_2_.refs_7_) | copy-start | bytes 2457604
  27.5 14.5 %collective-permute-start.6 = (bf16[64,3200]{1,0:T(8,128)(2,1)}, bf16[64,3200]{1,0:T(8,128)(2,1)}, u32[]{:S(2)}, u32[]{:S(2)}) collective-permute-start(bf16[64,3200]{1,0:T(8,128)(2,1)} %get-tuple-element.73), channel_id=1, source_target_pairs={{0,2},{1,3},{2,4},{3,5},{4,6},{5,7},{6,0},{7,1},{8,10},{9,11},{10,... | collective-permute-start | bytes 1228808 | tf_op jit(solution)/shard_map/ppermute | solution.py:40
  28.3 13.7 %collective-permute-start.7 = (bf16[64,3200]{1,0:T(8,128)(2,1)S(1)}, bf16[64,3200]{1,0:T(8,128)(2,1)}, u32[]{:S(2)}, u32[]{:S(2)}) collective-permute-start(bf16[64,3200]{1,0:T(8,128)(2,1)S(1)} %get-tuple-element.74), channel_id=1, source_target_pairs={{0,6},{1,7},{2,0},{3,1},{4,2},{5,3},{6,4},{7,5},{8,14},{9,15},{10,... | collective-permute-start | bytes 1228808 | tf_op jit(solution)/shard_map/ppermute | solution.py:40
  30.2 1.5 copy-start.15
  31.7 1.0 copy-start.20
  34.3 1.4 copy-start.6
  42.0 28.1 %collective-permute-start.8 = (bf16[160,4096]{1,0:T(8,128)(2,1)}, bf16[160,4096]{1,0:T(8,128)(2,1)S(1)}, u32[]{:S(2)}, u32[]{:S(2)}) collective-permute-start(bf16[160,4096]{1,0:T(8,128)(2,1)} %shard_map.169.refs_0_), channel_id=1, source_target_pairs={{0,2},{1,3},{2,4},{3,5},{4,6},{5,7},{6,0},{7,1},{8,10},{9,11},{10,... | collective-permute-start | bytes 3932168 | tf_op jit(solution)/shard_map/ppermute | solution.py:40
  42.0 32.6 %collective-permute-start.9 = (bf16[160,4096]{1,0:T(8,128)(2,1)}, bf16[160,4096]{1,0:T(8,128)(2,1)S(1)}, u32[]{:S(2)}, u32[]{:S(2)}) collective-permute-start(bf16[160,4096]{1,0:T(8,128)(2,1)} %shard_map.169.refs_0_), channel_id=1, source_target_pairs={{0,6},{1,7},{2,0},{3,1},{4,2},{5,3},{6,4},{7,5},{8,14},{9,15},{10,... | collective-permute-start | bytes 3932168 | tf_op jit(solution)/shard_map/ppermute | solution.py:40
  44.7 5.0 %copy-start.25 = (bf16[1,16,256]{2,1,0:T(8,128)(2,1)S(1)}, bf16[1,16,256]{2,1,0:T(8,128)(2,1)}, u32[]{:S(2)}) copy-start(bf16[1,16,256]{2,1,0:T(8,128)(2,1)} %param.22) | copy-start | bytes 24580
  44.7 5.0 %copy-start.26 = (bf16[1,16,256]{2,1,0:T(8,128)(2,1)S(1)}, bf16[1,16,256]{2,1,0:T(8,128)(2,1)}, u32[]{:S(2)}) copy-start(bf16[1,16,256]{2,1,0:T(8,128)(2,1)} %param.23) | copy-start | bytes 24580
  44.7 40.6 %all-to-all-start.1 = ((bf16[16,40,1792]{2,1,0:T(8,128)(2,1)}), bf16[16,40,1792]{2,1,0:T(8,128)(2,1)}, u32[]{:S(2)}, u32[]{:S(2)}) async-start(bf16[16,40,1792]{2,1,0:T(8,128)(2,1)} %bitcast.16), calls=%async_computation.1 | async-start | bytes 4587520 | tf_op jit(solution)/shard_map/all_to_all | solution.py:439
  70.1 15.2 %copy-start = (bf16[160,4096]{1,0:T(8,128)(2,1)}, bf16[160,4096]{1,0:T(8,128)(2,1)S(1)}, u32[]{:S(2)}) copy-start(bf16[160,4096]{1,0:T(8,128)(2,1)S(1)} %collective-permute-done.8.before_ref.refs_1_) | copy-start | bytes 3932164
  70.1 5.6 %collective-permute-start.5 = (bf16[32,256]{1,0:T(8,128)(2,1)S(1)}, bf16[32,256]{1,0:T(8,128)(2,1)S(1)}, u32[]{:S(2)}, u32[]{:S(2)}) collective-permute-start(bf16[32,256]{1,0:T(8,128)(2,1)S(1)} %pad_maximum_fusion), channel_id=1, source_target_pairs={{0,1},{1,0},{2,3},{3,2},{4,5},{5,4},{6,7},{7,6},{8,9},{9,8},{10,11... | collective-permute-start | bytes 49160 | tf_op jit(solution)/shard_map/ppermute | solution.py:45
  74.6 10.7 %copy-start.1 = (bf16[160,4096]{1,0:T(8,128)(2,1)}, bf16[160,4096]{1,0:T(8,128)(2,1)S(1)}, u32[]{:S(2)}) copy-start(bf16[160,4096]{1,0:T(8,128)(2,1)S(1)} %collective-permute-done.9.after_ref.refs_2_) | copy-start | bytes 3932164
  75.7 17.9 %collective-permute-start.10 = (bf16[80,4096]{1,0:T(8,128)(2,1)}, bf16[80,4096]{1,0:T(8,128)(2,1)}, u32[]{:S(2)}, u32[]{:S(2)}) collective-permute-start(bf16[80,4096]{1,0:T(8,128)(2,1)} %get-tuple-element.82), channel_id=1, source_target_pairs={{0,2},{1,3},{2,4},{3,5},{4,6},{5,7},{6,0},{7,1},{8,10},{9,11},{10,... | collective-permute-start | bytes 1966088 | tf_op jit(solution)/shard_map/ppermute | solution.py:40
  75.7 17.9 %collective-permute-start.11 = (bf16[80,4096]{1,0:T(8,128)(2,1)S(1)}, bf16[80,4096]{1,0:T(8,128)(2,1)}, u32[]{:S(2)}, u32[]{:S(2)}) collective-permute-start(bf16[80,4096]{1,0:T(8,128)(2,1)S(1)} %get-tuple-element.83), channel_id=1, source_target_pairs={{0,6},{1,7},{2,0},{3,1},{4,2},{5,3},{6,4},{7,5},{8,14},{9,15},{10,... | collective-permute-start | bytes 1966088 | tf_op jit(solution)/shard_map/ppermute | solution.py:40
  93.6 24.0 %collective-permute-start.12 = (bf16[160,3072]{1,0:T(8,128)(2,1)}, bf16[160,3072]{1,0:T(8,128)(2,1)S(1)}, u32[]{:S(2)}, u32[]{:S(2)}) collective-permute-start(bf16[160,3072]{1,0:T(8,128)(2,1)} %get-tuple-element.84.refs_0_.refs_5_), channel_id=1, source_target_pairs={{0,2},{1,3},{2,4},{3,5},{4,6},{5,7},{6,0},{7,1},{8,10},{9,11},{10,... | collective-permute-start | bytes 2949128 | tf_op jit(solution)/shard_map/ppermute | solution.py:40
  93.6 24.0 %collective-permute-start.13 = (bf16[160,3072]{1,0:T(8,128)(2,1)}, bf16[160,3072]{1,0:T(8,128)(2,1)S(1)}, u32[]{:S(2)}, u32[]{:S(2)}) collective-permute-start(bf16[160,3072]{1,0:T(8,128)(2,1)} %get-tuple-element.84.refs_0_.refs_5_), channel_id=1, source_target_pairs={{0,6},{1,7},{2,0},{3,1},{4,2},{5,3},{6,4},{7,5},{8,14},{9,15},{10,... | collective-permute-start | bytes 2949128 | tf_op jit(solution)/shard_map/ppermute | solution.py:40
  96.2 53.8 %all-to-all-start.2 = ((bf16[16,40,3072]{2,1,0:T(8,128)(2,1)}), bf16[16,40,3072]{2,1,0:T(8,128)(2,1)}, u32[]{:S(2)}, u32[]{:S(2)}) async-start(bf16[16,40,3072]{2,1,0:T(8,128)(2,1)} %bitcast.19), calls=%async_computation.2 | async-start | bytes 7864320 | tf_op jit(solution)/shard_map/all_to_all | solution.py:439
  117.6 13.9 %copy-start.4 = (bf16[160,3072]{1,0:T(8,128)(2,1)}, bf16[160,3072]{1,0:T(8,128)(2,1)S(1)}, u32[]{:S(2)}) copy-start(bf16[160,3072]{1,0:T(8,128)(2,1)S(1)} %collective-permute-done.12.before_ref.refs_1_.refs_6_) | copy-start | bytes 2949124
  117.6 13.9 %copy-start.5 = (bf16[160,3072]{1,0:T(8,128)(2,1)}, bf16[160,3072]{1,0:T(8,128)(2,1)S(1)}, u32[]{:S(2)}) copy-start(bf16[160,3072]{1,0:T(8,128)(2,1)S(1)} %collective-permute-done.13.after_ref.refs_2_.refs_7_) | copy-start | bytes 2949124
  117.7 13.8 %collective-permute-start.14 = (bf16[80,3072]{1,0:T(8,128)(2,1)S(1)}, bf16[80,3072]{1,0:T(8,128)(2,1)S(1)}, u32[]{:S(2)}, u32[]{:S(2)}) collective-permute-start(bf16[80,3072]{1,0:T(8,128)(2,1)S(1)} %get-tuple-element.90), channel_id=1, source_target_pairs={{0,2},{1,3},{2,4},{3,5},{4,6},{5,7},{6,0},{7,1},{8,10},{9,11},{10,... | collective-permute-start | bytes 1474568 | tf_op jit(solution)/shard_map/ppermute | solution.py:40
  117.8 13.7 %collective-permute-start.15 = (bf16[80,3072]{1,0:T(8,128)(2,1)S(1)}, bf16[80,3072]{1,0:T(8,128)(2,1)S(1)}, u32[]{:S(2)}, u32[]{:S(2)}) collective-permute-start(bf16[80,3072]{1,0:T(8,128)(2,1)S(1)} %get-tuple-element.91), channel_id=1, source_target_pairs={{0,6},{1,7},{2,0},{3,1},{4,2},{5,3},{6,4},{7,5},{8,14},{9,15},{10,... | collective-permute-start | bytes 1474568 | tf_op jit(solution)/shard_map/ppermute | solution.py:40
  131.5 2.8 %copy-start.23 = (bf16[80,3072]{1,0:T(8,128)(2,1)}, bf16[80,3072]{1,0:T(8,128)(2,1)S(1)}, u32[]{:S(2)}) copy-start(bf16[80,3072]{1,0:T(8,128)(2,1)S(1)} %collective-permute-done.14.refs_3_.refs_8_) | copy-start | bytes 1474564
  131.5 2.8 %copy-start.24 = (bf16[80,3072]{1,0:T(8,128)(2,1)}, bf16[80,3072]{1,0:T(8,128)(2,1)S(1)}, u32[]{:S(2)}) copy-start(bf16[80,3072]{1,0:T(8,128)(2,1)S(1)} %collective-permute-done.15.refs_4_.refs_9_) | copy-start | bytes 1474564
  131.5 29.6 %collective-permute-start.16 = (bf16[160,4096]{1,0:T(8,128)(2,1)}, bf16[160,4096]{1,0:T(8,128)(2,1)S(1)}, u32[]{:S(2)}, u32[]{:S(2)}) collective-permute-start(bf16[160,4096]{1,0:T(8,128)(2,1)} %get-tuple-element.95.refs_10_.refs_0_), channel_id=1, source_target_pairs={{0,2},{1,3},{2,4},{3,5},{4,6},{5,7},{6,0},{7,1},{8,10},{9,11},{10,... | collective-permute-start | bytes 3932168 | tf_op jit(solution)/shard_map/ppermute | solution.py:40
  131.6 29.6 %collective-permute-start.17 = (bf16[160,4096]{1,0:T(8,128)(2,1)}, bf16[160,4096]{1,0:T(8,128)(2,1)S(1)}, u32[]{:S(2)}, u32[]{:S(2)}) collective-permute-start(bf16[160,4096]{1,0:T(8,128)(2,1)} %get-tuple-element.95.refs_10_.refs_0_), channel_id=1, source_target_pairs={{0,6},{1,7},{2,0},{3,1},{4,2},{5,3},{6,4},{7,5},{8,14},{9,15},{10,... | collective-permute-start | bytes 3932168 | tf_op jit(solution)/shard_map/ppermute | solution.py:40
  161.1 2.9 %copy-start.2 = (bf16[160,4096]{1,0:T(8,128)(2,1)}, bf16[160,4096]{1,0:T(8,128)(2,1)S(1)}, u32[]{:S(2)}) copy-start(bf16[160,4096]{1,0:T(8,128)(2,1)S(1)} %collective-permute-done.16.before_ref.refs_11_.refs_1_) | copy-start | bytes 3932164
  161.1 2.9 %copy-start.3 = (bf16[160,4096]{1,0:T(8,128)(2,1)}, bf16[160,4096]{1,0:T(8,128)(2,1)S(1)}, u32[]{:S(2)}) copy-start(bf16[160,4096]{1,0:T(8,128)(2,1)S(1)} %collective-permute-done.17.after_ref.refs_12_.refs_2_) | copy-start | bytes 3932164
  161.2 14.5 %collective-permute-start.18 = (bf16[80,4096]{1,0:T(8,128)(2,1)S(1)}, bf16[80,4096]{1,0:T(8,128)(2,1)S(1)}, u32[]{:S(2)}, u32[]{:S(2)}) collective-permute-start(bf16[80,4096]{1,0:T(8,128)(2,1)S(1)} %get-tuple-element.108), channel_id=1, source_target_pairs={{0,2},{1,3},{2,4},{3,5},{4,6},{5,7},{6,0},{7,1},{8,10},{9,11},{10,... | collective-permute-start | bytes 1966088 | tf_op jit(solution)/shard_map/ppermute | solution.py:40
  161.3 14.4 %collective-permute-start.19 = (bf16[80,4096]{1,0:T(8,128)(2,1)S(1)}, bf16[80,4096]{1,0:T(8,128)(2,1)S(1)}, u32[]{:S(2)}, u32[]{:S(2)}) collective-permute-start(bf16[80,4096]{1,0:T(8,128)(2,1)S(1)} %get-tuple-element.109), channel_id=1, source_target_pairs={{0,6},{1,7},{2,0},{3,1},{4,2},{5,3},{6,4},{7,5},{8,14},{9,15},{10,... | collective-permute-start | bytes 1966088 | tf_op jit(solution)/shard_map/ppermute | solution.py:40
  175.7 0.8 copy-start.21
  175.7 1.1 copy-start.22
  182.0 5.9 %collective-permute-start.20 = (f32[32,640]{1,0:T(8,128)}, f32[32,640]{1,0:T(8,128)S(1)}, u32[]{:S(2)}, u32[]{:S(2)}) collective-permute-start(f32[32,640]{1,0:T(8,128)} %get-tuple-element.121.own_ref), channel_id=1, source_target_pairs={{0,2},{1,3},{2,4},{3,5},{4,6},{5,7},{6,0},{7,1},{8,10},{9,11},{10,... | collective-permute-start | bytes 245768 | tf_op jit(solution)/shard_map/ppermute | solution.py:40
  182.2 5.8 %collective-permute-start.21 = (f32[32,640]{1,0:T(8,128)}, f32[32,640]{1,0:T(8,128)S(1)}, u32[]{:S(2)}, u32[]{:S(2)}) collective-permute-start(f32[32,640]{1,0:T(8,128)} %get-tuple-element.121.own_ref), channel_id=1, source_target_pairs={{0,6},{1,7},{2,0},{3,1},{4,2},{5,3},{6,4},{7,5},{8,14},{9,15},{10,... | collective-permute-start | bytes 245768 | tf_op jit(solution)/shard_map/ppermute | solution.py:40
  184.8 5.0 %collective-permute-start.22 = (f32[32,640]{1,0:T(8,128)}, f32[32,640]{1,0:T(8,128)S(1)}, u32[]{:S(2)}, u32[]{:S(2)}) collective-permute-start(f32[32,640]{1,0:T(8,128)} %get-tuple-element.121.own_ref), channel_id=1, source_target_pairs={{0,4},{1,5},{2,6},{3,7},{4,0},{5,1},{6,2},{7,3},{8,12},{9,13},{10,... | collective-permute-start | bytes 245768 | tf_op jit(solution)/shard_map/ppermute | solution.py:40
  185.5 4.3 %copy-start.10 = (s32[640,1]{1,0:T(8,128)S(1)}, s32[640,1]{1,0:T(8,128)}, u32[]{:S(2)}) copy-start(s32[640,1]{1,0:T(8,128)} %constant.12.clone.came_ref) | copy-start | bytes 7684
  185.5 4.3 %copy-start.11 = (f32[32,640]{1,0:T(8,128)S(1)}, f32[32,640]{1,0:T(8,128)}, u32[]{:S(2)}) copy-start(f32[32,640]{1,0:T(8,128)} %get-tuple-element.121.own_ref) | copy-start | bytes 245764
  189.8 6.8 %copy-start.27 = (f32[32,256]{1,0:T(8,128)S(1)}, f32[32,256]{1,0:T(8,128)}, u32[]{:S(2)}) copy-start(f32[32,256]{1,0:T(8,128)} %get-tuple-element.125) | copy-start | bytes 98308
  189.8 8.0 %copy-start.12 = (f32[32,256]{1,0:T(8,128)S(1)}, f32[32,256]{1,0:T(8,128)}, u32[]{:S(2)}) copy-start(f32[32,256]{1,0:T(8,128)} %get-tuple-element.124.grads_ref) | copy-start | bytes 98308
  190.9 6.9 %collective-permute-start.23 = (f32[2,16,896]{2,1,0:T(8,128)S(1)}, f32[2,16,896]{2,1,0:T(8,128)S(1)}, u32[]{:S(2)}, u32[]{:S(2)}) collective-permute-start(f32[2,16,896]{2,1,0:T(8,128)S(1)} %get-tuple-element.123), channel_id=1, source_target_pairs={{0,1},{1,0},{2,3},{3,2},{4,5},{5,4},{6,7},{7,6},{8,9},{9,8},{10,11... | collective-permute-start | bytes 344072 | tf_op jit(solution)/shard_map/ppermute | solution.py:45
  196.6 1.2 collective-permute-start.24

commit v5 on v4

--- a/solution.py
+++ b/solution.py
@@ -3,7 +3,6 @@
 
 import jax
 import jax.numpy as jnp
-import numpy as np
 from jax import lax
 from jax.experimental import pallas as pl
 from jax.experimental.pallas import tpu as pltpu
@@ -49,15 +48,20 @@
     return shift_y(rows, 1), shift_y(rows, -1)
 
 
+def exchanged(value):
+    far = shift_y(value, 2)
+    return value, shift_y(value, 1), shift_y(value, -1), far
+
+
 def split_kernel(before_ref, after_ref, low_ref, high_ref):
     low_ref[...] = before_ref[...]
     high_ref[...] = after_ref[...]
 
 
-def second_step(before, after):
+def split_rows(before, after):
     rows, columns = before.shape[0] // 2, before.shape[1]
     part = pl.BlockSpec((rows, columns), lambda i: (0, 0))
-    low, high = call(
+    return call(
         split_kernel,
         (shape((rows, columns), before.dtype),) * 2,
         16,
@@ -66,7 +70,14 @@
         in_specs=[part, pl.BlockSpec((rows, columns), lambda i: (1, 0))],
         out_specs=(part,) * 2,
     )(before, after)
+
+
+def forward(low, high):
     return shift_y(low, 1), shift_y(high, -1)
+
+
+def second_step(before, after):
+    return forward(*split_rows(before, after))
 
 
 def shape(dims, dtype):
@@ -100,6 +111,25 @@
     raw_ref[:, late:] = codes[:, : raw_ref.shape[1] - late].astype(BF16)
 
 
+def index_parts(count, outer, inner):
+    row = lax.broadcasted_iota(jnp.int32, (count, 1), 0).astype(F32)
+    first = jnp.floor((row + 0.5) * (1.0 / (outer * inner)))
+    row = row - first * (outer * inner)
+    second = jnp.floor((row + 0.5) * (1.0 / inner))
+    return [part.astype(jnp.int32) for part in (first, second, row - second * inner)]
+
+
+def wanted(count, capacity):
+    expert, piece, slot = index_parts(count, 4, capacity)
+    return expert * capacity + slot, piece
+
+
+def order_of(count, capacity):
+    piece, source, slot = index_parts(count, count // (4 * capacity), capacity)
+    came = source * (4 * capacity) + piece * capacity + slot
+    return (lax.broadcasted_iota(jnp.int32, (count, count), 1) == came).astype(BF16)
+
+
 def code_kernel(experts, capacity, ids_ref, code_ref):
     ids = ids_ref[...]
     count = ids.shape[1]
@@ -113,11 +143,12 @@
     code_ref[...] = ids * capacity + slot
 
 
-def pack_kernel(spans, code_ref, want_ref, piece_ref, *refs):
+def pack_kernel(spans, capacity, code_ref, *refs):
     out = refs[-1]
-    hit = code_ref[...] == want_ref[...]
+    want, piece = wanted(out.shape[0], capacity)
+    hit = code_ref[...] == want
     placing = jnp.concatenate(
-        [(hit & (piece_ref[...] == q)).astype(BF16) for q in range(PIECES)], axis=1
+        [(hit & (piece == q)).astype(BF16) for q in range(PIECES)], axis=1
     )
     at = 0
     for rows, (first, size) in zip(refs, spans):
@@ -129,11 +160,9 @@
         at += part
 
 
-def unpack_kernel(got_ref, came_ref, *outs):
+def unpack_kernel(capacity, got_ref, *outs):
     count = got_ref.shape[0]
-    take = (
-        lax.broadcasted_iota(jnp.int32, (count, count), 1) == came_ref[...]
-    ).astype(BF16)
+    take = order_of(count, capacity)
     rows = count // PIECES
     at = 0
     for out in outs:
@@ -144,16 +173,17 @@
         at += part
 
 
-def pack_raw_kernel(want_ref, plane_ref, *refs):
+def pack_raw_kernel(capacity, *refs):
     pieces, codes, out, placing = refs[:5], refs[5:10], refs[10], refs[11]
 
     @pl.when(pl.program_id(0) == 0)
     def _():
         code = jnp.concatenate([piece[...] for piece in codes], axis=0).astype(F32)
         count = code.shape[0] // 4
+        want, plane = wanted(out.shape[0], capacity)
         for k in range(4):
             row = code[k * count : (k + 1) * count].T[:1].astype(jnp.int32)
-            hit = (row == want_ref[...]) & (plane_ref[...] == k)
+            hit = (row == want) & (plane == k)
             placing[:, k * count : (k + 1) * count] = hit.astype(BF16)
 
     stacked = jnp.concatenate([piece[...] for piece in pieces], axis=0)
@@ -214,12 +244,7 @@
     return high, (value - high.astype(F32)).astype(BF16)
 
 
-def order_of(came_ref):
-    count = came_ref.shape[0]
-    return (lax.broadcasted_iota(jnp.int32, (count, count), 1) == came_ref[...]).astype(BF16)
-
-
-def raw_kernel(got_ref, came_ref, down_o, down_p, first, total_ref, low_ref, total, low):
+def raw_kernel(capacity, got_ref, down_o, down_p, first, total_ref, low_ref, total, low):
     units = down_o.shape[0]
     step = pl.program_id(0)
 
@@ -235,7 +260,7 @@
 
     @pl.when(step == pl.num_programs(0) - 1)
     def _():
-        order = order_of(came_ref)
+        order = order_of(total.shape[0], capacity)
         for source, out in ((total, total_ref), (low, low_ref)):
             high_part, low_part = halves(source[...])
             out[...] = dot(order, high_part) + dot(order, low_part)
@@ -253,7 +278,7 @@
     prev, (factor_ref, hidden_ref, low_in_ref) = take(2), take(3)
     gb_o, gb_p, da_o, da_p = take(4)
     if last:
-        sums_before, *grads_before, sums_back = take(4)
+        sums_before, *grads_before = take(3)
     sums_ref, grads_o_ref, grads_p_ref, total, low = refs
     step = pl.program_id(0)
     units = down_o.shape[0]
@@ -283,9 +308,8 @@
         grads_b = contract_first(lowrank_back, hidden_ref[...])
         if last:
             done = sums_before.shape[1]
-            sums_ref[:rank, :done] = sums_before[...]
-            sums_ref[:rank, done:] = sums
-            sums_ref[rank:, :] = sums_back[...]
+            sums_ref[:, :done] = sums_before[...]
+            sums_ref[:, done:] = sums
         else:
             sums_ref[...] = sums
         for i, (out, top) in enumerate(((grads_o_ref, grads_o), (grads_p_ref, grads_p))):
@@ -338,25 +362,28 @@
                 copy.wait()
 
 
-def product_kernel(rest, me_ref, came_ref, tok_ref, cot_ref, own_ref, *refs):
-    others, (mine_ref, theirs_ref) = refs[:3], refs[3:]
+def product_kernel(rest, capacity, me_ref, tok_ref, cot_ref, *refs):
+    mine_ref, theirs_ref = refs[-2:]
     rank, span = mine_ref.shape[1], tok_ref.shape[1]
     slots = tok_ref.shape[0] // 4
     me = me_ref[0]
-    sums = own_ref[...]
-    for other, order in zip(others, ((2, 0, 3, 1), (1, 3, 0, 2), (3, 2, 1, 0))):
-        value = other[...]
-        sums = sums + jnp.concatenate([value[:, i * slots : (i + 1) * slots] for i in order], axis=1)
-    high, low = halves(sums)
+    totals = []
+    for own, *others in (refs[:4], refs[4:8]):
+        total = own[...]
+        for other, order in zip(others, ((2, 0, 3, 1), (1, 3, 0, 2), (3, 2, 1, 0))):
+            value = other[...]
+            total = total + jnp.concatenate(
+                [value[:, i * slots : (i + 1) * slots] for i in order], axis=1
+            )
+        totals.append(total)
     half = span // 2
     even = lax.rem(me, 2) == 0
     crossed = lax.broadcasted_iota(jnp.int32, (rank, span), 1) + lax.div(me, 2) * span >= rest
     for side, rows_ref in enumerate((tok_ref, cot_ref)):
-        at = slice(side * rank, (side + 1) * rank)
-        both = jnp.concatenate([high[at], low[at]], axis=0)
+        both = jnp.concatenate(halves(totals[side]), axis=0)
         rows = rows_ref[...]
         if side == 1:
-            both = jnp.concatenate([both, dot(both, order_of(came_ref)).astype(BF16)], axis=0)
+            both = jnp.concatenate([both, dot(both, order_of(rows.shape[0], capacity)).astype(BF16)], axis=0)
         wide = dot(both, rows)
         if side == 1:
             moved = wide[2 * rank : 3 * rank] + wide[3 * rank :]
@@ -403,18 +430,13 @@
     down_a, down_b = down_adapter_first[0], down_adapter_second[0]
     rank, units = gate_b.shape
 
-    at_row = np.arange(every, dtype=np.int32)[:, None]
-    want = at_row // (4 * capacity) * capacity + at_row % capacity
-    quarter = at_row // capacity % 4
-    came = at_row % slots // capacity * 4 * capacity + at_row // slots * capacity + at_row % capacity
-
     code = call(
         functools.partial(code_kernel, experts, capacity), shape((1, count), jnp.int32), 16, moved=1024
     )(chosen_expert_index.reshape(1, count))
     scaled, raw = call(
         scale_kernel,
         (shape((count, rest), BF16), shape((count, late + LANES), BF16)),
-        16,
+        VMEM_MIB,
         moved=4 * count * width,
     )(cotangent, router_weight.reshape(1, count), code)
     raw_steps = first_step(raw)
@@ -423,16 +445,16 @@
         spans = [(first, size) for _, first, size in sources]
         part = sum(size for _, size in spans) // PIECES
         return call(
-            functools.partial(pack_kernel, spans),
+            functools.partial(pack_kernel, spans, capacity),
             shape((every, part), BF16),
             32,
             flops=2 * every * PIECES * count * part,
             moved=2 * (PIECES * count + every) * part,
             grid=(1,),
-            in_specs=[whole(1, count), whole(every, 1), whole(every, 1)]
+            in_specs=[whole(1, count)]
             + [whole(*rows.shape) for rows, _, _ in sources],
             out_specs=whole(every, part),
-        )(code, want, quarter, *[rows for rows, _, _ in sources])
+        )(code, *[rows for rows, _, _ in sources])
 
     def across_dp(packed):
         sent = packed.reshape(experts, -1, packed.shape[1])
@@ -440,12 +462,12 @@
 
     def unpack(got, *sizes):
         return call(
-            unpack_kernel,
+            functools.partial(unpack_kernel, capacity),
             tuple(shape((slots, size), BF16) for size in sizes),
             VMEM_MIB,
             flops=2 * every * every * got.shape[1] // COVER,
             moved=4 * every * got.shape[1] // COVER,
-        )(got, came)
+        )(got)
 
     mine = (gate_w, up_w, down_w, jnp.concatenate([gate_b, down_a], axis=0))
     got = across_dp(pack(code, (tokens, *spans[0])))
@@ -463,21 +485,20 @@
     raw_pieces = (raw, *raw_steps, *raw_far)
     wide = late // PIECES
     packed_raw = call(
-        pack_raw_kernel,
+        functools.partial(pack_raw_kernel, capacity),
         shape((every, late), BF16),
         VMEM_MIB,
         flops=2 * every * 4 * count * late,
         moved=2 * (4 * count + every) * late,
         grid=(PIECES,),
-        in_specs=[whole(every, 1), whole(every, 1)]
-        + [pl.BlockSpec((piece.shape[0], wide), lambda i: (0, i)) for piece in raw_pieces]
+        in_specs=[pl.BlockSpec((piece.shape[0], wide), lambda i: (0, i)) for piece in raw_pieces]
         + [
             pl.BlockSpec((piece.shape[0], LANES), lambda i: (0, late // LANES))
             for piece in raw_pieces
         ],
         out_specs=pl.BlockSpec((every, wide), lambda i: (0, i)),
         scratch_shapes=[pltpu.VMEM((every, 4 * count), BF16)],
-    )(want, quarter, *raw_pieces, *raw_pieces)
+    )(*raw_pieces, *raw_pieces)
     got, theirs, packed_raw = tie((got, tuple(swap_core(w) for w in mine), packed_raw))
     gate_p, up_p, down_p, small_p = theirs
     small = (gate_b, small_p[:rank], down_a, small_p[rank:])
@@ -525,17 +546,18 @@
     rows_1, far_0 = tie((rows_1, far_0))
     got_raw = across_dp(packed_raw)
     steps_1 = first_step(rows_1)
-    steps_1, rows_0 = tie((steps_1, rows_0))
     pieces_0 = (rows_0, *steps_0, *far_0)
     part_0 = gate_up(0, pieces_0, None)
-    far_1 = second_step(*steps_1)
-    far_1, rows_2 = tie((far_1, rows_2))
+    steps_1, part_0 = tie((steps_1, part_0))
+    halves_1 = split_rows(*steps_1)
+    halves_1, rows_2 = tie((halves_1, rows_2))
+    far_1 = forward(*halves_1)
     steps_2 = first_step(rows_2)
     pieces_1 = (rows_1, *steps_1, *far_1)
     hidden, factor, low_in, sums_back = gate_up(1, pieces_1, part_0)
     depth = math.gcd(rest, late)
     back_0, low_0 = call(
-        raw_kernel,
+        functools.partial(raw_kernel, capacity),
         (totals[0], totals[2]),
         VMEM_MIB,
         flops=2 * every * late * 2 * units,
@@ -543,14 +565,14 @@
         grid=(late // depth,),
         in_specs=[
             pl.BlockSpec((every, depth), lambda i: (0, i)),
-            whole(every, 1),
             flat(units, depth, rest),
             flat(units, depth, rest),
             flat(rank, depth, rest),
         ],
         out_specs=(whole(every, 2 * units), whole(every, rank)),
         scratch_shapes=[scratch[0], scratch[2]],
-    )(got_raw, came, down_w, down_p, down_b)
+    )(got_raw, down_w, down_p, down_b)
+    sums_back = exchanged(sums_back)
     steps_2, hidden, back_0 = tie((steps_2, hidden, back_0))
     far_2 = second_step(*steps_2)
 
@@ -561,14 +583,14 @@
             return pl.BlockSpec((rows, columns), lambda i: (at // rows, 0))
 
         outs = (
-            shape((2 * rank if last else rank, every if last else rows), F32),
+            shape((rank, every if last else rows), F32),
             *[shape((2 * rank, units), F32)] * 2,
         )
         depth = rest // 2
         return call(
             functools.partial(back_kernel, last, len(pieces)),
             outs,
-            VMEM_MIB,
+            24 if last else 44,
             flops=2 * rows * rest * 2 * units,
             moved=2 * rest * (rows + 2 * units),
             grid=(rest // depth,),
@@ -582,9 +604,10 @@
             scratch_shapes=[pltpu.VMEM((rows, 2 * units), F32), pltpu.VMEM((rows, rank), F32)],
         )(*pieces, down_w, down_p, down_b, back_0, low_0, factor, hidden, low_in, *small, *before)
 
+    far_2, sums_back = tie((far_2, sums_back))
     pieces_2 = (rows_2, *steps_2, *far_2)
     near = back(False, pieces_2[:3], 0)
-    sums, grads, for_other = back(True, pieces_2[3:], 3 * slots, *near, sums_back)
+    sums, grads, for_other = back(True, pieces_2[3:], 3 * slots, *near)
 
     me = lax.axis_index("seq").astype(jnp.int32).reshape(1)
     share = width // lax.axis_size("seq")
@@ -600,15 +623,15 @@
         scratch_shapes=[pltpu.SemaphoreType.DMA((len(chunks),))],
     )(me, *chunks)
     own, other = call(
-        functools.partial(product_kernel, rest),
+        functools.partial(product_kernel, rest, capacity),
         (shape((2, rank, share), F32),) * 2,
         16,
         flops=8 * rank * every * share,
         moved=8 * every * share,
-        in_specs=[scalar, whole(every, 1)]
+        in_specs=[scalar]
         + [pl.BlockSpec(memory_space=pltpu.VMEM)] * 2
-        + [whole(2 * rank, every)] * 4,
-    )(me, came, tok, cot, sums, shift_y(sums, 1), shift_y(sums, -1), shift_y(sums, 2))
+        + [whole(rank, every)] * 8,
+    )(me, tok, cot, *exchanged(sums), *sums_back)
     return tuple(
         call(
             final_kernel,

time: 199 us -> 194 us (0.975)
  waiting for transfers between devices: 59.3 us -> 51.6 us
  starting transfers between devices: 56 us -> 63.6 us
  local copies, waits for them, and re-layouts: 10.4 us -> 6.86 us
    ppermute x19 -> x22, waiting for transfers between devices: 51.6 us -> 43.4 us  [shift_y(): return lax.ppermute(value, 'seq', pairs)]
    unnamed x56 -> x68, local copies, waits for them, and re-layouts: 9.75 us -> 6.25 us
    pallas_call x13, Pallas kernels: 44.5 us -> 41 us  [the longest x2 10.2 us: back(): call(functools.partial(back_kernel, last, len(pieces)), outs, 24 if last...]
    ppermute x19 -> x22, starting transfers between devices: 25.9 us -> 29.4 us  [shift_y(): return lax.ppermute(value, 'seq', pairs)]
    all_to_all x3, starting transfers between devices: 17.7 us -> 20.6 us  [across_dp(): lax.all_to_all(sent, 'dp', split_axis=0, concat_axis=0, tiled=True)]
  transfers between devices with their start and end apart: 28 -> 31, of which waited for: 10 -> 10; matrix products, arithmetic and copies ran while one was open for 0% -> 0% of each run, Pallas kernels for 32% -> 32%
where the time goes in v5:
time: 194 us; the launch traced here: 193 us
  Pallas kernels  70.4 us (36%)
  starting transfers between devices  63.6 us (33%)
  waiting for transfers between devices  51.6 us (27%)
  local copies, waits for them, and re-layouts  6.86 us (4%)
    ppermute x22, waiting for transfers between devices, shift_y(): return lax.ppermute(value, 'seq', pairs)  43.4 us
    ppermute x22, starting transfers between devices, shift_y(): return lax.ppermute(value, 'seq', pairs)  29.4 us
    pallas_call x2, Pallas kernels, gate_up(): call(functools.partial(gate_up_kernel, begins, last), outs, VMEM_MIB, flo...  22.9 us
    all_to_all x3, starting transfers between devices, across_dp(): lax.all_to_all(sent, 'dp', split_axis=0, concat_axis=0, tiled=True)  20.6 us
    ppermute x6, starting transfers between devices, swap_core(): return lax.ppermute(value, 'seq', [(i, i ^ 1) for i in range(size)])  13.7 us
    pallas_call x2, Pallas kernels, back(): call(functools.partial(back_kernel, last, len(pieces)), outs, 24 if last...  10.2 us
    pallas_call x1, Pallas kernels, body(): call(functools.partial(raw_kernel, capacity), (totals[0], totals[2]), VME...  8.86 us
    pallas_call x2, Pallas kernels, unpack(): call(functools.partial(unpack_kernel, capacity), tuple((shape((slots, siz...  8.51 us
  transfers between devices with their start and end apart: 31, of which 10 were waited for; matrix products, arithmetic and copies ran while one was open for 0% of the time, Pallas kernels for 32%

profile of v5, /device:TPU:1, one launch (start us, length us, event | category | flops | bytes accessed | tf_op | source)
XLA Modules:
  0.0 193.5 jit_solution(11824227741865022138)
XLA Ops:
  0.7 0.8 copy-done.24
  1.4 0.1 shard_map.138.code_ref
  1.6 0.5 copy-done.18
  2.1 3.2 %shard_map.140 = (bf16[128,4096]{1,0:T(8,128)(2,1)}, bf16[128,3200]{1,0:T(8,128)(2,1)}) custom-call(bf16[128,7168]{1,0:T(8,128)(2,1)} %cot_ref.1, f32[1,128]{1,0:T(1,128)} %bitcast.34, s32[1,128]{1,0:T(1,128)} %copy-done.18), custom_call_target="tpu_custom_call" | custom-call | bytes 29360128 | tf_op jit(solution)/shard_map/pallas_call | solution.py:436
  5.3 2.1 %collective-permute-start = (bf16[128,3200]{1,0:T(8,128)(2,1)}, bf16[128,3200]{1,0:T(8,128)(2,1)S(1)}, u32[]{:S(2)}, u32[]{:S(2)}) collective-permute-start(bf16[128,3200]{1,0:T(8,128)(2,1)} %get-tuple-element.73.refs_0_.refs_5_), channel_id=1, source_target_pairs={{0,2},{1,3},{2,4},{3,5},{4,6},{5,7},{6,0},{7,1},{8,10},{9,11},{10,... | collective-permute-start | bytes 2457608 | tf_op jit(solution)/shard_map/ppermute | solution.py:39
  7.5 1.4 collective-permute-start.1
  8.9 2.0 %shard_map.139 = bf16[640,1024]{1,0:T(8,128)(2,1)} custom-call(s32[1,128]{1,0:T(1,128)S(1)} %copy-done.19, bf16[128,7168]{1,0:T(8,128)(2,1)S(1)} %copy-done.21), custom_call_target="tpu_custom_call" | custom-call | flops 5368709120 | bytes 18874368 | tf_op jit(solution)/shard_map/pallas_call | solution.py:447
  11.0 7.6 %all-to-all-start = ((bf16[16,40,1024]{2,1,0:T(8,128)(2,1)}), bf16[16,40,1024]{2,1,0:T(8,128)(2,1)}, u32[]{:S(2)}, u32[]{:S(2)}) async-start(bf16[16,40,1024]{2,1,0:T(8,128)(2,1)} %bitcast.2), calls=%async_computation | async-start | bytes 2621440 | tf_op jit(solution)/shard_map/all_to_all | solution.py:461
  18.6 1.5 collective-permute-start.8
  20.1 0.1 collective-permute-start.6
  20.2 0.4 collective-permute-start.7
  20.6 6.4 %collective-permute-done.before_ref.refs_1_.refs_6_ = bf16[128,3200]{1,0:T(8,128)(2,1)S(1)} collective-permute-done((bf16[128,3200]{1,0:T(8,128)(2,1)}, bf16[128,3200]{1,0:T(8,128)(2,1)S(1)}, u32[]{:S(2)}, u32[]{:S(2)}) %collective-permute-start) | collective-permute-done | bytes 819232 | tf_op jit(solution)/shard_map/ppermute | solution.py:39
  27.0 1.0 shard_map.143
  28.1 0.9 collective-permute-start.2
  28.9 1.8 collective-permute-start.3
  30.8 1.2 copy-done.22
  32.0 1.5 shard_map.141
  33.6 1.3 copy-done.6
  34.9 1.7 all-to-all-done
  36.6 3.7 %shard_map.142.refs_0_ = bf16[160,4096]{1,0:T(8,128)(2,1)} custom-call(bf16[640,1024]{1,0:T(8,128)(2,1)} %bitcast.3.got_ref), custom_call_target="tpu_custom_call" | custom-call | flops 838860800 | bytes 2621440 | tf_op jit(solution)/shard_map/pallas_call | solution.py:464
  40.3 2.7 %collective-permute-start.5 = (bf16[160,4096]{1,0:T(8,128)(2,1)}, bf16[160,4096]{1,0:T(8,128)(2,1)S(1)}, u32[]{:S(2)}, u32[]{:S(2)}) collective-permute-start(bf16[160,4096]{1,0:T(8,128)(2,1)} %shard_map.142.refs_0_), channel_id=1, source_target_pairs={{0,6},{1,7},{2,0},{3,1},{4,2},{5,3},{6,4},{7,5},{8,14},{9,15},{10,... | collective-permute-start | bytes 3932168 | tf_op jit(solution)/shard_map/ppermute | solution.py:39
  43.0 6.5 %all-to-all-start.1 = ((bf16[16,40,1792]{2,1,0:T(8,128)(2,1)}), bf16[16,40,1792]{2,1,0:T(8,128)(2,1)}, u32[]{:S(2)}, u32[]{:S(2)}) async-start(bf16[16,40,1792]{2,1,0:T(8,128)(2,1)} %bitcast.16), calls=%async_computation.1 | async-start | bytes 4587520 | tf_op jit(solution)/shard_map/all_to_all | solution.py:461
  49.6 18.8 %collective-permute-done.4.before_ref.refs_1_ = bf16[160,4096]{1,0:T(8,128)(2,1)S(1)} collective-permute-done((bf16[160,4096]{1,0:T(8,128)(2,1)}, bf16[160,4096]{1,0:T(8,128)(2,1)S(1)}, u32[]{:S(2)}, u32[]{:S(2)}) %collective-permute-start.4) | collective-permute-done | bytes 1310752 | tf_op jit(solution)/shard_map/ppermute | solution.py:39
  68.4 4.5 %collective-permute-start.9 = (bf16[32,256]{1,0:T(8,128)(2,1)S(1)}, bf16[32,256]{1,0:T(8,128)(2,1)S(1)}, u32[]{:S(2)}, u32[]{:S(2)}) collective-permute-start(bf16[32,256]{1,0:T(8,128)(2,1)S(1)} %pad_maximum_fusion), channel_id=1, source_target_pairs={{0,1},{1,0},{2,3},{3,2},{4,5},{5,4},{6,7},{7,6},{8,9},{9,8},{10,11... | collective-permute-start | bytes 49160 | tf_op jit(solution)/shard_map/ppermute | solution.py:44
  72.9 1.0 shard_map.146
  74.0 2.7 %collective-permute-start.11 = (bf16[80,4096]{1,0:T(8,128)(2,1)S(1)}, bf16[80,4096]{1,0:T(8,128)(2,1)}, u32[]{:S(2)}, u32[]{:S(2)}) collective-permute-start(bf16[80,4096]{1,0:T(8,128)(2,1)S(1)} %get-tuple-element.91), channel_id=1, source_target_pairs={{0,6},{1,7},{2,0},{3,1},{4,2},{5,3},{6,4},{7,5},{8,14},{9,15},{10,... | collective-permute-start | bytes 1966088 | tf_op jit(solution)/shard_map/ppermute | solution.py:39
  76.7 6.5 %shard_map.144 = bf16[640,3072]{1,0:T(8,128)(2,1)} custom-call(bf16[128,3200]{1,0:T(8,128)(2,1)} %get-tuple-element.73.refs_0_.refs_5_, bf16[128,3200]{1,0:T(8,128)(2,1)} %copy-done.7, bf16[128,3200]{1,0:T(8,128)(2,1)} %copy-done.8, bf16[64,3200]{1,0:T(8,128)(2,1)} %collective-permute-done.2.refs_3_.refs_8_, ...), custom_call_target="tpu_custom_call" | custom-call | flops 16106127360 | bytes 56623104 | tf_op jit(solution)/shard_map/pallas_call | solution.py:487
  83.2 4.8 %shard_map.145 = (bf16[160,3072]{1,0:T(8,128)(2,1)}, bf16[160,4096]{1,0:T(8,128)(2,1)}) custom-call(bf16[640,1792]{1,0:T(8,128)(2,1)} %bitcast.6.got_ref), custom_call_target="tpu_custom_call" | custom-call | flops 1468006400 | bytes 4587520 | tf_op jit(solution)/shard_map/pallas_call | solution.py:464
  88.0 3.7 %collective-permute-done.10.refs_3_ = bf16[80,4096]{1,0:T(8,128)(2,1)} collective-permute-done((bf16[80,4096]{1,0:T(8,128)(2,1)}, bf16[80,4096]{1,0:T(8,128)(2,1)}, u32[]{:S(2)}, u32[]{:S(2)}) %collective-permute-start.10) | collective-permute-done | bytes 655392 | tf_op jit(solution)/shard_map/ppermute | solution.py:39
  91.8 2.7 %collective-permute-start.13 = (bf16[160,3072]{1,0:T(8,128)(2,1)}, bf16[160,3072]{1,0:T(8,128)(2,1)S(1)}, u32[]{:S(2)}, u32[]{:S(2)}) collective-permute-start(bf16[160,3072]{1,0:T(8,128)(2,1)} %get-tuple-element.94.refs_0_.refs_5_), channel_id=1, source_target_pairs={{0,6},{1,7},{2,0},{3,1},{4,2},{5,3},{6,4},{7,5},{8,14},{9,15},{10,... | collective-permute-start | bytes 2949128 | tf_op jit(solution)/shard_map/ppermute | solution.py:39
  94.5 6.4 %all-to-all-start.2 = ((bf16[16,40,3072]{2,1,0:T(8,128)(2,1)}), bf16[16,40,3072]{2,1,0:T(8,128)(2,1)}, u32[]{:S(2)}, u32[]{:S(2)}) async-start(bf16[16,40,3072]{2,1,0:T(8,128)(2,1)} %bitcast.33), calls=%async_computation.2 | async-start | bytes 7864320 | tf_op jit(solution)/shard_map/all_to_all | solution.py:461
  100.9 11.1 %shard_map.147 = (f32[640,512]{1,0:T(8,128)}, f32[640,512]{1,0:T(8,128)}, f32[640,16]{1,0:T(8,128)}) custom-call(bf16[160,4096]{1,0:T(8,128)(2,1)} %shard_map.142.refs_0_, bf16[160,4096]{1,0:T(8,128)(2,1)} %copy-done, bf16[160,4096]{1,0:T(8,128)(2,1)} %copy-done.1, bf16[80,4096]{1,0:T(8,128)(2,1)} %collective-permute-done.10.refs_3_, ...), custom_call_target="tpu_custom_call" | custom-call | flops 42949672960 | bytes 109051904 | tf_op jit(solution)/shard_map/pallas_call | solution.py:531
  111.9 3.8 %collective-permute-done.12.before_ref.refs_1_.refs_6_ = bf16[160,3072]{1,0:T(8,128)(2,1)S(1)} collective-permute-done((bf16[160,3072]{1,0:T(8,128)(2,1)}, bf16[160,3072]{1,0:T(8,128)(2,1)S(1)}, u32[]{:S(2)}, u32[]{:S(2)}) %collective-permute-start.12) | collective-permute-done | bytes 983072 | tf_op jit(solution)/shard_map/ppermute | solution.py:39
  115.8 0.1 shard_map.148
  115.8 0.1 collective-permute-start.14
  115.9 2.7 %collective-permute-start.15 = (bf16[80,3072]{1,0:T(8,128)(2,1)S(1)}, bf16[80,3072]{1,0:T(8,128)(2,1)S(1)}, u32[]{:S(2)}, u32[]{:S(2)}) collective-permute-start(bf16[80,3072]{1,0:T(8,128)(2,1)S(1)} %get-tuple-element.106), channel_id=1, source_target_pairs={{0,6},{1,7},{2,0},{3,1},{4,2},{5,3},{6,4},{7,5},{8,14},{9,15},{10,... | collective-permute-start | bytes 1474568 | tf_op jit(solution)/shard_map/ppermute | solution.py:39
  118.6 0.6 fusion
  119.2 2.7 %collective-permute-start.17 = (bf16[160,4096]{1,0:T(8,128)(2,1)}, bf16[160,4096]{1,0:T(8,128)(2,1)S(1)}, u32[]{:S(2)}, u32[]{:S(2)}) collective-permute-start(bf16[160,4096]{1,0:T(8,128)(2,1)} %get-tuple-element.107.refs_10_.refs_0_), channel_id=1, source_target_pairs={{0,6},{1,7},{2,0},{3,1},{4,2},{5,3},{6,4},{7,5},{8,14},{9,15},{10,... | collective-permute-start | bytes 3932168 | tf_op jit(solution)/shard_map/ppermute | solution.py:39
  121.9 6.4 %collective-permute-done.14.refs_3_.refs_8_ = bf16[80,3072]{1,0:T(8,128)(2,1)S(1)} collective-permute-done((bf16[80,3072]{1,0:T(8,128)(2,1)S(1)}, bf16[80,3072]{1,0:T(8,128)(2,1)S(1)}, u32[]{:S(2)}, u32[]{:S(2)}) %collective-permute-start.14) | collective-permute-done | bytes 491552 | tf_op jit(solution)/shard_map/ppermute | solution.py:39
  128.3 0.8 copy-done.32
  129.1 0.2 copy-done.33
  129.3 11.8 %shard_map.149 = (bf16[640,512]{1,0:T(8,128)(2,1)}, f32[640,512]{1,0:T(8,128)}, bf16[640,16]{1,0:T(8,128)(2,1)}, f32[16,640]{1,0:T(8,128)}) custom-call(bf16[160,3072]{1,0:T(8,128)(2,1)} %get-tuple-element.94.refs_0_.refs_5_, bf16[160,3072]{1,0:T(8,128)(2,1)} %copy-done.4, bf16[160,3072]{1,0:T(8,128)(2,1)} %copy-done.5, bf16[80,3072]{1,0:T(8,128)(2,1)} %copy-done.32, ...), custom_call_target="tpu_custom_call" | custom-call | flops 32212254720 | bytes 81788928 | tf_op jit(solution)/shard_map/pallas_call | solution.py:531
  141.1 0.2 collective-permute-start.20
  141.3 2.6 %collective-permute-start.21 = (f32[16,640]{1,0:T(8,128)}, f32[16,640]{1,0:T(8,128)S(1)}, u32[]{:S(2)}, u32[]{:S(2)}) collective-permute-start(f32[16,640]{1,0:T(8,128)} %get-tuple-element.134.refs_4_), channel_id=1, source_target_pairs={{0,6},{1,7},{2,0},{3,1},{4,2},{5,3},{6,4},{7,5},{8,14},{9,15},{10,... | collective-permute-start | bytes 122888 | tf_op jit(solution)/shard_map/ppermute | solution.py:39
  143.9 0.8 collective-permute-start.22
  144.6 5.3 %all-to-all-done.2 = bf16[16,40,3072]{2,1,0:T(8,128)(2,1)} async-done(((bf16[16,40,3072]{2,1,0:T(8,128)(2,1)}), bf16[16,40,3072]{2,1,0:T(8,128)(2,1)}, u32[]{:S(2)}, u32[]{:S(2)}) %all-to-all-start.2) | async-done | bytes 3932192 | tf_op jit(solution)/shard_map/all_to_all | solution.py:461
  149.9 8.9 %shard_map.150 = (f32[640,512]{1,0:T(8,128)}, f32[640,16]{1,0:T(8,128)}) custom-call(bf16[640,3072]{1,0:T(8,128)(2,1)} %bitcast.14.got_ref.refs_15_, bf16[256,7168]{1,0:T(8,128)(2,1)} %bitcast.26, bf16[256,7168]{1,0:T(8,128)(2,1)} %collective-permute-done.8.down_p.refs_4_.refs_3_, bf16[16,7168]{1,0:T(8,128)(2,1)} %bitcast.29), custom_call_target="tpu_custom_call" | custom-call | flops 16106127360 | bytes 56623104 | tf_op jit(solution)/shard_map/pallas_call | solution.py:559
  158.9 0.1 shard_map.151
  159.0 0.1 collective-permute-start.18
  159.1 2.7 %collective-permute-start.19 = (bf16[80,4096]{1,0:T(8,128)(2,1)S(1)}, bf16[80,4096]{1,0:T(8,128)(2,1)S(1)}, u32[]{:S(2)}, u32[]{:S(2)}) collective-permute-start(bf16[80,4096]{1,0:T(8,128)(2,1)S(1)} %get-tuple-element.119), channel_id=1, source_target_pairs={{0,6},{1,7},{2,0},{3,1},{4,2},{5,3},{6,4},{7,5},{8,14},{9,15},{10,... | collective-permute-start | bytes 1966088 | tf_op jit(solution)/shard_map/ppermute | solution.py:39
  161.8 1.3 copy-done.27
  163.1 6.0 %shard_map.153 = (f32[16,480]{1,0:T(8,128)S(1)}, f32[32,256]{1,0:T(8,128)S(1)}, f32[32,256]{1,0:T(8,128)S(1)}) custom-call(bf16[160,4096]{1,0:T(8,128)(2,1)} %get-tuple-element.107.refs_10_.refs_0_, bf16[160,4096]{1,0:T(8,128)(2,1)S(1)} %collective-permute-done.16.before_ref.refs_11_.refs_1_, ...), custom_call_target="tpu_custom_call" | custom-call | flops 16106127360 | bytes 65011712 | tf_op jit(solution)/shard_map/pallas_call | solution.py:590
  169.2 2.9 %collective-permute-done.18.refs_13_.refs_0_ = bf16[80,4096]{1,0:T(8,128)(2,1)S(1)} collective-permute-done((bf16[80,4096]{1,0:T(8,128)(2,1)S(1)}, bf16[80,4096]{1,0:T(8,128)(2,1)S(1)}, u32[]{:S(2)}, u32[]{:S(2)}) %collective-permute-start.18) | collective-permute-done | bytes 655392 | tf_op jit(solution)/shard_map/ppermute | solution.py:39
  172.2 4.1 %shard_map.154 = (f32[16,640]{1,0:T(8,128)S(1)}, f32[32,256]{1,0:T(8,128)S(1)}, f32[32,256]{1,0:T(8,128)S(1)}) custom-call(bf16[80,4096]{1,0:T(8,128)(2,1)S(1)} %collective-permute-done.18.refs_13_.refs_0_, bf16[80,4096]{1,0:T(8,128)(2,1)S(1)} %collective-permute-done.19.refs_14_.refs_1_, bf16[256,7168]{1,0:T(8,128)(2,1)S(1)} %bitcast.28, ...), custom_call_target="tpu_custom_call" | custom-call | flops 5368709120 | bytes 44040192 | tf_op jit(solution)/shard_map/pallas_call | solution.py:590
  176.3 0.1 collective-permute-start.23
  176.4 2.7 %collective-permute-start.24 = (f32[16,640]{1,0:T(8,128)S(1)}, f32[16,640]{1,0:T(8,128)S(1)}, u32[]{:S(2)}, u32[]{:S(2)}) collective-permute-start(f32[16,640]{1,0:T(8,128)S(1)} %get-tuple-element.133.refs_0_), channel_id=1, source_target_pairs={{0,6},{1,7},{2,0},{3,1},{4,2},{5,3},{6,4},{7,5},{8,14},{9,15},{10,... | collective-permute-start | bytes 122888 | tf_op jit(solution)/shard_map/ppermute | solution.py:39
  179.1 0.7 collective-permute-start.25
  179.7 2.4 %shard_map.152 = (bf16[640,1792]{1,0:T(8,128)(2,1)S(1)}, bf16[640,1792]{1,0:T(8,128)(2,1)S(1)}) custom-call(s32[1]{0:T(128)} %bitcast.me_ref, bf16[160,4096]{1,0:T(8,128)(2,1)} %shard_map.142.refs_0_, bf16[160,4096]{1,0:T(8,128)(2,1)} %copy-done, bf16[160,4096]{1,0:T(8,128)(2,1)} %copy-done.1, bf16[80,4096]{1,0:T(8,128)(2,1)} %collective-permute-done.10.refs_3_, ...), custom_call_target="tpu_custom_call" | custom-call | bytes 73400320 | tf_op jit(solution)/shard_map/pallas_call | solution.py:616
  182.2 1.2 collective-permute-done.25.refs_3_
  183.4 1.2 shard_map.155
  184.6 7.0 %collective-permute-start.26 = (f32[2,16,896]{2,1,0:T(8,128)S(1)}, f32[2,16,896]{2,1,0:T(8,128)S(1)}, u32[]{:S(2)}, u32[]{:S(2)}) collective-permute-start(f32[2,16,896]{2,1,0:T(8,128)S(1)} %get-tuple-element.139), channel_id=1, source_target_pairs={{0,1},{1,0},{2,3},{3,2},{4,5},{5,4},{6,7},{7,6},{8,9},{9,8},{10,11... | collective-permute-start | bytes 344072 | tf_op jit(solution)/shard_map/ppermute | solution.py:44
  191.6 0.1 collective-permute-start.27
  191.7 1.1 collective-permute-done.27.more_ref
  192.8 0.7 shard_map.156
  (87 shorter events, 0.2 us)
Async XLA Ops:
  0.6 8.3 %copy-start.21 = (bf16[128,7168]{1,0:T(8,128)(2,1)S(1)}, bf16[128,7168]{1,0:T(8,128)(2,1)}, u32[]{:S(2)}) copy-start(bf16[128,7168]{1,0:T(8,128)(2,1)} %refs_0_.3) | copy-start | bytes 5505028
  0.6 0.8 copy-start.24
  2.1 6.8 %copy-start.19 = (s32[1,128]{1,0:T(1,128)S(1)}, s32[1,128]{1,0:T(1,128)}, u32[]{:S(2)}) copy-start(s32[1,128]{1,0:T(1,128)} %copy-done.18) | copy-start | bytes 1540
  5.3 21.7 %collective-permute-start = (bf16[128,3200]{1,0:T(8,128)(2,1)}, bf16[128,3200]{1,0:T(8,128)(2,1)S(1)}, u32[]{:S(2)}, u32[]{:S(2)}) collective-permute-start(bf16[128,3200]{1,0:T(8,128)(2,1)} %get-tuple-element.73.refs_0_.refs_5_), channel_id=1, source_target_pairs={{0,2},{1,3},{2,4},{3,5},{4,6},{5,7},{6,0},{7,1},{8,10},{9,11},{10,... | collective-permute-start | bytes 2457608 | tf_op jit(solution)/shard_map/ppermute | solution.py:39
  7.5 19.6 %collective-permute-start.1 = (bf16[128,3200]{1,0:T(8,128)(2,1)}, bf16[128,3200]{1,0:T(8,128)(2,1)S(1)}, u32[]{:S(2)}, u32[]{:S(2)}) collective-permute-start(bf16[128,3200]{1,0:T(8,128)(2,1)} %get-tuple-element.73.refs_0_.refs_5_), channel_id=1, source_target_pairs={{0,6},{1,7},{2,0},{3,1},{4,2},{5,3},{6,4},{7,5},{8,14},{9,15},{10,... | collective-permute-start | bytes 2457608 | tf_op jit(solution)/shard_map/ppermute | solution.py:39
  11.0 25.7 %all-to-all-start = ((bf16[16,40,1024]{2,1,0:T(8,128)(2,1)}), bf16[16,40,1024]{2,1,0:T(8,128)(2,1)}, u32[]{:S(2)}, u32[]{:S(2)}) async-start(bf16[16,40,1024]{2,1,0:T(8,128)(2,1)} %bitcast.2), calls=%async_computation | async-start | bytes 2621440 | tf_op jit(solution)/shard_map/all_to_all | solution.py:461
  18.6 64.6 %collective-permute-start.8 = (bf16[256,7168]{1,0:T(8,128)(2,1)}, bf16[256,7168]{1,0:T(8,128)(2,1)}, u32[]{:S(2)}, u32[]{:S(2)}) collective-permute-start(bf16[256,7168]{1,0:T(8,128)(2,1)} %bitcast.25), channel_id=1, source_target_pairs={{0,1},{1,0},{2,3},{3,2},{4,5},{5,4},{6,7},{7,6},{8,9},{9,8},{10,11... | collective-permute-start | bytes 11010056 | tf_op jit(solution)/shard_map/ppermute | solution.py:44
  20.1 63.1 %collective-permute-start.6 = (bf16[7168,256]{1,0:T(8,128)(2,1)}, bf16[7168,256]{1,0:T(8,128)(2,1)}, u32[]{:S(2)}, u32[]{:S(2)}) collective-permute-start(bf16[7168,256]{1,0:T(8,128)(2,1)} %bitcast.35), channel_id=1, source_target_pairs={{0,1},{1,0},{2,3},{3,2},{4,5},{5,4},{6,7},{7,6},{8,9},{9,8},{10,11... | collective-permute-start | bytes 11010056 | tf_op jit(solution)/shard_map/ppermute | solution.py:44
  20.2 63.0 %collective-permute-start.7 = (bf16[7168,256]{1,0:T(8,128)(2,1)}, bf16[7168,256]{1,0:T(8,128)(2,1)}, u32[]{:S(2)}, u32[]{:S(2)}) collective-permute-start(bf16[7168,256]{1,0:T(8,128)(2,1)} %bitcast.38), channel_id=1, source_target_pairs={{0,1},{1,0},{2,3},{3,2},{4,5},{5,4},{6,7},{7,6},{8,9},{9,8},{10,11... | collective-permute-start | bytes 11010056 | tf_op jit(solution)/shard_map/ppermute | solution.py:44
  27.0 6.5 %copy-start.7 = (bf16[128,3200]{1,0:T(8,128)(2,1)}, bf16[128,3200]{1,0:T(8,128)(2,1)S(1)}, u32[]{:S(2)}) copy-start(bf16[128,3200]{1,0:T(8,128)(2,1)S(1)} %collective-permute-done.before_ref.refs_1_.refs_6_) | copy-start | bytes 2457604
  27.0 6.5 %copy-start.8 = (bf16[128,3200]{1,0:T(8,128)(2,1)}, bf16[128,3200]{1,0:T(8,128)(2,1)S(1)}, u32[]{:S(2)}) copy-start(bf16[128,3200]{1,0:T(8,128)(2,1)S(1)} %collective-permute-done.1.after_ref.refs_2_.refs_7_) | copy-start | bytes 2457604
  28.1 12.2 %collective-permute-start.2 = (bf16[64,3200]{1,0:T(8,128)(2,1)}, bf16[64,3200]{1,0:T(8,128)(2,1)}, u32[]{:S(2)}, u32[]{:S(2)}) collective-permute-start(bf16[64,3200]{1,0:T(8,128)(2,1)} %get-tuple-element.81), channel_id=1, source_target_pairs={{0,2},{1,3},{2,4},{3,5},{4,6},{5,7},{6,0},{7,1},{8,10},{9,11},{10,... | collective-permute-start | bytes 1228808 | tf_op jit(solution)/shard_map/ppermute | solution.py:39
  28.9 11.4 %collective-permute-start.3 = (bf16[64,3200]{1,0:T(8,128)(2,1)}, bf16[64,3200]{1,0:T(8,128)(2,1)}, u32[]{:S(2)}, u32[]{:S(2)}) collective-permute-start(bf16[64,3200]{1,0:T(8,128)(2,1)} %get-tuple-element.82), channel_id=1, source_target_pairs={{0,6},{1,7},{2,0},{3,1},{4,2},{5,3},{6,4},{7,5},{8,14},{9,15},{10,... | collective-permute-start | bytes 1228808 | tf_op jit(solution)/shard_map/ppermute | solution.py:39
  30.8 1.2 copy-start.22
  33.6 1.4 copy-start.6
  40.3 28.1 %collective-permute-start.4 = (bf16[160,4096]{1,0:T(8,128)(2,1)}, bf16[160,4096]{1,0:T(8,128)(2,1)S(1)}, u32[]{:S(2)}, u32[]{:S(2)}) collective-permute-start(bf16[160,4096]{1,0:T(8,128)(2,1)} %shard_map.142.refs_0_), channel_id=1, source_target_pairs={{0,2},{1,3},{2,4},{3,5},{4,6},{5,7},{6,0},{7,1},{8,10},{9,11},{10,... | collective-permute-start | bytes 3932168 | tf_op jit(solution)/shard_map/ppermute | solution.py:39
  40.3 32.6 %collective-permute-start.5 = (bf16[160,4096]{1,0:T(8,128)(2,1)}, bf16[160,4096]{1,0:T(8,128)(2,1)S(1)}, u32[]{:S(2)}, u32[]{:S(2)}) collective-permute-start(bf16[160,4096]{1,0:T(8,128)(2,1)} %shard_map.142.refs_0_), channel_id=1, source_target_pairs={{0,6},{1,7},{2,0},{3,1},{4,2},{5,3},{6,4},{7,5},{8,14},{9,15},{10,... | collective-permute-start | bytes 3932168 | tf_op jit(solution)/shard_map/ppermute | solution.py:39
  43.0 6.5 %copy-start.12 = (bf16[1,16,256]{2,1,0:T(8,128)(2,1)S(1)}, bf16[1,16,256]{2,1,0:T(8,128)(2,1)}, u32[]{:S(2)}) copy-start(bf16[1,16,256]{2,1,0:T(8,128)(2,1)} %param.19) | copy-start | bytes 24580
  43.0 6.6 %copy-start.14 = (bf16[1,16,256]{2,1,0:T(8,128)(2,1)S(1)}, bf16[1,16,256]{2,1,0:T(8,128)(2,1)}, u32[]{:S(2)}) copy-start(bf16[1,16,256]{2,1,0:T(8,128)(2,1)} %param.20) | copy-start | bytes 24580
  43.0 40.2 %all-to-all-start.1 = ((bf16[16,40,1792]{2,1,0:T(8,128)(2,1)}), bf16[16,40,1792]{2,1,0:T(8,128)(2,1)}, u32[]{:S(2)}, u32[]{:S(2)}) async-start(bf16[16,40,1792]{2,1,0:T(8,128)(2,1)} %bitcast.16), calls=%async_computation.1 | async-start | bytes 4587520 | tf_op jit(solution)/shard_map/all_to_all | solution.py:461
  68.4 14.8 %copy-start = (bf16[160,4096]{1,0:T(8,128)(2,1)}, bf16[160,4096]{1,0:T(8,128)(2,1)S(1)}, u32[]{:S(2)}) copy-start(bf16[160,4096]{1,0:T(8,128)(2,1)S(1)} %collective-permute-done.4.before_ref.refs_1_) | copy-start | bytes 3932164
  68.4 5.6 %collective-permute-start.9 = (bf16[32,256]{1,0:T(8,128)(2,1)S(1)}, bf16[32,256]{1,0:T(8,128)(2,1)S(1)}, u32[]{:S(2)}, u32[]{:S(2)}) collective-permute-start(bf16[32,256]{1,0:T(8,128)(2,1)S(1)} %pad_maximum_fusion), channel_id=1, source_target_pairs={{0,1},{1,0},{2,3},{3,2},{4,5},{5,4},{6,7},{7,6},{8,9},{9,8},{10,11... | collective-permute-start | bytes 49160 | tf_op jit(solution)/shard_map/ppermute | solution.py:44
  72.9 10.2 %copy-start.1 = (bf16[160,4096]{1,0:T(8,128)(2,1)}, bf16[160,4096]{1,0:T(8,128)(2,1)S(1)}, u32[]{:S(2)}) copy-start(bf16[160,4096]{1,0:T(8,128)(2,1)S(1)} %collective-permute-done.5.after_ref.refs_2_) | copy-start | bytes 3932164
  74.0 17.8 %collective-permute-start.10 = (bf16[80,4096]{1,0:T(8,128)(2,1)}, bf16[80,4096]{1,0:T(8,128)(2,1)}, u32[]{:S(2)}, u32[]{:S(2)}) collective-permute-start(bf16[80,4096]{1,0:T(8,128)(2,1)} %get-tuple-element.90), channel_id=1, source_target_pairs={{0,2},{1,3},{2,4},{3,5},{4,6},{5,7},{6,0},{7,1},{8,10},{9,11},{10,... | collective-permute-start | bytes 1966088 | tf_op jit(solution)/shard_map/ppermute | solution.py:39
  74.0 17.8 %collective-permute-start.11 = (bf16[80,4096]{1,0:T(8,128)(2,1)S(1)}, bf16[80,4096]{1,0:T(8,128)(2,1)}, u32[]{:S(2)}, u32[]{:S(2)}) collective-permute-start(bf16[80,4096]{1,0:T(8,128)(2,1)S(1)} %get-tuple-element.91), channel_id=1, source_target_pairs={{0,6},{1,7},{2,0},{3,1},{4,2},{5,3},{6,4},{7,5},{8,14},{9,15},{10,... | collective-permute-start | bytes 1966088 | tf_op jit(solution)/shard_map/ppermute | solution.py:39
  91.8 24.0 %collective-permute-start.12 = (bf16[160,3072]{1,0:T(8,128)(2,1)}, bf16[160,3072]{1,0:T(8,128)(2,1)S(1)}, u32[]{:S(2)}, u32[]{:S(2)}) collective-permute-start(bf16[160,3072]{1,0:T(8,128)(2,1)} %get-tuple-element.94.refs_0_.refs_5_), channel_id=1, source_target_pairs={{0,2},{1,3},{2,4},{3,5},{4,6},{5,7},{6,0},{7,1},{8,10},{9,11},{10,... | collective-permute-start | bytes 2949128 | tf_op jit(solution)/shard_map/ppermute | solution.py:39
  91.8 24.0 %collective-permute-start.13 = (bf16[160,3072]{1,0:T(8,128)(2,1)}, bf16[160,3072]{1,0:T(8,128)(2,1)S(1)}, u32[]{:S(2)}, u32[]{:S(2)}) collective-permute-start(bf16[160,3072]{1,0:T(8,128)(2,1)} %get-tuple-element.94.refs_0_.refs_5_), channel_id=1, source_target_pairs={{0,6},{1,7},{2,0},{3,1},{4,2},{5,3},{6,4},{7,5},{8,14},{9,15},{10,... | collective-permute-start | bytes 2949128 | tf_op jit(solution)/shard_map/ppermute | solution.py:39
  94.5 55.4 %all-to-all-start.2 = ((bf16[16,40,3072]{2,1,0:T(8,128)(2,1)}), bf16[16,40,3072]{2,1,0:T(8,128)(2,1)}, u32[]{:S(2)}, u32[]{:S(2)}) async-start(bf16[16,40,3072]{2,1,0:T(8,128)(2,1)} %bitcast.33), calls=%async_computation.2 | async-start | bytes 7864320 | tf_op jit(solution)/shard_map/all_to_all | solution.py:461
  115.8 3.4 %copy-start.4 = (bf16[160,3072]{1,0:T(8,128)(2,1)}, bf16[160,3072]{1,0:T(8,128)(2,1)S(1)}, u32[]{:S(2)}) copy-start(bf16[160,3072]{1,0:T(8,128)(2,1)S(1)} %collective-permute-done.12.before_ref.refs_1_.refs_6_) | copy-start | bytes 2949124
  115.8 2.8 %copy-start.5 = (bf16[160,3072]{1,0:T(8,128)(2,1)}, bf16[160,3072]{1,0:T(8,128)(2,1)S(1)}, u32[]{:S(2)}) copy-start(bf16[160,3072]{1,0:T(8,128)(2,1)S(1)} %collective-permute-done.13.after_ref.refs_2_.refs_7_) | copy-start | bytes 2949124
  115.8 12.5 %collective-permute-start.14 = (bf16[80,3072]{1,0:T(8,128)(2,1)S(1)}, bf16[80,3072]{1,0:T(8,128)(2,1)S(1)}, u32[]{:S(2)}, u32[]{:S(2)}) collective-permute-start(bf16[80,3072]{1,0:T(8,128)(2,1)S(1)} %get-tuple-element.105), channel_id=1, source_target_pairs={{0,2},{1,3},{2,4},{3,5},{4,6},{5,7},{6,0},{7,1},{8,10},{9,11},{10,... | collective-permute-start | bytes 1474568 | tf_op jit(solution)/shard_map/ppermute | solution.py:39
  115.9 12.4 %collective-permute-start.15 = (bf16[80,3072]{1,0:T(8,128)(2,1)S(1)}, bf16[80,3072]{1,0:T(8,128)(2,1)S(1)}, u32[]{:S(2)}, u32[]{:S(2)}) collective-permute-start(bf16[80,3072]{1,0:T(8,128)(2,1)S(1)} %get-tuple-element.106), channel_id=1, source_target_pairs={{0,6},{1,7},{2,0},{3,1},{4,2},{5,3},{6,4},{7,5},{8,14},{9,15},{10,... | collective-permute-start | bytes 1474568 | tf_op jit(solution)/shard_map/ppermute | solution.py:39
  119.2 39.6 %collective-permute-start.16 = (bf16[160,4096]{1,0:T(8,128)(2,1)}, bf16[160,4096]{1,0:T(8,128)(2,1)S(1)}, u32[]{:S(2)}, u32[]{:S(2)}) collective-permute-start(bf16[160,4096]{1,0:T(8,128)(2,1)} %get-tuple-element.107.refs_10_.refs_0_), channel_id=1, source_target_pairs={{0,2},{1,3},{2,4},{3,5},{4,6},{5,7},{6,0},{7,1},{8,10},{9,11},{10,... | collective-permute-start | bytes 3932168 | tf_op jit(solution)/shard_map/ppermute | solution.py:39
  119.2 39.7 %collective-permute-start.17 = (bf16[160,4096]{1,0:T(8,128)(2,1)}, bf16[160,4096]{1,0:T(8,128)(2,1)S(1)}, u32[]{:S(2)}, u32[]{:S(2)}) collective-permute-start(bf16[160,4096]{1,0:T(8,128)(2,1)} %get-tuple-element.107.refs_10_.refs_0_), channel_id=1, source_target_pairs={{0,6},{1,7},{2,0},{3,1},{4,2},{5,3},{6,4},{7,5},{8,14},{9,15},{10,... | collective-permute-start | bytes 3932168 | tf_op jit(solution)/shard_map/ppermute | solution.py:39
  128.3 0.8 copy-start.32
  128.3 1.0 copy-start.33
  141.1 28.0 %collective-permute-start.20 = (f32[16,640]{1,0:T(8,128)}, f32[16,640]{1,0:T(8,128)S(1)}, u32[]{:S(2)}, u32[]{:S(2)}) collective-permute-start(f32[16,640]{1,0:T(8,128)} %get-tuple-element.134.refs_4_), channel_id=1, source_target_pairs={{0,2},{1,3},{2,4},{3,5},{4,6},{5,7},{6,0},{7,1},{8,10},{9,11},{10,... | collective-permute-start | bytes 122888 | tf_op jit(solution)/shard_map/ppermute | solution.py:39
  141.3 27.9 %collective-permute-start.21 = (f32[16,640]{1,0:T(8,128)}, f32[16,640]{1,0:T(8,128)S(1)}, u32[]{:S(2)}, u32[]{:S(2)}) collective-permute-start(f32[16,640]{1,0:T(8,128)} %get-tuple-element.134.refs_4_), channel_id=1, source_target_pairs={{0,6},{1,7},{2,0},{3,1},{4,2},{5,3},{6,4},{7,5},{8,14},{9,15},{10,... | collective-permute-start | bytes 122888 | tf_op jit(solution)/shard_map/ppermute | solution.py:39
  143.9 25.3 %collective-permute-start.22 = (f32[16,640]{1,0:T(8,128)}, f32[16,640]{1,0:T(8,128)S(1)}, u32[]{:S(2)}, u32[]{:S(2)}) collective-permute-start(f32[16,640]{1,0:T(8,128)} %get-tuple-element.134.refs_4_), channel_id=1, source_target_pairs={{0,4},{1,5},{2,6},{3,7},{4,0},{5,1},{6,2},{7,3},{8,12},{9,13},{10,... | collective-permute-start | bytes 122888 | tf_op jit(solution)/shard_map/ppermute | solution.py:39
  149.9 11.8 %copy-start.31 = (bf16[640,16]{1,0:T(8,128)(2,1)S(1)}, bf16[640,16]{1,0:T(8,128)(2,1)}, u32[]{:S(2)}) copy-start(bf16[640,16]{1,0:T(8,128)(2,1)} %get-tuple-element.129.refs_10_.refs_9_) | copy-start | bytes 61444
  158.8 3.0 %copy-start.13 = (bf16[1,16,256]{2,1,0:T(8,128)(2,1)S(1)}, bf16[1,16,256]{2,1,0:T(8,128)(2,1)}, u32[]{:S(2)}) copy-start(bf16[1,16,256]{2,1,0:T(8,128)(2,1)} %param.19) | copy-start | bytes 24580
  158.8 3.0 %copy-start.15 = (bf16[1,16,256]{2,1,0:T(8,128)(2,1)S(1)}, bf16[1,16,256]{2,1,0:T(8,128)(2,1)}, u32[]{:S(2)}) copy-start(bf16[1,16,256]{2,1,0:T(8,128)(2,1)} %param.20) | copy-start | bytes 24580
  158.8 3.0 %copy-start.16 = (bf16[16,256]{1,0:T(8,128)(2,1)S(1)}, bf16[16,256]{1,0:T(8,128)(2,1)}, u32[]{:S(2)}) copy-start(bf16[16,256]{1,0:T(8,128)(2,1)} %get-tuple-element.142.refs_16_.refs_14_.refs_13_) | copy-start | bytes 24580
  158.8 3.0 %copy-start.17 = (bf16[16,256]{1,0:T(8,128)(2,1)S(1)}, bf16[16,256]{1,0:T(8,128)(2,1)}, u32[]{:S(2)}) copy-start(bf16[16,256]{1,0:T(8,128)(2,1)} %get-tuple-element.143.refs_14_.refs_12_.refs_11_) | copy-start | bytes 24580
  158.8 3.0 %copy-start.23 = (bf16[1,16,7168]{2,1,0:T(8,128)(2,1)S(1)}, bf16[1,16,7168]{2,1,0:T(8,128)(2,1)}, u32[]{:S(2)}) copy-start(bf16[1,16,7168]{2,1,0:T(8,128)(2,1)} %param.21) | copy-start | bytes 688132
  158.8 2.9 %copy-start.25 = (f32[640,512]{1,0:T(8,128)S(1)}, f32[640,512]{1,0:T(8,128)}, u32[]{:S(2)}) copy-start(f32[640,512]{1,0:T(8,128)} %get-tuple-element.127.refs_8_.refs_7_) | copy-start | bytes 3932164
  158.8 2.9 %copy-start.29 = (bf16[640,512]{1,0:T(8,128)(2,1)S(1)}, bf16[640,512]{1,0:T(8,128)(2,1)}, u32[]{:S(2)}) copy-start(bf16[640,512]{1,0:T(8,128)(2,1)} %get-tuple-element.128.refs_9_.refs_8_) | copy-start | bytes 1966084
  158.8 2.9 %copy-start.30 = (f32[640,16]{1,0:T(8,128)S(1)}, f32[640,16]{1,0:T(8,128)}, u32[]{:S(2)}) copy-start(f32[640,16]{1,0:T(8,128)} %get-tuple-element.126.refs_7_.refs_6_) | copy-start | bytes 122884
  158.8 10.3 %copy-start.2 = (bf16[160,4096]{1,0:T(8,128)(2,1)}, bf16[160,4096]{1,0:T(8,128)(2,1)S(1)}, u32[]{:S(2)}) copy-start(bf16[160,4096]{1,0:T(8,128)(2,1)S(1)} %collective-permute-done.16.before_ref.refs_11_.refs_1_) | copy-start | bytes 3932164
  158.9 10.3 %copy-start.3 = (bf16[160,4096]{1,0:T(8,128)(2,1)}, bf16[160,4096]{1,0:T(8,128)(2,1)S(1)}, u32[]{:S(2)}) copy-start(bf16[160,4096]{1,0:T(8,128)(2,1)S(1)} %collective-permute-done.17.after_ref.refs_12_.refs_2_) | copy-start | bytes 3932164
  159.0 13.2 %collective-permute-start.18 = (bf16[80,4096]{1,0:T(8,128)(2,1)S(1)}, bf16[80,4096]{1,0:T(8,128)(2,1)S(1)}, u32[]{:S(2)}, u32[]{:S(2)}) collective-permute-start(bf16[80,4096]{1,0:T(8,128)(2,1)S(1)} %get-tuple-element.118), channel_id=1, source_target_pairs={{0,2},{1,3},{2,4},{3,5},{4,6},{5,7},{6,0},{7,1},{8,10},{9,11},{10,... | collective-permute-start | bytes 1966088 | tf_op jit(solution)/shard_map/ppermute | solution.py:39
  159.1 13.1 %collective-permute-start.19 = (bf16[80,4096]{1,0:T(8,128)(2,1)S(1)}, bf16[80,4096]{1,0:T(8,128)(2,1)S(1)}, u32[]{:S(2)}, u32[]{:S(2)}) collective-permute-start(bf16[80,4096]{1,0:T(8,128)(2,1)S(1)} %get-tuple-element.119), channel_id=1, source_target_pairs={{0,6},{1,7},{2,0},{3,1},{4,2},{5,3},{6,4},{7,5},{8,14},{9,15},{10,... | collective-permute-start | bytes 1966088 | tf_op jit(solution)/shard_map/ppermute | solution.py:39
  161.8 1.3 copy-start.27
  163.1 9.0 %copy-start.20 = (bf16[1,256,7168]{2,1,0:T(8,128)(2,1)S(1)}, bf16[1,256,7168]{2,1,0:T(8,128)(2,1)}, u32[]{:S(2)}) copy-start(bf16[1,256,7168]{2,1,0:T(8,128)(2,1)} %param.17) | copy-start | bytes 11010052
  163.1 9.0 %copy-start.26 = (f32[640,512]{1,0:T(8,128)S(1)}, f32[640,512]{1,0:T(8,128)}, u32[]{:S(2)}) copy-start(f32[640,512]{1,0:T(8,128)} %get-tuple-element.127.refs_8_.refs_7_) | copy-start | bytes 3932164
  163.1 9.0 %copy-start.28 = (f32[640,512]{1,0:T(8,128)S(1)}, f32[640,512]{1,0:T(8,128)}, u32[]{:S(2)}) copy-start(f32[640,512]{1,0:T(8,128)} %get-tuple-element.125.refs_6_.refs_5_) | copy-start | bytes 3932164
  172.1 4.2 %copy-start.9 = (bf16[80,4096]{1,0:T(8,128)(2,1)}, bf16[80,4096]{1,0:T(8,128)(2,1)S(1)}, u32[]{:S(2)}) copy-start(bf16[80,4096]{1,0:T(8,128)(2,1)S(1)} %collective-permute-done.18.refs_13_.refs_0_) | copy-start | bytes 1966084
  172.1 4.2 %copy-start.10 = (bf16[80,4096]{1,0:T(8,128)(2,1)}, bf16[80,4096]{1,0:T(8,128)(2,1)S(1)}, u32[]{:S(2)}) copy-start(bf16[80,4096]{1,0:T(8,128)(2,1)S(1)} %collective-permute-done.19.refs_14_.refs_1_) | copy-start | bytes 1966084
  176.3 5.8 %collective-permute-start.23 = (f32[16,640]{1,0:T(8,128)S(1)}, f32[16,640]{1,0:T(8,128)S(1)}, u32[]{:S(2)}, u32[]{:S(2)}) collective-permute-start(f32[16,640]{1,0:T(8,128)S(1)} %get-tuple-element.133.refs_0_), channel_id=1, source_target_pairs={{0,2},{1,3},{2,4},{3,5},{4,6},{5,7},{6,0},{7,1},{8,10},{9,11},{10,... | collective-permute-start | bytes 122888 | tf_op jit(solution)/shard_map/ppermute | solution.py:39
  176.4 5.8 %collective-permute-start.24 = (f32[16,640]{1,0:T(8,128)S(1)}, f32[16,640]{1,0:T(8,128)S(1)}, u32[]{:S(2)}, u32[]{:S(2)}) collective-permute-start(f32[16,640]{1,0:T(8,128)S(1)} %get-tuple-element.133.refs_0_), channel_id=1, source_target_pairs={{0,6},{1,7},{2,0},{3,1},{4,2},{5,3},{6,4},{7,5},{8,14},{9,15},{10,... | collective-permute-start | bytes 122888 | tf_op jit(solution)/shard_map/ppermute | solution.py:39
  179.1 4.4 %collective-permute-start.25 = (f32[16,640]{1,0:T(8,128)S(1)}, f32[16,640]{1,0:T(8,128)S(1)}, u32[]{:S(2)}, u32[]{:S(2)}) collective-permute-start(f32[16,640]{1,0:T(8,128)S(1)} %get-tuple-element.133.refs_0_), channel_id=1, source_target_pairs={{0,4},{1,5},{2,6},{3,7},{4,0},{5,1},{6,2},{7,3},{8,12},{9,13},{10,... | collective-permute-start | bytes 122888 | tf_op jit(solution)/shard_map/ppermute | solution.py:39
  179.7 3.7 %copy-start.11 = (f32[16,640]{1,0:T(8,128)S(1)}, f32[16,640]{1,0:T(8,128)}, u32[]{:S(2)}) copy-start(f32[16,640]{1,0:T(8,128)} %get-tuple-element.134.refs_4_) | copy-start | bytes 122884
  184.6 8.2 %collective-permute-start.26 = (f32[2,16,896]{2,1,0:T(8,128)S(1)}, f32[2,16,896]{2,1,0:T(8,128)S(1)}, u32[]{:S(2)}, u32[]{:S(2)}) collective-permute-start(f32[2,16,896]{2,1,0:T(8,128)S(1)} %get-tuple-element.139), channel_id=1, source_target_pairs={{0,1},{1,0},{2,3},{3,2},{4,5},{5,4},{6,7},{7,6},{8,9},{9,8},{10,11... | collective-permute-start | bytes 344072 | tf_op jit(solution)/shard_map/ppermute | solution.py:44
  191.6 1.2 collective-permute-start.27
  (1 other events, 0.5 us)

commit v6 on v5

--- a/solution.py
+++ b/solution.py
@@ -98,15 +98,24 @@
     return pl.BlockSpec(dims, lambda *_: (0,) * len(dims))
 
 
-def scale_kernel(cot_ref, weight_ref, code_ref, rest_ref, raw_ref):
+def scale(weight_ref, cot_ref, out, size):
     count = weight_ref.shape[1]
     column = jnp.broadcast_to(weight_ref[...], (count, count)).T[:, :1]
-    rest = rest_ref.shape[1]
-    late = cot_ref.shape[1] - rest
-    for base, size, out in ((rest, late, raw_ref), (0, rest, rest_ref)):
-        for at in range(0, size, 512):
-            block = cot_ref[:, base + at : base + at + 512].astype(F32)
-            out[:, at : at + 512] = (block * column).astype(BF16)
+    for at in range(0, size, 512):
+        out[:, at : at + 512] = (cot_ref[:, at : at + 512].astype(F32) * column).astype(BF16)
+
+
+def scale_kernel(cot_ref, weight_ref, out_ref):
+    scale(weight_ref, cot_ref, out_ref, out_ref.shape[1])
+
+
+def scale_raw_kernel(cot_ref, weight_ref, code_ref, raw_ref, buffer, sem):
+    late = buffer.shape[1]
+    copy = pltpu.make_async_copy(cot_ref.at[:, pl.ds(cot_ref.shape[1] - late, late)], buffer, sem)
+    copy.start()
+    copy.wait()
+    scale(weight_ref, buffer, raw_ref, late)
+    count = code_ref.shape[1]
     codes = jnp.broadcast_to(code_ref[...], (count, count)).astype(F32).T
     raw_ref[:, late:] = codes[:, : raw_ref.shape[1] - late].astype(BF16)
 
@@ -433,12 +442,24 @@
     code = call(
         functools.partial(code_kernel, experts, capacity), shape((1, count), jnp.int32), 16, moved=1024
     )(chosen_expert_index.reshape(1, count))
-    scaled, raw = call(
+    weight = router_weight.reshape(1, count)
+    raw = call(
+        scale_raw_kernel,
+        shape((count, late + LANES), BF16),
+        VMEM_MIB,
+        moved=4 * count * late,
+        in_specs=[pl.BlockSpec(memory_space=pl.ANY), whole(1, count), whole(1, count)],
+        scratch_shapes=[pltpu.VMEM((count, late), BF16), pltpu.SemaphoreType.DMA],
+    )(cotangent, weight, code)
+    scaled = call(
         scale_kernel,
-        (shape((count, rest), BF16), shape((count, late + LANES), BF16)),
+        shape((count, rest), BF16),
         VMEM_MIB,
-        moved=4 * count * width,
-    )(cotangent, router_weight.reshape(1, count), code)
+        moved=4 * count * rest,
+        grid=(1,),
+        in_specs=[pl.BlockSpec((count, rest), lambda i: (0, 0)), whole(1, count)],
+        out_specs=whole(count, rest),
+    )(cotangent, weight)
     raw_steps = first_step(raw)
 
     def pack(code, *sources):
@@ -464,7 +485,7 @@
         return call(
             functools.partial(unpack_kernel, capacity),
             tuple(shape((slots, size), BF16) for size in sizes),
-            VMEM_MIB,
+            24 if len(sizes) == 1 else VMEM_MIB,
             flops=2 * every * every * got.shape[1] // COVER,
             moved=4 * every * got.shape[1] // COVER,
         )(got)

time: 194 us -> 194 us (level)
  waiting for transfers between devices: 51.6 us -> 48 us
  starting transfers between devices: 63.6 us -> 65.7 us
    ppermute x22, waiting for transfers between devices: 43.4 us -> 38.6 us  [shift_y(): return lax.ppermute(value, 'seq', pairs)]
    pallas_call x1 -> x2, Pallas kernels: 3.24 us -> 5.69 us  [the longest x1 3.02 us: body(): call(scale_raw_kernel, shape((count, late + LANES), BF16), VMEM_MIB, move...]
    all_to_all x3, starting transfers between devices: 20.6 us -> 22.6 us  [across_dp(): lax.all_to_all(sent, 'dp', split_axis=0, concat_axis=0, tiled=True)]
    unnamed x68 -> x70, local copies, waits for them, and re-layouts: 6.25 us -> 6.26 us
where the time goes in v6:
time: 194 us; the launch traced here: 193 us
  Pallas kernels  71.4 us (37%)
  starting transfers between devices  65.7 us (34%)
  waiting for transfers between devices  48 us (25%)
  local copies, waits for them, and re-layouts  6.86 us (4%)
    ppermute x22, waiting for transfers between devices, shift_y(): return lax.ppermute(value, 'seq', pairs)  38.6 us
    ppermute x22, starting transfers between devices, shift_y(): return lax.ppermute(value, 'seq', pairs)  29.5 us
    pallas_call x2, Pallas kernels, gate_up(): call(functools.partial(gate_up_kernel, begins, last), outs, VMEM_MIB, flo...  22.9 us
    all_to_all x3, starting transfers between devices, across_dp(): lax.all_to_all(sent, 'dp', split_axis=0, concat_axis=0, tiled=True)  22.6 us
    ppermute x6, starting transfers between devices, swap_core(): return lax.ppermute(value, 'seq', [(i, i ^ 1) for i in range(size)])  13.6 us
    pallas_call x2, Pallas kernels, back(): call(functools.partial(back_kernel, last, len(pieces)), outs, 24 if last...  10.1 us
    pallas_call x1, Pallas kernels, body(): call(functools.partial(raw_kernel, capacity), (totals[0], totals[2]), VME...  8.87 us
    all_to_all x3, waiting for transfers between devices, across_dp(): lax.all_to_all(sent, 'dp', split_axis=0, concat_axis=0, tiled=True)  8.19 us
  transfers between devices with their start and end apart: 31, of which 10 were waited for; matrix products, arithmetic and copies ran while one was open for 0% of the time, Pallas kernels for 32%

profile of v6, /device:TPU:1, one launch (start us, length us, event | category | flops | bytes accessed | tf_op | source)
XLA Modules:
  0.0 193.0 jit_solution(17321150749378685569)
XLA Ops:
  0.7 0.8 copy-done.25
  1.4 0.1 shard_map.138.code_ref
  1.6 0.5 copy-done.19
  2.1 3.0 %shard_map.140.refs_0_.refs_5_ = bf16[128,3200]{1,0:T(8,128)(2,1)} custom-call(bf16[128,7168]{1,0:T(8,128)(2,1)} %cot_ref.3, f32[1,128]{1,0:T(1,128)} %bitcast.35, s32[1,128]{1,0:T(1,128)} %copy-done.19), custom_call_target="tpu_custom_call" | custom-call | bytes 12582912 | tf_op jit(solution)/shard_map/pallas_call | solution.py:446
  5.1 2.2 %collective-permute-start = (bf16[128,3200]{1,0:T(8,128)(2,1)}, bf16[128,3200]{1,0:T(8,128)(2,1)S(1)}, u32[]{:S(2)}, u32[]{:S(2)}) collective-permute-start(bf16[128,3200]{1,0:T(8,128)(2,1)} %shard_map.140.refs_0_.refs_5_), channel_id=1, source_target_pairs={{0,2},{1,3},{2,4},{3,5},{4,6},{5,7},{6,0},{7,1},{8,10},{9,11},{10,... | collective-permute-start | bytes 2457608 | tf_op jit(solution)/shard_map/ppermute | solution.py:39
  7.3 1.5 collective-permute-start.1
  8.8 2.0 %shard_map.139 = bf16[640,1024]{1,0:T(8,128)(2,1)} custom-call(s32[1,128]{1,0:T(1,128)S(1)} %copy-done.20, bf16[128,7168]{1,0:T(8,128)(2,1)S(1)} %copy-done.22), custom_call_target="tpu_custom_call" | custom-call | flops 5368709120 | bytes 18874368 | tf_op jit(solution)/shard_map/pallas_call | solution.py:468
  10.9 7.6 %all-to-all-start = ((bf16[16,40,1024]{2,1,0:T(8,128)(2,1)}), bf16[16,40,1024]{2,1,0:T(8,128)(2,1)S(1)}, u32[]{:S(2)}, u32[]{:S(2)}) async-start(bf16[16,40,1024]{2,1,0:T(8,128)(2,1)} %bitcast.2), calls=%async_computation | async-start | bytes 2621440 | tf_op jit(solution)/shard_map/all_to_all | solution.py:482
  18.5 1.5 collective-permute-start.8
  20.0 0.1 collective-permute-start.6
  20.1 0.4 collective-permute-start.7
  20.5 2.7 %shard_map.141.refs_1_ = bf16[128,4096]{1,0:T(8,128)(2,1)} custom-call(bf16[128,7168]{1,0:T(8,128)(2,1)} %cot_ref.3, f32[1,128]{1,0:T(1,128)} %bitcast.36), custom_call_target="tpu_custom_call" | custom-call | bytes 16777216 | tf_op jit(solution)/shard_map/pallas_call | solution.py:454
  23.1 3.6 %collective-permute-done.before_ref.refs_1_.refs_6_ = bf16[128,3200]{1,0:T(8,128)(2,1)S(1)} collective-permute-done((bf16[128,3200]{1,0:T(8,128)(2,1)}, bf16[128,3200]{1,0:T(8,128)(2,1)S(1)}, u32[]{:S(2)}, u32[]{:S(2)}) %collective-permute-start) | collective-permute-done | bytes 819232 | tf_op jit(solution)/shard_map/ppermute | solution.py:39
  26.8 0.9 shard_map.144
  27.7 0.8 collective-permute-start.2
  28.5 1.9 collective-permute-start.3
  30.4 1.2 copy-done.7
  31.6 1.6 shard_map.142
  33.2 1.3 copy-done.6
  34.6 1.9 all-to-all-done
  36.4 2.4 %shard_map.143.refs_0_ = bf16[160,4096]{1,0:T(8,128)(2,1)} custom-call(bf16[640,1024]{1,0:T(8,128)(2,1)S(1)} %bitcast.17), custom_call_target="tpu_custom_call" | custom-call | flops 838860800 | bytes 2621440 | tf_op jit(solution)/shard_map/pallas_call | solution.py:485
  38.8 2.7 %collective-permute-start.5 = (bf16[160,4096]{1,0:T(8,128)(2,1)}, bf16[160,4096]{1,0:T(8,128)(2,1)S(1)}, u32[]{:S(2)}, u32[]{:S(2)}) collective-permute-start(bf16[160,4096]{1,0:T(8,128)(2,1)} %shard_map.143.refs_0_), channel_id=1, source_target_pairs={{0,6},{1,7},{2,0},{3,1},{4,2},{5,3},{6,4},{7,5},{8,14},{9,15},{10,... | collective-permute-start | bytes 3932168 | tf_op jit(solution)/shard_map/ppermute | solution.py:39
  41.5 7.6 %all-to-all-start.1 = ((bf16[16,40,1792]{2,1,0:T(8,128)(2,1)}), bf16[16,40,1792]{2,1,0:T(8,128)(2,1)}, u32[]{:S(2)}, u32[]{:S(2)}) async-start(bf16[16,40,1792]{2,1,0:T(8,128)(2,1)} %bitcast.16), calls=%async_computation.1 | async-start | bytes 4587520 | tf_op jit(solution)/shard_map/all_to_all | solution.py:482
  49.1 17.8 %collective-permute-done.4.before_ref.refs_1_ = bf16[160,4096]{1,0:T(8,128)(2,1)S(1)} collective-permute-done((bf16[160,4096]{1,0:T(8,128)(2,1)}, bf16[160,4096]{1,0:T(8,128)(2,1)S(1)}, u32[]{:S(2)}, u32[]{:S(2)}) %collective-permute-start.4) | collective-permute-done | bytes 1310752 | tf_op jit(solution)/shard_map/ppermute | solution.py:39
  66.9 4.6 %collective-permute-start.9 = (bf16[32,256]{1,0:T(8,128)(2,1)S(1)}, bf16[32,256]{1,0:T(8,128)(2,1)S(1)}, u32[]{:S(2)}, u32[]{:S(2)}) collective-permute-start(bf16[32,256]{1,0:T(8,128)(2,1)S(1)} %pad_maximum_fusion), channel_id=1, source_target_pairs={{0,1},{1,0},{2,3},{3,2},{4,5},{5,4},{6,7},{7,6},{8,9},{9,8},{10,11... | collective-permute-start | bytes 49160 | tf_op jit(solution)/shard_map/ppermute | solution.py:44
  71.4 1.0 shard_map.147
  72.5 2.7 %collective-permute-start.11 = (bf16[80,4096]{1,0:T(8,128)(2,1)S(1)}, bf16[80,4096]{1,0:T(8,128)(2,1)}, u32[]{:S(2)}, u32[]{:S(2)}) collective-permute-start(bf16[80,4096]{1,0:T(8,128)(2,1)S(1)} %get-tuple-element.87), channel_id=1, source_target_pairs={{0,6},{1,7},{2,0},{3,1},{4,2},{5,3},{6,4},{7,5},{8,14},{9,15},{10,... | collective-permute-start | bytes 1966088 | tf_op jit(solution)/shard_map/ppermute | solution.py:39
  75.2 6.5 %shard_map.145 = bf16[640,3072]{1,0:T(8,128)(2,1)} custom-call(bf16[128,3200]{1,0:T(8,128)(2,1)} %shard_map.140.refs_0_.refs_5_, bf16[128,3200]{1,0:T(8,128)(2,1)} %copy-done.8, bf16[128,3200]{1,0:T(8,128)(2,1)} %copy-done.9, bf16[64,3200]{1,0:T(8,128)(2,1)} %collective-permute-done.2.refs_3_.refs_8_, ...), custom_call_target="tpu_custom_call" | custom-call | flops 16106127360 | bytes 56623104 | tf_op jit(solution)/shard_map/pallas_call | solution.py:508
  81.7 4.8 %shard_map.146 = (bf16[160,3072]{1,0:T(8,128)(2,1)}, bf16[160,4096]{1,0:T(8,128)(2,1)}) custom-call(bf16[640,1792]{1,0:T(8,128)(2,1)} %bitcast.6.got_ref), custom_call_target="tpu_custom_call" | custom-call | flops 1468006400 | bytes 4587520 | tf_op jit(solution)/shard_map/pallas_call | solution.py:485
  86.6 3.7 %collective-permute-done.10.refs_3_ = bf16[80,4096]{1,0:T(8,128)(2,1)} collective-permute-done((bf16[80,4096]{1,0:T(8,128)(2,1)}, bf16[80,4096]{1,0:T(8,128)(2,1)}, u32[]{:S(2)}, u32[]{:S(2)}) %collective-permute-start.10) | collective-permute-done | bytes 655392 | tf_op jit(solution)/shard_map/ppermute | solution.py:39
  90.3 2.7 %collective-permute-start.13 = (bf16[160,3072]{1,0:T(8,128)(2,1)}, bf16[160,3072]{1,0:T(8,128)(2,1)S(1)}, u32[]{:S(2)}, u32[]{:S(2)}) collective-permute-start(bf16[160,3072]{1,0:T(8,128)(2,1)} %get-tuple-element.90.refs_0_.refs_5_), channel_id=1, source_target_pairs={{0,6},{1,7},{2,0},{3,1},{4,2},{5,3},{6,4},{7,5},{8,14},{9,15},{10,... | collective-permute-start | bytes 2949128 | tf_op jit(solution)/shard_map/ppermute | solution.py:39
  93.0 7.4 %all-to-all-start.2 = ((bf16[16,40,3072]{2,1,0:T(8,128)(2,1)}), bf16[16,40,3072]{2,1,0:T(8,128)(2,1)}, u32[]{:S(2)}, u32[]{:S(2)}) async-start(bf16[16,40,3072]{2,1,0:T(8,128)(2,1)} %bitcast.34), calls=%async_computation.2 | async-start | bytes 7864320 | tf_op jit(solution)/shard_map/all_to_all | solution.py:482
  100.4 11.1 %shard_map.148 = (f32[640,512]{1,0:T(8,128)}, f32[640,512]{1,0:T(8,128)}, f32[640,16]{1,0:T(8,128)}) custom-call(bf16[160,4096]{1,0:T(8,128)(2,1)} %shard_map.143.refs_0_, bf16[160,4096]{1,0:T(8,128)(2,1)} %copy-done, bf16[160,4096]{1,0:T(8,128)(2,1)} %copy-done.1, bf16[80,4096]{1,0:T(8,128)(2,1)} %collective-permute-done.10.refs_3_, ...), custom_call_target="tpu_custom_call" | custom-call | flops 42949672960 | bytes 109051904 | tf_op jit(solution)/shard_map/pallas_call | solution.py:552
  111.5 2.8 %collective-permute-done.12.before_ref.refs_1_.refs_6_ = bf16[160,3072]{1,0:T(8,128)(2,1)S(1)} collective-permute-done((bf16[160,3072]{1,0:T(8,128)(2,1)}, bf16[160,3072]{1,0:T(8,128)(2,1)S(1)}, u32[]{:S(2)}, u32[]{:S(2)}) %collective-permute-start.12) | collective-permute-done | bytes 983072 | tf_op jit(solution)/shard_map/ppermute | solution.py:39
  114.3 0.1 collective-permute-start.14
  114.4 2.7 %collective-permute-start.15 = (bf16[80,3072]{1,0:T(8,128)(2,1)S(1)}, bf16[80,3072]{1,0:T(8,128)(2,1)S(1)}, u32[]{:S(2)}, u32[]{:S(2)}) collective-permute-start(bf16[80,3072]{1,0:T(8,128)(2,1)S(1)} %get-tuple-element.102), channel_id=1, source_target_pairs={{0,6},{1,7},{2,0},{3,1},{4,2},{5,3},{6,4},{7,5},{8,14},{9,15},{10,... | collective-permute-start | bytes 1474568 | tf_op jit(solution)/shard_map/ppermute | solution.py:39
  117.1 0.6 fusion
  117.7 2.7 %collective-permute-start.17 = (bf16[160,4096]{1,0:T(8,128)(2,1)}, bf16[160,4096]{1,0:T(8,128)(2,1)S(1)}, u32[]{:S(2)}, u32[]{:S(2)}) collective-permute-start(bf16[160,4096]{1,0:T(8,128)(2,1)} %get-tuple-element.103.refs_10_.refs_0_), channel_id=1, source_target_pairs={{0,6},{1,7},{2,0},{3,1},{4,2},{5,3},{6,4},{7,5},{8,14},{9,15},{10,... | collective-permute-start | bytes 3932168 | tf_op jit(solution)/shard_map/ppermute | solution.py:39
  120.4 6.4 %collective-permute-done.14.refs_3_.refs_8_ = bf16[80,3072]{1,0:T(8,128)(2,1)S(1)} collective-permute-done((bf16[80,3072]{1,0:T(8,128)(2,1)S(1)}, bf16[80,3072]{1,0:T(8,128)(2,1)S(1)}, u32[]{:S(2)}, u32[]{:S(2)}) %collective-permute-start.14) | collective-permute-done | bytes 491552 | tf_op jit(solution)/shard_map/ppermute | solution.py:39
  126.8 0.8 copy-done.33
  127.6 0.2 copy-done.34
  127.8 11.8 %shard_map.150 = (bf16[640,512]{1,0:T(8,128)(2,1)}, f32[640,512]{1,0:T(8,128)}, bf16[640,16]{1,0:T(8,128)(2,1)}, f32[16,640]{1,0:T(8,128)}) custom-call(bf16[160,3072]{1,0:T(8,128)(2,1)} %get-tuple-element.90.refs_0_.refs_5_, bf16[160,3072]{1,0:T(8,128)(2,1)} %copy-done.4, bf16[160,3072]{1,0:T(8,128)(2,1)} %copy-done.5, bf16[80,3072]{1,0:T(8,128)(2,1)} %copy-done.33, ...), custom_call_target="tpu_custom_call" | custom-call | flops 32212254720 | bytes 81788928 | tf_op jit(solution)/shard_map/pallas_call | solution.py:552
  139.6 0.2 collective-permute-start.20
  139.8 2.6 %collective-permute-start.21 = (f32[16,640]{1,0:T(8,128)}, f32[16,640]{1,0:T(8,128)S(1)}, u32[]{:S(2)}, u32[]{:S(2)}) collective-permute-start(f32[16,640]{1,0:T(8,128)} %get-tuple-element.130.refs_4_), channel_id=1, source_target_pairs={{0,6},{1,7},{2,0},{3,1},{4,2},{5,3},{6,4},{7,5},{8,14},{9,15},{10,... | collective-permute-start | bytes 122888 | tf_op jit(solution)/shard_map/ppermute | solution.py:39
  142.4 0.8 collective-permute-start.22
  143.1 6.3 %all-to-all-done.2 = bf16[16,40,3072]{2,1,0:T(8,128)(2,1)} async-done(((bf16[16,40,3072]{2,1,0:T(8,128)(2,1)}), bf16[16,40,3072]{2,1,0:T(8,128)(2,1)}, u32[]{:S(2)}, u32[]{:S(2)}) %all-to-all-start.2) | async-done | bytes 3932192 | tf_op jit(solution)/shard_map/all_to_all | solution.py:482
  149.4 8.9 %shard_map.151 = (f32[640,512]{1,0:T(8,128)}, f32[640,16]{1,0:T(8,128)}) custom-call(bf16[640,3072]{1,0:T(8,128)(2,1)} %bitcast.14.got_ref.refs_15_, bf16[256,7168]{1,0:T(8,128)(2,1)} %bitcast.27, bf16[256,7168]{1,0:T(8,128)(2,1)} %collective-permute-done.8.down_p.refs_4_.refs_3_, bf16[16,7168]{1,0:T(8,128)(2,1)} %bitcast.30), custom_call_target="tpu_custom_call" | custom-call | flops 16106127360 | bytes 56623104 | tf_op jit(solution)/shard_map/pallas_call | solution.py:580
  158.4 0.1 shard_map.152
  158.5 0.1 collective-permute-start.18
  158.6 2.7 %collective-permute-start.19 = (bf16[80,4096]{1,0:T(8,128)(2,1)S(1)}, bf16[80,4096]{1,0:T(8,128)(2,1)S(1)}, u32[]{:S(2)}, u32[]{:S(2)}) collective-permute-start(bf16[80,4096]{1,0:T(8,128)(2,1)S(1)} %get-tuple-element.115), channel_id=1, source_target_pairs={{0,6},{1,7},{2,0},{3,1},{4,2},{5,3},{6,4},{7,5},{8,14},{9,15},{10,... | collective-permute-start | bytes 1966088 | tf_op jit(solution)/shard_map/ppermute | solution.py:39
  161.3 1.3 copy-done.28
  162.6 6.0 %shard_map.154 = (f32[16,480]{1,0:T(8,128)S(1)}, f32[32,256]{1,0:T(8,128)S(1)}, f32[32,256]{1,0:T(8,128)S(1)}) custom-call(bf16[160,4096]{1,0:T(8,128)(2,1)} %get-tuple-element.103.refs_10_.refs_0_, bf16[160,4096]{1,0:T(8,128)(2,1)S(1)} %collective-permute-done.16.before_ref.refs_11_.refs_1_, ...), custom_call_target="tpu_custom_call" | custom-call | flops 16106127360 | bytes 65011712 | tf_op jit(solution)/shard_map/pallas_call | solution.py:611
  168.7 3.0 %collective-permute-done.18.refs_13_.refs_0_ = bf16[80,4096]{1,0:T(8,128)(2,1)S(1)} collective-permute-done((bf16[80,4096]{1,0:T(8,128)(2,1)S(1)}, bf16[80,4096]{1,0:T(8,128)(2,1)S(1)}, u32[]{:S(2)}, u32[]{:S(2)}) %collective-permute-start.18) | collective-permute-done | bytes 655392 | tf_op jit(solution)/shard_map/ppermute | solution.py:39
  171.7 4.1 %shard_map.155 = (f32[16,640]{1,0:T(8,128)S(1)}, f32[32,256]{1,0:T(8,128)S(1)}, f32[32,256]{1,0:T(8,128)S(1)}) custom-call(bf16[80,4096]{1,0:T(8,128)(2,1)S(1)} %collective-permute-done.18.refs_13_.refs_0_, bf16[80,4096]{1,0:T(8,128)(2,1)S(1)} %collective-permute-done.19.refs_14_.refs_1_, bf16[256,7168]{1,0:T(8,128)(2,1)S(1)} %bitcast.29, ...), custom_call_target="tpu_custom_call" | custom-call | flops 5368709120 | bytes 44040192 | tf_op jit(solution)/shard_map/pallas_call | solution.py:611
  175.8 0.1 collective-permute-start.23
  175.9 2.7 %collective-permute-start.24 = (f32[16,640]{1,0:T(8,128)S(1)}, f32[16,640]{1,0:T(8,128)S(1)}, u32[]{:S(2)}, u32[]{:S(2)}) collective-permute-start(f32[16,640]{1,0:T(8,128)S(1)} %get-tuple-element.129.refs_0_), channel_id=1, source_target_pairs={{0,6},{1,7},{2,0},{3,1},{4,2},{5,3},{6,4},{7,5},{8,14},{9,15},{10,... | collective-permute-start | bytes 122888 | tf_op jit(solution)/shard_map/ppermute | solution.py:39
  178.6 0.7 collective-permute-start.25
  179.3 2.4 %shard_map.153 = (bf16[640,1792]{1,0:T(8,128)(2,1)S(1)}, bf16[640,1792]{1,0:T(8,128)(2,1)S(1)}) custom-call(s32[1]{0:T(128)} %bitcast.me_ref, bf16[160,4096]{1,0:T(8,128)(2,1)} %shard_map.143.refs_0_, bf16[160,4096]{1,0:T(8,128)(2,1)} %copy-done, bf16[160,4096]{1,0:T(8,128)(2,1)} %copy-done.1, bf16[80,4096]{1,0:T(8,128)(2,1)} %collective-permute-done.10.refs_3_, ...), custom_call_target="tpu_custom_call" | custom-call | bytes 73400320 | tf_op jit(solution)/shard_map/pallas_call | solution.py:637
  181.7 1.2 collective-permute-done.25.refs_3_
  182.9 1.2 shard_map.156
  184.1 7.0 %collective-permute-start.26 = (f32[2,16,896]{2,1,0:T(8,128)S(1)}, f32[2,16,896]{2,1,0:T(8,128)S(1)}, u32[]{:S(2)}, u32[]{:S(2)}) collective-permute-start(f32[2,16,896]{2,1,0:T(8,128)S(1)} %get-tuple-element.135), channel_id=1, source_target_pairs={{0,1},{1,0},{2,3},{3,2},{4,5},{5,4},{6,7},{7,6},{8,9},{9,8},{10,11... | collective-permute-start | bytes 344072 | tf_op jit(solution)/shard_map/ppermute | solution.py:44
  191.1 0.1 collective-permute-start.27
  191.2 1.1 collective-permute-done.27.more_ref
  192.3 0.7 shard_map.157
  (90 shorter events, 0.3 us)
Async XLA Ops:
  0.6 8.2 %copy-start.22 = (bf16[128,7168]{1,0:T(8,128)(2,1)S(1)}, bf16[128,7168]{1,0:T(8,128)(2,1)}, u32[]{:S(2)}) copy-start(bf16[128,7168]{1,0:T(8,128)(2,1)} %refs_0_.3) | copy-start | bytes 5505028
  2.1 6.8 %copy-start.20 = (s32[1,128]{1,0:T(1,128)S(1)}, s32[1,128]{1,0:T(1,128)}, u32[]{:S(2)}) copy-start(s32[1,128]{1,0:T(1,128)} %copy-done.19) | copy-start | bytes 1540
  5.1 21.7 %collective-permute-start = (bf16[128,3200]{1,0:T(8,128)(2,1)}, bf16[128,3200]{1,0:T(8,128)(2,1)S(1)}, u32[]{:S(2)}, u32[]{:S(2)}) collective-permute-start(bf16[128,3200]{1,0:T(8,128)(2,1)} %shard_map.140.refs_0_.refs_5_), channel_id=1, source_target_pairs={{0,2},{1,3},{2,4},{3,5},{4,6},{5,7},{6,0},{7,1},{8,10},{9,11},{10,... | collective-permute-start | bytes 2457608 | tf_op jit(solution)/shard_map/ppermute | solution.py:39
  7.3 19.5 %collective-permute-start.1 = (bf16[128,3200]{1,0:T(8,128)(2,1)}, bf16[128,3200]{1,0:T(8,128)(2,1)S(1)}, u32[]{:S(2)}, u32[]{:S(2)}) collective-permute-start(bf16[128,3200]{1,0:T(8,128)(2,1)} %shard_map.140.refs_0_.refs_5_), channel_id=1, source_target_pairs={{0,6},{1,7},{2,0},{3,1},{4,2},{5,3},{6,4},{7,5},{8,14},{9,15},{10,... | collective-permute-start | bytes 2457608 | tf_op jit(solution)/shard_map/ppermute | solution.py:39
  10.9 25.5 %all-to-all-start = ((bf16[16,40,1024]{2,1,0:T(8,128)(2,1)}), bf16[16,40,1024]{2,1,0:T(8,128)(2,1)S(1)}, u32[]{:S(2)}, u32[]{:S(2)}) async-start(bf16[16,40,1024]{2,1,0:T(8,128)(2,1)} %bitcast.2), calls=%async_computation | async-start | bytes 2621440 | tf_op jit(solution)/shard_map/all_to_all | solution.py:482
  18.5 63.2 %collective-permute-start.8 = (bf16[256,7168]{1,0:T(8,128)(2,1)}, bf16[256,7168]{1,0:T(8,128)(2,1)}, u32[]{:S(2)}, u32[]{:S(2)}) collective-permute-start(bf16[256,7168]{1,0:T(8,128)(2,1)} %bitcast.26), channel_id=1, source_target_pairs={{0,1},{1,0},{2,3},{3,2},{4,5},{5,4},{6,7},{7,6},{8,9},{9,8},{10,11... | collective-permute-start | bytes 11010056 | tf_op jit(solution)/shard_map/ppermute | solution.py:44
  20.0 61.8 %collective-permute-start.6 = (bf16[7168,256]{1,0:T(8,128)(2,1)}, bf16[7168,256]{1,0:T(8,128)(2,1)}, u32[]{:S(2)}, u32[]{:S(2)}) collective-permute-start(bf16[7168,256]{1,0:T(8,128)(2,1)} %bitcast.37), channel_id=1, source_target_pairs={{0,1},{1,0},{2,3},{3,2},{4,5},{5,4},{6,7},{7,6},{8,9},{9,8},{10,11... | collective-permute-start | bytes 11010056 | tf_op jit(solution)/shard_map/ppermute | solution.py:44
  20.1 10.3 %copy-start.23 = (bf16[128,7168]{1,0:T(8,128)(2,1)S(1)}, bf16[128,7168]{1,0:T(8,128)(2,1)}, u32[]{:S(2)}) copy-start(bf16[128,7168]{1,0:T(8,128)(2,1)} %refs_0_.3) | copy-start | bytes 5505028
  20.1 61.7 %collective-permute-start.7 = (bf16[7168,256]{1,0:T(8,128)(2,1)}, bf16[7168,256]{1,0:T(8,128)(2,1)}, u32[]{:S(2)}, u32[]{:S(2)}) collective-permute-start(bf16[7168,256]{1,0:T(8,128)(2,1)} %bitcast.40), channel_id=1, source_target_pairs={{0,1},{1,0},{2,3},{3,2},{4,5},{5,4},{6,7},{7,6},{8,9},{9,8},{10,11... | collective-permute-start | bytes 11010056 | tf_op jit(solution)/shard_map/ppermute | solution.py:44
  26.8 6.4 %copy-start.8 = (bf16[128,3200]{1,0:T(8,128)(2,1)}, bf16[128,3200]{1,0:T(8,128)(2,1)S(1)}, u32[]{:S(2)}) copy-start(bf16[128,3200]{1,0:T(8,128)(2,1)S(1)} %collective-permute-done.before_ref.refs_1_.refs_6_) | copy-start | bytes 2457604
  26.8 6.4 %copy-start.9 = (bf16[128,3200]{1,0:T(8,128)(2,1)}, bf16[128,3200]{1,0:T(8,128)(2,1)S(1)}, u32[]{:S(2)}) copy-start(bf16[128,3200]{1,0:T(8,128)(2,1)S(1)} %collective-permute-done.1.after_ref.refs_2_.refs_7_) | copy-start | bytes 2457604
  27.7 11.1 %collective-permute-start.2 = (bf16[64,3200]{1,0:T(8,128)(2,1)}, bf16[64,3200]{1,0:T(8,128)(2,1)}, u32[]{:S(2)}, u32[]{:S(2)}) collective-permute-start(bf16[64,3200]{1,0:T(8,128)(2,1)} %get-tuple-element.77), channel_id=1, source_target_pairs={{0,2},{1,3},{2,4},{3,5},{4,6},{5,7},{6,0},{7,1},{8,10},{9,11},{10,... | collective-permute-start | bytes 1228808 | tf_op jit(solution)/shard_map/ppermute | solution.py:39
  28.5 10.3 %collective-permute-start.3 = (bf16[64,3200]{1,0:T(8,128)(2,1)S(1)}, bf16[64,3200]{1,0:T(8,128)(2,1)}, u32[]{:S(2)}, u32[]{:S(2)}) collective-permute-start(bf16[64,3200]{1,0:T(8,128)(2,1)S(1)} %get-tuple-element.78), channel_id=1, source_target_pairs={{0,6},{1,7},{2,0},{3,1},{4,2},{5,3},{6,4},{7,5},{8,14},{9,15},{10,... | collective-permute-start | bytes 1228808 | tf_op jit(solution)/shard_map/ppermute | solution.py:39
  30.4 1.2 copy-start.7
  33.2 1.4 copy-start.6
  38.8 28.0 %collective-permute-start.4 = (bf16[160,4096]{1,0:T(8,128)(2,1)}, bf16[160,4096]{1,0:T(8,128)(2,1)S(1)}, u32[]{:S(2)}, u32[]{:S(2)}) collective-permute-start(bf16[160,4096]{1,0:T(8,128)(2,1)} %shard_map.143.refs_0_), channel_id=1, source_target_pairs={{0,2},{1,3},{2,4},{3,5},{4,6},{5,7},{6,0},{7,1},{8,10},{9,11},{10,... | collective-permute-start | bytes 3932168 | tf_op jit(solution)/shard_map/ppermute | solution.py:39
  38.8 32.6 %collective-permute-start.5 = (bf16[160,4096]{1,0:T(8,128)(2,1)}, bf16[160,4096]{1,0:T(8,128)(2,1)S(1)}, u32[]{:S(2)}, u32[]{:S(2)}) collective-permute-start(bf16[160,4096]{1,0:T(8,128)(2,1)} %shard_map.143.refs_0_), channel_id=1, source_target_pairs={{0,6},{1,7},{2,0},{3,1},{4,2},{5,3},{6,4},{7,5},{8,14},{9,15},{10,... | collective-permute-start | bytes 3932168 | tf_op jit(solution)/shard_map/ppermute | solution.py:39
  41.5 7.6 %copy-start.13 = (bf16[1,16,256]{2,1,0:T(8,128)(2,1)S(1)}, bf16[1,16,256]{2,1,0:T(8,128)(2,1)}, u32[]{:S(2)}) copy-start(bf16[1,16,256]{2,1,0:T(8,128)(2,1)} %param.19) | copy-start | bytes 24580
  41.5 7.6 %copy-start.15 = (bf16[1,16,256]{2,1,0:T(8,128)(2,1)S(1)}, bf16[1,16,256]{2,1,0:T(8,128)(2,1)}, u32[]{:S(2)}) copy-start(bf16[1,16,256]{2,1,0:T(8,128)(2,1)} %param.20) | copy-start | bytes 24580
  41.5 40.2 %all-to-all-start.1 = ((bf16[16,40,1792]{2,1,0:T(8,128)(2,1)}), bf16[16,40,1792]{2,1,0:T(8,128)(2,1)}, u32[]{:S(2)}, u32[]{:S(2)}) async-start(bf16[16,40,1792]{2,1,0:T(8,128)(2,1)} %bitcast.16), calls=%async_computation.1 | async-start | bytes 4587520 | tf_op jit(solution)/shard_map/all_to_all | solution.py:482
  66.9 14.8 %copy-start = (bf16[160,4096]{1,0:T(8,128)(2,1)}, bf16[160,4096]{1,0:T(8,128)(2,1)S(1)}, u32[]{:S(2)}) copy-start(bf16[160,4096]{1,0:T(8,128)(2,1)S(1)} %collective-permute-done.4.before_ref.refs_1_) | copy-start | bytes 3932164
  66.9 5.6 %collective-permute-start.9 = (bf16[32,256]{1,0:T(8,128)(2,1)S(1)}, bf16[32,256]{1,0:T(8,128)(2,1)S(1)}, u32[]{:S(2)}, u32[]{:S(2)}) collective-permute-start(bf16[32,256]{1,0:T(8,128)(2,1)S(1)} %pad_maximum_fusion), channel_id=1, source_target_pairs={{0,1},{1,0},{2,3},{3,2},{4,5},{5,4},{6,7},{7,6},{8,9},{9,8},{10,11... | collective-permute-start | bytes 49160 | tf_op jit(solution)/shard_map/ppermute | solution.py:44
  71.4 10.2 %copy-start.1 = (bf16[160,4096]{1,0:T(8,128)(2,1)}, bf16[160,4096]{1,0:T(8,128)(2,1)S(1)}, u32[]{:S(2)}) copy-start(bf16[160,4096]{1,0:T(8,128)(2,1)S(1)} %collective-permute-done.5.after_ref.refs_2_) | copy-start | bytes 3932164
  72.5 17.8 %collective-permute-start.10 = (bf16[80,4096]{1,0:T(8,128)(2,1)}, bf16[80,4096]{1,0:T(8,128)(2,1)}, u32[]{:S(2)}, u32[]{:S(2)}) collective-permute-start(bf16[80,4096]{1,0:T(8,128)(2,1)} %get-tuple-element.86), channel_id=1, source_target_pairs={{0,2},{1,3},{2,4},{3,5},{4,6},{5,7},{6,0},{7,1},{8,10},{9,11},{10,... | collective-permute-start | bytes 1966088 | tf_op jit(solution)/shard_map/ppermute | solution.py:39
  72.5 17.8 %collective-permute-start.11 = (bf16[80,4096]{1,0:T(8,128)(2,1)S(1)}, bf16[80,4096]{1,0:T(8,128)(2,1)}, u32[]{:S(2)}, u32[]{:S(2)}) collective-permute-start(bf16[80,4096]{1,0:T(8,128)(2,1)S(1)} %get-tuple-element.87), channel_id=1, source_target_pairs={{0,6},{1,7},{2,0},{3,1},{4,2},{5,3},{6,4},{7,5},{8,14},{9,15},{10,... | collective-permute-start | bytes 1966088 | tf_op jit(solution)/shard_map/ppermute | solution.py:39
  90.3 24.0 %collective-permute-start.12 = (bf16[160,3072]{1,0:T(8,128)(2,1)}, bf16[160,3072]{1,0:T(8,128)(2,1)S(1)}, u32[]{:S(2)}, u32[]{:S(2)}) collective-permute-start(bf16[160,3072]{1,0:T(8,128)(2,1)} %get-tuple-element.90.refs_0_.refs_5_), channel_id=1, source_target_pairs={{0,2},{1,3},{2,4},{3,5},{4,6},{5,7},{6,0},{7,1},{8,10},{9,11},{10,... | collective-permute-start | bytes 2949128 | tf_op jit(solution)/shard_map/ppermute | solution.py:39
  90.3 24.0 %collective-permute-start.13 = (bf16[160,3072]{1,0:T(8,128)(2,1)}, bf16[160,3072]{1,0:T(8,128)(2,1)S(1)}, u32[]{:S(2)}, u32[]{:S(2)}) collective-permute-start(bf16[160,3072]{1,0:T(8,128)(2,1)} %get-tuple-element.90.refs_0_.refs_5_), channel_id=1, source_target_pairs={{0,6},{1,7},{2,0},{3,1},{4,2},{5,3},{6,4},{7,5},{8,14},{9,15},{10,... | collective-permute-start | bytes 2949128 | tf_op jit(solution)/shard_map/ppermute | solution.py:39
  93.0 56.4 %all-to-all-start.2 = ((bf16[16,40,3072]{2,1,0:T(8,128)(2,1)}), bf16[16,40,3072]{2,1,0:T(8,128)(2,1)}, u32[]{:S(2)}, u32[]{:S(2)}) async-start(bf16[16,40,3072]{2,1,0:T(8,128)(2,1)} %bitcast.34), calls=%async_computation.2 | async-start | bytes 7864320 | tf_op jit(solution)/shard_map/all_to_all | solution.py:482
  114.3 3.4 %copy-start.4 = (bf16[160,3072]{1,0:T(8,128)(2,1)}, bf16[160,3072]{1,0:T(8,128)(2,1)S(1)}, u32[]{:S(2)}) copy-start(bf16[160,3072]{1,0:T(8,128)(2,1)S(1)} %collective-permute-done.12.before_ref.refs_1_.refs_6_) | copy-start | bytes 2949124
  114.3 2.8 %copy-start.5 = (bf16[160,3072]{1,0:T(8,128)(2,1)}, bf16[160,3072]{1,0:T(8,128)(2,1)S(1)}, u32[]{:S(2)}) copy-start(bf16[160,3072]{1,0:T(8,128)(2,1)S(1)} %collective-permute-done.13.after_ref.refs_2_.refs_7_) | copy-start | bytes 2949124
  114.3 12.5 %collective-permute-start.14 = (bf16[80,3072]{1,0:T(8,128)(2,1)S(1)}, bf16[80,3072]{1,0:T(8,128)(2,1)S(1)}, u32[]{:S(2)}, u32[]{:S(2)}) collective-permute-start(bf16[80,3072]{1,0:T(8,128)(2,1)S(1)} %get-tuple-element.101), channel_id=1, source_target_pairs={{0,2},{1,3},{2,4},{3,5},{4,6},{5,7},{6,0},{7,1},{8,10},{9,11},{10,... | collective-permute-start | bytes 1474568 | tf_op jit(solution)/shard_map/ppermute | solution.py:39
  114.4 12.4 %collective-permute-start.15 = (bf16[80,3072]{1,0:T(8,128)(2,1)S(1)}, bf16[80,3072]{1,0:T(8,128)(2,1)S(1)}, u32[]{:S(2)}, u32[]{:S(2)}) collective-permute-start(bf16[80,3072]{1,0:T(8,128)(2,1)S(1)} %get-tuple-element.102), channel_id=1, source_target_pairs={{0,6},{1,7},{2,0},{3,1},{4,2},{5,3},{6,4},{7,5},{8,14},{9,15},{10,... | collective-permute-start | bytes 1474568 | tf_op jit(solution)/shard_map/ppermute | solution.py:39
  117.7 40.7 %collective-permute-start.16 = (bf16[160,4096]{1,0:T(8,128)(2,1)}, bf16[160,4096]{1,0:T(8,128)(2,1)S(1)}, u32[]{:S(2)}, u32[]{:S(2)}) collective-permute-start(bf16[160,4096]{1,0:T(8,128)(2,1)} %get-tuple-element.103.refs_10_.refs_0_), channel_id=1, source_target_pairs={{0,2},{1,3},{2,4},{3,5},{4,6},{5,7},{6,0},{7,1},{8,10},{9,11},{10,... | collective-permute-start | bytes 3932168 | tf_op jit(solution)/shard_map/ppermute | solution.py:39
  117.7 40.7 %collective-permute-start.17 = (bf16[160,4096]{1,0:T(8,128)(2,1)}, bf16[160,4096]{1,0:T(8,128)(2,1)S(1)}, u32[]{:S(2)}, u32[]{:S(2)}) collective-permute-start(bf16[160,4096]{1,0:T(8,128)(2,1)} %get-tuple-element.103.refs_10_.refs_0_), channel_id=1, source_target_pairs={{0,6},{1,7},{2,0},{3,1},{4,2},{5,3},{6,4},{7,5},{8,14},{9,15},{10,... | collective-permute-start | bytes 3932168 | tf_op jit(solution)/shard_map/ppermute | solution.py:39
  126.8 0.8 copy-start.33
  126.8 1.0 copy-start.34
  139.6 29.1 %collective-permute-start.20 = (f32[16,640]{1,0:T(8,128)}, f32[16,640]{1,0:T(8,128)S(1)}, u32[]{:S(2)}, u32[]{:S(2)}) collective-permute-start(f32[16,640]{1,0:T(8,128)} %get-tuple-element.130.refs_4_), channel_id=1, source_target_pairs={{0,2},{1,3},{2,4},{3,5},{4,6},{5,7},{6,0},{7,1},{8,10},{9,11},{10,... | collective-permute-start | bytes 122888 | tf_op jit(solution)/shard_map/ppermute | solution.py:39
  139.8 28.9 %collective-permute-start.21 = (f32[16,640]{1,0:T(8,128)}, f32[16,640]{1,0:T(8,128)S(1)}, u32[]{:S(2)}, u32[]{:S(2)}) collective-permute-start(f32[16,640]{1,0:T(8,128)} %get-tuple-element.130.refs_4_), channel_id=1, source_target_pairs={{0,6},{1,7},{2,0},{3,1},{4,2},{5,3},{6,4},{7,5},{8,14},{9,15},{10,... | collective-permute-start | bytes 122888 | tf_op jit(solution)/shard_map/ppermute | solution.py:39
  142.4 26.3 %collective-permute-start.22 = (f32[16,640]{1,0:T(8,128)}, f32[16,640]{1,0:T(8,128)S(1)}, u32[]{:S(2)}, u32[]{:S(2)}) collective-permute-start(f32[16,640]{1,0:T(8,128)} %get-tuple-element.130.refs_4_), channel_id=1, source_target_pairs={{0,4},{1,5},{2,6},{3,7},{4,0},{5,1},{6,2},{7,3},{8,12},{9,13},{10,... | collective-permute-start | bytes 122888 | tf_op jit(solution)/shard_map/ppermute | solution.py:39
  149.4 11.8 %copy-start.32 = (bf16[640,16]{1,0:T(8,128)(2,1)S(1)}, bf16[640,16]{1,0:T(8,128)(2,1)}, u32[]{:S(2)}) copy-start(bf16[640,16]{1,0:T(8,128)(2,1)} %get-tuple-element.125.refs_10_.refs_9_) | copy-start | bytes 61444
  158.3 3.0 %copy-start.14 = (bf16[1,16,256]{2,1,0:T(8,128)(2,1)S(1)}, bf16[1,16,256]{2,1,0:T(8,128)(2,1)}, u32[]{:S(2)}) copy-start(bf16[1,16,256]{2,1,0:T(8,128)(2,1)} %param.19) | copy-start | bytes 24580
  158.3 3.0 %copy-start.16 = (bf16[1,16,256]{2,1,0:T(8,128)(2,1)S(1)}, bf16[1,16,256]{2,1,0:T(8,128)(2,1)}, u32[]{:S(2)}) copy-start(bf16[1,16,256]{2,1,0:T(8,128)(2,1)} %param.20) | copy-start | bytes 24580
  158.3 3.0 %copy-start.17 = (bf16[16,256]{1,0:T(8,128)(2,1)S(1)}, bf16[16,256]{1,0:T(8,128)(2,1)}, u32[]{:S(2)}) copy-start(bf16[16,256]{1,0:T(8,128)(2,1)} %get-tuple-element.138.refs_16_.refs_14_.refs_13_) | copy-start | bytes 24580
  158.3 3.0 %copy-start.18 = (bf16[16,256]{1,0:T(8,128)(2,1)S(1)}, bf16[16,256]{1,0:T(8,128)(2,1)}, u32[]{:S(2)}) copy-start(bf16[16,256]{1,0:T(8,128)(2,1)} %get-tuple-element.139.refs_14_.refs_12_.refs_11_) | copy-start | bytes 24580
  158.3 3.0 %copy-start.24 = (bf16[1,16,7168]{2,1,0:T(8,128)(2,1)S(1)}, bf16[1,16,7168]{2,1,0:T(8,128)(2,1)}, u32[]{:S(2)}) copy-start(bf16[1,16,7168]{2,1,0:T(8,128)(2,1)} %param.21) | copy-start | bytes 688132
  158.3 2.9 %copy-start.26 = (f32[640,512]{1,0:T(8,128)S(1)}, f32[640,512]{1,0:T(8,128)}, u32[]{:S(2)}) copy-start(f32[640,512]{1,0:T(8,128)} %get-tuple-element.123.refs_8_.refs_7_) | copy-start | bytes 3932164
  158.3 2.9 %copy-start.30 = (bf16[640,512]{1,0:T(8,128)(2,1)S(1)}, bf16[640,512]{1,0:T(8,128)(2,1)}, u32[]{:S(2)}) copy-start(bf16[640,512]{1,0:T(8,128)(2,1)} %get-tuple-element.124.refs_9_.refs_8_) | copy-start | bytes 1966084
  158.4 2.9 %copy-start.31 = (f32[640,16]{1,0:T(8,128)S(1)}, f32[640,16]{1,0:T(8,128)}, u32[]{:S(2)}) copy-start(f32[640,16]{1,0:T(8,128)} %get-tuple-element.122.refs_7_.refs_6_) | copy-start | bytes 122884
  158.4 10.3 %copy-start.2 = (bf16[160,4096]{1,0:T(8,128)(2,1)}, bf16[160,4096]{1,0:T(8,128)(2,1)S(1)}, u32[]{:S(2)}) copy-start(bf16[160,4096]{1,0:T(8,128)(2,1)S(1)} %collective-permute-done.16.before_ref.refs_11_.refs_1_) | copy-start | bytes 3932164
  158.4 10.3 %copy-start.3 = (bf16[160,4096]{1,0:T(8,128)(2,1)}, bf16[160,4096]{1,0:T(8,128)(2,1)S(1)}, u32[]{:S(2)}) copy-start(bf16[160,4096]{1,0:T(8,128)(2,1)S(1)} %collective-permute-done.17.after_ref.refs_12_.refs_2_) | copy-start | bytes 3932164
  158.5 13.2 %collective-permute-start.18 = (bf16[80,4096]{1,0:T(8,128)(2,1)S(1)}, bf16[80,4096]{1,0:T(8,128)(2,1)S(1)}, u32[]{:S(2)}, u32[]{:S(2)}) collective-permute-start(bf16[80,4096]{1,0:T(8,128)(2,1)S(1)} %get-tuple-element.114), channel_id=1, source_target_pairs={{0,2},{1,3},{2,4},{3,5},{4,6},{5,7},{6,0},{7,1},{8,10},{9,11},{10,... | collective-permute-start | bytes 1966088 | tf_op jit(solution)/shard_map/ppermute | solution.py:39
  158.6 13.1 %collective-permute-start.19 = (bf16[80,4096]{1,0:T(8,128)(2,1)S(1)}, bf16[80,4096]{1,0:T(8,128)(2,1)S(1)}, u32[]{:S(2)}, u32[]{:S(2)}) collective-permute-start(bf16[80,4096]{1,0:T(8,128)(2,1)S(1)} %get-tuple-element.115), channel_id=1, source_target_pairs={{0,6},{1,7},{2,0},{3,1},{4,2},{5,3},{6,4},{7,5},{8,14},{9,15},{10,... | collective-permute-start | bytes 1966088 | tf_op jit(solution)/shard_map/ppermute | solution.py:39
  161.3 1.3 copy-start.28
  162.6 9.0 %copy-start.21 = (bf16[1,256,7168]{2,1,0:T(8,128)(2,1)S(1)}, bf16[1,256,7168]{2,1,0:T(8,128)(2,1)}, u32[]{:S(2)}) copy-start(bf16[1,256,7168]{2,1,0:T(8,128)(2,1)} %param.17) | copy-start | bytes 11010052
  162.6 9.0 %copy-start.27 = (f32[640,512]{1,0:T(8,128)S(1)}, f32[640,512]{1,0:T(8,128)}, u32[]{:S(2)}) copy-start(f32[640,512]{1,0:T(8,128)} %get-tuple-element.123.refs_8_.refs_7_) | copy-start | bytes 3932164
  162.6 9.0 %copy-start.29 = (f32[640,512]{1,0:T(8,128)S(1)}, f32[640,512]{1,0:T(8,128)}, u32[]{:S(2)}) copy-start(f32[640,512]{1,0:T(8,128)} %get-tuple-element.121.refs_6_.refs_5_) | copy-start | bytes 3932164
  171.7 4.2 %copy-start.10 = (bf16[80,4096]{1,0:T(8,128)(2,1)}, bf16[80,4096]{1,0:T(8,128)(2,1)S(1)}, u32[]{:S(2)}) copy-start(bf16[80,4096]{1,0:T(8,128)(2,1)S(1)} %collective-permute-done.18.refs_13_.refs_0_) | copy-start | bytes 1966084
  171.7 4.2 %copy-start.11 = (bf16[80,4096]{1,0:T(8,128)(2,1)}, bf16[80,4096]{1,0:T(8,128)(2,1)S(1)}, u32[]{:S(2)}) copy-start(bf16[80,4096]{1,0:T(8,128)(2,1)S(1)} %collective-permute-done.19.refs_14_.refs_1_) | copy-start | bytes 1966084
  175.8 5.8 %collective-permute-start.23 = (f32[16,640]{1,0:T(8,128)S(1)}, f32[16,640]{1,0:T(8,128)S(1)}, u32[]{:S(2)}, u32[]{:S(2)}) collective-permute-start(f32[16,640]{1,0:T(8,128)S(1)} %get-tuple-element.129.refs_0_), channel_id=1, source_target_pairs={{0,2},{1,3},{2,4},{3,5},{4,6},{5,7},{6,0},{7,1},{8,10},{9,11},{10,... | collective-permute-start | bytes 122888 | tf_op jit(solution)/shard_map/ppermute | solution.py:39
  175.9 5.8 %collective-permute-start.24 = (f32[16,640]{1,0:T(8,128)S(1)}, f32[16,640]{1,0:T(8,128)S(1)}, u32[]{:S(2)}, u32[]{:S(2)}) collective-permute-start(f32[16,640]{1,0:T(8,128)S(1)} %get-tuple-element.129.refs_0_), channel_id=1, source_target_pairs={{0,6},{1,7},{2,0},{3,1},{4,2},{5,3},{6,4},{7,5},{8,14},{9,15},{10,... | collective-permute-start | bytes 122888 | tf_op jit(solution)/shard_map/ppermute | solution.py:39
  178.6 4.4 %collective-permute-start.25 = (f32[16,640]{1,0:T(8,128)S(1)}, f32[16,640]{1,0:T(8,128)S(1)}, u32[]{:S(2)}, u32[]{:S(2)}) collective-permute-start(f32[16,640]{1,0:T(8,128)S(1)} %get-tuple-element.129.refs_0_), channel_id=1, source_target_pairs={{0,4},{1,5},{2,6},{3,7},{4,0},{5,1},{6,2},{7,3},{8,12},{9,13},{10,... | collective-permute-start | bytes 122888 | tf_op jit(solution)/shard_map/ppermute | solution.py:39
  179.3 3.7 %copy-start.12 = (f32[16,640]{1,0:T(8,128)S(1)}, f32[16,640]{1,0:T(8,128)}, u32[]{:S(2)}) copy-start(f32[16,640]{1,0:T(8,128)} %get-tuple-element.130.refs_4_) | copy-start | bytes 122884
  184.1 8.2 %collective-permute-start.26 = (f32[2,16,896]{2,1,0:T(8,128)S(1)}, f32[2,16,896]{2,1,0:T(8,128)S(1)}, u32[]{:S(2)}, u32[]{:S(2)}) collective-permute-start(f32[2,16,896]{2,1,0:T(8,128)S(1)} %get-tuple-element.135), channel_id=1, source_target_pairs={{0,1},{1,0},{2,3},{3,2},{4,5},{5,4},{6,7},{7,6},{8,9},{9,8},{10,11... | collective-permute-start | bytes 344072 | tf_op jit(solution)/shard_map/ppermute | solution.py:44
  191.1 1.2 collective-permute-start.27
  (2 other events, 1.3 us)

commit v7 on v6

--- a/solution.py
+++ b/solution.py
@@ -553,7 +553,7 @@
             functools.partial(gate_up_kernel, begins, last),
             outs,
             VMEM_MIB,
-            flops=2 * every * size * 4 * units,
+            flops=every * size * 3 * units,
             moved=2 * size * (every + 4 * units),
             grid=(size // depth,),
             in_specs=piece_specs(pieces, depth)

time: 194 us -> 194 us (level)
    ppermute x22, waiting for transfers between devices: 38.6 us -> 46.7 us  [shift_y(): return lax.ppermute(value, 'seq', pairs)]
    all_to_all x3, waiting for transfers between devices: 8.19 us -> 1.89 us  [across_dp(): lax.all_to_all(sent, 'dp', split_axis=0, concat_axis=0, tiled=True)]
  transfers between devices with their start and end apart: 31 -> 31, of which waited for: 10 -> 9; matrix products, arithmetic and copies ran while one was open for 0% -> 0% of each run, Pallas kernels for 32% -> 32%
where the time goes in v7:
time: 194 us; the launch traced here: 193 us
  Pallas kernels  71.4 us (37%)
  starting transfers between devices  64.4 us (33%)
  waiting for transfers between devices  49.8 us (26%)
  local copies, waits for them, and re-layouts  6.85 us (4%)
    ppermute x22, waiting for transfers between devices, shift_y(): return lax.ppermute(value, 'seq', pairs)  46.7 us
    ppermute x22, starting transfers between devices, shift_y(): return lax.ppermute(value, 'seq', pairs)  29.2 us
    pallas_call x2, Pallas kernels, gate_up(): call(functools.partial(gate_up_kernel, begins, last), outs, VMEM_MIB, flo...  22.9 us
    all_to_all x3, starting transfers between devices, across_dp(): lax.all_to_all(sent, 'dp', split_axis=0, concat_axis=0, tiled=True)  22.6 us
    ppermute x6, starting transfers between devices, swap_core(): return lax.ppermute(value, 'seq', [(i, i ^ 1) for i in range(size)])  12.6 us
    pallas_call x2, Pallas kernels, back(): call(functools.partial(back_kernel, last, len(pieces)), outs, 24 if last...  10.2 us
    pallas_call x1, Pallas kernels, body(): call(functools.partial(raw_kernel, capacity), (totals[0], totals[2]), VME...  8.86 us
    pallas_call x2, Pallas kernels, unpack(): call(functools.partial(unpack_kernel, capacity), tuple((shape((slots, siz...  7.19 us
  transfers between devices with their start and end apart: 31, of which 9 were waited for; matrix products, arithmetic and copies ran while one was open for 0% of the time, Pallas kernels for 32%

profile of v7, /device:TPU:1, one launch (start us, length us, event | category | flops | bytes accessed | tf_op | source)
XLA Modules:
  0.0 193.4 jit_solution(17530934380075384247)
XLA Ops:
  0.7 0.8 copy-done.25
  1.4 0.1 shard_map.138.code_ref
  1.6 0.5 copy-done.19
  2.1 3.0 %shard_map.140.refs_0_.refs_5_ = bf16[128,3200]{1,0:T(8,128)(2,1)} custom-call(bf16[128,7168]{1,0:T(8,128)(2,1)} %cot_ref.3, f32[1,128]{1,0:T(1,128)} %bitcast.35, s32[1,128]{1,0:T(1,128)} %copy-done.19), custom_call_target="tpu_custom_call" | custom-call | bytes 12582912 | tf_op jit(solution)/shard_map/pallas_call | solution.py:446
  5.1 2.2 %collective-permute-start = (bf16[128,3200]{1,0:T(8,128)(2,1)}, bf16[128,3200]{1,0:T(8,128)(2,1)S(1)}, u32[]{:S(2)}, u32[]{:S(2)}) collective-permute-start(bf16[128,3200]{1,0:T(8,128)(2,1)} %shard_map.140.refs_0_.refs_5_), channel_id=1, source_target_pairs={{0,2},{1,3},{2,4},{3,5},{4,6},{5,7},{6,0},{7,1},{8,10},{9,11},{10,... | collective-permute-start | bytes 2457608 | tf_op jit(solution)/shard_map/ppermute | solution.py:39
  7.3 1.5 collective-permute-start.1
  8.8 2.0 %shard_map.139 = bf16[640,1024]{1,0:T(8,128)(2,1)} custom-call(s32[1,128]{1,0:T(1,128)S(1)} %copy-done.20, bf16[128,7168]{1,0:T(8,128)(2,1)S(1)} %copy-done.22), custom_call_target="tpu_custom_call" | custom-call | flops 5368709120 | bytes 18874368 | tf_op jit(solution)/shard_map/pallas_call | solution.py:468
  10.9 7.6 %all-to-all-start = ((bf16[16,40,1024]{2,1,0:T(8,128)(2,1)}), bf16[16,40,1024]{2,1,0:T(8,128)(2,1)S(1)}, u32[]{:S(2)}, u32[]{:S(2)}) async-start(bf16[16,40,1024]{2,1,0:T(8,128)(2,1)} %bitcast.2), calls=%async_computation | async-start | bytes 2621440 | tf_op jit(solution)/shard_map/all_to_all | solution.py:482
  18.5 1.5 collective-permute-start.8
  20.0 0.1 collective-permute-start.6
  20.1 0.4 collective-permute-start.7
  20.5 2.7 %shard_map.141.refs_1_ = bf16[128,4096]{1,0:T(8,128)(2,1)} custom-call(bf16[128,7168]{1,0:T(8,128)(2,1)} %cot_ref.3, f32[1,128]{1,0:T(1,128)} %bitcast.36), custom_call_target="tpu_custom_call" | custom-call | bytes 16777216 | tf_op jit(solution)/shard_map/pallas_call | solution.py:454
  23.1 3.6 %collective-permute-done.before_ref.refs_1_.refs_6_ = bf16[128,3200]{1,0:T(8,128)(2,1)S(1)} collective-permute-done((bf16[128,3200]{1,0:T(8,128)(2,1)}, bf16[128,3200]{1,0:T(8,128)(2,1)S(1)}, u32[]{:S(2)}, u32[]{:S(2)}) %collective-permute-start) | collective-permute-done | bytes 819232 | tf_op jit(solution)/shard_map/ppermute | solution.py:39
  26.8 0.9 shard_map.144
  27.7 0.8 collective-permute-start.2
  28.5 1.9 collective-permute-start.3
  30.4 1.2 copy-done.7
  31.6 1.6 shard_map.142
  33.2 1.3 copy-done.6
  34.6 1.9 all-to-all-done
  36.4 2.4 %shard_map.143.refs_0_ = bf16[160,4096]{1,0:T(8,128)(2,1)} custom-call(bf16[640,1024]{1,0:T(8,128)(2,1)S(1)} %bitcast.17), custom_call_target="tpu_custom_call" | custom-call | flops 838860800 | bytes 2621440 | tf_op jit(solution)/shard_map/pallas_call | solution.py:485
  38.8 2.7 %collective-permute-start.5 = (bf16[160,4096]{1,0:T(8,128)(2,1)}, bf16[160,4096]{1,0:T(8,128)(2,1)S(1)}, u32[]{:S(2)}, u32[]{:S(2)}) collective-permute-start(bf16[160,4096]{1,0:T(8,128)(2,1)} %shard_map.143.refs_0_), channel_id=1, source_target_pairs={{0,6},{1,7},{2,0},{3,1},{4,2},{5,3},{6,4},{7,5},{8,14},{9,15},{10,... | collective-permute-start | bytes 3932168 | tf_op jit(solution)/shard_map/ppermute | solution.py:39
  41.5 7.6 %all-to-all-start.1 = ((bf16[16,40,1792]{2,1,0:T(8,128)(2,1)}), bf16[16,40,1792]{2,1,0:T(8,128)(2,1)}, u32[]{:S(2)}, u32[]{:S(2)}) async-start(bf16[16,40,1792]{2,1,0:T(8,128)(2,1)} %bitcast.16), calls=%async_computation.1 | async-start | bytes 4587520 | tf_op jit(solution)/shard_map/all_to_all | solution.py:482
  49.1 17.8 %collective-permute-done.4.before_ref.refs_1_ = bf16[160,4096]{1,0:T(8,128)(2,1)S(1)} collective-permute-done((bf16[160,4096]{1,0:T(8,128)(2,1)}, bf16[160,4096]{1,0:T(8,128)(2,1)S(1)}, u32[]{:S(2)}, u32[]{:S(2)}) %collective-permute-start.4) | collective-permute-done | bytes 1310752 | tf_op jit(solution)/shard_map/ppermute | solution.py:39
  66.9 4.6 %collective-permute-start.9 = (bf16[32,256]{1,0:T(8,128)(2,1)S(1)}, bf16[32,256]{1,0:T(8,128)(2,1)S(1)}, u32[]{:S(2)}, u32[]{:S(2)}) collective-permute-start(bf16[32,256]{1,0:T(8,128)(2,1)S(1)} %pad_maximum_fusion), channel_id=1, source_target_pairs={{0,1},{1,0},{2,3},{3,2},{4,5},{5,4},{6,7},{7,6},{8,9},{9,8},{10,11... | collective-permute-start | bytes 49160 | tf_op jit(solution)/shard_map/ppermute | solution.py:44
  71.4 1.0 shard_map.147
  72.5 2.7 %collective-permute-start.11 = (bf16[80,4096]{1,0:T(8,128)(2,1)S(1)}, bf16[80,4096]{1,0:T(8,128)(2,1)}, u32[]{:S(2)}, u32[]{:S(2)}) collective-permute-start(bf16[80,4096]{1,0:T(8,128)(2,1)S(1)} %get-tuple-element.87), channel_id=1, source_target_pairs={{0,6},{1,7},{2,0},{3,1},{4,2},{5,3},{6,4},{7,5},{8,14},{9,15},{10,... | collective-permute-start | bytes 1966088 | tf_op jit(solution)/shard_map/ppermute | solution.py:39
  75.2 6.5 %shard_map.145 = bf16[640,3072]{1,0:T(8,128)(2,1)} custom-call(bf16[128,3200]{1,0:T(8,128)(2,1)} %shard_map.140.refs_0_.refs_5_, bf16[128,3200]{1,0:T(8,128)(2,1)} %copy-done.8, bf16[128,3200]{1,0:T(8,128)(2,1)} %copy-done.9, bf16[64,3200]{1,0:T(8,128)(2,1)} %collective-permute-done.2.refs_3_.refs_8_, ...), custom_call_target="tpu_custom_call" | custom-call | flops 16106127360 | bytes 56623104 | tf_op jit(solution)/shard_map/pallas_call | solution.py:508
  81.7 7.4 %all-to-all-start.2 = ((bf16[16,40,3072]{2,1,0:T(8,128)(2,1)}), bf16[16,40,3072]{2,1,0:T(8,128)(2,1)}, u32[]{:S(2)}, u32[]{:S(2)}) async-start(bf16[16,40,3072]{2,1,0:T(8,128)(2,1)} %bitcast.34), calls=%async_computation.2 | async-start | bytes 7864320 | tf_op jit(solution)/shard_map/all_to_all | solution.py:482
  89.2 4.8 %shard_map.146 = (bf16[160,3072]{1,0:T(8,128)(2,1)}, bf16[160,4096]{1,0:T(8,128)(2,1)}) custom-call(bf16[640,1792]{1,0:T(8,128)(2,1)} %bitcast.6.got_ref), custom_call_target="tpu_custom_call" | custom-call | flops 1468006400 | bytes 4587520 | tf_op jit(solution)/shard_map/pallas_call | solution.py:485
  94.0 2.7 %collective-permute-start.13 = (bf16[160,3072]{1,0:T(8,128)(2,1)}, bf16[160,3072]{1,0:T(8,128)(2,1)S(1)}, u32[]{:S(2)}, u32[]{:S(2)}) collective-permute-start(bf16[160,3072]{1,0:T(8,128)(2,1)} %get-tuple-element.90.refs_0_.refs_5_), channel_id=1, source_target_pairs={{0,6},{1,7},{2,0},{3,1},{4,2},{5,3},{6,4},{7,5},{8,14},{9,15},{10,... | collective-permute-start | bytes 2949128 | tf_op jit(solution)/shard_map/ppermute | solution.py:39
  96.7 11.0 %shard_map.148 = (f32[640,512]{1,0:T(8,128)}, f32[640,512]{1,0:T(8,128)}, f32[640,16]{1,0:T(8,128)}) custom-call(bf16[160,4096]{1,0:T(8,128)(2,1)} %shard_map.143.refs_0_, bf16[160,4096]{1,0:T(8,128)(2,1)} %copy-done, bf16[160,4096]{1,0:T(8,128)(2,1)} %copy-done.1, bf16[80,4096]{1,0:T(8,128)(2,1)} %collective-permute-done.10.refs_3_, ...), custom_call_target="tpu_custom_call" | custom-call | flops 16106127360 | bytes 109051904 | tf_op jit(solution)/shard_map/pallas_call | solution.py:552
  107.7 10.2 %collective-permute-done.12.before_ref.refs_1_.refs_6_ = bf16[160,3072]{1,0:T(8,128)(2,1)S(1)} collective-permute-done((bf16[160,3072]{1,0:T(8,128)(2,1)}, bf16[160,3072]{1,0:T(8,128)(2,1)S(1)}, u32[]{:S(2)}, u32[]{:S(2)}) %collective-permute-start.12) | collective-permute-done | bytes 983072 | tf_op jit(solution)/shard_map/ppermute | solution.py:39
  117.9 0.1 shard_map.149
  118.0 0.1 collective-permute-start.14
  118.0 2.7 %collective-permute-start.15 = (bf16[80,3072]{1,0:T(8,128)(2,1)S(1)}, bf16[80,3072]{1,0:T(8,128)(2,1)S(1)}, u32[]{:S(2)}, u32[]{:S(2)}) collective-permute-start(bf16[80,3072]{1,0:T(8,128)(2,1)S(1)} %get-tuple-element.102), channel_id=1, source_target_pairs={{0,6},{1,7},{2,0},{3,1},{4,2},{5,3},{6,4},{7,5},{8,14},{9,15},{10,... | collective-permute-start | bytes 1474568 | tf_op jit(solution)/shard_map/ppermute | solution.py:39
  120.7 0.6 fusion
  121.3 2.7 %collective-permute-start.17 = (bf16[160,4096]{1,0:T(8,128)(2,1)}, bf16[160,4096]{1,0:T(8,128)(2,1)S(1)}, u32[]{:S(2)}, u32[]{:S(2)}) collective-permute-start(bf16[160,4096]{1,0:T(8,128)(2,1)} %get-tuple-element.103.refs_10_.refs_0_), channel_id=1, source_target_pairs={{0,6},{1,7},{2,0},{3,1},{4,2},{5,3},{6,4},{7,5},{8,14},{9,15},{10,... | collective-permute-start | bytes 3932168 | tf_op jit(solution)/shard_map/ppermute | solution.py:39
  124.0 6.4 %collective-permute-done.14.refs_3_.refs_8_ = bf16[80,3072]{1,0:T(8,128)(2,1)S(1)} collective-permute-done((bf16[80,3072]{1,0:T(8,128)(2,1)S(1)}, bf16[80,3072]{1,0:T(8,128)(2,1)S(1)}, u32[]{:S(2)}, u32[]{:S(2)}) %collective-permute-start.14) | collective-permute-done | bytes 491552 | tf_op jit(solution)/shard_map/ppermute | solution.py:39
  130.4 0.8 copy-done.34
  131.2 0.1 copy-done.33
  131.3 11.8 %shard_map.150 = (bf16[640,512]{1,0:T(8,128)(2,1)}, f32[640,512]{1,0:T(8,128)}, bf16[640,16]{1,0:T(8,128)(2,1)}, f32[16,640]{1,0:T(8,128)}) custom-call(bf16[160,3072]{1,0:T(8,128)(2,1)} %get-tuple-element.90.refs_0_.refs_5_, bf16[160,3072]{1,0:T(8,128)(2,1)} %copy-done.4, bf16[160,3072]{1,0:T(8,128)(2,1)} %copy-done.5, bf16[80,3072]{1,0:T(8,128)(2,1)} %copy-done.33, ...), custom_call_target="tpu_custom_call" | custom-call | flops 12079595520 | bytes 81788928 | tf_op jit(solution)/shard_map/pallas_call | solution.py:552
  143.2 0.2 collective-permute-start.20
  143.4 2.5 %collective-permute-start.21 = (f32[16,640]{1,0:T(8,128)}, f32[16,640]{1,0:T(8,128)S(1)}, u32[]{:S(2)}, u32[]{:S(2)}) collective-permute-start(f32[16,640]{1,0:T(8,128)} %get-tuple-element.130.refs_4_), channel_id=1, source_target_pairs={{0,6},{1,7},{2,0},{3,1},{4,2},{5,3},{6,4},{7,5},{8,14},{9,15},{10,... | collective-permute-start | bytes 122888 | tf_op jit(solution)/shard_map/ppermute | solution.py:39
  145.9 0.8 collective-permute-start.22
  146.7 8.9 %shard_map.151 = (f32[640,512]{1,0:T(8,128)}, f32[640,16]{1,0:T(8,128)}) custom-call(bf16[640,3072]{1,0:T(8,128)(2,1)} %bitcast.14.got_ref.refs_15_, bf16[256,7168]{1,0:T(8,128)(2,1)} %bitcast.27, bf16[256,7168]{1,0:T(8,128)(2,1)} %collective-permute-done.8.down_p.refs_4_.refs_3_, bf16[16,7168]{1,0:T(8,128)(2,1)} %bitcast.30), custom_call_target="tpu_custom_call" | custom-call | flops 16106127360 | bytes 56623104 | tf_op jit(solution)/shard_map/pallas_call | solution.py:580
  155.6 2.7 %collective-permute-done.16.before_ref.refs_11_.refs_1_ = bf16[160,4096]{1,0:T(8,128)(2,1)S(1)} collective-permute-done((bf16[160,4096]{1,0:T(8,128)(2,1)}, bf16[160,4096]{1,0:T(8,128)(2,1)S(1)}, u32[]{:S(2)}, u32[]{:S(2)}) %collective-permute-start.16) | collective-permute-done | bytes 1310752 | tf_op jit(solution)/shard_map/ppermute | solution.py:39
  158.4 0.1 shard_map.152
  158.4 0.3 collective-permute-start.18
  158.8 2.7 %collective-permute-start.19 = (bf16[80,4096]{1,0:T(8,128)(2,1)S(1)}, bf16[80,4096]{1,0:T(8,128)(2,1)S(1)}, u32[]{:S(2)}, u32[]{:S(2)}) collective-permute-start(bf16[80,4096]{1,0:T(8,128)(2,1)S(1)} %get-tuple-element.115), channel_id=1, source_target_pairs={{0,6},{1,7},{2,0},{3,1},{4,2},{5,3},{6,4},{7,5},{8,14},{9,15},{10,... | collective-permute-start | bytes 1966088 | tf_op jit(solution)/shard_map/ppermute | solution.py:39
  161.5 1.3 copy-done.28
  162.8 6.0 %shard_map.154 = (f32[16,480]{1,0:T(8,128)S(1)}, f32[32,256]{1,0:T(8,128)S(1)}, f32[32,256]{1,0:T(8,128)S(1)}) custom-call(bf16[160,4096]{1,0:T(8,128)(2,1)} %get-tuple-element.103.refs_10_.refs_0_, bf16[160,4096]{1,0:T(8,128)(2,1)S(1)} %collective-permute-done.16.before_ref.refs_11_.refs_1_, ...), custom_call_target="tpu_custom_call" | custom-call | flops 16106127360 | bytes 65011712 | tf_op jit(solution)/shard_map/pallas_call | solution.py:611
  168.9 4.2 %collective-permute-done.18.refs_13_.refs_0_ = bf16[80,4096]{1,0:T(8,128)(2,1)S(1)} collective-permute-done((bf16[80,4096]{1,0:T(8,128)(2,1)S(1)}, bf16[80,4096]{1,0:T(8,128)(2,1)S(1)}, u32[]{:S(2)}, u32[]{:S(2)}) %collective-permute-start.18) | collective-permute-done | bytes 655392 | tf_op jit(solution)/shard_map/ppermute | solution.py:39
  173.1 4.1 %shard_map.155 = (f32[16,640]{1,0:T(8,128)S(1)}, f32[32,256]{1,0:T(8,128)S(1)}, f32[32,256]{1,0:T(8,128)S(1)}) custom-call(bf16[80,4096]{1,0:T(8,128)(2,1)S(1)} %collective-permute-done.18.refs_13_.refs_0_, bf16[80,4096]{1,0:T(8,128)(2,1)S(1)} %collective-permute-done.19.refs_14_.refs_1_, bf16[256,7168]{1,0:T(8,128)(2,1)S(1)} %bitcast.29, ...), custom_call_target="tpu_custom_call" | custom-call | flops 5368709120 | bytes 44040192 | tf_op jit(solution)/shard_map/pallas_call | solution.py:611
  177.3 0.4 collective-permute-start.23
  177.7 2.3 %collective-permute-start.24 = (f32[16,640]{1,0:T(8,128)S(1)}, f32[16,640]{1,0:T(8,128)S(1)}, u32[]{:S(2)}, u32[]{:S(2)}) collective-permute-start(f32[16,640]{1,0:T(8,128)S(1)} %get-tuple-element.129.refs_0_), channel_id=1, source_target_pairs={{0,6},{1,7},{2,0},{3,1},{4,2},{5,3},{6,4},{7,5},{8,14},{9,15},{10,... | collective-permute-start | bytes 122888 | tf_op jit(solution)/shard_map/ppermute | solution.py:39
  180.0 0.1 collective-permute-start.25
  180.1 2.4 %shard_map.153 = (bf16[640,1792]{1,0:T(8,128)(2,1)S(1)}, bf16[640,1792]{1,0:T(8,128)(2,1)S(1)}) custom-call(s32[1]{0:T(128)} %bitcast.me_ref, bf16[160,4096]{1,0:T(8,128)(2,1)} %shard_map.143.refs_0_, bf16[160,4096]{1,0:T(8,128)(2,1)} %copy-done, bf16[160,4096]{1,0:T(8,128)(2,1)} %copy-done.1, bf16[80,4096]{1,0:T(8,128)(2,1)} %collective-permute-done.10.refs_3_, ...), custom_call_target="tpu_custom_call" | custom-call | bytes 73400320 | tf_op jit(solution)/shard_map/pallas_call | solution.py:637
  182.6 1.8 collective-permute-done.25.refs_3_
  184.4 1.2 shard_map.156
  185.6 5.9 %collective-permute-start.26 = (f32[2,16,896]{2,1,0:T(8,128)S(1)}, f32[2,16,896]{2,1,0:T(8,128)S(1)}, u32[]{:S(2)}, u32[]{:S(2)}) collective-permute-start(f32[2,16,896]{2,1,0:T(8,128)S(1)} %get-tuple-element.135), channel_id=1, source_target_pairs={{0,1},{1,0},{2,3},{3,2},{4,5},{5,4},{6,7},{7,6},{8,9},{9,8},{10,11... | collective-permute-start | bytes 344072 | tf_op jit(solution)/shard_map/ppermute | solution.py:44
  191.5 0.1 collective-permute-start.27
  191.6 1.1 collective-permute-done.27.more_ref
  192.7 0.7 shard_map.157
  (90 shorter events, 0.2 us)
Async XLA Ops:
  0.6 8.2 %copy-start.22 = (bf16[128,7168]{1,0:T(8,128)(2,1)S(1)}, bf16[128,7168]{1,0:T(8,128)(2,1)}, u32[]{:S(2)}) copy-start(bf16[128,7168]{1,0:T(8,128)(2,1)} %refs_0_.3) | copy-start | bytes 5505028
  2.1 6.8 %copy-start.20 = (s32[1,128]{1,0:T(1,128)S(1)}, s32[1,128]{1,0:T(1,128)}, u32[]{:S(2)}) copy-start(s32[1,128]{1,0:T(1,128)} %copy-done.19) | copy-start | bytes 1540
  5.1 21.7 %collective-permute-start = (bf16[128,3200]{1,0:T(8,128)(2,1)}, bf16[128,3200]{1,0:T(8,128)(2,1)S(1)}, u32[]{:S(2)}, u32[]{:S(2)}) collective-permute-start(bf16[128,3200]{1,0:T(8,128)(2,1)} %shard_map.140.refs_0_.refs_5_), channel_id=1, source_target_pairs={{0,2},{1,3},{2,4},{3,5},{4,6},{5,7},{6,0},{7,1},{8,10},{9,11},{10,... | collective-permute-start | bytes 2457608 | tf_op jit(solution)/shard_map/ppermute | solution.py:39
  7.3 19.5 %collective-permute-start.1 = (bf16[128,3200]{1,0:T(8,128)(2,1)}, bf16[128,3200]{1,0:T(8,128)(2,1)S(1)}, u32[]{:S(2)}, u32[]{:S(2)}) collective-permute-start(bf16[128,3200]{1,0:T(8,128)(2,1)} %shard_map.140.refs_0_.refs_5_), channel_id=1, source_target_pairs={{0,6},{1,7},{2,0},{3,1},{4,2},{5,3},{6,4},{7,5},{8,14},{9,15},{10,... | collective-permute-start | bytes 2457608 | tf_op jit(solution)/shard_map/ppermute | solution.py:39
  10.9 25.5 %all-to-all-start = ((bf16[16,40,1024]{2,1,0:T(8,128)(2,1)}), bf16[16,40,1024]{2,1,0:T(8,128)(2,1)S(1)}, u32[]{:S(2)}, u32[]{:S(2)}) async-start(bf16[16,40,1024]{2,1,0:T(8,128)(2,1)} %bitcast.2), calls=%async_computation | async-start | bytes 2621440 | tf_op jit(solution)/shard_map/all_to_all | solution.py:482
  18.5 63.2 %collective-permute-start.8 = (bf16[256,7168]{1,0:T(8,128)(2,1)}, bf16[256,7168]{1,0:T(8,128)(2,1)}, u32[]{:S(2)}, u32[]{:S(2)}) collective-permute-start(bf16[256,7168]{1,0:T(8,128)(2,1)} %bitcast.26), channel_id=1, source_target_pairs={{0,1},{1,0},{2,3},{3,2},{4,5},{5,4},{6,7},{7,6},{8,9},{9,8},{10,11... | collective-permute-start | bytes 11010056 | tf_op jit(solution)/shard_map/ppermute | solution.py:44
  20.0 61.8 %collective-permute-start.6 = (bf16[7168,256]{1,0:T(8,128)(2,1)}, bf16[7168,256]{1,0:T(8,128)(2,1)}, u32[]{:S(2)}, u32[]{:S(2)}) collective-permute-start(bf16[7168,256]{1,0:T(8,128)(2,1)} %bitcast.37), channel_id=1, source_target_pairs={{0,1},{1,0},{2,3},{3,2},{4,5},{5,4},{6,7},{7,6},{8,9},{9,8},{10,11... | collective-permute-start | bytes 11010056 | tf_op jit(solution)/shard_map/ppermute | solution.py:44
  20.1 10.3 %copy-start.23 = (bf16[128,7168]{1,0:T(8,128)(2,1)S(1)}, bf16[128,7168]{1,0:T(8,128)(2,1)}, u32[]{:S(2)}) copy-start(bf16[128,7168]{1,0:T(8,128)(2,1)} %refs_0_.3) | copy-start | bytes 5505028
  20.1 61.7 %collective-permute-start.7 = (bf16[7168,256]{1,0:T(8,128)(2,1)}, bf16[7168,256]{1,0:T(8,128)(2,1)}, u32[]{:S(2)}, u32[]{:S(2)}) collective-permute-start(bf16[7168,256]{1,0:T(8,128)(2,1)} %bitcast.40), channel_id=1, source_target_pairs={{0,1},{1,0},{2,3},{3,2},{4,5},{5,4},{6,7},{7,6},{8,9},{9,8},{10,11... | collective-permute-start | bytes 11010056 | tf_op jit(solution)/shard_map/ppermute | solution.py:44
  26.8 6.4 %copy-start.8 = (bf16[128,3200]{1,0:T(8,128)(2,1)}, bf16[128,3200]{1,0:T(8,128)(2,1)S(1)}, u32[]{:S(2)}) copy-start(bf16[128,3200]{1,0:T(8,128)(2,1)S(1)} %collective-permute-done.before_ref.refs_1_.refs_6_) | copy-start | bytes 2457604
  26.8 6.4 %copy-start.9 = (bf16[128,3200]{1,0:T(8,128)(2,1)}, bf16[128,3200]{1,0:T(8,128)(2,1)S(1)}, u32[]{:S(2)}) copy-start(bf16[128,3200]{1,0:T(8,128)(2,1)S(1)} %collective-permute-done.1.after_ref.refs_2_.refs_7_) | copy-start | bytes 2457604
  27.7 11.1 %collective-permute-start.2 = (bf16[64,3200]{1,0:T(8,128)(2,1)}, bf16[64,3200]{1,0:T(8,128)(2,1)}, u32[]{:S(2)}, u32[]{:S(2)}) collective-permute-start(bf16[64,3200]{1,0:T(8,128)(2,1)} %get-tuple-element.77), channel_id=1, source_target_pairs={{0,2},{1,3},{2,4},{3,5},{4,6},{5,7},{6,0},{7,1},{8,10},{9,11},{10,... | collective-permute-start | bytes 1228808 | tf_op jit(solution)/shard_map/ppermute | solution.py:39
  28.5 10.3 %collective-permute-start.3 = (bf16[64,3200]{1,0:T(8,128)(2,1)S(1)}, bf16[64,3200]{1,0:T(8,128)(2,1)}, u32[]{:S(2)}, u32[]{:S(2)}) collective-permute-start(bf16[64,3200]{1,0:T(8,128)(2,1)S(1)} %get-tuple-element.78), channel_id=1, source_target_pairs={{0,6},{1,7},{2,0},{3,1},{4,2},{5,3},{6,4},{7,5},{8,14},{9,15},{10,... | collective-permute-start | bytes 1228808 | tf_op jit(solution)/shard_map/ppermute | solution.py:39
  30.4 1.2 copy-start.7
  33.2 1.4 copy-start.6
  38.8 28.0 %collective-permute-start.4 = (bf16[160,4096]{1,0:T(8,128)(2,1)}, bf16[160,4096]{1,0:T(8,128)(2,1)S(1)}, u32[]{:S(2)}, u32[]{:S(2)}) collective-permute-start(bf16[160,4096]{1,0:T(8,128)(2,1)} %shard_map.143.refs_0_), channel_id=1, source_target_pairs={{0,2},{1,3},{2,4},{3,5},{4,6},{5,7},{6,0},{7,1},{8,10},{9,11},{10,... | collective-permute-start | bytes 3932168 | tf_op jit(solution)/shard_map/ppermute | solution.py:39
  38.8 32.6 %collective-permute-start.5 = (bf16[160,4096]{1,0:T(8,128)(2,1)}, bf16[160,4096]{1,0:T(8,128)(2,1)S(1)}, u32[]{:S(2)}, u32[]{:S(2)}) collective-permute-start(bf16[160,4096]{1,0:T(8,128)(2,1)} %shard_map.143.refs_0_), channel_id=1, source_target_pairs={{0,6},{1,7},{2,0},{3,1},{4,2},{5,3},{6,4},{7,5},{8,14},{9,15},{10,... | collective-permute-start | bytes 3932168 | tf_op jit(solution)/shard_map/ppermute | solution.py:39
  41.5 7.6 %copy-start.13 = (bf16[1,16,256]{2,1,0:T(8,128)(2,1)S(1)}, bf16[1,16,256]{2,1,0:T(8,128)(2,1)}, u32[]{:S(2)}) copy-start(bf16[1,16,256]{2,1,0:T(8,128)(2,1)} %param.19) | copy-start | bytes 24580
  41.5 7.6 %copy-start.15 = (bf16[1,16,256]{2,1,0:T(8,128)(2,1)S(1)}, bf16[1,16,256]{2,1,0:T(8,128)(2,1)}, u32[]{:S(2)}) copy-start(bf16[1,16,256]{2,1,0:T(8,128)(2,1)} %param.20) | copy-start | bytes 24580
  41.5 40.2 %all-to-all-start.1 = ((bf16[16,40,1792]{2,1,0:T(8,128)(2,1)}), bf16[16,40,1792]{2,1,0:T(8,128)(2,1)}, u32[]{:S(2)}, u32[]{:S(2)}) async-start(bf16[16,40,1792]{2,1,0:T(8,128)(2,1)} %bitcast.16), calls=%async_computation.1 | async-start | bytes 4587520 | tf_op jit(solution)/shard_map/all_to_all | solution.py:482
  66.9 14.8 %copy-start = (bf16[160,4096]{1,0:T(8,128)(2,1)}, bf16[160,4096]{1,0:T(8,128)(2,1)S(1)}, u32[]{:S(2)}) copy-start(bf16[160,4096]{1,0:T(8,128)(2,1)S(1)} %collective-permute-done.4.before_ref.refs_1_) | copy-start | bytes 3932164
  66.9 5.6 %collective-permute-start.9 = (bf16[32,256]{1,0:T(8,128)(2,1)S(1)}, bf16[32,256]{1,0:T(8,128)(2,1)S(1)}, u32[]{:S(2)}, u32[]{:S(2)}) collective-permute-start(bf16[32,256]{1,0:T(8,128)(2,1)S(1)} %pad_maximum_fusion), channel_id=1, source_target_pairs={{0,1},{1,0},{2,3},{3,2},{4,5},{5,4},{6,7},{7,6},{8,9},{9,8},{10,11... | collective-permute-start | bytes 49160 | tf_op jit(solution)/shard_map/ppermute | solution.py:44
  71.4 10.2 %copy-start.1 = (bf16[160,4096]{1,0:T(8,128)(2,1)}, bf16[160,4096]{1,0:T(8,128)(2,1)S(1)}, u32[]{:S(2)}) copy-start(bf16[160,4096]{1,0:T(8,128)(2,1)S(1)} %collective-permute-done.5.after_ref.refs_2_) | copy-start | bytes 3932164
  72.5 21.5 %collective-permute-start.10 = (bf16[80,4096]{1,0:T(8,128)(2,1)}, bf16[80,4096]{1,0:T(8,128)(2,1)}, u32[]{:S(2)}, u32[]{:S(2)}) collective-permute-start(bf16[80,4096]{1,0:T(8,128)(2,1)} %get-tuple-element.86), channel_id=1, source_target_pairs={{0,2},{1,3},{2,4},{3,5},{4,6},{5,7},{6,0},{7,1},{8,10},{9,11},{10,... | collective-permute-start | bytes 1966088 | tf_op jit(solution)/shard_map/ppermute | solution.py:39
  72.5 21.5 %collective-permute-start.11 = (bf16[80,4096]{1,0:T(8,128)(2,1)S(1)}, bf16[80,4096]{1,0:T(8,128)(2,1)}, u32[]{:S(2)}, u32[]{:S(2)}) collective-permute-start(bf16[80,4096]{1,0:T(8,128)(2,1)S(1)} %get-tuple-element.87), channel_id=1, source_target_pairs={{0,6},{1,7},{2,0},{3,1},{4,2},{5,3},{6,4},{7,5},{8,14},{9,15},{10,... | collective-permute-start | bytes 1966088 | tf_op jit(solution)/shard_map/ppermute | solution.py:39
  81.7 65.0 %all-to-all-start.2 = ((bf16[16,40,3072]{2,1,0:T(8,128)(2,1)}), bf16[16,40,3072]{2,1,0:T(8,128)(2,1)}, u32[]{:S(2)}, u32[]{:S(2)}) async-start(bf16[16,40,3072]{2,1,0:T(8,128)(2,1)} %bitcast.34), calls=%async_computation.2 | async-start | bytes 7864320 | tf_op jit(solution)/shard_map/all_to_all | solution.py:482
  94.0 23.9 %collective-permute-start.12 = (bf16[160,3072]{1,0:T(8,128)(2,1)}, bf16[160,3072]{1,0:T(8,128)(2,1)S(1)}, u32[]{:S(2)}, u32[]{:S(2)}) collective-permute-start(bf16[160,3072]{1,0:T(8,128)(2,1)} %get-tuple-element.90.refs_0_.refs_5_), channel_id=1, source_target_pairs={{0,2},{1,3},{2,4},{3,5},{4,6},{5,7},{6,0},{7,1},{8,10},{9,11},{10,... | collective-permute-start | bytes 2949128 | tf_op jit(solution)/shard_map/ppermute | solution.py:39
  94.0 23.9 %collective-permute-start.13 = (bf16[160,3072]{1,0:T(8,128)(2,1)}, bf16[160,3072]{1,0:T(8,128)(2,1)S(1)}, u32[]{:S(2)}, u32[]{:S(2)}) collective-permute-start(bf16[160,3072]{1,0:T(8,128)(2,1)} %get-tuple-element.90.refs_0_.refs_5_), channel_id=1, source_target_pairs={{0,6},{1,7},{2,0},{3,1},{4,2},{5,3},{6,4},{7,5},{8,14},{9,15},{10,... | collective-permute-start | bytes 2949128 | tf_op jit(solution)/shard_map/ppermute | solution.py:39
  117.9 13.3 %copy-start.4 = (bf16[160,3072]{1,0:T(8,128)(2,1)}, bf16[160,3072]{1,0:T(8,128)(2,1)S(1)}, u32[]{:S(2)}) copy-start(bf16[160,3072]{1,0:T(8,128)(2,1)S(1)} %collective-permute-done.12.before_ref.refs_1_.refs_6_) | copy-start | bytes 2949124
  117.9 13.3 %copy-start.5 = (bf16[160,3072]{1,0:T(8,128)(2,1)}, bf16[160,3072]{1,0:T(8,128)(2,1)S(1)}, u32[]{:S(2)}) copy-start(bf16[160,3072]{1,0:T(8,128)(2,1)S(1)} %collective-permute-done.13.after_ref.refs_2_.refs_7_) | copy-start | bytes 2949124
  118.0 12.4 %collective-permute-start.14 = (bf16[80,3072]{1,0:T(8,128)(2,1)S(1)}, bf16[80,3072]{1,0:T(8,128)(2,1)S(1)}, u32[]{:S(2)}, u32[]{:S(2)}) collective-permute-start(bf16[80,3072]{1,0:T(8,128)(2,1)S(1)} %get-tuple-element.101), channel_id=1, source_target_pairs={{0,2},{1,3},{2,4},{3,5},{4,6},{5,7},{6,0},{7,1},{8,10},{9,11},{10,... | collective-permute-start | bytes 1474568 | tf_op jit(solution)/shard_map/ppermute | solution.py:39
  118.0 12.3 %collective-permute-start.15 = (bf16[80,3072]{1,0:T(8,128)(2,1)S(1)}, bf16[80,3072]{1,0:T(8,128)(2,1)S(1)}, u32[]{:S(2)}, u32[]{:S(2)}) collective-permute-start(bf16[80,3072]{1,0:T(8,128)(2,1)S(1)} %get-tuple-element.102), channel_id=1, source_target_pairs={{0,6},{1,7},{2,0},{3,1},{4,2},{5,3},{6,4},{7,5},{8,14},{9,15},{10,... | collective-permute-start | bytes 1474568 | tf_op jit(solution)/shard_map/ppermute | solution.py:39
  121.3 37.0 %collective-permute-start.16 = (bf16[160,4096]{1,0:T(8,128)(2,1)}, bf16[160,4096]{1,0:T(8,128)(2,1)S(1)}, u32[]{:S(2)}, u32[]{:S(2)}) collective-permute-start(bf16[160,4096]{1,0:T(8,128)(2,1)} %get-tuple-element.103.refs_10_.refs_0_), channel_id=1, source_target_pairs={{0,2},{1,3},{2,4},{3,5},{4,6},{5,7},{6,0},{7,1},{8,10},{9,11},{10,... | collective-permute-start | bytes 3932168 | tf_op jit(solution)/shard_map/ppermute | solution.py:39
  121.3 37.0 %collective-permute-start.17 = (bf16[160,4096]{1,0:T(8,128)(2,1)}, bf16[160,4096]{1,0:T(8,128)(2,1)S(1)}, u32[]{:S(2)}, u32[]{:S(2)}) collective-permute-start(bf16[160,4096]{1,0:T(8,128)(2,1)} %get-tuple-element.103.refs_10_.refs_0_), channel_id=1, source_target_pairs={{0,6},{1,7},{2,0},{3,1},{4,2},{5,3},{6,4},{7,5},{8,14},{9,15},{10,... | collective-permute-start | bytes 3932168 | tf_op jit(solution)/shard_map/ppermute | solution.py:39
  130.4 1.0 copy-start.33
  130.4 0.8 copy-start.34
  143.2 25.7 %collective-permute-start.20 = (f32[16,640]{1,0:T(8,128)}, f32[16,640]{1,0:T(8,128)S(1)}, u32[]{:S(2)}, u32[]{:S(2)}) collective-permute-start(f32[16,640]{1,0:T(8,128)} %get-tuple-element.130.refs_4_), channel_id=1, source_target_pairs={{0,2},{1,3},{2,4},{3,5},{4,6},{5,7},{6,0},{7,1},{8,10},{9,11},{10,... | collective-permute-start | bytes 122888 | tf_op jit(solution)/shard_map/ppermute | solution.py:39
  143.4 25.5 %collective-permute-start.21 = (f32[16,640]{1,0:T(8,128)}, f32[16,640]{1,0:T(8,128)S(1)}, u32[]{:S(2)}, u32[]{:S(2)}) collective-permute-start(f32[16,640]{1,0:T(8,128)} %get-tuple-element.130.refs_4_), channel_id=1, source_target_pairs={{0,6},{1,7},{2,0},{3,1},{4,2},{5,3},{6,4},{7,5},{8,14},{9,15},{10,... | collective-permute-start | bytes 122888 | tf_op jit(solution)/shard_map/ppermute | solution.py:39
  145.9 23.0 %collective-permute-start.22 = (f32[16,640]{1,0:T(8,128)}, f32[16,640]{1,0:T(8,128)S(1)}, u32[]{:S(2)}, u32[]{:S(2)}) collective-permute-start(f32[16,640]{1,0:T(8,128)} %get-tuple-element.130.refs_4_), channel_id=1, source_target_pairs={{0,4},{1,5},{2,6},{3,7},{4,0},{5,1},{6,2},{7,3},{8,12},{9,13},{10,... | collective-permute-start | bytes 122888 | tf_op jit(solution)/shard_map/ppermute | solution.py:39
  146.7 14.7 %copy-start.32 = (bf16[640,16]{1,0:T(8,128)(2,1)S(1)}, bf16[640,16]{1,0:T(8,128)(2,1)}, u32[]{:S(2)}) copy-start(bf16[640,16]{1,0:T(8,128)(2,1)} %get-tuple-element.125.refs_10_.refs_9_) | copy-start | bytes 61444
  155.6 5.9 %copy-start.14 = (bf16[1,16,256]{2,1,0:T(8,128)(2,1)S(1)}, bf16[1,16,256]{2,1,0:T(8,128)(2,1)}, u32[]{:S(2)}) copy-start(bf16[1,16,256]{2,1,0:T(8,128)(2,1)} %param.19) | copy-start | bytes 24580
  155.6 5.9 %copy-start.16 = (bf16[1,16,256]{2,1,0:T(8,128)(2,1)S(1)}, bf16[1,16,256]{2,1,0:T(8,128)(2,1)}, u32[]{:S(2)}) copy-start(bf16[1,16,256]{2,1,0:T(8,128)(2,1)} %param.20) | copy-start | bytes 24580
  155.6 5.9 %copy-start.17 = (bf16[16,256]{1,0:T(8,128)(2,1)S(1)}, bf16[16,256]{1,0:T(8,128)(2,1)}, u32[]{:S(2)}) copy-start(bf16[16,256]{1,0:T(8,128)(2,1)} %get-tuple-element.138.refs_16_.refs_14_.refs_13_) | copy-start | bytes 24580
  155.6 5.9 %copy-start.18 = (bf16[16,256]{1,0:T(8,128)(2,1)S(1)}, bf16[16,256]{1,0:T(8,128)(2,1)}, u32[]{:S(2)}) copy-start(bf16[16,256]{1,0:T(8,128)(2,1)} %get-tuple-element.139.refs_14_.refs_12_.refs_11_) | copy-start | bytes 24580
  155.6 5.9 %copy-start.24 = (bf16[1,16,7168]{2,1,0:T(8,128)(2,1)S(1)}, bf16[1,16,7168]{2,1,0:T(8,128)(2,1)}, u32[]{:S(2)}) copy-start(bf16[1,16,7168]{2,1,0:T(8,128)(2,1)} %param.21) | copy-start | bytes 688132
  155.6 5.9 %copy-start.26 = (f32[640,512]{1,0:T(8,128)S(1)}, f32[640,512]{1,0:T(8,128)}, u32[]{:S(2)}) copy-start(f32[640,512]{1,0:T(8,128)} %get-tuple-element.123.refs_8_.refs_7_) | copy-start | bytes 3932164
  155.6 5.9 %copy-start.30 = (bf16[640,512]{1,0:T(8,128)(2,1)S(1)}, bf16[640,512]{1,0:T(8,128)(2,1)}, u32[]{:S(2)}) copy-start(bf16[640,512]{1,0:T(8,128)(2,1)} %get-tuple-element.124.refs_9_.refs_8_) | copy-start | bytes 1966084
  155.6 5.9 %copy-start.31 = (f32[640,16]{1,0:T(8,128)S(1)}, f32[640,16]{1,0:T(8,128)}, u32[]{:S(2)}) copy-start(f32[640,16]{1,0:T(8,128)} %get-tuple-element.122.refs_7_.refs_6_) | copy-start | bytes 122884
  158.4 10.5 %copy-start.2 = (bf16[160,4096]{1,0:T(8,128)(2,1)}, bf16[160,4096]{1,0:T(8,128)(2,1)S(1)}, u32[]{:S(2)}) copy-start(bf16[160,4096]{1,0:T(8,128)(2,1)S(1)} %collective-permute-done.16.before_ref.refs_11_.refs_1_) | copy-start | bytes 3932164
  158.4 10.5 %copy-start.3 = (bf16[160,4096]{1,0:T(8,128)(2,1)}, bf16[160,4096]{1,0:T(8,128)(2,1)S(1)}, u32[]{:S(2)}) copy-start(bf16[160,4096]{1,0:T(8,128)(2,1)S(1)} %collective-permute-done.17.after_ref.refs_12_.refs_2_) | copy-start | bytes 3932164
  158.4 14.7 %collective-permute-start.18 = (bf16[80,4096]{1,0:T(8,128)(2,1)S(1)}, bf16[80,4096]{1,0:T(8,128)(2,1)S(1)}, u32[]{:S(2)}, u32[]{:S(2)}) collective-permute-start(bf16[80,4096]{1,0:T(8,128)(2,1)S(1)} %get-tuple-element.114), channel_id=1, source_target_pairs={{0,2},{1,3},{2,4},{3,5},{4,6},{5,7},{6,0},{7,1},{8,10},{9,11},{10,... | collective-permute-start | bytes 1966088 | tf_op jit(solution)/shard_map/ppermute | solution.py:39
  158.8 14.3 %collective-permute-start.19 = (bf16[80,4096]{1,0:T(8,128)(2,1)S(1)}, bf16[80,4096]{1,0:T(8,128)(2,1)S(1)}, u32[]{:S(2)}, u32[]{:S(2)}) collective-permute-start(bf16[80,4096]{1,0:T(8,128)(2,1)S(1)} %get-tuple-element.115), channel_id=1, source_target_pairs={{0,6},{1,7},{2,0},{3,1},{4,2},{5,3},{6,4},{7,5},{8,14},{9,15},{10,... | collective-permute-start | bytes 1966088 | tf_op jit(solution)/shard_map/ppermute | solution.py:39
  161.5 1.3 copy-start.28
  162.8 10.3 %copy-start.21 = (bf16[1,256,7168]{2,1,0:T(8,128)(2,1)S(1)}, bf16[1,256,7168]{2,1,0:T(8,128)(2,1)}, u32[]{:S(2)}) copy-start(bf16[1,256,7168]{2,1,0:T(8,128)(2,1)} %param.17) | copy-start | bytes 11010052
  162.8 10.3 %copy-start.27 = (f32[640,512]{1,0:T(8,128)S(1)}, f32[640,512]{1,0:T(8,128)}, u32[]{:S(2)}) copy-start(f32[640,512]{1,0:T(8,128)} %get-tuple-element.123.refs_8_.refs_7_) | copy-start | bytes 3932164
  162.8 10.3 %copy-start.29 = (f32[640,512]{1,0:T(8,128)S(1)}, f32[640,512]{1,0:T(8,128)}, u32[]{:S(2)}) copy-start(f32[640,512]{1,0:T(8,128)} %get-tuple-element.121.refs_6_.refs_5_) | copy-start | bytes 3932164
  173.1 4.2 %copy-start.10 = (bf16[80,4096]{1,0:T(8,128)(2,1)}, bf16[80,4096]{1,0:T(8,128)(2,1)S(1)}, u32[]{:S(2)}) copy-start(bf16[80,4096]{1,0:T(8,128)(2,1)S(1)} %collective-permute-done.18.refs_13_.refs_0_) | copy-start | bytes 1966084
  173.1 4.2 %copy-start.11 = (bf16[80,4096]{1,0:T(8,128)(2,1)}, bf16[80,4096]{1,0:T(8,128)(2,1)S(1)}, u32[]{:S(2)}) copy-start(bf16[80,4096]{1,0:T(8,128)(2,1)S(1)} %collective-permute-done.19.refs_14_.refs_1_) | copy-start | bytes 1966084
  177.3 5.3 %collective-permute-start.23 = (f32[16,640]{1,0:T(8,128)S(1)}, f32[16,640]{1,0:T(8,128)S(1)}, u32[]{:S(2)}, u32[]{:S(2)}) collective-permute-start(f32[16,640]{1,0:T(8,128)S(1)} %get-tuple-element.129.refs_0_), channel_id=1, source_target_pairs={{0,2},{1,3},{2,4},{3,5},{4,6},{5,7},{6,0},{7,1},{8,10},{9,11},{10,... | collective-permute-start | bytes 122888 | tf_op jit(solution)/shard_map/ppermute | solution.py:39
  177.7 4.9 %collective-permute-start.24 = (f32[16,640]{1,0:T(8,128)S(1)}, f32[16,640]{1,0:T(8,128)S(1)}, u32[]{:S(2)}, u32[]{:S(2)}) collective-permute-start(f32[16,640]{1,0:T(8,128)S(1)} %get-tuple-element.129.refs_0_), channel_id=1, source_target_pairs={{0,6},{1,7},{2,0},{3,1},{4,2},{5,3},{6,4},{7,5},{8,14},{9,15},{10,... | collective-permute-start | bytes 122888 | tf_op jit(solution)/shard_map/ppermute | solution.py:39
  180.0 4.4 %collective-permute-start.25 = (f32[16,640]{1,0:T(8,128)S(1)}, f32[16,640]{1,0:T(8,128)S(1)}, u32[]{:S(2)}, u32[]{:S(2)}) collective-permute-start(f32[16,640]{1,0:T(8,128)S(1)} %get-tuple-element.129.refs_0_), channel_id=1, source_target_pairs={{0,4},{1,5},{2,6},{3,7},{4,0},{5,1},{6,2},{7,3},{8,12},{9,13},{10,... | collective-permute-start | bytes 122888 | tf_op jit(solution)/shard_map/ppermute | solution.py:39
  180.1 4.3 %copy-start.12 = (f32[16,640]{1,0:T(8,128)S(1)}, f32[16,640]{1,0:T(8,128)}, u32[]{:S(2)}) copy-start(f32[16,640]{1,0:T(8,128)} %get-tuple-element.130.refs_4_) | copy-start | bytes 122884
  185.6 7.2 %collective-permute-start.26 = (f32[2,16,896]{2,1,0:T(8,128)S(1)}, f32[2,16,896]{2,1,0:T(8,128)S(1)}, u32[]{:S(2)}, u32[]{:S(2)}) collective-permute-start(f32[2,16,896]{2,1,0:T(8,128)S(1)} %get-tuple-element.135), channel_id=1, source_target_pairs={{0,1},{1,0},{2,3},{3,2},{4,5},{5,4},{6,7},{7,6},{8,9},{9,8},{10,11... | collective-permute-start | bytes 344072 | tf_op jit(solution)/shard_map/ppermute | solution.py:44
  191.5 1.2 collective-permute-start.27
  (2 other events, 1.3 us)
